TPU v7x, 32 devices: a whole 2x2x4 slice. The times are simulated.
32 devices in a mesh: groups: 2 (over y), ang: 4 (over z), tm: 4 (over x, core).
Axes of the slice: x: 2, y: 2, z: 4, core: 2. Of those that a mesh axis runs over, the one named last changes fastest.
Arguments:
- field: bfloat16 [4, 256, 512, 512], P('groups', 'ang', None, 'tm'), parts along dimension 0, may hold values from -6 to 6
- radial_tables: bfloat16 [16, 8, 64, 64], replicated, may hold values from -0.75 to 0.75
- weights: float32 [512], replicated, may hold values from 0.3 to 3
- order_map: int32 [256], P('ang'), may hold values from 0 to 15
- curvature: float32 [256, 512], P('ang'), may hold values from 0.05 to 0.5
- walk_off: float32 [256, 512], P('ang'), may hold values from -0.5 to 0.5
Outputs:
- stepped: bfloat16 [4, 256, 512, 512], P('groups', 'ang', None, 'tm'), parts along dimension 0
There are 2 independent parts, one for each index of `groups`. A program takes and returns all parts, laid end to end along the dimension named above; an argument that names none is the same for every part. Nothing has to cross between parts.
All inputs are finite; a program needn't handle non-finite values.
Results may differ from a plain program's by a relative error of at most 0.008.
Values may be sent and summed in bfloat16 or wider, within the bound.
No kernel may reach another device: no remote copies, remote signals or barrier semaphores. Data moves between devices by JAX's collectives and lax.ppermute only.
A program may use at most 448 MiB of HBM per device.

v0:
```python
import math

import jax
import jax.numpy as jnp
from jax import lax
from jax.sharding import PartitionSpec as P

ORDERS = 256


kerr_gamma = 0.00390625


def with_halo(block, sides, width):
    for axis, dim in sides:
        count = lax.axis_size(axis)
        forward = [(i, i + 1) for i in range(count - 1)]
        forward.append((count - 1, 0))
        backward = [(target, source) for source, target in forward]
        low = lax.ppermute(
            lax.slice_in_dim(block, block.shape[dim] - width, None, axis=dim), axis, forward
        )
        high = lax.ppermute(lax.slice_in_dim(block, 0, width, axis=dim), axis, backward)
        block = jnp.concatenate([low, block, high], axis=dim)
    return block


def angle_tables(count):
    index = jnp.arange(count, dtype=jnp.int32)
    phase = (index[:, None] * index[None, :] % count).astype(jnp.float32) * (2.0 * math.pi / count)
    cosine = jnp.cos(phase)
    sine = jnp.sin(phase)
    forward = jnp.concatenate(
        [jnp.concatenate([cosine, -sine], 1), jnp.concatenate([sine, cosine], 1)], 0
    )
    backward = jnp.concatenate(
        [jnp.concatenate([cosine, sine], 1), jnp.concatenate([-sine, cosine], 1)], 0
    )
    return (forward.astype(jnp.bfloat16), backward.astype(jnp.bfloat16))


def local_kerr(pieces, forward, backward):
    orders = pieces.shape[1]
    flat = pieces.reshape(2 * orders, -1)
    angular = jnp.dot(forward, flat, preferred_element_type=jnp.float32)
    power = angular[:orders] ** 2 + angular[orders:] ** 2
    kerr = jnp.concatenate(
        [-kerr_gamma * power * angular[orders:], kerr_gamma * power * angular[:orders]], 0
    )
    kerr = kerr.astype(jnp.bfloat16)
    back = jnp.dot(backward, kerr, preferred_element_type=jnp.float32) * (1.0 / orders)
    return back.astype(jnp.bfloat16).reshape(pieces.shape)


def per_device(field, radial_tables, weights, order_map, curvature, walk_off):
    local_orders = field.shape[1]
    radial = field.shape[2]
    steps_dev = field.shape[3]
    nblocks = radial_tables.shape[1]
    block = radial_tables.shape[2]
    padded = with_halo(field, (("tm", 3),), 1).astype(jnp.float32)
    middle = padded[..., 1:-1]
    right = padded[..., 2:]
    left = padded[..., :-2]
    second = right - 2.0 * middle + left
    first = 0.5 * (right - left)
    beta = curvature[:, :, None]
    delta = walk_off[:, :, None]
    real = middle[0] - beta * second[1] + delta * first[0]
    imag = middle[1] + beta * second[0] + delta * first[1]
    moved = jnp.stack([real, imag])
    moved_low = moved.astype(jnp.bfloat16).reshape(2, local_orders, nblocks, block, steps_dev)
    tables = jnp.take(radial_tables, order_map, axis=0)
    scaled = radial_tables.astype(jnp.float32) * weights.reshape(nblocks, block)[None, :, :, None]
    analysis = jnp.take(scaled.astype(jnp.bfloat16), order_map, axis=0)
    points = jnp.einsum("mbqn,cmbnt->cmbqt", tables, moved_low, preferred_element_type=jnp.float32)
    points = points.reshape(2, local_orders, radial, steps_dev).astype(jnp.bfloat16)
    forward, backward = angle_tables(ORDERS)
    back = local_kerr(
        lax.all_to_all(points, "ang", split_axis=2, concat_axis=1, tiled=True), forward, backward
    )
    returned = lax.all_to_all(back, "ang", split_axis=1, concat_axis=2, tiled=True)
    returned = returned.reshape(2, local_orders, nblocks, block, steps_dev)
    increment = jnp.einsum(
        "mbqn,cmbqt->cmbnt", analysis, returned, preferred_element_type=jnp.float32
    )
    increment = increment.reshape(2, local_orders, radial, steps_dev)
    return (moved + increment).astype(jnp.bfloat16)


def solution(mesh):
    in_specs = (P("groups", "ang", None, "tm"), P(), P(), P("ang"), P("ang", None), P("ang", None))
    out_specs = P("groups", "ang", None, "tm")
    return jax.shard_map(
        per_device, mesh=mesh, in_specs=in_specs, out_specs=out_specs, check_vma=False
    )
```

profile of v0, /device:TPU:24, one launch (start us, length us, event | category | flops | bytes accessed | tf_op | source)
XLA Modules:
  0.0 1254.5 jit_solution(11552785081753718057)
XLA Ops:
  0.0 25.5 %fusion.60 = (bf16[2,64,512,1]{3,2,1,0:T(8,128)(2,1)}, bf16[2,64,512,1]{3,2,1,0:T(8,128)(2,1)}) fusion(bf16[2,64,512,128]{3,2,1,0:T(8,128)(2,1)} %param.8), kind=kLoop, calls=%fused_computation.78 | loop fusion | bytes 524288 | tf_op jit(solution)/shard_map/slice | solution.py:21
  25.5 13.8 %copy.37 = bf16[2,64,512,1]{2,1,3,0:T(8,128)(2,1)S(1)} copy(bf16[2,64,512,1]{3,2,1,0:T(8,128)(2,1)} %get-tuple-element.16) | data formatting | bytes 262144
  39.4 13.7 %copy.38 = bf16[2,64,512,1]{2,1,3,0:T(8,128)(2,1)S(1)} copy(bf16[2,64,512,1]{3,2,1,0:T(8,128)(2,1)} %get-tuple-element.17) | data formatting | bytes 262144
  53.1 1.8 collective-permute-start.1
  54.9 0.6 copy-done.4
  55.5 5.5 gather_fusion
  61.0 11.8 copy.21
  72.8 11.5 copy.22
  84.2 39.8 %maximum_convert_fusion = f32[2,64,512,130]{3,2,1,0:T(8,128)} fusion(bf16[2,64,512,1]{3,2,1,0:T(8,128)(2,1)} %copy.22, bf16[2,64,512,128]{3,2,1,0:T(8,128)(2,1)} %param.8, bf16[2,64,512,1]{3,2,1,0:T(8,128)(2,1)} %copy.21), kind=kLoop, calls=%fused_computation.5 | loop fusion | flops 51118080 | bytes 51118080 | tf_op jit(solution)/shard_map/convert_element_type | solution.py:61
  124.1 75.0 %fusion.1 = (f32[2,64,512,128]{3,2,1,0:T(8,128)}, f32[2,64,512,128]{3,2,1,0:T(8,128)}) fusion(f32[2,64,512,130]{3,2,1,0:T(8,128)} %maximum_convert_fusion), kind=kLoop, calls=%fused_computation.4 | loop fusion | flops 41943040 | bytes 167772160 | tf_op jit(solution)/shard_map/add | solution.py:65
  199.1 59.9 %fusion.56 = (bf16[1,64,512,128]{3,2,1,0:T(8,128)(2,1)}, f32[1,64,512,128]{3,2,1,0:T(8,128)}, bf16[1,64,512,128]{3,2,1,0:T(8,128)(2,1)}, f32[1,64,512,128]{3,2,1,0:T(8,128)}) fusion(f32[2,64,512,128]{3,2,1,0:T(8,128)} %get-tuple-element.13, f32[64,512]{1,0:T(8,128)S(1)} %copy-done.2, f32[2,64,512,128]{3,2,1,0:T(8,128)} %get-tuple-element.12, ...), kind=kLoop, calls=%fused_computation.76 | loop fusion | flops 41943040 | bytes 151257088 | tf_op jit(solution)/shard_map/convert.5
  259.0 16.8 %convert_bitcast_fusion = bf16[2,64,8,64,128]{4,3,0,2,1:T(8,128)(2,1)} fusion(bf16[1,64,8,64,128]{4,3,0,2,1:T(8,128)(2,1)} %bitcast.39, bf16[1,64,8,64,128]{4,3,0,2,1:T(8,128)(2,1)} %bitcast.38, bf16[64,8,64,64]{3,2,1,0:T(8,128)(2,1)} %gather_fusion, pred[64]{0:T(512)(128)(4,1)S(1)} %compare_and_fusion), kind=kOutput, calls=%fused_computation.33 | convolution fusion | flops 1117782016 | bytes 37748800 | tf_op jit(solution)/shard_map/mbqn,cmbnt->cmbqt/dot_general | solution.py:76
  275.8 8.2 copy.23
  284.1 38.2 %copy.24 = bf16[2,64,512,128]{3,1,0,2:T(8,128)(2,1)} copy(bf16[2,64,512,128]{3,2,1,0:T(8,128)(2,1)S(1)} %bitcast.36) | data formatting | bytes 33554432 | tf_op jit(solution)/shard_map/convert_element_type | solution.py:77
  322.2 7.0 all-to-all-start
  329.2 1.0 fusion.50
  330.2 1.1 negate_convert_fusion
  331.3 359.0 %all-to-all-done = bf16[2,64,512,128]{3,1,0,2:T(8,128)(2,1)} async-done(((bf16[2,64,512,128]{3,1,0,2:T(8,128)(2,1)}), bf16[2,64,512,128]{3,1,0,2:T(8,128)(2,1)}, u32[]{:S(2)}, u32[]{:S(2)}) %all-to-all-start) | async-done | bytes 16777248 | tf_op jit(solution)/shard_map/all_to_all | solution.py:80
  690.3 18.6 %copy.25 = bf16[2,64,4,128,128]{4,3,1,2,0:T(8,128)(2,1)} copy(bf16[2,64,4,128,128]{4,1,0,3,2:T(8,128)(2,1)} %bitcast.6) | data formatting | bytes 33554432 | tf_op jit(solution)/shard_map/all_to_all | solution.py:80
  708.9 43.0 %fusion.3 = f32[512,16384]{1,0:T(8,128)} fusion(bf16[64,8,128,128]{3,2,1,0:T(8,128)(2,1)} %bitcast.34, bf16[256,256]{1,0:T(8,128)(2,1)S(1)} %get-tuple-element.19, bf16[256,256]{1,0:T(8,128)(2,1)S(1)} %fusion.50, bf16[256,256]{1,0:T(8,128)(2,1)S(1)} %get-tuple-element.18), kind=kOutput, calls=%fused_computation.10 | convolution fusion | flops 8592031744 | bytes 50724864 | tf_op jit(solution)/shard_map/dot_general | solution.py:45
  751.9 15.1 %multiply_convert_fusion.2 = (bf16[256,16384]{1,0:T(8,128)(2,1)S(1)}, bf16[256,16384]{1,0:T(8,128)(2,1)}) fusion(f32[512,16384]{1,0:T(8,128)} %fusion.3), kind=kLoop, calls=%fused_computation.31 | loop fusion | flops 37748736 | bytes 50331648 | tf_op jit(solution)/shard_map/convert
  766.9 14.7 %fusion.30 = bf16[64,8,128,128]{3,1,2,0:T(8,128)(2,1)} fusion(bf16[256,16384]{1,0:T(8,128)(2,1)} %get-tuple-element.15, bf16[256,16384]{1,0:T(8,128)(2,1)S(1)} %get-tuple-element.14, bf16[256,256]{1,0:T(8,128)(2,1)S(1)} %get-tuple-element.19, bf16[256,256]{1,0:T(8,128)(2,1)S(1)} %get-tuple-element.18, bf16[256,256]{1,0:T(8,128)(2,1)S(1)} %fusion.50), kind=kOutput, calls=%fused_computation.41 | convolution fusion | flops 8642363392 | bytes 33947648 | tf_op jit(solution)/shard_map/dot_general | solution.py:51
  781.6 9.8 copy.40
  791.4 6.5 copy.26
  798.0 9.5 all-to-all-start.1
  807.5 2.3 multiply_convert_fusion.3
  809.8 7.2 gather_fusion.1
  817.0 350.7 %all-to-all-done.1 = bf16[2,256,128,128]{3,2,0,1:T(8,128)(2,1)} async-done(((bf16[2,256,128,128]{3,2,0,1:T(8,128)(2,1)}), bf16[2,256,128,128]{3,2,0,1:T(8,128)(2,1)}, u32[]{:S(2)}, u32[]{:S(2)}) %all-to-all-start.1) | async-done | bytes 16777248 | tf_op jit(solution)/shard_map/all_to_all | solution.py:82
  1167.8 14.2 %copy.28 = bf16[2,64,4,128,128]{4,3,2,1,0:T(8,128)(2,1)} copy(bf16[2,64,4,128,128]{4,3,0,1,2:T(8,128)(2,1)} %bitcast.10) | data formatting | bytes 33554432 | tf_op jit(solution)/shard_map/all_to_all | solution.py:82
  1182.0 21.2 %fusion.19 = f32[2,64,8,64,128]{4,3,0,2,1:T(8,128)} fusion(bf16[2,64,8,64,128]{4,3,2,1,0:T(8,128)(2,1)} %bitcast.35, bf16[64,8,64,64]{3,2,1,0:T(8,128)(2,1)} %gather_fusion.1, pred[64]{0:T(512)(128)(4,1)S(1)} %compare_and_fusion), kind=kOutput, calls=%fused_computation.34 | convolution fusion | flops 1075838976 | bytes 54526016 | tf_op jit(solution)/shard_map/mbqn,cmbqt->cmbnt/dot_general | solution.py:84
  1203.2 23.5 %copy.31 = f32[2,64,8,64,128]{4,3,2,1,0:T(8,128)} copy(f32[2,64,8,64,128]{4,3,0,2,1:T(8,128)} %fusion.19) | data formatting | bytes 67108864 | tf_op jit(solution)/shard_map/mbqn,cmbqt->cmbnt/transpose | solution.py:84
  1226.7 27.4 %fusion.2 = bf16[2,64,512,128]{3,2,1,0:T(8,128)(2,1)} fusion(f32[1,64,512,128]{3,2,1,0:T(8,128)} %get-tuple-element.11, f32[1,64,512,128]{3,2,1,0:T(8,128)} %get-tuple-element.7, f32[2,64,8,64,128]{4,3,2,1,0:T(8,128)} %copy.31), kind=kLoop, calls=%fused_computation.7 | loop fusion | flops 25165824 | bytes 83886080 | tf_op jit(solution)/shard_map/convert_element_type | solution.py:88
  (20 shorter events, 0.2 us)
Async XLA Ops:
  25.5 29.4 %copy-start.6 = (s32[64]{0:T(128)S(1)}, s32[64]{0:T(128)}, u32[]{:S(2)}) copy-start(s32[64]{0:T(128)} %param.11) | copy-start | bytes 772
  25.5 30.0 %copy-start = (bf16[16,8,64,64]{3,2,1,0:T(8,128)(2,1)S(1)}, bf16[16,8,64,64]{3,2,1,0:T(8,128)(2,1)}, u32[]{:S(2)}) copy-start(bf16[16,8,64,64]{3,2,1,0:T(8,128)(2,1)} %param.9) | copy-start | bytes 3145732
  39.3 21.7 %collective-permute-start = (bf16[2,64,512,1]{2,1,3,0:T(8,128)(2,1)S(1)}, bf16[2,64,512,1]{2,1,3,0:T(8,128)(2,1)S(1)}, u32[]{:S(2)}, u32[]{:S(2)}) collective-permute-start(bf16[2,64,512,1]{2,1,3,0:T(8,128)(2,1)S(1)} %copy.37), channel_id=1, source_target_pairs={{0,1},{1,2},{2,3},{3,0},{4,5},{5,6},{6,7},{7,4},{8,9},{9,10},{10,1... | collective-permute-start | bytes 393224 | tf_op jit(solution)/shard_map/ppermute | solution.py:20
  53.1 19.7 %collective-permute-start.1 = (bf16[2,64,512,1]{2,1,3,0:T(8,128)(2,1)S(1)}, bf16[2,64,512,1]{2,1,3,0:T(8,128)(2,1)S(1)}, u32[]{:S(2)}, u32[]{:S(2)}) collective-permute-start(bf16[2,64,512,1]{2,1,3,0:T(8,128)(2,1)S(1)} %copy.38), channel_id=1, source_target_pairs={{1,0},{2,1},{3,2},{0,3},{5,4},{6,5},{7,6},{4,7},{9,8},{10,9},{11,1... | collective-permute-start | bytes 393224 | tf_op jit(solution)/shard_map/ppermute | solution.py:23
  54.9 0.6 copy-start.4
  124.1 75.0 %copy-start.2 = (f32[64,512]{1,0:T(8,128)S(1)}, f32[64,512]{1,0:T(8,128)}, u32[]{:S(2)}) copy-start(f32[64,512]{1,0:T(8,128)} %param.13) | copy-start | bytes 393220
  124.1 75.0 %copy-start.3 = (f32[64,512]{1,0:T(8,128)S(1)}, f32[64,512]{1,0:T(8,128)}, u32[]{:S(2)}) copy-start(f32[64,512]{1,0:T(8,128)} %param.12) | copy-start | bytes 393220
  322.2 368.0 %all-to-all-start = ((bf16[2,64,512,128]{3,1,0,2:T(8,128)(2,1)}), bf16[2,64,512,128]{3,1,0,2:T(8,128)(2,1)}, u32[]{:S(2)}, u32[]{:S(2)}) async-start(bf16[2,64,512,128]{3,1,0,2:T(8,128)(2,1)} %copy.24), calls=%async_computation | async-start | bytes 33554432 | tf_op jit(solution)/shard_map/all_to_all | solution.py:80
  797.9 9.5 copy-start.5
  798.0 9.5 copy-start.1
  798.0 369.8 %all-to-all-start.1 = ((bf16[2,256,128,128]{3,2,0,1:T(8,128)(2,1)}), bf16[2,256,128,128]{3,2,0,1:T(8,128)(2,1)}, u32[]{:S(2)}, u32[]{:S(2)}) async-start(bf16[2,256,128,128]{3,2,0,1:T(8,128)(2,1)} %copy.26), calls=%async_computation.1 | async-start | bytes 33554432 | tf_op jit(solution)/shard_map/all_to_all | solution.py:82
where the time goes:
time: 1270 us; the launch traced here: 1250 us
  waiting for transfers between devices  710 us (56%)
  other arithmetic  222 us (17%)
  local copies, waits for them, and re-layouts  209 us (16%)
  matrix products  95.7 us (8%)
  starting transfers between devices  18.2 us (1%)
    all_to_all x1, waiting for transfers between devices, per_device(): lax.all_to_all(points, 'ang', split_axis=2, concat_axis=1, tiled=True)  359 us
    all_to_all x1, waiting for transfers between devices, per_device(): lax.all_to_all(back, 'ang', split_axis=1, concat_axis=2, tiled=True)  351 us
    another operation x4, other arithmetic  77 us
    add x1, other arithmetic, per_device(): second = right - 2.0 * middle + left  75 us
    convert_element_type x2, local copies, waits for them, and re-layouts, per_device(): points.reshape(2, local_orders, radial, steps_dev).astype(jnp.bfloat16)  46.4 us
    dot_general x1, matrix products, local_kerr(): angular = jnp.dot(forward, flat, preferred_element_type=jnp.float32)  43 us
    convert_element_type x1, other arithmetic, per_device(): padded = with_halo(field, (('tm', 3),), 1).astype(jnp.float32)  39.8 us
    unnamed x17, local copies, waits for them, and re-layouts  37.9 us
  transfers between devices with their start and end apart: 4, of which 2 were waited for; matrix products, arithmetic and copies ran while one was open for 3% of the time, Pallas kernels for 0%

commit v1 on v0

v1 whole, which is shorter than its diff:
```python
import functools
import math

import jax
import jax.numpy as jnp
import numpy as np
from jax import lax
from jax.experimental import pallas as pl
from jax.experimental.pallas import tpu as pltpu
from jax.sharding import PartitionSpec as P

ORDERS = 256
LANES = 128
ROWS = 16

kerr_gamma = 0.00390625


def angle_matrices(count):
    index = np.arange(count, dtype=np.int32)
    phase = (index[:, None] * index[None, :] % count).astype(np.float32) * np.float32(
        2.0 * math.pi / count
    )
    cosine, sine = np.cos(phase), np.sin(phase)
    forward = np.block([[cosine, -sine], [sine, cosine]])
    backward = np.block([[cosine, sine], [-sine, cosine]])
    return forward.astype(jnp.bfloat16), backward.astype(jnp.bfloat16)


def ring(axis, shift):
    count = lax.axis_size(axis)
    return [(i, (i + shift) % count) for i in range(count)]


def lane_index(rows):
    return lax.broadcasted_iota(jnp.int32, (rows, LANES), 1)


def roll(x, shift):
    return pltpu.roll(x, shift, 1)


def params():
    return pltpu.CompilerParams(vmem_limit_bytes=40 * 1024 * 1024)


def cost(flops, size):
    return pl.CostEstimate(flops=flops, bytes_accessed=size, transcendentals=0)


def anywhere(count):
    return [pl.BlockSpec(memory_space=pl.ANY)] * count


def edges(field, first, count, block, deps=()):
    parts, orders = field.shape[:2]
    groups = orders // ROWS

    def kernel(x_ref, *refs):
        o_ref, acc = refs[-2:]
        g = pl.program_id(1)
        slot = ((lane_index(block) + 1) >> 1) & (LANES // 2 - 1)
        for c in range(parts):
            kept = acc[c]
            for i in range(ROWS):
                m = g * ROWS + i
                row = roll(x_ref[c, i].astype(jnp.float32), 2 * m)
                kept = jnp.where(slot == m, row, kept)
            acc[c] = kept

        @pl.when(g == groups - 1)
        def _():
            o_ref[...] = acc[...].astype(o_ref.dtype)

    return pl.pallas_call(
        kernel,
        out_shape=jax.ShapeDtypeStruct((parts, count * block, LANES), field.dtype),
        grid=(count, groups),
        in_specs=[pl.BlockSpec((parts, ROWS, block, LANES), lambda j, g: (0, g, j + first, 0))]
        + anywhere(len(deps)),
        out_specs=pl.BlockSpec((parts, block, LANES), lambda j, g: (0, j, 0)),
        scratch_shapes=[pltpu.VMEM((parts, block, LANES), jnp.float32)],
        compiler_params=params(),
        cost_estimate=cost(0, parts * orders * count * block * LANES * 2),
        name="edges",
    )(field, *deps)


def join_halo(low, high):
    lane = lane_index(low.shape[0])
    low, high = low.astype(jnp.float32), high.astype(jnp.float32)
    return jnp.where((lane & 1) == 0, roll(low, 1), roll(high, LANES - 1))


def columns(ref, start, block):
    base = start // LANES * LANES
    turned = jnp.transpose(ref[:, base : base + LANES])
    return turned[start - base : start - base + block]


def move(x, halo, beta, delta, m):
    lane = lane_index(beta.shape[0])
    second, first = [], []
    for c in range(2):
        ends = roll(halo[c], (LANES - 2 * m) & (LANES - 1))
        left = jnp.where(lane == 0, ends, roll(x[c], 1))
        right = jnp.where(lane == LANES - 1, ends, roll(x[c], LANES - 1))
        second.append(right - 2.0 * x[c] + left)
        first.append(0.5 * (right - left))
    real = x[0] - beta * second[1] + delta * first[0]
    imag = x[1] + beta * second[0] + delta * first[1]
    return real, imag


def synthesize(field, low, high, halo_at, tables, curvature, walk_off, order_map, me, b, count, deps):
    parts, orders, radial, steps = field.shape
    kinds, _, block, _ = tables.shape
    share = block // count
    groups = orders // ROWS

    def kernel(map_ref, me_ref, x_ref, low_ref, high_ref, tab_ref, beta_ref, delta_ref, *refs):
        outs, acc = refs[len(deps) : -1], refs[-1]
        g = pl.program_id(0)
        beta = columns(beta_ref, b * block, block)
        delta = columns(delta_ref, b * block, block)
        halo = [join_halo(low_ref[c], high_ref[c]) for c in range(parts)]
        for i in range(ROWS):
            m = g * ROWS + i
            x = [x_ref[c, i].astype(jnp.float32) for c in range(parts)]
            moved = move(x, halo, beta[:, i : i + 1], delta[:, i : i + 1], m)
            moved = jnp.concatenate(moved, 1).astype(jnp.bfloat16)
            points = jnp.dot(
                tab_ref[map_ref[m], 0], moved, preferred_element_type=jnp.float32
            )
            for c in range(parts):
                acc[c, pl.ds(i, block, stride=ROWS), :] = points[:, c * LANES : (c + 1) * LANES]
        for s in range(count):
            owner = lax.rem(me_ref[0] + s, count)
            for q in range(share):
                row = pl.multiple_of((owner * share + q) * ROWS, ROWS)
                for c in range(parts):
                    outs[s][q, c] = acc[c, pl.ds(row, ROWS), :].astype(jnp.bfloat16)

    piece = jax.ShapeDtypeStruct((share, parts, orders, LANES), jnp.bfloat16)
    size = parts * orders * block * LANES * 2
    return pl.pallas_call(
        kernel,
        out_shape=[piece] * count,
        grid_spec=pltpu.PrefetchScalarGridSpec(
            num_scalar_prefetch=2,
            grid=(groups,),
            in_specs=[
                pl.BlockSpec((parts, ROWS, block, LANES), lambda g, *_: (0, g, b, 0)),
                pl.BlockSpec((parts, block, LANES), lambda g, *_: (0, halo_at, 0)),
                pl.BlockSpec((parts, block, LANES), lambda g, *_: (0, halo_at, 0)),
                pl.BlockSpec((kinds, 1, block, block), lambda g, *_: (0, b, 0, 0)),
                pl.BlockSpec((ROWS, radial), lambda g, *_: (g, 0)),
                pl.BlockSpec((ROWS, radial), lambda g, *_: (g, 0)),
            ]
            + anywhere(len(deps)),
            out_specs=[
                pl.BlockSpec((share, parts, ROWS, LANES), lambda g, *_: (0, 0, g, 0))
            ]
            * count,
            scratch_shapes=[pltpu.VMEM((parts, block * ROWS, LANES), jnp.float32)],
        ),
        compiler_params=params(),
        cost_estimate=cost(2 * size * block, 2 * size),
        name="synthesize",
    )(order_map, me, field, low, high, tables, curvature, walk_off, *deps)


def kerr_step(pieces, forward, backward, me, deps):
    count = len(pieces)
    share, parts, orders, _ = pieces[0].shape
    every = count * orders
    width = 2

    def kernel(me_ref, f_ref, b_ref, *refs):
        ins = refs[:count]
        outs, flat, back = refs[count + len(deps) : -2], refs[-2], refs[-1]
        for s in range(count):
            source = lax.rem(me_ref[0] + count - s, count)
            for c in range(parts):
                row = pl.multiple_of(c * every + source * orders, orders)
                for q in range(width):
                    flat[pl.ds(row, orders), q * LANES : (q + 1) * LANES] = ins[s][q, c]
        angular = jnp.dot(f_ref[...], flat[...], preferred_element_type=jnp.float32)
        real, imag = angular[:every], angular[every:]
        power = kerr_gamma * (real * real + imag * imag)
        kerr = jnp.concatenate([-power * imag, power * real], 0).astype(jnp.bfloat16)
        back[...] = (
            jnp.dot(b_ref[...], kerr, preferred_element_type=jnp.float32) * (1.0 / every)
        ).astype(jnp.bfloat16)
        for s in range(count):
            owner = lax.rem(me_ref[0] + s, count)
            for c in range(parts):
                row = pl.multiple_of(c * every + owner * orders, orders)
                for q in range(width):
                    outs[s][q, c] = back[pl.ds(row, orders), q * LANES : (q + 1) * LANES]

    block = pl.BlockSpec((width, parts, orders, LANES), lambda q, *_: (q, 0, 0, 0))
    whole = pl.BlockSpec((parts * every, parts * every), lambda q, *_: (0, 0))
    lanes = share * LANES
    return pl.pallas_call(
        kernel,
        out_shape=[jax.ShapeDtypeStruct(pieces[0].shape, jnp.bfloat16)] * count,
        grid_spec=pltpu.PrefetchScalarGridSpec(
            num_scalar_prefetch=1,
            grid=(share // width,),
            in_specs=[whole, whole] + [block] * count + anywhere(len(deps)),
            out_specs=[block] * count,
            scratch_shapes=[
                pltpu.VMEM((parts * every, width * LANES), jnp.bfloat16),
                pltpu.VMEM((parts * every, width * LANES), jnp.bfloat16),
            ],
        ),
        compiler_params=params(),
        cost_estimate=cost(4 * (parts * every) ** 2 * lanes, 4 * parts * every * lanes),
        name="kerr",
    )(me, forward, backward, *pieces, *deps)


def analyze(
    pieces, field, low, high, halo_at, tables, curvature, walk_off, order_map, me, b, out, deps
):
    count = len(pieces)
    parts, orders, radial, steps = field.shape
    kinds, _, block, _ = tables.shape
    share = block // count
    groups = orders // ROWS
    held = () if out is None else (out,)

    def kernel(map_ref, me_ref, *refs):
        ins = refs[:count]
        x_ref, low_ref, high_ref, tab_ref, beta_ref, delta_ref = refs[count : count + 6]
        o_ref, acc = refs[-2:]
        g = pl.program_id(0)
        for s in range(count):
            source = lax.rem(me_ref[0] + count - s, count)
            for q in range(share):
                row = pl.multiple_of((source * share + q) * ROWS, ROWS)
                for c in range(parts):
                    acc[c, pl.ds(row, ROWS), :] = ins[s][q, c].astype(jnp.float32)
        beta = columns(beta_ref, b * block, block)
        delta = columns(delta_ref, b * block, block)
        halo = [join_halo(low_ref[c], high_ref[c]) for c in range(parts)]
        for i in range(ROWS):
            m = g * ROWS + i
            x = [x_ref[c, i].astype(jnp.float32) for c in range(parts)]
            moved = move(x, halo, beta[:, i : i + 1], delta[:, i : i + 1], m)
            back = [acc[c, pl.ds(i, block, stride=ROWS), :] for c in range(parts)]
            back = jnp.concatenate(back, 1).astype(jnp.bfloat16)
            increment = jnp.dot(
                tab_ref[map_ref[m], 0], back, preferred_element_type=jnp.float32
            )
            for c in range(parts):
                total = moved[c] + increment[:, c * LANES : (c + 1) * LANES]
                o_ref[c, i] = total.astype(jnp.bfloat16)

    size = parts * orders * block * LANES * 2
    return pl.pallas_call(
        kernel,
        out_shape=jax.ShapeDtypeStruct(field.shape, field.dtype),
        grid_spec=pltpu.PrefetchScalarGridSpec(
            num_scalar_prefetch=2,
            grid=(groups,),
            in_specs=[
                pl.BlockSpec((share, parts, ROWS, LANES), lambda g, *_: (0, 0, g, 0))
            ]
            * count
            + [
                pl.BlockSpec((parts, ROWS, block, LANES), lambda g, *_: (0, g, b, 0)),
                pl.BlockSpec((parts, block, LANES), lambda g, *_: (0, halo_at, 0)),
                pl.BlockSpec((parts, block, LANES), lambda g, *_: (0, halo_at, 0)),
                pl.BlockSpec((kinds, 1, block, block), lambda g, *_: (0, b, 0, 0)),
                pl.BlockSpec((ROWS, radial), lambda g, *_: (g, 0)),
                pl.BlockSpec((ROWS, radial), lambda g, *_: (g, 0)),
            ]
            + anywhere(len(held) + len(deps)),
            out_specs=pl.BlockSpec((parts, ROWS, block, LANES), lambda g, *_: (0, g, b, 0)),
            scratch_shapes=[pltpu.VMEM((parts, block * ROWS, LANES), jnp.float32)],
        ),
        input_output_aliases={2 + count + 6: 0} if held else {},
        compiler_params=params(),
        cost_estimate=cost(2 * size * block, 3 * size),
        name="analyze",
    )(
        order_map, me, *pieces, field, low, high, tables, curvature, walk_off, *held, *deps
    )


def exchange(pieces):
    return [pieces[0]] + [
        lax.ppermute(pieces[s], "ang", ring("ang", s)) for s in range(1, len(pieces))
    ]


def pipelined(field, radial_tables, weights, order_map, curvature, walk_off):
    count = lax.axis_size("ang")
    nblocks, block = radial_tables.shape[1:3]
    me = lax.axis_index("ang").astype(jnp.int32).reshape(1)
    forward, backward = (jnp.asarray(table) for table in angle_matrices(ORDERS))
    scaled = radial_tables.astype(jnp.float32) * weights.reshape(nblocks, block)[None, :, :, None]
    analysis = scaled.astype(jnp.bfloat16).transpose(0, 1, 3, 2)
    halos = []

    def halo(first, some, deps=()):
        ends = edges(field, first, some, block, deps)
        low = lax.ppermute(ends, "tm", ring("tm", 1))
        high = lax.ppermute(ends, "tm", ring("tm", -1))
        for j in range(some):
            halos.append((low, high, j))

    def points(b, deps=()):
        low, high, at = halos[b]
        return synthesize(
            field, low, high, at, radial_tables, curvature, walk_off, order_map, me, b, count, deps
        )

    sent, returned = {}, {}
    halo(0, 1)
    own = points(0)
    sent[0] = exchange(own)
    halo(1, nblocks - 1, own[:1])
    own = points(1, own[:1])
    sent[1] = exchange(own)
    out, last = None, own
    for b in range(nblocks):
        back = kerr_step(sent.pop(b), forward, backward, me, last[:1])
        returned[b] = exchange(back)
        last = back
        if b >= 1:
            low, high, at = halos[b - 1]
            out = analyze(
                returned.pop(b - 1), field, low, high, at, analysis, curvature, walk_off,
                order_map, me, b - 1, out, last[:1],
            )
        if b + 2 < nblocks:
            own = points(b + 2, last[:1])
            sent[b + 2] = exchange(own)
            last = own
    low, high, at = halos[nblocks - 1]
    return analyze(
        returned.pop(nblocks - 1), field, low, high, at, analysis, curvature, walk_off,
        order_map, me, nblocks - 1, out, (),
    )


def with_halo(block, axis, dim):
    low = lax.ppermute(
        lax.slice_in_dim(block, block.shape[dim] - 1, None, axis=dim), axis, ring(axis, 1)
    )
    high = lax.ppermute(lax.slice_in_dim(block, 0, 1, axis=dim), axis, ring(axis, -1))
    return jnp.concatenate([low, block, high], axis=dim)


def local_kerr(pieces, forward, backward):
    orders = pieces.shape[1]
    flat = pieces.reshape(2 * orders, -1)
    angular = jnp.dot(forward, flat, preferred_element_type=jnp.float32)
    power = angular[:orders] ** 2 + angular[orders:] ** 2
    kerr = jnp.concatenate(
        [-kerr_gamma * power * angular[orders:], kerr_gamma * power * angular[:orders]], 0
    )
    kerr = kerr.astype(jnp.bfloat16)
    back = jnp.dot(backward, kerr, preferred_element_type=jnp.float32) * (1.0 / orders)
    return back.astype(jnp.bfloat16).reshape(pieces.shape)


def whole_arrays(field, radial_tables, weights, order_map, curvature, walk_off):
    local_orders, radial, steps_dev = field.shape[1:]
    nblocks, block = radial_tables.shape[1:3]
    padded = with_halo(field, "tm", 3).astype(jnp.float32)
    middle = padded[..., 1:-1]
    right = padded[..., 2:]
    left = padded[..., :-2]
    second = right - 2.0 * middle + left
    first = 0.5 * (right - left)
    beta = curvature[:, :, None]
    delta = walk_off[:, :, None]
    real = middle[0] - beta * second[1] + delta * first[0]
    imag = middle[1] + beta * second[0] + delta * first[1]
    moved = jnp.stack([real, imag])
    moved_low = moved.astype(jnp.bfloat16).reshape(2, local_orders, nblocks, block, steps_dev)
    tables = jnp.take(radial_tables, order_map, axis=0)
    scaled = radial_tables.astype(jnp.float32) * weights.reshape(nblocks, block)[None, :, :, None]
    analysis = jnp.take(scaled.astype(jnp.bfloat16), order_map, axis=0)
    points = jnp.einsum("mbqn,cmbnt->cmbqt", tables, moved_low, preferred_element_type=jnp.float32)
    points = points.reshape(2, local_orders, radial, steps_dev).astype(jnp.bfloat16)
    forward, backward = (jnp.asarray(table) for table in angle_matrices(ORDERS))
    back = local_kerr(
        lax.all_to_all(points, "ang", split_axis=2, concat_axis=1, tiled=True), forward, backward
    )
    returned = lax.all_to_all(back, "ang", split_axis=1, concat_axis=2, tiled=True)
    returned = returned.reshape(2, local_orders, nblocks, block, steps_dev)
    increment = jnp.einsum(
        "mbqn,cmbqt->cmbnt", analysis, returned, preferred_element_type=jnp.float32
    )
    increment = increment.reshape(2, local_orders, radial, steps_dev)
    return (moved + increment).astype(jnp.bfloat16)


def per_device(field, radial_tables, weights, order_map, curvature, walk_off):
    parts, orders, radial, steps = field.shape
    nblocks, block = radial_tables.shape[1:3]
    count = lax.axis_size("ang")
    fits = (
        steps == LANES
        and orders % ROWS == 0
        and 2 * orders <= LANES
        and block % (2 * count) == 0
        and radial % LANES == 0
        and LANES % block == 0
        and nblocks >= 2
    )
    plan = pipelined if fits else whole_arrays
    return plan(field, radial_tables, weights, order_map, curvature, walk_off)


def solution(mesh):
    in_specs = (P("groups", "ang", None, "tm"), P(), P(), P("ang"), P("ang", None), P("ang", None))
    out_specs = P("groups", "ang", None, "tm")
    return jax.shard_map(
        per_device, mesh=mesh, in_specs=in_specs, out_specs=out_specs, check_vma=False
    )
```

time: 1270 us -> 753 us (0.59); the launches traced: 1250 us -> 751 us
  waiting for transfers between devices: 710 us -> 341 us
  other arithmetic: 222 us -> 2.17 us
  Pallas kernels: 0 us -> 200 us
  local copies, waits for them, and re-layouts: 209 us -> 12.7 us
  starting transfers between devices: 18.2 us -> 194 us
  matrix products: 95.7 us -> 0 us
    all_to_all x2 -> x0, waiting for transfers between devices: 710 us -> none  [the longest x1 359 us: per_device(): lax.all_to_all(points, 'ang', split_axis=2, concat_axis=1, tiled=True)]
    ppermute x2 -> x52, waiting for transfers between devices: 0.01 us -> 341 us  [the longest x48 334 us: exchange(): lax.ppermute(pieces[s], 'ang', ring('ang', s))]
    pallas_call x0 -> x26, Pallas kernels: none -> 200 us  [the longest x8 60.1 us: analyze(): pl.pallas_call(kernel, out_shape=jax.ShapeDtypeStruct(field.shape, field....]
    ppermute x2 -> x52, starting transfers between devices: 1.84 us -> 194 us  [the longest x48 190 us: exchange(): lax.ppermute(pieces[s], 'ang', ring('ang', s))]
    dot_general x4 -> x0, matrix products: 95.7 us -> none  [the longest x1 43 us: local_kerr(): angular = jnp.dot(forward, flat, preferred_element_type=jnp.float32)]
    another operation x4 -> x0, other arithmetic: 77 us -> none
    add x1 -> x0, other arithmetic: 75 us -> none  [per_device(): second = right - 2.0 * middle + left]
    convert_element_type x3 -> x0, other arithmetic: 69.5 us -> none  [the longest x1 39.8 us: per_device(): padded = with_halo(field, (('tm', 3),), 1).astype(jnp.float32)]
  transfers between devices with their start and end apart: 4 -> 52, of which waited for: 2 -> 16; matrix products, arithmetic and copies ran while one was open for 3% -> 1% of each run, Pallas kernels for 0% -> 24%
where the time goes in v1:
time: 753 us; the launch traced here: 751 us
  waiting for transfers between devices  341 us (45%)
  Pallas kernels  200 us (27%)
  starting transfers between devices  194 us (26%)
  local copies, waits for them, and re-layouts  12.7 us (2%)
    ppermute x48, waiting for transfers between devices, exchange(): lax.ppermute(pieces[s], 'ang', ring('ang', s))  334 us
    ppermute x48, starting transfers between devices, exchange(): lax.ppermute(pieces[s], 'ang', ring('ang', s))  190 us
    pallas_call x8, Pallas kernels, analyze(): pl.pallas_call(kernel, out_shape=jax.ShapeDtypeStruct(field.shape, field....  60.1 us
    pallas_call x8, Pallas kernels, kerr_step(): pl.pallas_call(kernel, out_shape=[jax.ShapeDtypeStruct(pieces[0].shape, j...  59.6 us
    pallas_call x8, Pallas kernels, synthesize(): pl.pallas_call(kernel, out_shape=[piece] * count, grid_spec=pltpu.Prefetc...  58.9 us
    pallas_call x2, Pallas kernels, edges(): pl.pallas_call(kernel, out_shape=jax.ShapeDtypeStruct((parts, count * blo...  21.7 us
  transfers between devices with their start and end apart: 52, of which 16 were waited for; matrix products, arithmetic and copies ran while one was open for 1% of the time, Pallas kernels for 24%

profile of v1, /device:TPU:24, one launch (start us, length us, event | category | flops | bytes accessed | tf_op | source)
XLA Modules:
  0.0 750.9 jit_solution(13802165784344193545)
XLA Ops:
  16.1 18.7 %edges.3 = bf16[2,448,128]{2,1,0:T(8,128)(2,1)S(1)} custom-call(bf16[2,64,512,128]{3,2,1,0:T(8,128)(2,1)} %refs_4_.15, bf16[16,2,64,128]{3,2,1,0:T(8,128)(2,1)S(1)} %get-tuple-element.69.refs_0_), custom_call_target="tpu_custom_call" | custom-call | bytes 14680064 | tf_op jit(solution)/shard_map/edges/pallas_call | solution.py:75
  53.9 7.7 %collective-permute-done.8.refs_2_ = bf16[16,2,64,128]{3,2,1,0:T(8,128)(2,1)S(1)} collective-permute-done((bf16[16,2,64,128]{3,2,1,0:T(8,128)(2,1)S(1)}, bf16[16,2,64,128]{3,2,1,0:T(8,128)(2,1)S(1)}, u32[]{:S(2)}, u32[]{:S(2)}) %collective-permute-start.8) | collective-permute-done | bytes 524320 | tf_op jit(solution)/shard_map/ppermute | solution.py:295
  69.1 24.0 %collective-permute-start.50 = (bf16[16,2,64,128]{3,2,1,0:T(8,128)(2,1)S(1)}, bf16[16,2,64,128]{3,2,1,0:T(8,128)(2,1)S(1)}, u32[]{:S(2)}, u32[]{:S(2)}) collective-permute-start(bf16[16,2,64,128]{3,2,1,0:T(8,128)(2,1)S(1)} %get-tuple-element.131), channel_id=1, source_target_pairs={{0,8},{4,12},{8,0},{12,4},{1,9},{5,13},{9,1},{13,5},{2,10},{6,14},... | collective-permute-start | bytes 1572872 | tf_op jit(solution)/shard_map/ppermute | solution.py:295
  102.3 26.7 %collective-permute-done.5.refs_2_ = bf16[16,2,64,128]{3,2,1,0:T(8,128)(2,1)S(1)} collective-permute-done((bf16[16,2,64,128]{3,2,1,0:T(8,128)(2,1)S(1)}, bf16[16,2,64,128]{3,2,1,0:T(8,128)(2,1)S(1)}, u32[]{:S(2)}, u32[]{:S(2)}) %collective-permute-start.5) | collective-permute-done | bytes 524320 | tf_op jit(solution)/shard_map/ppermute | solution.py:295
  137.9 25.4 %collective-permute-start.15 = (bf16[16,2,64,128]{3,2,1,0:T(8,128)(2,1)S(1)}, bf16[16,2,64,128]{3,2,1,0:T(8,128)(2,1)S(1)}, u32[]{:S(2)}, u32[]{:S(2)}) collective-permute-start(bf16[16,2,64,128]{3,2,1,0:T(8,128)(2,1)S(1)} %get-tuple-element.86), channel_id=1, source_target_pairs={{0,12},{4,0},{8,4},{12,8},{1,13},{5,1},{9,5},{13,9},{2,14},{6,2},{... | collective-permute-start | bytes 1572872 | tf_op jit(solution)/shard_map/ppermute | solution.py:295
  163.4 10.7 %collective-permute-done.50.refs_2_ = bf16[16,2,64,128]{3,2,1,0:T(8,128)(2,1)S(1)} collective-permute-done((bf16[16,2,64,128]{3,2,1,0:T(8,128)(2,1)S(1)}, bf16[16,2,64,128]{3,2,1,0:T(8,128)(2,1)S(1)}, u32[]{:S(2)}, u32[]{:S(2)}) %collective-permute-start.50) | collective-permute-done | bytes 524320 | tf_op jit(solution)/shard_map/ppermute | solution.py:295
  176.4 9.4 %collective-permute-start.48 = (bf16[16,2,64,128]{3,2,1,0:T(8,128)(2,1)S(1)}, bf16[16,2,64,128]{3,2,1,0:T(8,128)(2,1)S(1)}, u32[]{:S(2)}, u32[]{:S(2)}) collective-permute-start(bf16[16,2,64,128]{3,2,1,0:T(8,128)(2,1)S(1)} %get-tuple-element.129), channel_id=1, source_target_pairs={{0,12},{4,0},{8,4},{12,8},{1,13},{5,1},{9,5},{13,9},{2,14},{6,2},{... | collective-permute-start | bytes 1572872 | tf_op jit(solution)/shard_map/ppermute | solution.py:295
  193.3 25.8 %collective-permute-done.14.refs_2_ = bf16[16,2,64,128]{3,2,1,0:T(8,128)(2,1)S(1)} collective-permute-done((bf16[16,2,64,128]{3,2,1,0:T(8,128)(2,1)S(1)}, bf16[16,2,64,128]{3,2,1,0:T(8,128)(2,1)S(1)}, u32[]{:S(2)}, u32[]{:S(2)}) %collective-permute-start.14) | collective-permute-done | bytes 524320 | tf_op jit(solution)/shard_map/ppermute | solution.py:295
  221.4 10.2 %collective-permute-start.12 = (bf16[16,2,64,128]{3,2,1,0:T(8,128)(2,1)S(1)}, bf16[16,2,64,128]{3,2,1,0:T(8,128)(2,1)S(1)}, u32[]{:S(2)}, u32[]{:S(2)}) collective-permute-start(bf16[16,2,64,128]{3,2,1,0:T(8,128)(2,1)S(1)} %get-tuple-element.83), channel_id=1, source_target_pairs={{0,12},{4,0},{8,4},{12,8},{1,13},{5,1},{9,5},{13,9},{2,14},{6,2},{... | collective-permute-start | bytes 1572872 | tf_op jit(solution)/shard_map/ppermute | solution.py:295
  238.9 25.1 %collective-permute-done.47.refs_2_ = bf16[16,2,64,128]{3,2,1,0:T(8,128)(2,1)S(1)} collective-permute-done((bf16[16,2,64,128]{3,2,1,0:T(8,128)(2,1)S(1)}, bf16[16,2,64,128]{3,2,1,0:T(8,128)(2,1)S(1)}, u32[]{:S(2)}, u32[]{:S(2)}) %collective-permute-start.47) | collective-permute-done | bytes 524320 | tf_op jit(solution)/shard_map/ppermute | solution.py:295
  275.8 33.2 %collective-permute-done.11.refs_2_ = bf16[16,2,64,128]{3,2,1,0:T(8,128)(2,1)S(1)} collective-permute-done((bf16[16,2,64,128]{3,2,1,0:T(8,128)(2,1)S(1)}, bf16[16,2,64,128]{3,2,1,0:T(8,128)(2,1)S(1)}, u32[]{:S(2)}, u32[]{:S(2)}) %collective-permute-start.11) | collective-permute-done | bytes 524320 | tf_op jit(solution)/shard_map/ppermute | solution.py:295
  320.8 33.2 %collective-permute-done.44.refs_2_ = bf16[16,2,64,128]{3,2,1,0:T(8,128)(2,1)S(1)} collective-permute-done((bf16[16,2,64,128]{3,2,1,0:T(8,128)(2,1)S(1)}, bf16[16,2,64,128]{3,2,1,0:T(8,128)(2,1)S(1)}, u32[]{:S(2)}, u32[]{:S(2)}) %collective-permute-start.44) | collective-permute-done | bytes 524320 | tf_op jit(solution)/shard_map/ppermute | solution.py:295
  365.8 33.2 %collective-permute-done.20.refs_2_ = bf16[16,2,64,128]{3,2,1,0:T(8,128)(2,1)S(1)} collective-permute-done((bf16[16,2,64,128]{3,2,1,0:T(8,128)(2,1)S(1)}, bf16[16,2,64,128]{3,2,1,0:T(8,128)(2,1)S(1)}, u32[]{:S(2)}, u32[]{:S(2)}) %collective-permute-start.20) | collective-permute-done | bytes 524320 | tf_op jit(solution)/shard_map/ppermute | solution.py:295
  401.2 10.3 %collective-permute-start.18 = (bf16[16,2,64,128]{3,2,1,0:T(8,128)(2,1)S(1)}, bf16[16,2,64,128]{3,2,1,0:T(8,128)(2,1)S(1)}, u32[]{:S(2)}, u32[]{:S(2)}) collective-permute-start(bf16[16,2,64,128]{3,2,1,0:T(8,128)(2,1)S(1)} %get-tuple-element.93), channel_id=1, source_target_pairs={{0,12},{4,0},{8,4},{12,8},{1,13},{5,1},{9,5},{13,9},{2,14},{6,2},{... | collective-permute-start | bytes 1572872 | tf_op jit(solution)/shard_map/ppermute | solution.py:295
  426.2 17.8 %collective-permute-done.41.refs_2_ = bf16[16,2,64,128]{3,2,1,0:T(8,128)(2,1)S(1)} collective-permute-done((bf16[16,2,64,128]{3,2,1,0:T(8,128)(2,1)S(1)}, bf16[16,2,64,128]{3,2,1,0:T(8,128)(2,1)S(1)}, u32[]{:S(2)}, u32[]{:S(2)}) %collective-permute-start.41) | collective-permute-done | bytes 524320 | tf_op jit(solution)/shard_map/ppermute | solution.py:295
  448.3 29.4 %collective-permute-done.17.refs_2_ = bf16[16,2,64,128]{3,2,1,0:T(8,128)(2,1)S(1)} collective-permute-done((bf16[16,2,64,128]{3,2,1,0:T(8,128)(2,1)S(1)}, bf16[16,2,64,128]{3,2,1,0:T(8,128)(2,1)S(1)}, u32[]{:S(2)}, u32[]{:S(2)}) %collective-permute-start.17) | collective-permute-done | bytes 524320 | tf_op jit(solution)/shard_map/ppermute | solution.py:295
  477.8 33.1 %collective-permute-start.27 = (bf16[16,2,64,128]{3,2,1,0:T(8,128)(2,1)S(1)}, bf16[16,2,64,128]{3,2,1,0:T(8,128)(2,1)S(1)}, u32[]{:S(2)}, u32[]{:S(2)}) collective-permute-start(bf16[16,2,64,128]{3,2,1,0:T(8,128)(2,1)S(1)} %get-tuple-element.106), channel_id=1, source_target_pairs={{0,12},{4,0},{8,4},{12,8},{1,13},{5,1},{9,5},{13,9},{2,14},{6,2},{... | collective-permute-start | bytes 1572872 | tf_op jit(solution)/shard_map/ppermute | solution.py:295
  529.6 26.9 %collective-permute-done.26.refs_2_ = bf16[16,2,64,128]{3,2,1,0:T(8,128)(2,1)S(1)} collective-permute-done((bf16[16,2,64,128]{3,2,1,0:T(8,128)(2,1)S(1)}, bf16[16,2,64,128]{3,2,1,0:T(8,128)(2,1)S(1)}, u32[]{:S(2)}, u32[]{:S(2)}) %collective-permute-start.26) | collective-permute-done | bytes 524320 | tf_op jit(solution)/shard_map/ppermute | solution.py:295
  556.5 21.9 %collective-permute-start.24 = (bf16[16,2,64,128]{3,2,1,0:T(8,128)(2,1)S(1)}, bf16[16,2,64,128]{3,2,1,0:T(8,128)(2,1)S(1)}, u32[]{:S(2)}, u32[]{:S(2)}) collective-permute-start(bf16[16,2,64,128]{3,2,1,0:T(8,128)(2,1)S(1)} %get-tuple-element.103), channel_id=1, source_target_pairs={{0,12},{4,0},{8,4},{12,8},{1,13},{5,1},{9,5},{13,9},{2,14},{6,2},{... | collective-permute-start | bytes 1572872 | tf_op jit(solution)/shard_map/ppermute | solution.py:295
  578.3 8.0 %kerr.14 = (bf16[16,2,64,128]{3,2,1,0:T(8,128)(2,1)S(1)}, bf16[16,2,64,128]{3,2,1,0:T(8,128)(2,1)S(1)}, bf16[16,2,64,128]{3,2,1,0:T(8,128)(2,1)}, bf16[16,2,64,128]{3,2,1,0:T(8,128)(2,1)}) custom-call(s32[1]{0:T(128)} %bitcast.me_ref, bf16[512,512]{1,0:T(8,128)(2,1)S(1)} %copy-done.57, bf16[512,512]{1,0:T(8,128)(2,1)S(1)} %copy-done.56, ...), custom_call_target="tpu_custom_call" | custom-call | flops 2147483648 | bytes 4194304 | tf_op jit(solution)/shard_map/kerr/pallas_call | solution.py:205
  595.3 39.8 %collective-permute-done.23.refs_2_ = bf16[16,2,64,128]{3,2,1,0:T(8,128)(2,1)S(1)} collective-permute-done((bf16[16,2,64,128]{3,2,1,0:T(8,128)(2,1)S(1)}, bf16[16,2,64,128]{3,2,1,0:T(8,128)(2,1)S(1)}, u32[]{:S(2)}, u32[]{:S(2)}) %collective-permute-start.23) | collective-permute-done | bytes 524320 | tf_op jit(solution)/shard_map/ppermute | solution.py:295
  635.2 8.1 %kerr.15 = (bf16[16,2,64,128]{3,2,1,0:T(8,128)(2,1)S(1)}, bf16[16,2,64,128]{3,2,1,0:T(8,128)(2,1)}, bf16[16,2,64,128]{3,2,1,0:T(8,128)(2,1)}, bf16[16,2,64,128]{3,2,1,0:T(8,128)(2,1)}) custom-call(s32[1]{0:T(128)} %bitcast.me_ref, bf16[512,512]{1,0:T(8,128)(2,1)S(1)} %copy-done.57, bf16[512,512]{1,0:T(8,128)(2,1)S(1)} %copy-done.56, ...), custom_call_target="tpu_custom_call" | custom-call | flops 2147483648 | bytes 4194304 | tf_op jit(solution)/shard_map/kerr/pallas_call | solution.py:205
  644.1 24.7 %collective-permute-done.35.refs_2_ = bf16[16,2,64,128]{3,2,1,0:T(8,128)(2,1)S(1)} collective-permute-done((bf16[16,2,64,128]{3,2,1,0:T(8,128)(2,1)S(1)}, bf16[16,2,64,128]{3,2,1,0:T(8,128)(2,1)S(1)}, u32[]{:S(2)}, u32[]{:S(2)}) %collective-permute-start.35) | collective-permute-done | bytes 524320 | tf_op jit(solution)/shard_map/ppermute | solution.py:295
  671.9 9.5 %collective-permute-start.30 = (bf16[16,2,64,128]{3,2,1,0:T(8,128)(2,1)}, bf16[16,2,64,128]{3,2,1,0:T(8,128)(2,1)}, u32[]{:S(2)}, u32[]{:S(2)}) collective-permute-start(bf16[16,2,64,128]{3,2,1,0:T(8,128)(2,1)} %get-tuple-element.111), channel_id=1, source_target_pairs={{0,12},{4,0},{8,4},{12,8},{1,13},{5,1},{9,5},{13,9},{2,14},{6,2},{... | collective-permute-start | bytes 1572872 | tf_op jit(solution)/shard_map/ppermute | solution.py:295
  690.5 7.5 analyze.8.refs_10_
  698.0 7.5 analyze.9.refs_10_
  705.5 7.5 analyze.10.refs_10_
  713.1 7.5 analyze.11.refs_10_
  720.6 7.5 analyze.12.refs_10_
  728.2 7.5 analyze.13.refs_10_
  735.7 7.6 %analyze.14.refs_10_ = bf16[2,64,512,128]{3,2,1,0:T(8,128)(2,1)} custom-call(s32[64]{0:T(128)S(1)} %copy-done.55, s32[1]{0:T(128)} %bitcast.me_ref, bf16[16,2,64,128]{3,2,1,0:T(8,128)(2,1)S(1)} %copy-done.12, bf16[16,2,64,128]{3,2,1,0:T(8,128)(2,1)S(1)} %copy-done.52, ...), custom_call_target="tpu_custom_call", output_to_operand_aliasing={{}: (12, {})} | custom-call | flops 268435456 | bytes 6291456 | tf_op jit(solution)/shard_map/analyze/pallas_call | solution.py:262
  743.2 7.6 %analyze.15 = bf16[2,64,512,128]{3,2,1,0:T(8,128)(2,1)} custom-call(s32[64]{0:T(128)S(1)} %copy-done.55, s32[1]{0:T(128)} %bitcast.me_ref, bf16[16,2,64,128]{3,2,1,0:T(8,128)(2,1)S(1)} %copy-done.14, bf16[16,2,64,128]{3,2,1,0:T(8,128)(2,1)} %collective-permute-done.28.refs_1_, ...), custom_call_target="tpu_custom_call", output_to_operand_aliasing={{}: (12, {})} | custom-call | flops 268435456 | bytes 6291456 | tf_op jit(solution)/shard_map/analyze/pallas_call | solution.py:262
  (219 shorter events, 177.1 us)
Async XLA Ops:
  52.7 76.4 %collective-permute-start.5 = (bf16[16,2,64,128]{3,2,1,0:T(8,128)(2,1)S(1)}, bf16[16,2,64,128]{3,2,1,0:T(8,128)(2,1)S(1)}, u32[]{:S(2)}, u32[]{:S(2)}) collective-permute-start(bf16[16,2,64,128]{3,2,1,0:T(8,128)(2,1)S(1)} %get-tuple-element.72), channel_id=1, source_target_pairs={{0,8},{4,12},{8,0},{12,4},{1,9},{5,13},{9,1},{13,5},{2,10},{6,14},... | collective-permute-start | bytes 1572872 | tf_op jit(solution)/shard_map/ppermute | solution.py:295
  52.7 76.4 %collective-permute-start.6 = (bf16[16,2,64,128]{3,2,1,0:T(8,128)(2,1)S(1)}, bf16[16,2,64,128]{3,2,1,0:T(8,128)(2,1)S(1)}, u32[]{:S(2)}, u32[]{:S(2)}) collective-permute-start(bf16[16,2,64,128]{3,2,1,0:T(8,128)(2,1)S(1)} %get-tuple-element.73), channel_id=1, source_target_pairs={{0,12},{4,0},{8,4},{12,8},{1,13},{5,1},{9,5},{13,9},{2,14},{6,2},{... | collective-permute-start | bytes 1572872 | tf_op jit(solution)/shard_map/ppermute | solution.py:295
  69.1 105.0 %collective-permute-start.50 = (bf16[16,2,64,128]{3,2,1,0:T(8,128)(2,1)S(1)}, bf16[16,2,64,128]{3,2,1,0:T(8,128)(2,1)S(1)}, u32[]{:S(2)}, u32[]{:S(2)}) collective-permute-start(bf16[16,2,64,128]{3,2,1,0:T(8,128)(2,1)S(1)} %get-tuple-element.131), channel_id=1, source_target_pairs={{0,8},{4,12},{8,0},{12,4},{1,9},{5,13},{9,1},{13,5},{2,10},{6,14},... | collective-permute-start | bytes 1572872 | tf_op jit(solution)/shard_map/ppermute | solution.py:295
  100.3 73.7 %collective-permute-start.51 = (bf16[16,2,64,128]{3,2,1,0:T(8,128)(2,1)S(1)}, bf16[16,2,64,128]{3,2,1,0:T(8,128)(2,1)S(1)}, u32[]{:S(2)}, u32[]{:S(2)}) collective-permute-start(bf16[16,2,64,128]{3,2,1,0:T(8,128)(2,1)S(1)} %get-tuple-element.132), channel_id=1, source_target_pairs={{0,12},{4,0},{8,4},{12,8},{1,13},{5,1},{9,5},{13,9},{2,14},{6,2},{... | collective-permute-start | bytes 1572872 | tf_op jit(solution)/shard_map/ppermute | solution.py:295
  129.1 89.9 %collective-permute-start.14 = (bf16[16,2,64,128]{3,2,1,0:T(8,128)(2,1)S(1)}, bf16[16,2,64,128]{3,2,1,0:T(8,128)(2,1)S(1)}, u32[]{:S(2)}, u32[]{:S(2)}) collective-permute-start(bf16[16,2,64,128]{3,2,1,0:T(8,128)(2,1)S(1)} %get-tuple-element.85), channel_id=1, source_target_pairs={{0,8},{4,12},{8,0},{12,4},{1,9},{5,13},{9,1},{13,5},{2,10},{6,14},... | collective-permute-start | bytes 1572872 | tf_op jit(solution)/shard_map/ppermute | solution.py:295
  137.9 81.1 %collective-permute-start.15 = (bf16[16,2,64,128]{3,2,1,0:T(8,128)(2,1)S(1)}, bf16[16,2,64,128]{3,2,1,0:T(8,128)(2,1)S(1)}, u32[]{:S(2)}, u32[]{:S(2)}) collective-permute-start(bf16[16,2,64,128]{3,2,1,0:T(8,128)(2,1)S(1)} %get-tuple-element.86), channel_id=1, source_target_pairs={{0,12},{4,0},{8,4},{12,8},{1,13},{5,1},{9,5},{13,9},{2,14},{6,2},{... | collective-permute-start | bytes 1572872 | tf_op jit(solution)/shard_map/ppermute | solution.py:295
  174.9 89.1 %collective-permute-start.47 = (bf16[16,2,64,128]{3,2,1,0:T(8,128)(2,1)S(1)}, bf16[16,2,64,128]{3,2,1,0:T(8,128)(2,1)S(1)}, u32[]{:S(2)}, u32[]{:S(2)}) collective-permute-start(bf16[16,2,64,128]{3,2,1,0:T(8,128)(2,1)S(1)} %get-tuple-element.128), channel_id=1, source_target_pairs={{0,8},{4,12},{8,0},{12,4},{1,9},{5,13},{9,1},{13,5},{2,10},{6,14},... | collective-permute-start | bytes 1572872 | tf_op jit(solution)/shard_map/ppermute | solution.py:295
  176.4 87.6 %collective-permute-start.48 = (bf16[16,2,64,128]{3,2,1,0:T(8,128)(2,1)S(1)}, bf16[16,2,64,128]{3,2,1,0:T(8,128)(2,1)S(1)}, u32[]{:S(2)}, u32[]{:S(2)}) collective-permute-start(bf16[16,2,64,128]{3,2,1,0:T(8,128)(2,1)S(1)} %get-tuple-element.129), channel_id=1, source_target_pairs={{0,12},{4,0},{8,4},{12,8},{1,13},{5,1},{9,5},{13,9},{2,14},{6,2},{... | collective-permute-start | bytes 1572872 | tf_op jit(solution)/shard_map/ppermute | solution.py:295
  219.0 90.0 %collective-permute-start.11 = (bf16[16,2,64,128]{3,2,1,0:T(8,128)(2,1)S(1)}, bf16[16,2,64,128]{3,2,1,0:T(8,128)(2,1)S(1)}, u32[]{:S(2)}, u32[]{:S(2)}) collective-permute-start(bf16[16,2,64,128]{3,2,1,0:T(8,128)(2,1)S(1)} %get-tuple-element.82), channel_id=1, source_target_pairs={{0,8},{4,12},{8,0},{12,4},{1,9},{5,13},{9,1},{13,5},{2,10},{6,14},... | collective-permute-start | bytes 1572872 | tf_op jit(solution)/shard_map/ppermute | solution.py:295
  221.4 87.6 %collective-permute-start.12 = (bf16[16,2,64,128]{3,2,1,0:T(8,128)(2,1)S(1)}, bf16[16,2,64,128]{3,2,1,0:T(8,128)(2,1)S(1)}, u32[]{:S(2)}, u32[]{:S(2)}) collective-permute-start(bf16[16,2,64,128]{3,2,1,0:T(8,128)(2,1)S(1)} %get-tuple-element.83), channel_id=1, source_target_pairs={{0,12},{4,0},{8,4},{12,8},{1,13},{5,1},{9,5},{13,9},{2,14},{6,2},{... | collective-permute-start | bytes 1572872 | tf_op jit(solution)/shard_map/ppermute | solution.py:295
  264.0 90.0 %collective-permute-start.44 = (bf16[16,2,64,128]{3,2,1,0:T(8,128)(2,1)S(1)}, bf16[16,2,64,128]{3,2,1,0:T(8,128)(2,1)S(1)}, u32[]{:S(2)}, u32[]{:S(2)}) collective-permute-start(bf16[16,2,64,128]{3,2,1,0:T(8,128)(2,1)S(1)} %get-tuple-element.125), channel_id=1, source_target_pairs={{0,8},{4,12},{8,0},{12,4},{1,9},{5,13},{9,1},{13,5},{2,10},{6,14},... | collective-permute-start | bytes 1572872 | tf_op jit(solution)/shard_map/ppermute | solution.py:295
  272.9 88.5 %collective-permute-start.45 = (bf16[16,2,64,128]{3,2,1,0:T(8,128)(2,1)S(1)}, bf16[16,2,64,128]{3,2,1,0:T(8,128)(2,1)S(1)}, u32[]{:S(2)}, u32[]{:S(2)}) collective-permute-start(bf16[16,2,64,128]{3,2,1,0:T(8,128)(2,1)S(1)} %get-tuple-element.126), channel_id=1, source_target_pairs={{0,12},{4,0},{8,4},{12,8},{1,13},{5,1},{9,5},{13,9},{2,14},{6,2},{... | collective-permute-start | bytes 1572872 | tf_op jit(solution)/shard_map/ppermute | solution.py:295
  309.0 90.0 %collective-permute-start.20 = (bf16[16,2,64,128]{3,2,1,0:T(8,128)(2,1)S(1)}, bf16[16,2,64,128]{3,2,1,0:T(8,128)(2,1)S(1)}, u32[]{:S(2)}, u32[]{:S(2)}) collective-permute-start(bf16[16,2,64,128]{3,2,1,0:T(8,128)(2,1)S(1)} %get-tuple-element.95), channel_id=1, source_target_pairs={{0,8},{4,12},{8,0},{12,4},{1,9},{5,13},{9,1},{13,5},{2,10},{6,14},... | collective-permute-start | bytes 1572872 | tf_op jit(solution)/shard_map/ppermute | solution.py:295
  317.8 81.2 %collective-permute-start.21 = (bf16[16,2,64,128]{3,2,1,0:T(8,128)(2,1)S(1)}, bf16[16,2,64,128]{3,2,1,0:T(8,128)(2,1)S(1)}, u32[]{:S(2)}, u32[]{:S(2)}) collective-permute-start(bf16[16,2,64,128]{3,2,1,0:T(8,128)(2,1)S(1)} %get-tuple-element.96), channel_id=1, source_target_pairs={{0,12},{4,0},{8,4},{12,8},{1,13},{5,1},{9,5},{13,9},{2,14},{6,2},{... | collective-permute-start | bytes 1572872 | tf_op jit(solution)/shard_map/ppermute | solution.py:295
  361.5 82.5 %collective-permute-start.41 = (bf16[16,2,64,128]{3,2,1,0:T(8,128)(2,1)S(1)}, bf16[16,2,64,128]{3,2,1,0:T(8,128)(2,1)S(1)}, u32[]{:S(2)}, u32[]{:S(2)}) collective-permute-start(bf16[16,2,64,128]{3,2,1,0:T(8,128)(2,1)S(1)} %get-tuple-element.122), channel_id=1, source_target_pairs={{0,8},{4,12},{8,0},{12,4},{1,9},{5,13},{9,1},{13,5},{2,10},{6,14},... | collective-permute-start | bytes 1572872 | tf_op jit(solution)/shard_map/ppermute | solution.py:295
  361.5 82.4 %collective-permute-start.42 = (bf16[16,2,64,128]{3,2,1,0:T(8,128)(2,1)S(1)}, bf16[16,2,64,128]{3,2,1,0:T(8,128)(2,1)S(1)}, u32[]{:S(2)}, u32[]{:S(2)}) collective-permute-start(bf16[16,2,64,128]{3,2,1,0:T(8,128)(2,1)S(1)} %get-tuple-element.123), channel_id=1, source_target_pairs={{0,12},{4,0},{8,4},{12,8},{1,13},{5,1},{9,5},{13,9},{2,14},{6,2},{... | collective-permute-start | bytes 1572872 | tf_op jit(solution)/shard_map/ppermute | solution.py:295
  399.0 78.8 %collective-permute-start.17 = (bf16[16,2,64,128]{3,2,1,0:T(8,128)(2,1)S(1)}, bf16[16,2,64,128]{3,2,1,0:T(8,128)(2,1)S(1)}, u32[]{:S(2)}, u32[]{:S(2)}) collective-permute-start(bf16[16,2,64,128]{3,2,1,0:T(8,128)(2,1)S(1)} %get-tuple-element.92), channel_id=1, source_target_pairs={{0,8},{4,12},{8,0},{12,4},{1,9},{5,13},{9,1},{13,5},{2,10},{6,14},... | collective-permute-start | bytes 1572872 | tf_op jit(solution)/shard_map/ppermute | solution.py:295
  401.2 76.6 %collective-permute-start.18 = (bf16[16,2,64,128]{3,2,1,0:T(8,128)(2,1)S(1)}, bf16[16,2,64,128]{3,2,1,0:T(8,128)(2,1)S(1)}, u32[]{:S(2)}, u32[]{:S(2)}) collective-permute-start(bf16[16,2,64,128]{3,2,1,0:T(8,128)(2,1)S(1)} %get-tuple-element.93), channel_id=1, source_target_pairs={{0,12},{4,0},{8,4},{12,8},{1,13},{5,1},{9,5},{13,9},{2,14},{6,2},{... | collective-permute-start | bytes 1572872 | tf_op jit(solution)/shard_map/ppermute | solution.py:295
  443.9 81.7 %collective-permute-start.37 = (bf16[16,2,64,128]{3,2,1,0:T(8,128)(2,1)S(1)}, bf16[16,2,64,128]{3,2,1,0:T(8,128)(2,1)S(1)}, u32[]{:S(2)}, u32[]{:S(2)}) collective-permute-start(bf16[16,2,64,128]{3,2,1,0:T(8,128)(2,1)S(1)} %get-tuple-element.118), channel_id=1, source_target_pairs={{0,4},{4,8},{8,12},{12,0},{1,5},{5,9},{9,13},{13,1},{2,6},{6,10},{... | collective-permute-start | bytes 1572872 | tf_op jit(solution)/shard_map/ppermute | solution.py:295
  444.0 84.2 %collective-permute-start.38 = (bf16[16,2,64,128]{3,2,1,0:T(8,128)(2,1)S(1)}, bf16[16,2,64,128]{3,2,1,0:T(8,128)(2,1)S(1)}, u32[]{:S(2)}, u32[]{:S(2)}) collective-permute-start(bf16[16,2,64,128]{3,2,1,0:T(8,128)(2,1)S(1)} %get-tuple-element.119), channel_id=1, source_target_pairs={{0,8},{4,12},{8,0},{12,4},{1,9},{5,13},{9,1},{13,5},{2,10},{6,14},... | collective-permute-start | bytes 1572872 | tf_op jit(solution)/shard_map/ppermute | solution.py:295
  445.4 84.1 %collective-permute-start.25 = (bf16[16,2,64,128]{3,2,1,0:T(8,128)(2,1)S(1)}, bf16[16,2,64,128]{3,2,1,0:T(8,128)(2,1)S(1)}, u32[]{:S(2)}, u32[]{:S(2)}) collective-permute-start(bf16[16,2,64,128]{3,2,1,0:T(8,128)(2,1)S(1)} %get-tuple-element.104), channel_id=1, source_target_pairs={{0,4},{4,8},{8,12},{12,0},{1,5},{5,9},{9,13},{13,1},{2,6},{6,10},{... | collective-permute-start | bytes 1572872 | tf_op jit(solution)/shard_map/ppermute | solution.py:295
  477.8 78.7 %collective-permute-start.26 = (bf16[16,2,64,128]{3,2,1,0:T(8,128)(2,1)S(1)}, bf16[16,2,64,128]{3,2,1,0:T(8,128)(2,1)S(1)}, u32[]{:S(2)}, u32[]{:S(2)}) collective-permute-start(bf16[16,2,64,128]{3,2,1,0:T(8,128)(2,1)S(1)} %get-tuple-element.105), channel_id=1, source_target_pairs={{0,8},{4,12},{8,0},{12,4},{1,9},{5,13},{9,1},{13,5},{2,10},{6,14},... | collective-permute-start | bytes 1572872 | tf_op jit(solution)/shard_map/ppermute | solution.py:295
  477.8 78.7 %collective-permute-start.27 = (bf16[16,2,64,128]{3,2,1,0:T(8,128)(2,1)S(1)}, bf16[16,2,64,128]{3,2,1,0:T(8,128)(2,1)S(1)}, u32[]{:S(2)}, u32[]{:S(2)}) collective-permute-start(bf16[16,2,64,128]{3,2,1,0:T(8,128)(2,1)S(1)} %get-tuple-element.106), channel_id=1, source_target_pairs={{0,12},{4,0},{8,4},{12,8},{1,13},{5,1},{9,5},{13,9},{2,14},{6,2},{... | collective-permute-start | bytes 1572872 | tf_op jit(solution)/shard_map/ppermute | solution.py:295
  556.5 78.7 %collective-permute-start.23 = (bf16[16,2,64,128]{3,2,1,0:T(8,128)(2,1)S(1)}, bf16[16,2,64,128]{3,2,1,0:T(8,128)(2,1)S(1)}, u32[]{:S(2)}, u32[]{:S(2)}) collective-permute-start(bf16[16,2,64,128]{3,2,1,0:T(8,128)(2,1)S(1)} %get-tuple-element.102), channel_id=1, source_target_pairs={{0,8},{4,12},{8,0},{12,4},{1,9},{5,13},{9,1},{13,5},{2,10},{6,14},... | collective-permute-start | bytes 1572872 | tf_op jit(solution)/shard_map/ppermute | solution.py:295
  556.5 78.7 %collective-permute-start.24 = (bf16[16,2,64,128]{3,2,1,0:T(8,128)(2,1)S(1)}, bf16[16,2,64,128]{3,2,1,0:T(8,128)(2,1)S(1)}, u32[]{:S(2)}, u32[]{:S(2)}) collective-permute-start(bf16[16,2,64,128]{3,2,1,0:T(8,128)(2,1)S(1)} %get-tuple-element.103), channel_id=1, source_target_pairs={{0,12},{4,0},{8,4},{12,8},{1,13},{5,1},{9,5},{13,9},{2,14},{6,2},{... | collective-permute-start | bytes 1572872 | tf_op jit(solution)/shard_map/ppermute | solution.py:295
  586.4 82.4 %collective-permute-start.35 = (bf16[16,2,64,128]{3,2,1,0:T(8,128)(2,1)S(1)}, bf16[16,2,64,128]{3,2,1,0:T(8,128)(2,1)S(1)}, u32[]{:S(2)}, u32[]{:S(2)}) collective-permute-start(bf16[16,2,64,128]{3,2,1,0:T(8,128)(2,1)S(1)} %get-tuple-element.116), channel_id=1, source_target_pairs={{0,8},{4,12},{8,0},{12,4},{1,9},{5,13},{9,1},{13,5},{2,10},{6,14},... | collective-permute-start | bytes 1572872 | tf_op jit(solution)/shard_map/ppermute | solution.py:295
  591.5 78.1 %collective-permute-start.36 = (bf16[16,2,64,128]{3,2,1,0:T(8,128)(2,1)S(1)}, bf16[16,2,64,128]{3,2,1,0:T(8,128)(2,1)S(1)}, u32[]{:S(2)}, u32[]{:S(2)}) collective-permute-start(bf16[16,2,64,128]{3,2,1,0:T(8,128)(2,1)S(1)} %get-tuple-element.117), channel_id=1, source_target_pairs={{0,12},{4,0},{8,4},{12,8},{1,13},{5,1},{9,5},{13,9},{2,14},{6,2},{... | collective-permute-start | bytes 1572872 | tf_op jit(solution)/shard_map/ppermute | solution.py:295
  591.5 79.6 %collective-permute-start.31 = (bf16[16,2,64,128]{3,2,1,0:T(8,128)(2,1)S(1)}, bf16[16,2,64,128]{3,2,1,0:T(8,128)(2,1)S(1)}, u32[]{:S(2)}, u32[]{:S(2)}) collective-permute-start(bf16[16,2,64,128]{3,2,1,0:T(8,128)(2,1)S(1)} %get-tuple-element.112), channel_id=1, source_target_pairs={{0,4},{4,8},{8,12},{12,0},{1,5},{5,9},{9,13},{13,1},{2,6},{6,10},{... | collective-permute-start | bytes 1572872 | tf_op jit(solution)/shard_map/ppermute | solution.py:295
  635.2 100.5 %collective-permute-start.32 = (bf16[16,2,64,128]{3,2,1,0:T(8,128)(2,1)}, bf16[16,2,64,128]{3,2,1,0:T(8,128)(2,1)}, u32[]{:S(2)}, u32[]{:S(2)}) collective-permute-start(bf16[16,2,64,128]{3,2,1,0:T(8,128)(2,1)} %get-tuple-element.113), channel_id=1, source_target_pairs={{0,8},{4,12},{8,0},{12,4},{1,9},{5,13},{9,1},{13,5},{2,10},{6,14},... | collective-permute-start | bytes 1572872 | tf_op jit(solution)/shard_map/ppermute | solution.py:295
  635.2 100.5 %collective-permute-start.33 = (bf16[16,2,64,128]{3,2,1,0:T(8,128)(2,1)}, bf16[16,2,64,128]{3,2,1,0:T(8,128)(2,1)}, u32[]{:S(2)}, u32[]{:S(2)}) collective-permute-start(bf16[16,2,64,128]{3,2,1,0:T(8,128)(2,1)} %get-tuple-element.114), channel_id=1, source_target_pairs={{0,12},{4,0},{8,4},{12,8},{1,13},{5,1},{9,5},{13,9},{2,14},{6,2},{... | collective-permute-start | bytes 1572872 | tf_op jit(solution)/shard_map/ppermute | solution.py:295
  669.6 73.6 %collective-permute-start.28 = (bf16[16,2,64,128]{3,2,1,0:T(8,128)(2,1)}, bf16[16,2,64,128]{3,2,1,0:T(8,128)(2,1)}, u32[]{:S(2)}, u32[]{:S(2)}) collective-permute-start(bf16[16,2,64,128]{3,2,1,0:T(8,128)(2,1)} %get-tuple-element.109), channel_id=1, source_target_pairs={{0,4},{4,8},{8,12},{12,0},{1,5},{5,9},{9,13},{13,1},{2,6},{6,10},{... | collective-permute-start | bytes 1572872 | tf_op jit(solution)/shard_map/ppermute | solution.py:295
  670.5 72.8 %collective-permute-start.29 = (bf16[16,2,64,128]{3,2,1,0:T(8,128)(2,1)}, bf16[16,2,64,128]{3,2,1,0:T(8,128)(2,1)}, u32[]{:S(2)}, u32[]{:S(2)}) collective-permute-start(bf16[16,2,64,128]{3,2,1,0:T(8,128)(2,1)} %get-tuple-element.110), channel_id=1, source_target_pairs={{0,8},{4,12},{8,0},{12,4},{1,9},{5,13},{9,1},{13,5},{2,10},{6,14},... | collective-permute-start | bytes 1572872 | tf_op jit(solution)/shard_map/ppermute | solution.py:295
  (79 other events, 3501.8 us)

commit v2 on v1

--- a/solution.py
+++ b/solution.py
@@ -52,18 +52,22 @@
     return [pl.BlockSpec(memory_space=pl.ANY)] * count
 
 
-def edges(field, first, count, block, deps=()):
-    parts, orders = field.shape[:2]
-    groups = orders // ROWS
+def token():
+    return jax.ShapeDtypeStruct((8, LANES), jnp.float32)
+
+
+def edges(field, first, count, block, span, after):
+    parts = field.shape[0]
+    base, groups = span[0] // ROWS, span[1] // ROWS
 
     def kernel(x_ref, *refs):
-        o_ref, acc = refs[-2:]
+        o_ref, _, acc = refs[-3:]
         g = pl.program_id(1)
         slot = ((lane_index(block) + 1) >> 1) & (LANES // 2 - 1)
         for c in range(parts):
             kept = acc[c]
             for i in range(ROWS):
-                m = g * ROWS + i
+                m = (g + base) * ROWS + i
                 row = roll(x_ref[c, i].astype(jnp.float32), 2 * m)
                 kept = jnp.where(slot == m, row, kept)
             acc[c] = kept
@@ -74,16 +78,21 @@
 
     return pl.pallas_call(
         kernel,
-        out_shape=jax.ShapeDtypeStruct((parts, count * block, LANES), field.dtype),
+        out_shape=[
+            jax.ShapeDtypeStruct((parts, count * block, LANES), field.dtype),
+            token(),
+        ],
         grid=(count, groups),
-        in_specs=[pl.BlockSpec((parts, ROWS, block, LANES), lambda j, g: (0, g, j + first, 0))]
-        + anywhere(len(deps)),
-        out_specs=pl.BlockSpec((parts, block, LANES), lambda j, g: (0, j, 0)),
+        in_specs=[
+            pl.BlockSpec((parts, ROWS, block, LANES), lambda j, g: (0, g + base, j + first, 0))
+        ]
+        + anywhere(len(after)),
+        out_specs=[pl.BlockSpec((parts, block, LANES), lambda j, g: (0, j, 0))] + anywhere(1),
         scratch_shapes=[pltpu.VMEM((parts, block, LANES), jnp.float32)],
         compiler_params=params(),
-        cost_estimate=cost(0, parts * orders * count * block * LANES * 2),
+        cost_estimate=cost(0, parts * span[1] * count * block * LANES * 2),
         name="edges",
-    )(field, *deps)
+    )(field, *after)
 
 
 def join_halo(low, high):
@@ -112,22 +121,34 @@
     return real, imag
 
 
-def synthesize(field, low, high, halo_at, tables, curvature, walk_off, order_map, me, b, count, deps):
-    parts, orders, radial, steps = field.shape
+def radial_specs(parts, kinds, block, radial, b, halo_at, base):
+    return [
+        pl.BlockSpec((parts, ROWS, block, LANES), lambda g, *_: (0, g + base, b, 0)),
+        pl.BlockSpec((parts, block, LANES), lambda g, *_: (0, halo_at, 0)),
+        pl.BlockSpec((parts, block, LANES), lambda g, *_: (0, halo_at, 0)),
+        pl.BlockSpec((kinds, 1, block, block), lambda g, *_: (0, b, 0, 0)),
+        pl.BlockSpec((ROWS, radial), lambda g, *_: (g + base, 0)),
+        pl.BlockSpec((ROWS, radial), lambda g, *_: (g + base, 0)),
+    ]
+
+
+def synthesize(field, halo, tables, curvature, walk_off, order_map, me, b, count, span, after):
+    low, high, halo_at = halo
+    parts, _, radial, _ = field.shape
     kinds, _, block, _ = tables.shape
     share = block // count
-    groups = orders // ROWS
+    base, groups = span[0] // ROWS, span[1] // ROWS
 
     def kernel(map_ref, me_ref, x_ref, low_ref, high_ref, tab_ref, beta_ref, delta_ref, *refs):
-        outs, acc = refs[len(deps) : -1], refs[-1]
+        outs, acc = refs[len(after) : len(after) + count], refs[-1]
         g = pl.program_id(0)
         beta = columns(beta_ref, b * block, block)
         delta = columns(delta_ref, b * block, block)
-        halo = [join_halo(low_ref[c], high_ref[c]) for c in range(parts)]
+        ends = [join_halo(low_ref[c], high_ref[c]) for c in range(parts)]
         for i in range(ROWS):
-            m = g * ROWS + i
+            m = (g + base) * ROWS + i
             x = [x_ref[c, i].astype(jnp.float32) for c in range(parts)]
-            moved = move(x, halo, beta[:, i : i + 1], delta[:, i : i + 1], m)
+            moved = move(x, ends, beta[:, i : i + 1], delta[:, i : i + 1], m)
             moved = jnp.concatenate(moved, 1).astype(jnp.bfloat16)
             points = jnp.dot(
                 tab_ref[map_ref[m], 0], moved, preferred_element_type=jnp.float32
@@ -141,50 +162,51 @@
                 for c in range(parts):
                     outs[s][q, c] = acc[c, pl.ds(row, ROWS), :].astype(jnp.bfloat16)
 
-    piece = jax.ShapeDtypeStruct((share, parts, orders, LANES), jnp.bfloat16)
-    size = parts * orders * block * LANES * 2
-    return pl.pallas_call(
+    piece = jax.ShapeDtypeStruct((share, parts, span[1], LANES), jnp.bfloat16)
+    size = parts * span[1] * block * LANES * 2
+    *pieces, done = pl.pallas_call(
         kernel,
-        out_shape=[piece] * count,
+        out_shape=[piece] * count + [token()],
         grid_spec=pltpu.PrefetchScalarGridSpec(
             num_scalar_prefetch=2,
             grid=(groups,),
-            in_specs=[
-                pl.BlockSpec((parts, ROWS, block, LANES), lambda g, *_: (0, g, b, 0)),
-                pl.BlockSpec((parts, block, LANES), lambda g, *_: (0, halo_at, 0)),
-                pl.BlockSpec((parts, block, LANES), lambda g, *_: (0, halo_at, 0)),
-                pl.BlockSpec((kinds, 1, block, block), lambda g, *_: (0, b, 0, 0)),
-                pl.BlockSpec((ROWS, radial), lambda g, *_: (g, 0)),
-                pl.BlockSpec((ROWS, radial), lambda g, *_: (g, 0)),
-            ]
-            + anywhere(len(deps)),
+            in_specs=radial_specs(parts, kinds, block, radial, b, halo_at, base)
+            + anywhere(len(after)),
             out_specs=[
                 pl.BlockSpec((share, parts, ROWS, LANES), lambda g, *_: (0, 0, g, 0))
             ]
-            * count,
+            * count
+            + anywhere(1),
             scratch_shapes=[pltpu.VMEM((parts, block * ROWS, LANES), jnp.float32)],
         ),
         compiler_params=params(),
         cost_estimate=cost(2 * size * block, 2 * size),
         name="synthesize",
-    )(order_map, me, field, low, high, tables, curvature, walk_off, *deps)
-
-
-def kerr_step(pieces, forward, backward, me, deps):
-    count = len(pieces)
-    share, parts, orders, _ = pieces[0].shape
+    )(order_map, me, field, low, high, tables, curvature, walk_off, *after)
+    return pieces, done
+
+
+def kerr_step(pieces, spans, out_spans, forward, backward, me, after):
+    count = len(pieces[0])
+    share, parts = pieces[0][0].shape[:2]
+    orders = sum(size for _, size in spans)
     every = count * orders
     width = 2
+    ins_count, outs_count = count * len(spans), count * len(out_spans)
 
     def kernel(me_ref, f_ref, b_ref, *refs):
-        ins = refs[:count]
-        outs, flat, back = refs[count + len(deps) : -2], refs[-2], refs[-1]
-        for s in range(count):
-            source = lax.rem(me_ref[0] + count - s, count)
-            for c in range(parts):
-                row = pl.multiple_of(c * every + source * orders, orders)
-                for q in range(width):
-                    flat[pl.ds(row, orders), q * LANES : (q + 1) * LANES] = ins[s][q, c]
+        ins = refs[:ins_count]
+        outs = refs[ins_count + len(after) : ins_count + len(after) + outs_count]
+        flat, back = refs[-2:]
+        for k, (start, size) in enumerate(spans):
+            for s in range(count):
+                source = lax.rem(me_ref[0] + count - s, count)
+                for c in range(parts):
+                    row = pl.multiple_of(c * every + source * orders + start, ROWS)
+                    for q in range(width):
+                        flat[pl.ds(row, size), q * LANES : (q + 1) * LANES] = ins[
+                            k * count + s
+                        ][q, c]
         angular = jnp.dot(f_ref[...], flat[...], preferred_element_type=jnp.float32)
         real, imag = angular[:every], angular[every:]
         power = kerr_gamma * (real * real + imag * imag)
@@ -192,24 +214,38 @@
         back[...] = (
             jnp.dot(b_ref[...], kerr, preferred_element_type=jnp.float32) * (1.0 / every)
         ).astype(jnp.bfloat16)
-        for s in range(count):
-            owner = lax.rem(me_ref[0] + s, count)
-            for c in range(parts):
-                row = pl.multiple_of(c * every + owner * orders, orders)
-                for q in range(width):
-                    outs[s][q, c] = back[pl.ds(row, orders), q * LANES : (q + 1) * LANES]
-
-    block = pl.BlockSpec((width, parts, orders, LANES), lambda q, *_: (q, 0, 0, 0))
+        for k, (start, size) in enumerate(out_spans):
+            for s in range(count):
+                owner = lax.rem(me_ref[0] + s, count)
+                for c in range(parts):
+                    row = pl.multiple_of(c * every + owner * orders + start, ROWS)
+                    for q in range(width):
+                        outs[k * count + s][q, c] = back[
+                            pl.ds(row, size), q * LANES : (q + 1) * LANES
+                        ]
+
+    def blocks(some):
+        return [
+            pl.BlockSpec((width, parts, size, LANES), lambda q, *_: (q, 0, 0, 0))
+            for _, size in some
+            for _ in range(count)
+        ]
+
     whole = pl.BlockSpec((parts * every, parts * every), lambda q, *_: (0, 0))
     lanes = share * LANES
-    return pl.pallas_call(
+    *back, done = pl.pallas_call(
         kernel,
-        out_shape=[jax.ShapeDtypeStruct(pieces[0].shape, jnp.bfloat16)] * count,
+        out_shape=[
+            jax.ShapeDtypeStruct((share, parts, size, LANES), jnp.bfloat16)
+            for _, size in out_spans
+            for _ in range(count)
+        ]
+        + [token()],
         grid_spec=pltpu.PrefetchScalarGridSpec(
             num_scalar_prefetch=1,
             grid=(share // width,),
-            in_specs=[whole, whole] + [block] * count + anywhere(len(deps)),
-            out_specs=[block] * count,
+            in_specs=[whole, whole] + blocks(spans) + anywhere(len(after)),
+            out_specs=blocks(out_spans) + anywhere(1),
             scratch_shapes=[
                 pltpu.VMEM((parts * every, width * LANES), jnp.bfloat16),
                 pltpu.VMEM((parts * every, width * LANES), jnp.bfloat16),
@@ -218,23 +254,25 @@
         compiler_params=params(),
         cost_estimate=cost(4 * (parts * every) ** 2 * lanes, 4 * parts * every * lanes),
         name="kerr",
-    )(me, forward, backward, *pieces, *deps)
+    )(me, forward, backward, *(piece for group in pieces for piece in group), *after)
+    return [back[k * count : (k + 1) * count] for k in range(len(out_spans))], done
 
 
 def analyze(
-    pieces, field, low, high, halo_at, tables, curvature, walk_off, order_map, me, b, out, deps
+    pieces, field, halo, tables, curvature, walk_off, order_map, me, b, span, out, after
 ):
+    low, high, halo_at = halo
     count = len(pieces)
-    parts, orders, radial, steps = field.shape
+    parts, _, radial, _ = field.shape
     kinds, _, block, _ = tables.shape
     share = block // count
-    groups = orders // ROWS
+    base, groups = span[0] // ROWS, span[1] // ROWS
     held = () if out is None else (out,)
 
     def kernel(map_ref, me_ref, *refs):
         ins = refs[:count]
         x_ref, low_ref, high_ref, tab_ref, beta_ref, delta_ref = refs[count : count + 6]
-        o_ref, acc = refs[-2:]
+        o_ref, _, acc = refs[-3:]
         g = pl.program_id(0)
         for s in range(count):
             source = lax.rem(me_ref[0] + count - s, count)
@@ -244,11 +282,11 @@
                     acc[c, pl.ds(row, ROWS), :] = ins[s][q, c].astype(jnp.float32)
         beta = columns(beta_ref, b * block, block)
         delta = columns(delta_ref, b * block, block)
-        halo = [join_halo(low_ref[c], high_ref[c]) for c in range(parts)]
+        ends = [join_halo(low_ref[c], high_ref[c]) for c in range(parts)]
         for i in range(ROWS):
-            m = g * ROWS + i
+            m = (g + base) * ROWS + i
             x = [x_ref[c, i].astype(jnp.float32) for c in range(parts)]
-            moved = move(x, halo, beta[:, i : i + 1], delta[:, i : i + 1], m)
+            moved = move(x, ends, beta[:, i : i + 1], delta[:, i : i + 1], m)
             back = [acc[c, pl.ds(i, block, stride=ROWS), :] for c in range(parts)]
             back = jnp.concatenate(back, 1).astype(jnp.bfloat16)
             increment = jnp.dot(
@@ -258,10 +296,10 @@
                 total = moved[c] + increment[:, c * LANES : (c + 1) * LANES]
                 o_ref[c, i] = total.astype(jnp.bfloat16)
 
-    size = parts * orders * block * LANES * 2
+    size = parts * span[1] * block * LANES * 2
     return pl.pallas_call(
         kernel,
-        out_shape=jax.ShapeDtypeStruct(field.shape, field.dtype),
+        out_shape=[jax.ShapeDtypeStruct(field.shape, field.dtype), token()],
         grid_spec=pltpu.PrefetchScalarGridSpec(
             num_scalar_prefetch=2,
             grid=(groups,),
@@ -269,16 +307,12 @@
                 pl.BlockSpec((share, parts, ROWS, LANES), lambda g, *_: (0, 0, g, 0))
             ]
             * count
-            + [
-                pl.BlockSpec((parts, ROWS, block, LANES), lambda g, *_: (0, g, b, 0)),
-                pl.BlockSpec((parts, block, LANES), lambda g, *_: (0, halo_at, 0)),
-                pl.BlockSpec((parts, block, LANES), lambda g, *_: (0, halo_at, 0)),
-                pl.BlockSpec((kinds, 1, block, block), lambda g, *_: (0, b, 0, 0)),
-                pl.BlockSpec((ROWS, radial), lambda g, *_: (g, 0)),
-                pl.BlockSpec((ROWS, radial), lambda g, *_: (g, 0)),
+            + radial_specs(parts, kinds, block, radial, b, halo_at, base)
+            + anywhere(len(held) + len(after)),
+            out_specs=[
+                pl.BlockSpec((parts, ROWS, block, LANES), lambda g, *_: (0, g + base, b, 0))
             ]
-            + anywhere(len(held) + len(deps)),
-            out_specs=pl.BlockSpec((parts, ROWS, block, LANES), lambda g, *_: (0, g, b, 0)),
+            + anywhere(1),
             scratch_shapes=[pltpu.VMEM((parts, block * ROWS, LANES), jnp.float32)],
         ),
         input_output_aliases={2 + count + 6: 0} if held else {},
@@ -286,7 +320,7 @@
         cost_estimate=cost(2 * size * block, 3 * size),
         name="analyze",
     )(
-        order_map, me, *pieces, field, low, high, tables, curvature, walk_off, *held, *deps
+        order_map, me, *pieces, field, low, high, tables, curvature, walk_off, *held, *after
     )
 
 
@@ -296,55 +330,74 @@
     ]
 
 
+def spans_of(sizes):
+    starts = [sum(sizes[:k]) for k in range(len(sizes))]
+    return list(zip(starts, sizes, strict=True))
+
+
 def pipelined(field, radial_tables, weights, order_map, curvature, walk_off):
     count = lax.axis_size("ang")
+    orders = field.shape[1]
     nblocks, block = radial_tables.shape[1:3]
     me = lax.axis_index("ang").astype(jnp.int32).reshape(1)
     forward, backward = (jnp.asarray(table) for table in angle_matrices(ORDERS))
     scaled = radial_tables.astype(jnp.float32) * weights.reshape(nblocks, block)[None, :, :, None]
     analysis = scaled.astype(jnp.bfloat16).transpose(0, 1, 3, 2)
-    halos = []
-
-    def halo(first, some, deps=()):
-        ends = edges(field, first, some, block, deps)
+    whole = spans_of([orders])
+    head = spans_of([ROWS, orders - ROWS]) if orders > ROWS else whole
+    tail = spans_of([orders // 2, orders // 4, orders // 4]) if orders % (4 * ROWS) == 0 else whole
+    spans = {0: head}
+    out_spans = {nblocks - 1: tail}
+    after = ()
+    halos, sent, returned = {}, {}, {}
+    out = None
+
+    def halo(first, some, span, after):
+        ends, done = edges(field, first, some, block, span, after)
         low = lax.ppermute(ends, "tm", ring("tm", 1))
         high = lax.ppermute(ends, "tm", ring("tm", -1))
-        for j in range(some):
-            halos.append((low, high, j))
-
-    def points(b, deps=()):
-        low, high, at = halos[b]
-        return synthesize(
-            field, low, high, at, radial_tables, curvature, walk_off, order_map, me, b, count, deps
+        return [(low, high, j) for j in range(some)], (done,)
+
+    def points(b, span, ends, after):
+        own, done = synthesize(
+            field, ends, radial_tables, curvature, walk_off, order_map, me, b, count, span, after
         )
-
-    sent, returned = {}, {}
-    halo(0, 1)
-    own = points(0)
-    sent[0] = exchange(own)
-    halo(1, nblocks - 1, own[:1])
-    own = points(1, own[:1])
-    sent[1] = exchange(own)
-    out, last = None, own
+        sent.setdefault(b, []).append(exchange(own))
+        return (done,)
+
+    def turn(b, after):
+        back, done = kerr_step(
+            sent.pop(b), spans.get(b, whole), out_spans.get(b, whole), forward, backward, me, after
+        )
+        returned[b] = [exchange(group) for group in back]
+        return (done,)
+
+    def finish(b, out, after):
+        for span, group in zip(out_spans.get(b, whole), returned.pop(b), strict=True):
+            out, done = analyze(
+                group, field, halos[b], analysis, curvature, walk_off, order_map, me, b, span,
+                out, after,
+            )
+            after = (done,)
+        return out, after
+
+    early, after = halo(0, 1, head[0], after)
+    (halos[0],), after = halo(0, 1, whole[0], after)
+    for k, span in enumerate(head):
+        after = points(0, span, early[0] if k == 0 else halos[0], after)
+    (halos[1],), after = halo(1, 1, whole[0], after)
+    after = points(1, whole[0], halos[1], after)
+    if nblocks > 2:
+        rest, after = halo(2, nblocks - 2, whole[0], after)
+        halos.update(zip(range(2, nblocks), rest, strict=True))
     for b in range(nblocks):
-        back = kerr_step(sent.pop(b), forward, backward, me, last[:1])
-        returned[b] = exchange(back)
-        last = back
+        after = turn(b, after)
         if b >= 1:
-            low, high, at = halos[b - 1]
-            out = analyze(
-                returned.pop(b - 1), field, low, high, at, analysis, curvature, walk_off,
-                order_map, me, b - 1, out, last[:1],
-            )
+            out, after = finish(b - 1, out, after)
         if b + 2 < nblocks:
-            own = points(b + 2, last[:1])
-            sent[b + 2] = exchange(own)
-            last = own
-    low, high, at = halos[nblocks - 1]
-    return analyze(
-        returned.pop(nblocks - 1), field, low, high, at, analysis, curvature, walk_off,
-        order_map, me, nblocks - 1, out, (),
-    )
+            after = points(b + 2, whole[0], halos[b + 2], after)
+    out, after = finish(nblocks - 1, out, after)
+    return out
 
 
 def with_halo(block, axis, dim):

time: 753 us -> 777 us (1.032); the launches traced: 751 us -> 763 us
  starting transfers between devices: 194 us -> 322 us
  waiting for transfers between devices: 341 us -> 220 us
  Pallas kernels: 200 us -> 209 us
    ppermute x48 -> x57, starting transfers between devices: 190 us -> 318 us  [exchange(): lax.ppermute(pieces[s], 'ang', ring('ang', s))]
    ppermute x48 -> x57, waiting for transfers between devices: 334 us -> 210 us  [exchange(): lax.ppermute(pieces[s], 'ang', ring('ang', s))]
    pallas_call x26 -> x31, Pallas kernels: 200 us -> 209 us  [the longest x10 64.3 us: analyze(): pl.pallas_call(kernel, out_shape=[jax.ShapeDtypeStruct(field.shape, field...]
  transfers between devices with their start and end apart: 52 -> 65, of which waited for: 16 -> 18; matrix products, arithmetic and copies ran while one was open for 1% -> 1% of each run, Pallas kernels for 24% -> 25%
where the time goes in v2:
time: 777 us; the launch traced here: 763 us
  starting transfers between devices  322 us (41%)
  waiting for transfers between devices  220 us (28%)
  Pallas kernels  209 us (27%)
  local copies, waits for them, and re-layouts  9.07 us (1%)
    ppermute x57, starting transfers between devices, exchange(): lax.ppermute(pieces[s], 'ang', ring('ang', s))  318 us
    ppermute x57, waiting for transfers between devices, exchange(): lax.ppermute(pieces[s], 'ang', ring('ang', s))  210 us
    pallas_call x10, Pallas kernels, analyze(): pl.pallas_call(kernel, out_shape=[jax.ShapeDtypeStruct(field.shape, field...  64.3 us
    pallas_call x9, Pallas kernels, synthesize(): pl.pallas_call(kernel, out_shape=[piece] * count + [token()], grid_spec=p...  60.9 us
    pallas_call x8, Pallas kernels, kerr_step(): pl.pallas_call(kernel, out_shape=[jax.ShapeDtypeStruct((share, parts, siz...  60.6 us
    pallas_call x4, Pallas kernels, edges(): pl.pallas_call(kernel, out_shape=[jax.ShapeDtypeStruct((parts, count * bl...  23 us
  transfers between devices with their start and end apart: 65, of which 18 were waited for; matrix products, arithmetic and copies ran while one was open for 1% of the time, Pallas kernels for 25%

profile of v2, /device:TPU:24, one launch (start us, length us, event | category | flops | bytes accessed | tf_op | source)
XLA Modules:
  0.0 763.1 jit_solution(6098599497503870089)
XLA Ops:
  30.3 15.4 %collective-permute-done.11.refs_1_ = bf16[16,2,16,128]{3,2,1,0:T(8,128)(2,1)S(1)} collective-permute-done((bf16[16,2,16,128]{3,2,1,0:T(8,128)(2,1)S(1)}, bf16[16,2,16,128]{3,2,1,0:T(8,128)(2,1)S(1)}, u32[]{:S(2)}, u32[]{:S(2)}) %collective-permute-start.11) | collective-permute-done | bytes 131104 | tf_op jit(solution)/shard_map/ppermute | solution.py:329
  45.7 16.6 %collective-permute-start.13 = (bf16[16,2,16,128]{3,2,1,0:T(8,128)(2,1)S(1)}, bf16[16,2,16,128]{3,2,1,0:T(8,128)(2,1)S(1)}, u32[]{:S(2)}, u32[]{:S(2)}) collective-permute-start(bf16[16,2,16,128]{3,2,1,0:T(8,128)(2,1)S(1)} %get-tuple-element.142), channel_id=1, source_target_pairs={{0,12},{4,0},{8,4},{12,8},{1,13},{5,1},{9,5},{13,9},{2,14},{6,2},{... | collective-permute-start | bytes 393224 | tf_op jit(solution)/shard_map/ppermute | solution.py:329
  71.3 16.0 %edges.7 = (bf16[2,384,128]{2,1,0:T(8,128)(2,1)S(1)}, f32[8,128]{1,0:T(8,128)S(1)}) custom-call(bf16[2,64,512,128]{3,2,1,0:T(8,128)(2,1)} %refs_4_.19, f32[8,128]{1,0:T(8,128)S(1)} %get-tuple-element.133.refs_0_), custom_call_target="tpu_custom_call" | custom-call | bytes 12582912 | tf_op jit(solution)/shard_map/edges/pallas_call | solution.py:79
  88.0 8.0 %kerr.8 = (bf16[16,2,64,128]{3,2,1,0:T(8,128)(2,1)S(1)}, bf16[16,2,64,128]{3,2,1,0:T(8,128)(2,1)S(1)}, bf16[16,2,64,128]{3,2,1,0:T(8,128)(2,1)S(1)}, bf16[16,2,64,128]{3,2,1,0:T(8,128)(2,1)}, f32[8,128]{1,0:T(8,128)S(1)}) custom-call(s32[1]{0:T(128)} %bitcast.me_ref, bf16[512,512]{1,0:T(8,128)(2,1)S(1)} %copy-done.16, bf16[512,512]{1,0:T(8,128)(2,1)S(1)} %copy-done.14, ...), custom_call_target="tpu_custom_call" | custom-call | flops 2147483648 | bytes 4194304 | tf_op jit(solution)/shard_map/kerr/pallas_call | solution.py:236
  105.2 7.9 %synthesize.12 = (bf16[16,2,64,128]{3,2,1,0:T(8,128)(2,1)S(1)}, bf16[16,2,64,128]{3,2,1,0:T(8,128)(2,1)}, bf16[16,2,64,128]{3,2,1,0:T(8,128)(2,1)}, bf16[16,2,64,128]{3,2,1,0:T(8,128)(2,1)}, f32[8,128]{1,0:T(8,128)S(1)}) custom-call(s32[64]{0:T(128)S(1)} %copy-done.9, s32[1]{0:T(128)} %bitcast.me_ref, bf16[2,64,512,128]{3,2,1,0:T(8,128)(2,1)} %refs_4_.19, ...), custom_call_target="tpu_custom_call" | custom-call | flops 268435456 | bytes 4194304 | tf_op jit(solution)/shard_map/synthesize/pallas_call | solution.py:167
  115.6 24.7 %collective-permute-done.9.refs_2_ = bf16[16,2,64,128]{3,2,1,0:T(8,128)(2,1)S(1)} collective-permute-done((bf16[16,2,64,128]{3,2,1,0:T(8,128)(2,1)S(1)}, bf16[16,2,64,128]{3,2,1,0:T(8,128)(2,1)S(1)}, u32[]{:S(2)}, u32[]{:S(2)}) %collective-permute-start.9) | collective-permute-done | bytes 524320 | tf_op jit(solution)/shard_map/ppermute | solution.py:329
  142.7 32.8 %collective-permute-start.25 = (bf16[16,2,64,128]{3,2,1,0:T(8,128)(2,1)}, bf16[16,2,64,128]{3,2,1,0:T(8,128)(2,1)}, u32[]{:S(2)}, u32[]{:S(2)}) collective-permute-start(bf16[16,2,64,128]{3,2,1,0:T(8,128)(2,1)} %get-tuple-element.163), channel_id=1, source_target_pairs={{0,12},{4,0},{8,4},{12,8},{1,13},{5,1},{9,5},{13,9},{2,14},{6,2},{... | collective-permute-start | bytes 1572872 | tf_op jit(solution)/shard_map/ppermute | solution.py:329
  175.4 8.0 %kerr.9 = (bf16[16,2,64,128]{3,2,1,0:T(8,128)(2,1)S(1)}, bf16[16,2,64,128]{3,2,1,0:T(8,128)(2,1)}, bf16[16,2,64,128]{3,2,1,0:T(8,128)(2,1)S(1)}, bf16[16,2,64,128]{3,2,1,0:T(8,128)(2,1)S(1)}, f32[8,128]{1,0:T(8,128)S(1)}) custom-call(s32[1]{0:T(128)} %bitcast.me_ref, bf16[512,512]{1,0:T(8,128)(2,1)S(1)} %copy-done.16, bf16[512,512]{1,0:T(8,128)(2,1)S(1)} %copy-done.14, ...), custom_call_target="tpu_custom_call" | custom-call | flops 2147483648 | bytes 4194304 | tf_op jit(solution)/shard_map/kerr/pallas_call | solution.py:236
  189.1 30.7 %collective-permute-start.19 = (bf16[16,2,64,128]{3,2,1,0:T(8,128)(2,1)}, bf16[16,2,64,128]{3,2,1,0:T(8,128)(2,1)S(1)}, u32[]{:S(2)}, u32[]{:S(2)}) collective-permute-start(bf16[16,2,64,128]{3,2,1,0:T(8,128)(2,1)} %copy-done.12), channel_id=1, source_target_pairs={{0,12},{4,0},{8,4},{12,8},{1,13},{5,1},{9,5},{13,9},{2,14},{6,2},{... | collective-permute-start | bytes 1572872 | tf_op jit(solution)/shard_map/ppermute | solution.py:329
  225.1 7.5 analyze.10
  241.6 23.0 %collective-permute-start.34 = (bf16[16,2,64,128]{3,2,1,0:T(8,128)(2,1)S(1)}, bf16[16,2,64,128]{3,2,1,0:T(8,128)(2,1)S(1)}, u32[]{:S(2)}, u32[]{:S(2)}) collective-permute-start(bf16[16,2,64,128]{3,2,1,0:T(8,128)(2,1)S(1)} %get-tuple-element.180), channel_id=1, source_target_pairs={{0,12},{4,0},{8,4},{12,8},{1,13},{5,1},{9,5},{13,9},{2,14},{6,2},{... | collective-permute-start | bytes 1572872 | tf_op jit(solution)/shard_map/ppermute | solution.py:329
  264.6 8.3 %kerr.10 = (bf16[16,2,64,128]{3,2,1,0:T(8,128)(2,1)S(1)}, bf16[16,2,64,128]{3,2,1,0:T(8,128)(2,1)S(1)}, bf16[16,2,64,128]{3,2,1,0:T(8,128)(2,1)S(1)}, bf16[16,2,64,128]{3,2,1,0:T(8,128)(2,1)S(1)}, f32[8,128]{1,0:T(8,128)S(1)}) custom-call(s32[1]{0:T(128)} %bitcast.me_ref, bf16[512,512]{1,0:T(8,128)(2,1)S(1)} %copy-done.17, bf16[512,512]{1,0:T(8,128)(2,1)S(1)} %copy-done.15, ...), custom_call_target="tpu_custom_call" | custom-call | flops 2147483648 | bytes 4194304 | tf_op jit(solution)/shard_map/kerr/pallas_call | solution.py:236
  290.0 19.5 %collective-permute-start.31 = (bf16[16,2,64,128]{3,2,1,0:T(8,128)(2,1)S(1)}, bf16[16,2,64,128]{3,2,1,0:T(8,128)(2,1)S(1)}, u32[]{:S(2)}, u32[]{:S(2)}) collective-permute-start(bf16[16,2,64,128]{3,2,1,0:T(8,128)(2,1)S(1)} %get-tuple-element.175), channel_id=1, source_target_pairs={{0,12},{4,0},{8,4},{12,8},{1,13},{5,1},{9,5},{13,9},{2,14},{6,2},{... | collective-permute-start | bytes 1572872 | tf_op jit(solution)/shard_map/ppermute | solution.py:329
  309.5 10.7 %collective-permute-done.33.refs_2_ = bf16[16,2,64,128]{3,2,1,0:T(8,128)(2,1)S(1)} collective-permute-done((bf16[16,2,64,128]{3,2,1,0:T(8,128)(2,1)S(1)}, bf16[16,2,64,128]{3,2,1,0:T(8,128)(2,1)S(1)}, u32[]{:S(2)}, u32[]{:S(2)}) %collective-permute-start.33) | collective-permute-done | bytes 524320 | tf_op jit(solution)/shard_map/ppermute | solution.py:329
  327.5 26.9 %collective-permute-start.28 = (bf16[16,2,64,128]{3,2,1,0:T(8,128)(2,1)S(1)}, bf16[16,2,64,128]{3,2,1,0:T(8,128)(2,1)S(1)}, u32[]{:S(2)}, u32[]{:S(2)}) collective-permute-start(bf16[16,2,64,128]{3,2,1,0:T(8,128)(2,1)S(1)} %get-tuple-element.171), channel_id=1, source_target_pairs={{0,12},{4,0},{8,4},{12,8},{1,13},{5,1},{9,5},{13,9},{2,14},{6,2},{... | collective-permute-start | bytes 1572872 | tf_op jit(solution)/shard_map/ppermute | solution.py:329
  354.4 10.7 %collective-permute-done.30.refs_2_ = bf16[16,2,64,128]{3,2,1,0:T(8,128)(2,1)S(1)} collective-permute-done((bf16[16,2,64,128]{3,2,1,0:T(8,128)(2,1)S(1)}, bf16[16,2,64,128]{3,2,1,0:T(8,128)(2,1)S(1)}, u32[]{:S(2)}, u32[]{:S(2)}) %collective-permute-start.30) | collective-permute-done | bytes 524320 | tf_op jit(solution)/shard_map/ppermute | solution.py:329
  365.1 34.2 %collective-permute-start.40 = (bf16[16,2,64,128]{3,2,1,0:T(8,128)(2,1)S(1)}, bf16[16,2,64,128]{3,2,1,0:T(8,128)(2,1)S(1)}, u32[]{:S(2)}, u32[]{:S(2)}) collective-permute-start(bf16[16,2,64,128]{3,2,1,0:T(8,128)(2,1)S(1)} %get-tuple-element.192), channel_id=1, source_target_pairs={{0,12},{4,0},{8,4},{12,8},{1,13},{5,1},{9,5},{13,9},{2,14},{6,2},{... | collective-permute-start | bytes 1572872 | tf_op jit(solution)/shard_map/ppermute | solution.py:329
  399.3 7.5 analyze.12
  415.8 28.5 %collective-permute-start.43 = (bf16[16,2,64,128]{3,2,1,0:T(8,128)(2,1)S(1)}, bf16[16,2,64,128]{3,2,1,0:T(8,128)(2,1)S(1)}, u32[]{:S(2)}, u32[]{:S(2)}) collective-permute-start(bf16[16,2,64,128]{3,2,1,0:T(8,128)(2,1)S(1)} %get-tuple-element.199), channel_id=1, source_target_pairs={{0,12},{4,0},{8,4},{12,8},{1,13},{5,1},{9,5},{13,9},{2,14},{6,2},{... | collective-permute-start | bytes 1572872 | tf_op jit(solution)/shard_map/ppermute | solution.py:329
  470.1 19.2 %collective-permute-start.37 = (bf16[16,2,64,128]{3,2,1,0:T(8,128)(2,1)S(1)}, bf16[16,2,64,128]{3,2,1,0:T(8,128)(2,1)S(1)}, u32[]{:S(2)}, u32[]{:S(2)}) collective-permute-start(bf16[16,2,64,128]{3,2,1,0:T(8,128)(2,1)S(1)} %get-tuple-element.188), channel_id=1, source_target_pairs={{0,12},{4,0},{8,4},{12,8},{1,13},{5,1},{9,5},{13,9},{2,14},{6,2},{... | collective-permute-start | bytes 1572872 | tf_op jit(solution)/shard_map/ppermute | solution.py:329
  489.2 10.7 %collective-permute-done.42.refs_2_ = bf16[16,2,64,128]{3,2,1,0:T(8,128)(2,1)S(1)} collective-permute-done((bf16[16,2,64,128]{3,2,1,0:T(8,128)(2,1)S(1)}, bf16[16,2,64,128]{3,2,1,0:T(8,128)(2,1)S(1)}, u32[]{:S(2)}, u32[]{:S(2)}) %collective-permute-start.42) | collective-permute-done | bytes 524320 | tf_op jit(solution)/shard_map/ppermute | solution.py:329
  510.7 11.7 %collective-permute-done.36.refs_2_ = bf16[16,2,64,128]{3,2,1,0:T(8,128)(2,1)S(1)} collective-permute-done((bf16[16,2,64,128]{3,2,1,0:T(8,128)(2,1)S(1)}, bf16[16,2,64,128]{3,2,1,0:T(8,128)(2,1)S(1)}, u32[]{:S(2)}, u32[]{:S(2)}) %collective-permute-start.36) | collective-permute-done | bytes 524320 | tf_op jit(solution)/shard_map/ppermute | solution.py:329
  522.4 20.1 %collective-permute-start.52 = (bf16[16,2,64,128]{3,2,1,0:T(8,128)(2,1)S(1)}, bf16[16,2,64,128]{3,2,1,0:T(8,128)(2,1)S(1)}, u32[]{:S(2)}, u32[]{:S(2)}) collective-permute-start(bf16[16,2,64,128]{3,2,1,0:T(8,128)(2,1)S(1)} %get-tuple-element.216), channel_id=1, source_target_pairs={{0,12},{4,0},{8,4},{12,8},{1,13},{5,1},{9,5},{13,9},{2,14},{6,2},{... | collective-permute-start | bytes 1572872 | tf_op jit(solution)/shard_map/ppermute | solution.py:329
  542.5 13.1 %collective-permute-start.48 = (bf16[16,2,64,128]{3,2,1,0:T(8,128)(2,1)S(1)}, bf16[16,2,64,128]{3,2,1,0:T(8,128)(2,1)S(1)}, u32[]{:S(2)}, u32[]{:S(2)}) collective-permute-start(bf16[16,2,64,128]{3,2,1,0:T(8,128)(2,1)S(1)} %get-tuple-element.210), channel_id=1, source_target_pairs={{0,8},{4,12},{8,0},{12,4},{1,9},{5,13},{9,1},{13,5},{2,10},{6,14},... | collective-permute-start | bytes 1572872 | tf_op jit(solution)/shard_map/ppermute | solution.py:329
  555.6 7.5 analyze.14
  574.4 43.5 %collective-permute-done.51.refs_2_ = bf16[16,2,64,128]{3,2,1,0:T(8,128)(2,1)S(1)} collective-permute-done((bf16[16,2,64,128]{3,2,1,0:T(8,128)(2,1)S(1)}, bf16[16,2,64,128]{3,2,1,0:T(8,128)(2,1)S(1)}, u32[]{:S(2)}, u32[]{:S(2)}) %collective-permute-start.51) | collective-permute-done | bytes 524320 | tf_op jit(solution)/shard_map/ppermute | solution.py:329
  625.3 9.5 %collective-permute-done.48.refs_2_ = bf16[16,2,64,128]{3,2,1,0:T(8,128)(2,1)S(1)} collective-permute-done((bf16[16,2,64,128]{3,2,1,0:T(8,128)(2,1)S(1)}, bf16[16,2,64,128]{3,2,1,0:T(8,128)(2,1)S(1)}, u32[]{:S(2)}, u32[]{:S(2)}) %collective-permute-start.48) | collective-permute-done | bytes 524320 | tf_op jit(solution)/shard_map/ppermute | solution.py:329
  642.3 13.0 %collective-permute-done.45.refs_2_ = bf16[16,2,64,128]{3,2,1,0:T(8,128)(2,1)S(1)} collective-permute-done((bf16[16,2,64,128]{3,2,1,0:T(8,128)(2,1)S(1)}, bf16[16,2,64,128]{3,2,1,0:T(8,128)(2,1)S(1)}, u32[]{:S(2)}, u32[]{:S(2)}) %collective-permute-start.45) | collective-permute-done | bytes 524320 | tf_op jit(solution)/shard_map/ppermute | solution.py:329
  669.9 33.4 %collective-permute-done.56.refs_1_ = bf16[16,2,16,128]{3,2,1,0:T(8,128)(2,1)S(1)} collective-permute-done((bf16[16,2,16,128]{3,2,1,0:T(8,128)(2,1)S(1)}, bf16[16,2,16,128]{3,2,1,0:T(8,128)(2,1)S(1)}, u32[]{:S(2)}, u32[]{:S(2)}) %collective-permute-start.56) | collective-permute-done | bytes 131104 | tf_op jit(solution)/shard_map/ppermute | solution.py:329
  703.4 14.5 %collective-permute-start.60 = (bf16[16,2,32,128]{3,2,1,0:T(8,128)(2,1)S(1)}, bf16[16,2,32,128]{3,2,1,0:T(8,128)(2,1)S(1)}, u32[]{:S(2)}, u32[]{:S(2)}) collective-permute-start(bf16[16,2,32,128]{3,2,1,0:T(8,128)(2,1)S(1)} %get-tuple-element.230), channel_id=1, source_target_pairs={{0,8},{4,12},{8,0},{12,4},{1,9},{5,13},{9,1},{13,5},{2,10},{6,14},... | collective-permute-start | bytes 786440 | tf_op jit(solution)/shard_map/ppermute | solution.py:329
  719.0 19.0 %collective-permute-done.60.refs_2_ = bf16[16,2,32,128]{3,2,1,0:T(8,128)(2,1)S(1)} collective-permute-done((bf16[16,2,32,128]{3,2,1,0:T(8,128)(2,1)S(1)}, bf16[16,2,32,128]{3,2,1,0:T(8,128)(2,1)S(1)}, u32[]{:S(2)}, u32[]{:S(2)}) %collective-permute-start.60) | collective-permute-done | bytes 262176 | tf_op jit(solution)/shard_map/ppermute | solution.py:329
  743.3 7.5 analyze.16
  (170 shorter events, 202.4 us)
Async XLA Ops:
  16.2 71.1 %collective-permute-start.14 = (bf16[16,2,48,128]{3,2,1,0:T(8,128)(2,1)S(1)}, bf16[16,2,48,128]{3,2,1,0:T(8,128)(2,1)S(1)}, u32[]{:S(2)}, u32[]{:S(2)}) collective-permute-start(bf16[16,2,48,128]{3,2,1,0:T(8,128)(2,1)S(1)} %get-tuple-element.144), channel_id=1, source_target_pairs={{0,4},{4,8},{8,12},{12,0},{1,5},{5,9},{9,13},{13,1},{2,6},{6,10},{... | collective-permute-start | bytes 1179656 | tf_op jit(solution)/shard_map/ppermute | solution.py:329
  16.5 70.9 %collective-permute-start.15 = (bf16[16,2,48,128]{3,2,1,0:T(8,128)(2,1)S(1)}, bf16[16,2,48,128]{3,2,1,0:T(8,128)(2,1)S(1)}, u32[]{:S(2)}, u32[]{:S(2)}) collective-permute-start(bf16[16,2,48,128]{3,2,1,0:T(8,128)(2,1)S(1)} %get-tuple-element.145), channel_id=1, source_target_pairs={{0,8},{4,12},{8,0},{12,4},{1,9},{5,13},{9,1},{13,5},{2,10},{6,14},... | collective-permute-start | bytes 1179656 | tf_op jit(solution)/shard_map/ppermute | solution.py:329
  18.2 69.8 %collective-permute-start.16 = (bf16[16,2,48,128]{3,2,1,0:T(8,128)(2,1)S(1)}, bf16[16,2,48,128]{3,2,1,0:T(8,128)(2,1)S(1)}, u32[]{:S(2)}, u32[]{:S(2)}) collective-permute-start(bf16[16,2,48,128]{3,2,1,0:T(8,128)(2,1)S(1)} %get-tuple-element.146), channel_id=1, source_target_pairs={{0,12},{4,0},{8,4},{12,8},{1,13},{5,1},{9,5},{13,9},{2,14},{6,2},{... | collective-permute-start | bytes 1179656 | tf_op jit(solution)/shard_map/ppermute | solution.py:329
  69.8 70.5 %collective-permute-start.9 = (bf16[16,2,64,128]{3,2,1,0:T(8,128)(2,1)S(1)}, bf16[16,2,64,128]{3,2,1,0:T(8,128)(2,1)S(1)}, u32[]{:S(2)}, u32[]{:S(2)}) collective-permute-start(bf16[16,2,64,128]{3,2,1,0:T(8,128)(2,1)S(1)} %get-tuple-element.137), channel_id=1, source_target_pairs={{0,8},{4,12},{8,0},{12,4},{1,9},{5,13},{9,1},{13,5},{2,10},{6,14},... | collective-permute-start | bytes 1572872 | tf_op jit(solution)/shard_map/ppermute | solution.py:329
  105.2 80.1 %collective-permute-start.21 = (bf16[16,2,64,128]{3,2,1,0:T(8,128)(2,1)S(1)}, bf16[16,2,64,128]{3,2,1,0:T(8,128)(2,1)S(1)}, u32[]{:S(2)}, u32[]{:S(2)}) collective-permute-start(bf16[16,2,64,128]{3,2,1,0:T(8,128)(2,1)S(1)} %get-tuple-element.156), channel_id=1, source_target_pairs={{0,8},{4,12},{8,0},{12,4},{1,9},{5,13},{9,1},{13,5},{2,10},{6,14},... | collective-permute-start | bytes 1572872 | tf_op jit(solution)/shard_map/ppermute | solution.py:329
  113.9 74.9 %collective-permute-start.22 = (bf16[16,2,64,128]{3,2,1,0:T(8,128)(2,1)}, bf16[16,2,64,128]{3,2,1,0:T(8,128)(2,1)}, u32[]{:S(2)}, u32[]{:S(2)}) collective-permute-start(bf16[16,2,64,128]{3,2,1,0:T(8,128)(2,1)} %get-tuple-element.157), channel_id=1, source_target_pairs={{0,12},{4,0},{8,4},{12,8},{1,13},{5,1},{9,5},{13,9},{2,14},{6,2},{... | collective-permute-start | bytes 1572872 | tf_op jit(solution)/shard_map/ppermute | solution.py:329
  140.4 99.7 %collective-permute-start.24 = (bf16[16,2,64,128]{3,2,1,0:T(8,128)(2,1)}, bf16[16,2,64,128]{3,2,1,0:T(8,128)(2,1)}, u32[]{:S(2)}, u32[]{:S(2)}) collective-permute-start(bf16[16,2,64,128]{3,2,1,0:T(8,128)(2,1)} %get-tuple-element.162), channel_id=1, source_target_pairs={{0,8},{4,12},{8,0},{12,4},{1,9},{5,13},{9,1},{13,5},{2,10},{6,14},... | collective-permute-start | bytes 1572872 | tf_op jit(solution)/shard_map/ppermute | solution.py:329
  142.7 97.5 %collective-permute-start.25 = (bf16[16,2,64,128]{3,2,1,0:T(8,128)(2,1)}, bf16[16,2,64,128]{3,2,1,0:T(8,128)(2,1)}, u32[]{:S(2)}, u32[]{:S(2)}) collective-permute-start(bf16[16,2,64,128]{3,2,1,0:T(8,128)(2,1)} %get-tuple-element.163), channel_id=1, source_target_pairs={{0,12},{4,0},{8,4},{12,8},{1,13},{5,1},{9,5},{13,9},{2,14},{6,2},{... | collective-permute-start | bytes 1572872 | tf_op jit(solution)/shard_map/ppermute | solution.py:329
  188.8 86.4 %collective-permute-start.18 = (bf16[16,2,64,128]{3,2,1,0:T(8,128)(2,1)}, bf16[16,2,64,128]{3,2,1,0:T(8,128)(2,1)S(1)}, u32[]{:S(2)}, u32[]{:S(2)}) collective-permute-start(bf16[16,2,64,128]{3,2,1,0:T(8,128)(2,1)} %copy-done.13), channel_id=1, source_target_pairs={{0,8},{4,12},{8,0},{12,4},{1,9},{5,13},{9,1},{13,5},{2,10},{6,14},... | collective-permute-start | bytes 1572872 | tf_op jit(solution)/shard_map/ppermute | solution.py:329
  189.1 86.1 %collective-permute-start.19 = (bf16[16,2,64,128]{3,2,1,0:T(8,128)(2,1)}, bf16[16,2,64,128]{3,2,1,0:T(8,128)(2,1)S(1)}, u32[]{:S(2)}, u32[]{:S(2)}) collective-permute-start(bf16[16,2,64,128]{3,2,1,0:T(8,128)(2,1)} %copy-done.12), channel_id=1, source_target_pairs={{0,12},{4,0},{8,4},{12,8},{1,13},{5,1},{9,5},{13,9},{2,14},{6,2},{... | collective-permute-start | bytes 1572872 | tf_op jit(solution)/shard_map/ppermute | solution.py:329
  240.2 80.0 %collective-permute-start.33 = (bf16[16,2,64,128]{3,2,1,0:T(8,128)(2,1)S(1)}, bf16[16,2,64,128]{3,2,1,0:T(8,128)(2,1)S(1)}, u32[]{:S(2)}, u32[]{:S(2)}) collective-permute-start(bf16[16,2,64,128]{3,2,1,0:T(8,128)(2,1)S(1)} %get-tuple-element.179), channel_id=1, source_target_pairs={{0,8},{4,12},{8,0},{12,4},{1,9},{5,13},{9,1},{13,5},{2,10},{6,14},... | collective-permute-start | bytes 1572872 | tf_op jit(solution)/shard_map/ppermute | solution.py:329
  241.6 78.5 %collective-permute-start.34 = (bf16[16,2,64,128]{3,2,1,0:T(8,128)(2,1)S(1)}, bf16[16,2,64,128]{3,2,1,0:T(8,128)(2,1)S(1)}, u32[]{:S(2)}, u32[]{:S(2)}) collective-permute-start(bf16[16,2,64,128]{3,2,1,0:T(8,128)(2,1)S(1)} %get-tuple-element.180), channel_id=1, source_target_pairs={{0,12},{4,0},{8,4},{12,8},{1,13},{5,1},{9,5},{13,9},{2,14},{6,2},{... | collective-permute-start | bytes 1572872 | tf_op jit(solution)/shard_map/ppermute | solution.py:329
  275.2 89.9 %collective-permute-start.30 = (bf16[16,2,64,128]{3,2,1,0:T(8,128)(2,1)S(1)}, bf16[16,2,64,128]{3,2,1,0:T(8,128)(2,1)S(1)}, u32[]{:S(2)}, u32[]{:S(2)}) collective-permute-start(bf16[16,2,64,128]{3,2,1,0:T(8,128)(2,1)S(1)} %get-tuple-element.174), channel_id=1, source_target_pairs={{0,8},{4,12},{8,0},{12,4},{1,9},{5,13},{9,1},{13,5},{2,10},{6,14},... | collective-permute-start | bytes 1572872 | tf_op jit(solution)/shard_map/ppermute | solution.py:329
  290.0 75.1 %collective-permute-start.31 = (bf16[16,2,64,128]{3,2,1,0:T(8,128)(2,1)S(1)}, bf16[16,2,64,128]{3,2,1,0:T(8,128)(2,1)S(1)}, u32[]{:S(2)}, u32[]{:S(2)}) collective-permute-start(bf16[16,2,64,128]{3,2,1,0:T(8,128)(2,1)S(1)} %get-tuple-element.175), channel_id=1, source_target_pairs={{0,12},{4,0},{8,4},{12,8},{1,13},{5,1},{9,5},{13,9},{2,14},{6,2},{... | collective-permute-start | bytes 1572872 | tf_op jit(solution)/shard_map/ppermute | solution.py:329
  320.1 94.1 %collective-permute-start.27 = (bf16[16,2,64,128]{3,2,1,0:T(8,128)(2,1)S(1)}, bf16[16,2,64,128]{3,2,1,0:T(8,128)(2,1)S(1)}, u32[]{:S(2)}, u32[]{:S(2)}) collective-permute-start(bf16[16,2,64,128]{3,2,1,0:T(8,128)(2,1)S(1)} %get-tuple-element.170), channel_id=1, source_target_pairs={{0,8},{4,12},{8,0},{12,4},{1,9},{5,13},{9,1},{13,5},{2,10},{6,14},... | collective-permute-start | bytes 1572872 | tf_op jit(solution)/shard_map/ppermute | solution.py:329
  327.5 86.9 %collective-permute-start.28 = (bf16[16,2,64,128]{3,2,1,0:T(8,128)(2,1)S(1)}, bf16[16,2,64,128]{3,2,1,0:T(8,128)(2,1)S(1)}, u32[]{:S(2)}, u32[]{:S(2)}) collective-permute-start(bf16[16,2,64,128]{3,2,1,0:T(8,128)(2,1)S(1)} %get-tuple-element.171), channel_id=1, source_target_pairs={{0,12},{4,0},{8,4},{12,8},{1,13},{5,1},{9,5},{13,9},{2,14},{6,2},{... | collective-permute-start | bytes 1572872 | tf_op jit(solution)/shard_map/ppermute | solution.py:329
  365.1 89.9 %collective-permute-start.39 = (bf16[16,2,64,128]{3,2,1,0:T(8,128)(2,1)S(1)}, bf16[16,2,64,128]{3,2,1,0:T(8,128)(2,1)S(1)}, u32[]{:S(2)}, u32[]{:S(2)}) collective-permute-start(bf16[16,2,64,128]{3,2,1,0:T(8,128)(2,1)S(1)} %get-tuple-element.191), channel_id=1, source_target_pairs={{0,8},{4,12},{8,0},{12,4},{1,9},{5,13},{9,1},{13,5},{2,10},{6,14},... | collective-permute-start | bytes 1572872 | tf_op jit(solution)/shard_map/ppermute | solution.py:329
  365.1 90.1 %collective-permute-start.40 = (bf16[16,2,64,128]{3,2,1,0:T(8,128)(2,1)S(1)}, bf16[16,2,64,128]{3,2,1,0:T(8,128)(2,1)S(1)}, u32[]{:S(2)}, u32[]{:S(2)}) collective-permute-start(bf16[16,2,64,128]{3,2,1,0:T(8,128)(2,1)S(1)} %get-tuple-element.192), channel_id=1, source_target_pairs={{0,12},{4,0},{8,4},{12,8},{1,13},{5,1},{9,5},{13,9},{2,14},{6,2},{... | collective-permute-start | bytes 1572872 | tf_op jit(solution)/shard_map/ppermute | solution.py:329
  414.3 85.6 %collective-permute-start.42 = (bf16[16,2,64,128]{3,2,1,0:T(8,128)(2,1)S(1)}, bf16[16,2,64,128]{3,2,1,0:T(8,128)(2,1)S(1)}, u32[]{:S(2)}, u32[]{:S(2)}) collective-permute-start(bf16[16,2,64,128]{3,2,1,0:T(8,128)(2,1)S(1)} %get-tuple-element.198), channel_id=1, source_target_pairs={{0,8},{4,12},{8,0},{12,4},{1,9},{5,13},{9,1},{13,5},{2,10},{6,14},... | collective-permute-start | bytes 1572872 | tf_op jit(solution)/shard_map/ppermute | solution.py:329
  415.8 84.1 %collective-permute-start.43 = (bf16[16,2,64,128]{3,2,1,0:T(8,128)(2,1)S(1)}, bf16[16,2,64,128]{3,2,1,0:T(8,128)(2,1)S(1)}, u32[]{:S(2)}, u32[]{:S(2)}) collective-permute-start(bf16[16,2,64,128]{3,2,1,0:T(8,128)(2,1)S(1)} %get-tuple-element.199), channel_id=1, source_target_pairs={{0,12},{4,0},{8,4},{12,8},{1,13},{5,1},{9,5},{13,9},{2,14},{6,2},{... | collective-permute-start | bytes 1572872 | tf_op jit(solution)/shard_map/ppermute | solution.py:329
  455.2 67.2 %collective-permute-start.36 = (bf16[16,2,64,128]{3,2,1,0:T(8,128)(2,1)S(1)}, bf16[16,2,64,128]{3,2,1,0:T(8,128)(2,1)S(1)}, u32[]{:S(2)}, u32[]{:S(2)}) collective-permute-start(bf16[16,2,64,128]{3,2,1,0:T(8,128)(2,1)S(1)} %get-tuple-element.187), channel_id=1, source_target_pairs={{0,8},{4,12},{8,0},{12,4},{1,9},{5,13},{9,1},{13,5},{2,10},{6,14},... | collective-permute-start | bytes 1572872 | tf_op jit(solution)/shard_map/ppermute | solution.py:329
  470.1 72.4 %collective-permute-start.37 = (bf16[16,2,64,128]{3,2,1,0:T(8,128)(2,1)S(1)}, bf16[16,2,64,128]{3,2,1,0:T(8,128)(2,1)S(1)}, u32[]{:S(2)}, u32[]{:S(2)}) collective-permute-start(bf16[16,2,64,128]{3,2,1,0:T(8,128)(2,1)S(1)} %get-tuple-element.188), channel_id=1, source_target_pairs={{0,12},{4,0},{8,4},{12,8},{1,13},{5,1},{9,5},{13,9},{2,14},{6,2},{... | collective-permute-start | bytes 1572872 | tf_op jit(solution)/shard_map/ppermute | solution.py:329
  507.2 56.0 %collective-permute-start.47 = (bf16[16,2,64,128]{3,2,1,0:T(8,128)(2,1)S(1)}, bf16[16,2,64,128]{3,2,1,0:T(8,128)(2,1)S(1)}, u32[]{:S(2)}, u32[]{:S(2)}) collective-permute-start(bf16[16,2,64,128]{3,2,1,0:T(8,128)(2,1)S(1)} %get-tuple-element.209), channel_id=1, source_target_pairs={{0,4},{4,8},{8,12},{12,0},{1,5},{5,9},{9,13},{13,1},{2,6},{6,10},{... | collective-permute-start | bytes 1572872 | tf_op jit(solution)/shard_map/ppermute | solution.py:329
  507.2 63.3 %collective-permute-start.50 = (bf16[16,2,64,128]{3,2,1,0:T(8,128)(2,1)S(1)}, bf16[16,2,64,128]{3,2,1,0:T(8,128)(2,1)S(1)}, u32[]{:S(2)}, u32[]{:S(2)}) collective-permute-start(bf16[16,2,64,128]{3,2,1,0:T(8,128)(2,1)S(1)} %get-tuple-element.214), channel_id=1, source_target_pairs={{0,4},{4,8},{8,12},{12,0},{1,5},{5,9},{9,13},{13,1},{2,6},{6,10},{... | collective-permute-start | bytes 1572872 | tf_op jit(solution)/shard_map/ppermute | solution.py:329
  508.2 109.8 %collective-permute-start.51 = (bf16[16,2,64,128]{3,2,1,0:T(8,128)(2,1)S(1)}, bf16[16,2,64,128]{3,2,1,0:T(8,128)(2,1)S(1)}, u32[]{:S(2)}, u32[]{:S(2)}) collective-permute-start(bf16[16,2,64,128]{3,2,1,0:T(8,128)(2,1)S(1)} %get-tuple-element.215), channel_id=1, source_target_pairs={{0,8},{4,12},{8,0},{12,4},{1,9},{5,13},{9,1},{13,5},{2,10},{6,14},... | collective-permute-start | bytes 1572872 | tf_op jit(solution)/shard_map/ppermute | solution.py:329
  522.4 95.6 %collective-permute-start.52 = (bf16[16,2,64,128]{3,2,1,0:T(8,128)(2,1)S(1)}, bf16[16,2,64,128]{3,2,1,0:T(8,128)(2,1)S(1)}, u32[]{:S(2)}, u32[]{:S(2)}) collective-permute-start(bf16[16,2,64,128]{3,2,1,0:T(8,128)(2,1)S(1)} %get-tuple-element.216), channel_id=1, source_target_pairs={{0,12},{4,0},{8,4},{12,8},{1,13},{5,1},{9,5},{13,9},{2,14},{6,2},{... | collective-permute-start | bytes 1572872 | tf_op jit(solution)/shard_map/ppermute | solution.py:329
  542.5 92.3 %collective-permute-start.48 = (bf16[16,2,64,128]{3,2,1,0:T(8,128)(2,1)S(1)}, bf16[16,2,64,128]{3,2,1,0:T(8,128)(2,1)S(1)}, u32[]{:S(2)}, u32[]{:S(2)}) collective-permute-start(bf16[16,2,64,128]{3,2,1,0:T(8,128)(2,1)S(1)} %get-tuple-element.210), channel_id=1, source_target_pairs={{0,8},{4,12},{8,0},{12,4},{1,9},{5,13},{9,1},{13,5},{2,10},{6,14},... | collective-permute-start | bytes 1572872 | tf_op jit(solution)/shard_map/ppermute | solution.py:329
  563.1 71.7 %collective-permute-start.49 = (bf16[16,2,64,128]{3,2,1,0:T(8,128)(2,1)S(1)}, bf16[16,2,64,128]{3,2,1,0:T(8,128)(2,1)S(1)}, u32[]{:S(2)}, u32[]{:S(2)}) collective-permute-start(bf16[16,2,64,128]{3,2,1,0:T(8,128)(2,1)S(1)} %get-tuple-element.211), channel_id=1, source_target_pairs={{0,12},{4,0},{8,4},{12,8},{1,13},{5,1},{9,5},{13,9},{2,14},{6,2},{... | collective-permute-start | bytes 1572872 | tf_op jit(solution)/shard_map/ppermute | solution.py:329
  570.6 71.7 %collective-permute-start.44 = (bf16[16,2,64,128]{3,2,1,0:T(8,128)(2,1)S(1)}, bf16[16,2,64,128]{3,2,1,0:T(8,128)(2,1)S(1)}, u32[]{:S(2)}, u32[]{:S(2)}) collective-permute-start(bf16[16,2,64,128]{3,2,1,0:T(8,128)(2,1)S(1)} %get-tuple-element.205), channel_id=1, source_target_pairs={{0,4},{4,8},{8,12},{12,0},{1,5},{5,9},{9,13},{13,1},{2,6},{6,10},{... | collective-permute-start | bytes 1572872 | tf_op jit(solution)/shard_map/ppermute | solution.py:329
  662.6 75.4 %collective-permute-start.62 = (bf16[16,2,64,128]{3,2,1,0:T(8,128)(2,1)S(1)}, bf16[16,2,64,128]{3,2,1,0:T(8,128)(2,1)S(1)}, u32[]{:S(2)}, u32[]{:S(2)}) collective-permute-start(bf16[16,2,64,128]{3,2,1,0:T(8,128)(2,1)S(1)} %get-tuple-element.233), channel_id=1, source_target_pairs={{0,4},{4,8},{8,12},{12,0},{1,5},{5,9},{9,13},{13,1},{2,6},{6,10},{... | collective-permute-start | bytes 1572872 | tf_op jit(solution)/shard_map/ppermute | solution.py:329
  665.6 76.3 %collective-permute-start.63 = (bf16[16,2,64,128]{3,2,1,0:T(8,128)(2,1)S(1)}, bf16[16,2,64,128]{3,2,1,0:T(8,128)(2,1)S(1)}, u32[]{:S(2)}, u32[]{:S(2)}) collective-permute-start(bf16[16,2,64,128]{3,2,1,0:T(8,128)(2,1)S(1)} %get-tuple-element.234), channel_id=1, source_target_pairs={{0,8},{4,12},{8,0},{12,4},{1,9},{5,13},{9,1},{13,5},{2,10},{6,14},... | collective-permute-start | bytes 1572872 | tf_op jit(solution)/shard_map/ppermute | solution.py:329
  666.1 76.9 %collective-permute-start.64 = (bf16[16,2,64,128]{3,2,1,0:T(8,128)(2,1)S(1)}, bf16[16,2,64,128]{3,2,1,0:T(8,128)(2,1)S(1)}, u32[]{:S(2)}, u32[]{:S(2)}) collective-permute-start(bf16[16,2,64,128]{3,2,1,0:T(8,128)(2,1)S(1)} %get-tuple-element.235), channel_id=1, source_target_pairs={{0,12},{4,0},{8,4},{12,8},{1,13},{5,1},{9,5},{13,9},{2,14},{6,2},{... | collective-permute-start | bytes 1572872 | tf_op jit(solution)/shard_map/ppermute | solution.py:329
  (52 other events, 1298.0 us)

commit v3 on v2

--- a/solution.py
+++ b/solution.py
@@ -132,15 +132,15 @@
     ]
 
 
-def synthesize(field, halo, tables, curvature, walk_off, order_map, me, b, count, span, after):
+def synthesize(field, halo, tables, curvature, walk_off, order_map, b, count, span, after):
     low, high, halo_at = halo
     parts, _, radial, _ = field.shape
     kinds, _, block, _ = tables.shape
     share = block // count
     base, groups = span[0] // ROWS, span[1] // ROWS
 
-    def kernel(map_ref, me_ref, x_ref, low_ref, high_ref, tab_ref, beta_ref, delta_ref, *refs):
-        outs, acc = refs[len(after) : len(after) + count], refs[-1]
+    def kernel(map_ref, x_ref, low_ref, high_ref, tab_ref, beta_ref, delta_ref, *refs):
+        o_ref, _, acc = refs[-3:]
         g = pl.program_id(0)
         beta = columns(beta_ref, b * block, block)
         delta = columns(delta_ref, b * block, block)
@@ -155,58 +155,51 @@
             )
             for c in range(parts):
                 acc[c, pl.ds(i, block, stride=ROWS), :] = points[:, c * LANES : (c + 1) * LANES]
-        for s in range(count):
-            owner = lax.rem(me_ref[0] + s, count)
+        for d in range(count):
             for q in range(share):
-                row = pl.multiple_of((owner * share + q) * ROWS, ROWS)
+                row = (d * share + q) * ROWS
                 for c in range(parts):
-                    outs[s][q, c] = acc[c, pl.ds(row, ROWS), :].astype(jnp.bfloat16)
-
-    piece = jax.ShapeDtypeStruct((share, parts, span[1], LANES), jnp.bfloat16)
+                    o_ref[d, q, c] = acc[c, row : row + ROWS, :].astype(jnp.bfloat16)
+
     size = parts * span[1] * block * LANES * 2
-    *pieces, done = pl.pallas_call(
+    return pl.pallas_call(
         kernel,
-        out_shape=[piece] * count + [token()],
+        out_shape=[
+            jax.ShapeDtypeStruct((count, share, parts, span[1], LANES), jnp.bfloat16),
+            token(),
+        ],
         grid_spec=pltpu.PrefetchScalarGridSpec(
-            num_scalar_prefetch=2,
+            num_scalar_prefetch=1,
             grid=(groups,),
             in_specs=radial_specs(parts, kinds, block, radial, b, halo_at, base)
             + anywhere(len(after)),
             out_specs=[
-                pl.BlockSpec((share, parts, ROWS, LANES), lambda g, *_: (0, 0, g, 0))
+                pl.BlockSpec((count, share, parts, ROWS, LANES), lambda g, *_: (0, 0, 0, g, 0))
             ]
-            * count
             + anywhere(1),
             scratch_shapes=[pltpu.VMEM((parts, block * ROWS, LANES), jnp.float32)],
         ),
         compiler_params=params(),
         cost_estimate=cost(2 * size * block, 2 * size),
         name="synthesize",
-    )(order_map, me, field, low, high, tables, curvature, walk_off, *after)
-    return pieces, done
-
-
-def kerr_step(pieces, spans, out_spans, forward, backward, me, after):
-    count = len(pieces[0])
-    share, parts = pieces[0][0].shape[:2]
+    )(order_map, field, low, high, tables, curvature, walk_off, *after)
+
+
+def kerr_step(pieces, spans, out_spans, forward, backward, after):
+    count, share, parts = pieces[0].shape[:3]
     orders = sum(size for _, size in spans)
     every = count * orders
     width = 2
-    ins_count, outs_count = count * len(spans), count * len(out_spans)
-
-    def kernel(me_ref, f_ref, b_ref, *refs):
-        ins = refs[:ins_count]
-        outs = refs[ins_count + len(after) : ins_count + len(after) + outs_count]
-        flat, back = refs[-2:]
+
+    def kernel(f_ref, b_ref, *refs):
+        ins, flat, back = refs[: len(spans)], refs[-2], refs[-1]
+        outs = refs[len(spans) + len(after) : -3]
         for k, (start, size) in enumerate(spans):
-            for s in range(count):
-                source = lax.rem(me_ref[0] + count - s, count)
+            for d in range(count):
                 for c in range(parts):
-                    row = pl.multiple_of(c * every + source * orders + start, ROWS)
+                    row = c * every + d * orders + start
                     for q in range(width):
-                        flat[pl.ds(row, size), q * LANES : (q + 1) * LANES] = ins[
-                            k * count + s
-                        ][q, c]
+                        flat[row : row + size, q * LANES : (q + 1) * LANES] = ins[k][d, q, c]
         angular = jnp.dot(f_ref[...], flat[...], preferred_element_type=jnp.float32)
         real, imag = angular[:every], angular[every:]
         power = kerr_gamma * (real * real + imag * imag)
@@ -215,71 +208,60 @@
             jnp.dot(b_ref[...], kerr, preferred_element_type=jnp.float32) * (1.0 / every)
         ).astype(jnp.bfloat16)
         for k, (start, size) in enumerate(out_spans):
-            for s in range(count):
-                owner = lax.rem(me_ref[0] + s, count)
+            for d in range(count):
                 for c in range(parts):
-                    row = pl.multiple_of(c * every + owner * orders + start, ROWS)
+                    row = c * every + d * orders + start
                     for q in range(width):
-                        outs[k * count + s][q, c] = back[
-                            pl.ds(row, size), q * LANES : (q + 1) * LANES
-                        ]
+                        outs[k][d, q, c] = back[row : row + size, q * LANES : (q + 1) * LANES]
 
     def blocks(some):
         return [
-            pl.BlockSpec((width, parts, size, LANES), lambda q, *_: (q, 0, 0, 0))
+            pl.BlockSpec((count, width, parts, size, LANES), lambda q: (0, q, 0, 0, 0))
             for _, size in some
-            for _ in range(count)
         ]
 
-    whole = pl.BlockSpec((parts * every, parts * every), lambda q, *_: (0, 0))
+    whole = pl.BlockSpec((parts * every, parts * every), lambda q: (0, 0))
     lanes = share * LANES
     *back, done = pl.pallas_call(
         kernel,
         out_shape=[
-            jax.ShapeDtypeStruct((share, parts, size, LANES), jnp.bfloat16)
+            jax.ShapeDtypeStruct((count, share, parts, size, LANES), jnp.bfloat16)
             for _, size in out_spans
-            for _ in range(count)
         ]
         + [token()],
-        grid_spec=pltpu.PrefetchScalarGridSpec(
-            num_scalar_prefetch=1,
-            grid=(share // width,),
-            in_specs=[whole, whole] + blocks(spans) + anywhere(len(after)),
-            out_specs=blocks(out_spans) + anywhere(1),
-            scratch_shapes=[
-                pltpu.VMEM((parts * every, width * LANES), jnp.bfloat16),
-                pltpu.VMEM((parts * every, width * LANES), jnp.bfloat16),
-            ],
-        ),
+        grid=(share // width,),
+        in_specs=[whole, whole] + blocks(spans) + anywhere(len(after)),
+        out_specs=blocks(out_spans) + anywhere(1),
+        scratch_shapes=[
+            pltpu.VMEM((parts * every, width * LANES), jnp.bfloat16),
+            pltpu.VMEM((parts * every, width * LANES), jnp.bfloat16),
+        ],
         compiler_params=params(),
         cost_estimate=cost(4 * (parts * every) ** 2 * lanes, 4 * parts * every * lanes),
         name="kerr",
-    )(me, forward, backward, *(piece for group in pieces for piece in group), *after)
-    return [back[k * count : (k + 1) * count] for k in range(len(out_spans))], done
-
-
-def analyze(
-    pieces, field, halo, tables, curvature, walk_off, order_map, me, b, span, out, after
-):
+    )(forward, backward, *pieces, *after)
+    return back, done
+
+
+def analyze(piece, field, halo, tables, curvature, walk_off, order_map, b, span, out, after):
     low, high, halo_at = halo
-    count = len(pieces)
+    count = piece.shape[0]
     parts, _, radial, _ = field.shape
     kinds, _, block, _ = tables.shape
     share = block // count
     base, groups = span[0] // ROWS, span[1] // ROWS
     held = () if out is None else (out,)
 
-    def kernel(map_ref, me_ref, *refs):
-        ins = refs[:count]
-        x_ref, low_ref, high_ref, tab_ref, beta_ref, delta_ref = refs[count : count + 6]
+    def kernel(
+        map_ref, p_ref, x_ref, low_ref, high_ref, tab_ref, beta_ref, delta_ref, *refs
+    ):
         o_ref, _, acc = refs[-3:]
         g = pl.program_id(0)
-        for s in range(count):
-            source = lax.rem(me_ref[0] + count - s, count)
+        for d in range(count):
             for q in range(share):
-                row = pl.multiple_of((source * share + q) * ROWS, ROWS)
+                row = (d * share + q) * ROWS
                 for c in range(parts):
-                    acc[c, pl.ds(row, ROWS), :] = ins[s][q, c].astype(jnp.float32)
+                    acc[c, row : row + ROWS, :] = p_ref[d, q, c].astype(jnp.float32)
         beta = columns(beta_ref, b * block, block)
         delta = columns(delta_ref, b * block, block)
         ends = [join_halo(low_ref[c], high_ref[c]) for c in range(parts)]
@@ -301,12 +283,11 @@
         kernel,
         out_shape=[jax.ShapeDtypeStruct(field.shape, field.dtype), token()],
         grid_spec=pltpu.PrefetchScalarGridSpec(
-            num_scalar_prefetch=2,
+            num_scalar_prefetch=1,
             grid=(groups,),
             in_specs=[
-                pl.BlockSpec((share, parts, ROWS, LANES), lambda g, *_: (0, 0, g, 0))
+                pl.BlockSpec((count, share, parts, ROWS, LANES), lambda g, *_: (0, 0, 0, g, 0))
             ]
-            * count
             + radial_specs(parts, kinds, block, radial, b, halo_at, base)
             + anywhere(len(held) + len(after)),
             out_specs=[
@@ -315,19 +296,15 @@
             + anywhere(1),
             scratch_shapes=[pltpu.VMEM((parts, block * ROWS, LANES), jnp.float32)],
         ),
-        input_output_aliases={2 + count + 6: 0} if held else {},
+        input_output_aliases={8: 0} if held else {},
         compiler_params=params(),
         cost_estimate=cost(2 * size * block, 3 * size),
         name="analyze",
-    )(
-        order_map, me, *pieces, field, low, high, tables, curvature, walk_off, *held, *after
-    )
+    )(order_map, piece, field, low, high, tables, curvature, walk_off, *held, *after)
 
 
 def exchange(pieces):
-    return [pieces[0]] + [
-        lax.ppermute(pieces[s], "ang", ring("ang", s)) for s in range(1, len(pieces))
-    ]
+    return lax.all_to_all(pieces, "ang", split_axis=0, concat_axis=0, tiled=True)
 
 
 def spans_of(sizes):
@@ -339,7 +316,6 @@
     count = lax.axis_size("ang")
     orders = field.shape[1]
     nblocks, block = radial_tables.shape[1:3]
-    me = lax.axis_index("ang").astype(jnp.int32).reshape(1)
     forward, backward = (jnp.asarray(table) for table in angle_matrices(ORDERS))
     scaled = radial_tables.astype(jnp.float32) * weights.reshape(nblocks, block)[None, :, :, None]
     analysis = scaled.astype(jnp.bfloat16).transpose(0, 1, 3, 2)
@@ -360,14 +336,14 @@
 
     def points(b, span, ends, after):
         own, done = synthesize(
-            field, ends, radial_tables, curvature, walk_off, order_map, me, b, count, span, after
+            field, ends, radial_tables, curvature, walk_off, order_map, b, count, span, after
         )
         sent.setdefault(b, []).append(exchange(own))
         return (done,)
 
     def turn(b, after):
         back, done = kerr_step(
-            sent.pop(b), spans.get(b, whole), out_spans.get(b, whole), forward, backward, me, after
+            sent.pop(b), spans.get(b, whole), out_spans.get(b, whole), forward, backward, after
         )
         returned[b] = [exchange(group) for group in back]
         return (done,)
@@ -375,7 +351,7 @@
     def finish(b, out, after):
         for span, group in zip(out_spans.get(b, whole), returned.pop(b), strict=True):
             out, done = analyze(
-                group, field, halos[b], analysis, curvature, walk_off, order_map, me, b, span,
+                group, field, halos[b], analysis, curvature, walk_off, order_map, b, span,
                 out, after,
             )
             after = (done,)

time: 777 us -> 885 us (1.14)
  starting transfers between devices: 322 us -> 95.4 us
  blocking collectives: 0 us -> 200 us
  waiting for transfers between devices: 220 us -> 329 us
  local copies, waits for them, and re-layouts: 9.07 us -> 37.6 us
    ppermute x57 -> x0, starting transfers between devices: 318 us -> none  [exchange(): lax.ppermute(pieces[s], 'ang', ring('ang', s))]
    all_to_all x0 -> x14, waiting for transfers between devices: none -> 315 us  [exchange(): lax.all_to_all(pieces, 'ang', split_axis=0, concat_axis=0, tiled=True)]
    ppermute x57 -> x0, waiting for transfers between devices: 210 us -> none  [exchange(): lax.ppermute(pieces[s], 'ang', ring('ang', s))]
    all_to_all x0 -> x5, blocking collectives: none -> 200 us  [exchange(): lax.all_to_all(pieces, 'ang', split_axis=0, concat_axis=0, tiled=True)]
    all_to_all x0 -> x14, starting transfers between devices: none -> 92.4 us  [exchange(): lax.all_to_all(pieces, 'ang', split_axis=0, concat_axis=0, tiled=True)]
    unnamed x39 -> x103, local copies, waits for them, and re-layouts: 9 us -> 37.5 us
  transfers between devices with their start and end apart: 65 -> 22, of which waited for: 18 -> 20; matrix products, arithmetic and copies ran while one was open for 1% -> 1% of each run, Pallas kernels for 25% -> 23%
where the time goes in v3:
time: 885 us; the launch traced here: 879 us
  waiting for transfers between devices  329 us (37%)
  Pallas kernels  215 us (24%)
  blocking collectives  200 us (23%)
  starting transfers between devices  95.4 us (11%)
  local copies, waits for them, and re-layouts  37.6 us (4%)
    all_to_all x14, waiting for transfers between devices, exchange(): lax.all_to_all(pieces, 'ang', split_axis=0, concat_axis=0, tiled=True)  315 us
    all_to_all x5, blocking collectives, exchange(): lax.all_to_all(pieces, 'ang', split_axis=0, concat_axis=0, tiled=True)  200 us
    all_to_all x14, starting transfers between devices, exchange(): lax.all_to_all(pieces, 'ang', split_axis=0, concat_axis=0, tiled=True)  92.4 us
    pallas_call x8, Pallas kernels, kerr_step(): pl.pallas_call(kernel, out_shape=[jax.ShapeDtypeStruct((count, share, par...  66.9 us
    pallas_call x10, Pallas kernels, analyze(): pl.pallas_call(kernel, out_shape=[jax.ShapeDtypeStruct(field.shape, field...  64.5 us
    pallas_call x9, Pallas kernels, synthesize(): pl.pallas_call(kernel, out_shape=[jax.ShapeDtypeStruct((count, share, par...  60.1 us
    unnamed x103, local copies, waits for them, and re-layouts  37.5 us
    pallas_call x4, Pallas kernels, edges(): pl.pallas_call(kernel, out_shape=[jax.ShapeDtypeStruct((parts, count * bl...  23.1 us
  transfers between devices with their start and end apart: 22, of which 20 were waited for; matrix products, arithmetic and copies ran while one was open for 1% of the time, Pallas kernels for 23%

profile of v3, /device:TPU:24, one launch (start us, length us, event | category | flops | bytes accessed | tf_op | source)
XLA Modules:
  0.0 879.2 jit_solution(10535356369437683855)
XLA Ops:
  49.2 19.0 %all-to-all-done.2.refs_1_ = bf16[4,16,2,48,128]{4,3,2,1,0:T(8,128)(2,1)} async-done(((bf16[4,16,2,48,128]{4,3,2,1,0:T(8,128)(2,1)}), bf16[4,16,2,48,128]{4,3,2,1,0:T(8,128)(2,1)}, u32[]{:S(2)}, u32[]{:S(2)}) %all-to-all-start.2) | async-done | bytes 1572896 | tf_op jit(solution)/shard_map/all_to_all | solution.py:307
  75.0 16.1 %edges.7 = (bf16[2,384,128]{2,1,0:T(8,128)(2,1)S(1)}, f32[8,128]{1,0:T(8,128)S(1)}) custom-call(bf16[2,64,512,128]{3,2,1,0:T(8,128)(2,1)} %x_ref.45, f32[8,128]{1,0:T(8,128)S(1)} %get-tuple-element.76.refs_0_), custom_call_target="tpu_custom_call" | custom-call | bytes 12582912 | tf_op jit(solution)/shard_map/edges/pallas_call | solution.py:79
  91.9 8.3 kerr.8
  101.5 19.0 %all-to-all-done.refs_0_ = bf16[4,16,2,64,128]{4,3,2,1,0:T(8,128)(2,1)} async-done(((bf16[4,16,2,64,128]{4,3,2,1,0:T(8,128)(2,1)}), bf16[4,16,2,64,128]{4,3,2,1,0:T(8,128)(2,1)}, u32[]{:S(2)}, u32[]{:S(2)}) %all-to-all-start) | async-done | bytes 2097184 | tf_op jit(solution)/shard_map/all_to_all | solution.py:307
  143.4 29.4 %all-to-all-done.4.p_ref = bf16[4,16,2,64,128]{4,3,2,1,0:T(8,128)(2,1)} async-done(((bf16[4,16,2,64,128]{4,3,2,1,0:T(8,128)(2,1)}), bf16[4,16,2,64,128]{4,3,2,1,0:T(8,128)(2,1)}, u32[]{:S(2)}, u32[]{:S(2)}) %all-to-all-start.4) | async-done | bytes 2097184 | tf_op jit(solution)/shard_map/all_to_all | solution.py:307
  181.7 8.3 kerr.9
  191.4 33.7 %all-to-all-done.5.refs_0_ = bf16[4,16,2,64,128]{4,3,2,1,0:T(8,128)(2,1)} async-done(((bf16[4,16,2,64,128]{4,3,2,1,0:T(8,128)(2,1)}), bf16[4,16,2,64,128]{4,3,2,1,0:T(8,128)(2,1)}, u32[]{:S(2)}, u32[]{:S(2)}) %all-to-all-start.5) | async-done | bytes 2097184 | tf_op jit(solution)/shard_map/all_to_all | solution.py:307
  236.7 7.6 analyze.10
  244.4 7.4 synthesize.13
  253.1 8.3 kerr.10
  262.9 14.4 %all-to-all-done.3.p_ref = bf16[4,16,2,64,128]{4,3,2,1,0:T(8,128)(2,1)} async-done(((bf16[4,16,2,64,128]{4,3,2,1,0:T(8,128)(2,1)}), bf16[4,16,2,64,128]{4,3,2,1,0:T(8,128)(2,1)}, u32[]{:S(2)}, u32[]{:S(2)}) %all-to-all-start.3) | async-done | bytes 2097184 | tf_op jit(solution)/shard_map/all_to_all | solution.py:307
  277.3 52.2 %all_to_all.95.p_ref = bf16[4,16,2,64,128]{4,3,2,1,0:T(8,128)(2,1)} all-to-all(bf16[4,16,2,64,128]{4,3,2,1,0:T(8,128)(2,1)} %copy-done.25), channel_id=1, replica_groups=mesh['groups'=2,'ang'=4,'tm'=4] {'ang'}, dimensions={0} | all-to-all | bytes 4194304 | tf_op jit(solution)/shard_map/all_to_all | solution.py:307
  336.2 7.6 analyze.11
  352.5 28.8 %all-to-all-done.8.refs_0_ = bf16[4,16,2,64,128]{4,3,2,1,0:T(8,128)(2,1)} async-done(((bf16[4,16,2,64,128]{4,3,2,1,0:T(8,128)(2,1)}), bf16[4,16,2,64,128]{4,3,2,1,0:T(8,128)(2,1)}, u32[]{:S(2)}, u32[]{:S(2)}) %all-to-all-start.8) | async-done | bytes 2097184 | tf_op jit(solution)/shard_map/all_to_all | solution.py:307
  390.1 8.3 kerr.11
  399.8 33.6 %all-to-all-done.6.refs_0_ = bf16[4,16,2,64,128]{4,3,2,1,0:T(8,128)(2,1)} async-done(((bf16[4,16,2,64,128]{4,3,2,1,0:T(8,128)(2,1)}), bf16[4,16,2,64,128]{4,3,2,1,0:T(8,128)(2,1)}, u32[]{:S(2)}, u32[]{:S(2)}) %all-to-all-start.6) | async-done | bytes 2097184 | tf_op jit(solution)/shard_map/all_to_all | solution.py:307
  449.2 7.4 synthesize.15
  457.9 27.8 %all-to-all-done.10.p_ref = bf16[4,16,2,64,128]{4,3,2,1,0:T(8,128)(2,1)} async-done(((bf16[4,16,2,64,128]{4,3,2,1,0:T(8,128)(2,1)}), bf16[4,16,2,64,128]{4,3,2,1,0:T(8,128)(2,1)}, u32[]{:S(2)}, u32[]{:S(2)}) %all-to-all-start.10) | async-done | bytes 2097184 | tf_op jit(solution)/shard_map/all_to_all | solution.py:307
  494.6 8.3 kerr.12
  504.3 33.6 %all-to-all-done.11.refs_0_ = bf16[4,16,2,64,128]{4,3,2,1,0:T(8,128)(2,1)} async-done(((bf16[4,16,2,64,128]{4,3,2,1,0:T(8,128)(2,1)}), bf16[4,16,2,64,128]{4,3,2,1,0:T(8,128)(2,1)}, u32[]{:S(2)}, u32[]{:S(2)}) %all-to-all-start.11) | async-done | bytes 2097184 | tf_op jit(solution)/shard_map/all_to_all | solution.py:307
  544.7 7.6 analyze.13
  561.0 8.3 kerr.13
  570.7 19.4 %all-to-all-done.9.p_ref = bf16[4,16,2,64,128]{4,3,2,1,0:T(8,128)(2,1)} async-done(((bf16[4,16,2,64,128]{4,3,2,1,0:T(8,128)(2,1)}), bf16[4,16,2,64,128]{4,3,2,1,0:T(8,128)(2,1)}, u32[]{:S(2)}, u32[]{:S(2)}) %all-to-all-start.9) | async-done | bytes 2097184 | tf_op jit(solution)/shard_map/all_to_all | solution.py:307
  590.1 52.1 %all_to_all.96.p_ref = bf16[4,16,2,64,128]{4,3,2,1,0:T(8,128)(2,1)} all-to-all(bf16[4,16,2,64,128]{4,3,2,1,0:T(8,128)(2,1)} %copy-done.26), channel_id=1, replica_groups=mesh['groups'=2,'ang'=4,'tm'=4] {'ang'}, dimensions={0} | all-to-all | bytes 4194304 | tf_op jit(solution)/shard_map/all_to_all | solution.py:307
  649.0 7.6 analyze.14
  665.5 28.6 %all-to-all-done.14.refs_0_ = bf16[4,16,2,64,128]{4,3,2,1,0:T(8,128)(2,1)} async-done(((bf16[4,16,2,64,128]{4,3,2,1,0:T(8,128)(2,1)}), bf16[4,16,2,64,128]{4,3,2,1,0:T(8,128)(2,1)}, u32[]{:S(2)}, u32[]{:S(2)}) %all-to-all-start.14) | async-done | bytes 2097184 | tf_op jit(solution)/shard_map/all_to_all | solution.py:307
  702.9 8.5 kerr.14
  720.1 26.2 %all-to-all-done.12.refs_0_ = bf16[4,16,2,64,128]{4,3,2,1,0:T(8,128)(2,1)} async-done(((bf16[4,16,2,64,128]{4,3,2,1,0:T(8,128)(2,1)}), bf16[4,16,2,64,128]{4,3,2,1,0:T(8,128)(2,1)}, u32[]{:S(2)}, u32[]{:S(2)}) %all-to-all-start.12) | async-done | bytes 2097184 | tf_op jit(solution)/shard_map/all_to_all | solution.py:307
  748.3 8.4 kerr.15
  756.7 17.3 %all_to_all.97.p_ref = bf16[4,16,2,16,128]{4,3,2,1,0:T(8,128)(2,1)} all-to-all(bf16[4,16,2,16,128]{4,3,2,1,0:T(8,128)(2,1)S(1)} %get-tuple-element.119), channel_id=1, replica_groups=mesh['groups'=2,'ang'=4,'tm'=4] {'ang'}, dimensions={0} | all-to-all | bytes 1048576 | tf_op jit(solution)/shard_map/all_to_all | solution.py:307
  774.1 27.9 %all_to_all.98.p_ref = bf16[4,16,2,32,128]{4,3,2,1,0:T(8,128)(2,1)} all-to-all(bf16[4,16,2,32,128]{4,3,2,1,0:T(8,128)(2,1)S(1)} %get-tuple-element.120), channel_id=1, replica_groups=mesh['groups'=2,'ang'=4,'tm'=4] {'ang'}, dimensions={0} | all-to-all | bytes 2097152 | tf_op jit(solution)/shard_map/all_to_all | solution.py:307
  802.0 50.5 %all_to_all.99.p_ref = bf16[4,16,2,64,128]{4,3,2,1,0:T(8,128)(2,1)} all-to-all(bf16[4,16,2,64,128]{4,3,2,1,0:T(8,128)(2,1)S(1)} %copy-done.18), channel_id=1, replica_groups=mesh['groups'=2,'ang'=4,'tm'=4] {'ang'}, dimensions={0} | all-to-all | bytes 4194304 | tf_op jit(solution)/shard_map/all_to_all | solution.py:307
  (153 shorter events, 237.0 us)
Async XLA Ops:
  1.2 4.0 collective-permute-start.3
  2.2 3.3 collective-permute-start.2
  9.3 17.8 %all-to-all-start.1 = ((bf16[4,16,2,16,128]{4,3,2,1,0:T(8,128)(2,1)}), bf16[4,16,2,16,128]{4,3,2,1,0:T(8,128)(2,1)S(1)}, u32[]{:S(2)}, u32[]{:S(2)}) async-start(bf16[4,16,2,16,128]{4,3,2,1,0:T(8,128)(2,1)} %copy-done.30), calls=%async_computation.1 | async-start | bytes 1048576 | tf_op jit(solution)/shard_map/all_to_all | solution.py:307
  14.4 2.6 collective-permute-start.1
  15.2 3.3 collective-permute-start
  27.1 41.1 %all-to-all-start.2 = ((bf16[4,16,2,48,128]{4,3,2,1,0:T(8,128)(2,1)}), bf16[4,16,2,48,128]{4,3,2,1,0:T(8,128)(2,1)}, u32[]{:S(2)}, u32[]{:S(2)}) async-start(bf16[4,16,2,48,128]{4,3,2,1,0:T(8,128)(2,1)} %copy-done.28), calls=%async_computation.2 | async-start | bytes 3145728 | tf_op jit(solution)/shard_map/all_to_all | solution.py:307
  36.6 2.2 collective-permute-start.5
  37.2 3.3 collective-permute-start.4
  68.2 52.2 %all-to-all-start = ((bf16[4,16,2,64,128]{4,3,2,1,0:T(8,128)(2,1)}), bf16[4,16,2,64,128]{4,3,2,1,0:T(8,128)(2,1)}, u32[]{:S(2)}, u32[]{:S(2)}) async-start(bf16[4,16,2,64,128]{4,3,2,1,0:T(8,128)(2,1)} %copy-done.21), calls=%async_computation | async-start | bytes 4194304 | tf_op jit(solution)/shard_map/all_to_all | solution.py:307
  75.0 16.8 %copy-start.34 = (bf16[512,512]{1,0:T(8,128)(2,1)S(1)}, bf16[512,512]{1,0:T(8,128)(2,1)}, u32[]{:S(2)}) copy-start(bf16[512,512]{1,0:T(8,128)(2,1)} %constant.5.clone.b_ref) | copy-start | bytes 1572868
  75.0 16.8 %copy-start.42 = (bf16[512,512]{1,0:T(8,128)(2,1)S(1)}, bf16[512,512]{1,0:T(8,128)(2,1)}, u32[]{:S(2)}) copy-start(bf16[512,512]{1,0:T(8,128)(2,1)} %constant.4.clone.f_ref) | copy-start | bytes 1572868
  120.5 52.3 %all-to-all-start.4 = ((bf16[4,16,2,64,128]{4,3,2,1,0:T(8,128)(2,1)}), bf16[4,16,2,64,128]{4,3,2,1,0:T(8,128)(2,1)}, u32[]{:S(2)}, u32[]{:S(2)}) async-start(bf16[4,16,2,64,128]{4,3,2,1,0:T(8,128)(2,1)} %copy-done.12), calls=%async_computation.4 | async-start | bytes 4194304 | tf_op jit(solution)/shard_map/all_to_all | solution.py:307
  127.4 4.6 collective-permute-start.7
  127.7 7.0 collective-permute-start.6
  172.8 52.2 %all-to-all-start.5 = ((bf16[4,16,2,64,128]{4,3,2,1,0:T(8,128)(2,1)}), bf16[4,16,2,64,128]{4,3,2,1,0:T(8,128)(2,1)}, u32[]{:S(2)}, u32[]{:S(2)}) async-start(bf16[4,16,2,64,128]{4,3,2,1,0:T(8,128)(2,1)} %copy-done.22), calls=%async_computation.5 | async-start | bytes 4194304 | tf_op jit(solution)/shard_map/all_to_all | solution.py:307
  225.1 52.2 %all-to-all-start.3 = ((bf16[4,16,2,64,128]{4,3,2,1,0:T(8,128)(2,1)}), bf16[4,16,2,64,128]{4,3,2,1,0:T(8,128)(2,1)}, u32[]{:S(2)}, u32[]{:S(2)}) async-start(bf16[4,16,2,64,128]{4,3,2,1,0:T(8,128)(2,1)} %copy-done.13), calls=%async_computation.3 | async-start | bytes 4194304 | tf_op jit(solution)/shard_map/all_to_all | solution.py:307
  244.4 8.7 copy-start.36
  244.4 8.7 copy-start.44
  329.4 51.8 %all-to-all-start.8 = ((bf16[4,16,2,64,128]{4,3,2,1,0:T(8,128)(2,1)}), bf16[4,16,2,64,128]{4,3,2,1,0:T(8,128)(2,1)}, u32[]{:S(2)}, u32[]{:S(2)}) async-start(bf16[4,16,2,64,128]{4,3,2,1,0:T(8,128)(2,1)} %copy-done.14), calls=%async_computation.8 | async-start | bytes 4194304 | tf_op jit(solution)/shard_map/all_to_all | solution.py:307
  381.2 52.2 %all-to-all-start.6 = ((bf16[4,16,2,64,128]{4,3,2,1,0:T(8,128)(2,1)}), bf16[4,16,2,64,128]{4,3,2,1,0:T(8,128)(2,1)}, u32[]{:S(2)}, u32[]{:S(2)}) async-start(bf16[4,16,2,64,128]{4,3,2,1,0:T(8,128)(2,1)} %copy-done.23), calls=%async_computation.6 | async-start | bytes 4194304 | tf_op jit(solution)/shard_map/all_to_all | solution.py:307
  433.4 52.2 %all-to-all-start.10 = ((bf16[4,16,2,64,128]{4,3,2,1,0:T(8,128)(2,1)}), bf16[4,16,2,64,128]{4,3,2,1,0:T(8,128)(2,1)}, u32[]{:S(2)}, u32[]{:S(2)}) async-start(bf16[4,16,2,64,128]{4,3,2,1,0:T(8,128)(2,1)} %copy-done.19), calls=%async_computation.10 | async-start | bytes 4194304 | tf_op jit(solution)/shard_map/all_to_all | solution.py:307
  485.6 52.2 %all-to-all-start.11 = ((bf16[4,16,2,64,128]{4,3,2,1,0:T(8,128)(2,1)}), bf16[4,16,2,64,128]{4,3,2,1,0:T(8,128)(2,1)}, u32[]{:S(2)}, u32[]{:S(2)}) async-start(bf16[4,16,2,64,128]{4,3,2,1,0:T(8,128)(2,1)} %copy-done.24), calls=%async_computation.11 | async-start | bytes 4194304 | tf_op jit(solution)/shard_map/all_to_all | solution.py:307
  537.9 52.2 %all-to-all-start.9 = ((bf16[4,16,2,64,128]{4,3,2,1,0:T(8,128)(2,1)}), bf16[4,16,2,64,128]{4,3,2,1,0:T(8,128)(2,1)}, u32[]{:S(2)}, u32[]{:S(2)}) async-start(bf16[4,16,2,64,128]{4,3,2,1,0:T(8,128)(2,1)} %copy-done.16), calls=%async_computation.9 | async-start | bytes 4194304 | tf_op jit(solution)/shard_map/all_to_all | solution.py:307
  544.7 7.6 copy-start.4
  552.3 8.6 copy-start.39
  552.3 8.6 copy-start.47
  642.2 51.8 %all-to-all-start.14 = ((bf16[4,16,2,64,128]{4,3,2,1,0:T(8,128)(2,1)}), bf16[4,16,2,64,128]{4,3,2,1,0:T(8,128)(2,1)}, u32[]{:S(2)}, u32[]{:S(2)}) async-start(bf16[4,16,2,64,128]{4,3,2,1,0:T(8,128)(2,1)} %copy-done.15), calls=%async_computation.14 | async-start | bytes 4194304 | tf_op jit(solution)/shard_map/all_to_all | solution.py:307
  694.0 52.2 %all-to-all-start.12 = ((bf16[4,16,2,64,128]{4,3,2,1,0:T(8,128)(2,1)}), bf16[4,16,2,64,128]{4,3,2,1,0:T(8,128)(2,1)}, u32[]{:S(2)}, u32[]{:S(2)}) async-start(bf16[4,16,2,64,128]{4,3,2,1,0:T(8,128)(2,1)} %copy-done.20), calls=%async_computation.12 | async-start | bytes 4194304 | tf_op jit(solution)/shard_map/all_to_all | solution.py:307
  702.9 9.8 %copy-start.9 = (bf16[4,16,2,64,128]{4,3,2,1,0:T(8,128)(2,1)S(1)}, bf16[4,16,2,64,128]{4,3,2,1,0:T(8,128)(2,1)}, u32[]{:S(2)}) copy-start(bf16[4,16,2,64,128]{4,3,2,1,0:T(8,128)(2,1)} %all_to_all.96.p_ref) | copy-start | bytes 6291460
  756.7 95.8 %copy-start.29 = (bf16[4,16,2,16,128]{4,3,2,1,0:T(8,128)(2,1)}, bf16[4,16,2,16,128]{4,3,2,1,0:T(8,128)(2,1)S(1)}, u32[]{:S(2)}) copy-start(bf16[4,16,2,16,128]{4,3,2,1,0:T(8,128)(2,1)S(1)} %get-tuple-element.118) | copy-start | bytes 1572868
  756.7 45.3 %copy-start.18 = (bf16[4,16,2,64,128]{4,3,2,1,0:T(8,128)(2,1)S(1)}, bf16[4,16,2,64,128]{4,3,2,1,0:T(8,128)(2,1)}, u32[]{:S(2)}) copy-start(bf16[4,16,2,64,128]{4,3,2,1,0:T(8,128)(2,1)} %copy-done.17) | copy-start | bytes 6291460
  852.5 23.1 %all-to-all-start.15 = ((bf16[4,16,2,16,128]{4,3,2,1,0:T(8,128)(2,1)}), bf16[4,16,2,16,128]{4,3,2,1,0:T(8,128)(2,1)S(1)}, u32[]{:S(2)}, u32[]{:S(2)}) async-start(bf16[4,16,2,16,128]{4,3,2,1,0:T(8,128)(2,1)} %copy-done.29), calls=%async_computation.15 | async-start | bytes 1048576 | tf_op jit(solution)/shard_map/all_to_all | solution.py:307
  (41 other events, 100.3 us)

commit v4 on v2

--- a/solution.py
+++ b/solution.py
@@ -344,9 +344,8 @@
     scaled = radial_tables.astype(jnp.float32) * weights.reshape(nblocks, block)[None, :, :, None]
     analysis = scaled.astype(jnp.bfloat16).transpose(0, 1, 3, 2)
     whole = spans_of([orders])
-    head = spans_of([ROWS, orders - ROWS]) if orders > ROWS else whole
-    tail = spans_of([orders // 2, orders // 4, orders // 4]) if orders % (4 * ROWS) == 0 else whole
-    spans = {0: head}
+    tail = spans_of([orders - ROWS, ROWS]) if orders > ROWS else whole
+    spans = {}
     out_spans = {nblocks - 1: tail}
     after = ()
     halos, sent, returned = {}, {}, {}
@@ -381,16 +380,16 @@
             after = (done,)
         return out, after
 
-    early, after = halo(0, 1, head[0], after)
     (halos[0],), after = halo(0, 1, whole[0], after)
-    for k, span in enumerate(head):
-        after = points(0, span, early[0] if k == 0 else halos[0], after)
+    after = points(0, whole[0], halos[0], after)
     (halos[1],), after = halo(1, 1, whole[0], after)
     after = points(1, whole[0], halos[1], after)
     if nblocks > 2:
         rest, after = halo(2, nblocks - 2, whole[0], after)
         halos.update(zip(range(2, nblocks), rest, strict=True))
     for b in range(nblocks):
+        if b >= nblocks - 1:
+            after = after + tuple(returned[b - 1][0][1:2])
         after = turn(b, after)
         if b >= 1:
             out, after = finish(b - 1, out, after)

time: 777 us -> 743 us (0.956); the launches traced: 763 us -> 742 us
  waiting for transfers between devices: 220 us -> 183 us
  starting transfers between devices: 322 us -> 350 us
    ppermute x57 -> x51, waiting for transfers between devices: 210 us -> 172 us  [exchange(): lax.ppermute(pieces[s], 'ang', ring('ang', s))]
    ppermute x57 -> x51, starting transfers between devices: 318 us -> 348 us  [exchange(): lax.ppermute(pieces[s], 'ang', ring('ang', s))]
    pallas_call x10 -> x9, Pallas kernels: 64.3 us -> 62.1 us  [analyze(): pl.pallas_call(kernel, out_shape=[jax.ShapeDtypeStruct(field.shape, field...]
    pallas_call x9 -> x8, Pallas kernels: 60.9 us -> 59.8 us  [synthesize(): pl.pallas_call(kernel, out_shape=[piece] * count + [token()], grid_spec=p...]
    pallas_call x4 -> x3, Pallas kernels: 23 us -> 22 us  [edges(): pl.pallas_call(kernel, out_shape=[jax.ShapeDtypeStruct((parts, count * bl...]
  transfers between devices with their start and end apart: 65 -> 57, of which waited for: 18 -> 20; matrix products, arithmetic and copies ran while one was open for 1% -> 0% of each run, Pallas kernels for 25% -> 26%
where the time goes in v4:
time: 743 us; the launch traced here: 742 us
  starting transfers between devices  350 us (47%)
  Pallas kernels  204 us (27%)
  waiting for transfers between devices  183 us (25%)
    ppermute x51, starting transfers between devices, exchange(): lax.ppermute(pieces[s], 'ang', ring('ang', s))  348 us
    ppermute x51, waiting for transfers between devices, exchange(): lax.ppermute(pieces[s], 'ang', ring('ang', s))  172 us
    pallas_call x9, Pallas kernels, analyze(): pl.pallas_call(kernel, out_shape=[jax.ShapeDtypeStruct(field.shape, field...  62.1 us
    pallas_call x8, Pallas kernels, kerr_step(): pl.pallas_call(kernel, out_shape=[jax.ShapeDtypeStruct((share, parts, siz...  59.9 us
    pallas_call x8, Pallas kernels, synthesize(): pl.pallas_call(kernel, out_shape=[piece] * count + [token()], grid_spec=p...  59.8 us
    pallas_call x3, Pallas kernels, edges(): pl.pallas_call(kernel, out_shape=[jax.ShapeDtypeStruct((parts, count * bl...  22 us
  transfers between devices with their start and end apart: 57, of which 20 were waited for; matrix products, arithmetic and copies ran while one was open for 0% of the time, Pallas kernels for 26%

profile of v4, /device:TPU:24, one launch (start us, length us, event | category | flops | bytes accessed | tf_op | source)
XLA Modules:
  0.0 741.6 jit_solution(1031981669396223874)
XLA Ops:
  23.3 8.0 %synthesize.9 = (bf16[16,2,64,128]{3,2,1,0:T(8,128)(2,1)S(1)}, bf16[16,2,64,128]{3,2,1,0:T(8,128)(2,1)}, bf16[16,2,64,128]{3,2,1,0:T(8,128)(2,1)}, bf16[16,2,64,128]{3,2,1,0:T(8,128)(2,1)}, f32[8,128]{1,0:T(8,128)S(1)}) custom-call(s32[64]{0:T(128)S(1)} %copy-done.3, s32[1]{0:T(128)} %bitcast.me_ref, bf16[2,64,512,128]{3,2,1,0:T(8,128)(2,1)} %refs_4_.17, ...), custom_call_target="tpu_custom_call" | custom-call | flops 268435456 | bytes 4194304 | tf_op jit(solution)/shard_map/synthesize/pallas_call | solution.py:167
  31.3 16.2 %edges.5 = (bf16[2,384,128]{2,1,0:T(8,128)(2,1)S(1)}, f32[8,128]{1,0:T(8,128)S(1)}) custom-call(bf16[2,64,512,128]{3,2,1,0:T(8,128)(2,1)} %refs_4_.17, f32[8,128]{1,0:T(8,128)S(1)} %get-tuple-element.117.refs_0_), custom_call_target="tpu_custom_call" | custom-call | bytes 12582912 | tf_op jit(solution)/shard_map/edges/pallas_call | solution.py:79
  51.5 11.7 %collective-permute-done.10.refs_2_ = bf16[16,2,64,128]{3,2,1,0:T(8,128)(2,1)S(1)} collective-permute-done((bf16[16,2,64,128]{3,2,1,0:T(8,128)(2,1)S(1)}, bf16[16,2,64,128]{3,2,1,0:T(8,128)(2,1)S(1)}, u32[]{:S(2)}, u32[]{:S(2)}) %collective-permute-start.10) | collective-permute-done | bytes 524320 | tf_op jit(solution)/shard_map/ppermute | solution.py:329
  63.2 8.0 %kerr.8 = (bf16[16,2,64,128]{3,2,1,0:T(8,128)(2,1)S(1)}, bf16[16,2,64,128]{3,2,1,0:T(8,128)(2,1)}, bf16[16,2,64,128]{3,2,1,0:T(8,128)(2,1)}, bf16[16,2,64,128]{3,2,1,0:T(8,128)(2,1)S(1)}, f32[8,128]{1,0:T(8,128)S(1)}) custom-call(s32[1]{0:T(128)} %bitcast.me_ref, bf16[512,512]{1,0:T(8,128)(2,1)S(1)} %copy-done.10, bf16[512,512]{1,0:T(8,128)(2,1)S(1)} %copy-done.8, ...), custom_call_target="tpu_custom_call" | custom-call | flops 2147483648 | bytes 4194304 | tf_op jit(solution)/shard_map/kerr/pallas_call | solution.py:236
  80.9 17.9 %collective-permute-start.16 = (bf16[16,2,64,128]{3,2,1,0:T(8,128)(2,1)}, bf16[16,2,64,128]{3,2,1,0:T(8,128)(2,1)}, u32[]{:S(2)}, u32[]{:S(2)}) collective-permute-start(bf16[16,2,64,128]{3,2,1,0:T(8,128)(2,1)} %get-tuple-element.136), channel_id=1, source_target_pairs={{0,8},{4,12},{8,0},{12,4},{1,9},{5,13},{9,1},{13,5},{2,10},{6,14},... | collective-permute-start | bytes 1572872 | tf_op jit(solution)/shard_map/ppermute | solution.py:329
  101.5 7.7 %synthesize.10 = (bf16[16,2,64,128]{3,2,1,0:T(8,128)(2,1)S(1)}, bf16[16,2,64,128]{3,2,1,0:T(8,128)(2,1)S(1)}, bf16[16,2,64,128]{3,2,1,0:T(8,128)(2,1)S(1)}, bf16...) custom-call(s32[64]{0:T(128)S(1)} %copy-done.3, s32[1]{0:T(128)} %bitcast.me_ref, bf16[2,64,512,128]{3,2,1,0:T(8,128)(2,1)} %refs_4_.17, ...), custom_call_target="tpu_custom_call" | custom-call | flops 268435456 | bytes 4194304 | tf_op jit(solution)/shard_map/synthesize/pallas_call | solution.py:167
  111.3 19.5 %collective-permute-done.7.refs_2_ = bf16[16,2,64,128]{3,2,1,0:T(8,128)(2,1)} collective-permute-done((bf16[16,2,64,128]{3,2,1,0:T(8,128)(2,1)}, bf16[16,2,64,128]{3,2,1,0:T(8,128)(2,1)}, u32[]{:S(2)}, u32[]{:S(2)}) %collective-permute-start.7) | collective-permute-done | bytes 524320 | tf_op jit(solution)/shard_map/ppermute | solution.py:329
  130.8 10.5 %collective-permute-start.19 = (bf16[16,2,64,128]{3,2,1,0:T(8,128)(2,1)S(1)}, bf16[16,2,64,128]{3,2,1,0:T(8,128)(2,1)S(1)}, u32[]{:S(2)}, u32[]{:S(2)}) collective-permute-start(bf16[16,2,64,128]{3,2,1,0:T(8,128)(2,1)S(1)} %get-tuple-element.142), channel_id=1, source_target_pairs={{0,8},{4,12},{8,0},{12,4},{1,9},{5,13},{9,1},{13,5},{2,10},{6,14},... | collective-permute-start | bytes 1572872 | tf_op jit(solution)/shard_map/ppermute | solution.py:329
  141.3 23.8 %collective-permute-start.20 = (bf16[16,2,64,128]{3,2,1,0:T(8,128)(2,1)S(1)}, bf16[16,2,64,128]{3,2,1,0:T(8,128)(2,1)S(1)}, u32[]{:S(2)}, u32[]{:S(2)}) collective-permute-start(bf16[16,2,64,128]{3,2,1,0:T(8,128)(2,1)S(1)} %get-tuple-element.143), channel_id=1, source_target_pairs={{0,12},{4,0},{8,4},{12,8},{1,13},{5,1},{9,5},{13,9},{2,14},{6,2},{... | collective-permute-start | bytes 1572872 | tf_op jit(solution)/shard_map/ppermute | solution.py:329
  165.1 8.3 %kerr.9 = (bf16[16,2,64,128]{3,2,1,0:T(8,128)(2,1)S(1)}, bf16[16,2,64,128]{3,2,1,0:T(8,128)(2,1)S(1)}, bf16[16,2,64,128]{3,2,1,0:T(8,128)(2,1)S(1)}, bf16[16,2,64,128]{3,2,1,0:T(8,128)(2,1)S(1)}, f32[8,128]{1,0:T(8,128)S(1)}) custom-call(s32[1]{0:T(128)} %bitcast.me_ref, bf16[512,512]{1,0:T(8,128)(2,1)S(1)} %copy-done.11, bf16[512,512]{1,0:T(8,128)(2,1)S(1)} %copy-done.9, ...), custom_call_target="tpu_custom_call" | custom-call | flops 2147483648 | bytes 4194304 | tf_op jit(solution)/shard_map/kerr/pallas_call | solution.py:236
  191.5 18.4 %collective-permute-start.14 = (bf16[16,2,64,128]{3,2,1,0:T(8,128)(2,1)S(1)}, bf16[16,2,64,128]{3,2,1,0:T(8,128)(2,1)S(1)}, u32[]{:S(2)}, u32[]{:S(2)}) collective-permute-start(bf16[16,2,64,128]{3,2,1,0:T(8,128)(2,1)S(1)} %get-tuple-element.133), channel_id=1, source_target_pairs={{0,12},{4,0},{8,4},{12,8},{1,13},{5,1},{9,5},{13,9},{2,14},{6,2},{... | collective-permute-start | bytes 1572872 | tf_op jit(solution)/shard_map/ppermute | solution.py:329
  209.9 10.7 %collective-permute-done.19.refs_2_ = bf16[16,2,64,128]{3,2,1,0:T(8,128)(2,1)S(1)} collective-permute-done((bf16[16,2,64,128]{3,2,1,0:T(8,128)(2,1)S(1)}, bf16[16,2,64,128]{3,2,1,0:T(8,128)(2,1)S(1)}, u32[]{:S(2)}, u32[]{:S(2)}) %collective-permute-start.19) | collective-permute-done | bytes 524320 | tf_op jit(solution)/shard_map/ppermute | solution.py:329
  231.4 11.7 %collective-permute-done.13.refs_2_ = bf16[16,2,64,128]{3,2,1,0:T(8,128)(2,1)S(1)} collective-permute-done((bf16[16,2,64,128]{3,2,1,0:T(8,128)(2,1)S(1)}, bf16[16,2,64,128]{3,2,1,0:T(8,128)(2,1)S(1)}, u32[]{:S(2)}, u32[]{:S(2)}) %collective-permute-start.13) | collective-permute-done | bytes 524320 | tf_op jit(solution)/shard_map/ppermute | solution.py:329
  243.1 19.9 %collective-permute-start.29 = (bf16[16,2,64,128]{3,2,1,0:T(8,128)(2,1)S(1)}, bf16[16,2,64,128]{3,2,1,0:T(8,128)(2,1)S(1)}, u32[]{:S(2)}, u32[]{:S(2)}) collective-permute-start(bf16[16,2,64,128]{3,2,1,0:T(8,128)(2,1)S(1)} %get-tuple-element.160), channel_id=1, source_target_pairs={{0,12},{4,0},{8,4},{12,8},{1,13},{5,1},{9,5},{13,9},{2,14},{6,2},{... | collective-permute-start | bytes 1572872 | tf_op jit(solution)/shard_map/ppermute | solution.py:329
  263.0 13.1 %collective-permute-start.25 = (bf16[16,2,64,128]{3,2,1,0:T(8,128)(2,1)S(1)}, bf16[16,2,64,128]{3,2,1,0:T(8,128)(2,1)S(1)}, u32[]{:S(2)}, u32[]{:S(2)}) collective-permute-start(bf16[16,2,64,128]{3,2,1,0:T(8,128)(2,1)S(1)} %get-tuple-element.154), channel_id=1, source_target_pairs={{0,8},{4,12},{8,0},{12,4},{1,9},{5,13},{9,1},{13,5},{2,10},{6,14},... | collective-permute-start | bytes 1572872 | tf_op jit(solution)/shard_map/ppermute | solution.py:329
  294.7 43.9 %collective-permute-done.28.refs_2_ = bf16[16,2,64,128]{3,2,1,0:T(8,128)(2,1)S(1)} collective-permute-done((bf16[16,2,64,128]{3,2,1,0:T(8,128)(2,1)S(1)}, bf16[16,2,64,128]{3,2,1,0:T(8,128)(2,1)S(1)}, u32[]{:S(2)}, u32[]{:S(2)}) %collective-permute-start.28) | collective-permute-done | bytes 524320 | tf_op jit(solution)/shard_map/ppermute | solution.py:329
  345.9 9.6 %collective-permute-done.25.refs_2_ = bf16[16,2,64,128]{3,2,1,0:T(8,128)(2,1)S(1)} collective-permute-done((bf16[16,2,64,128]{3,2,1,0:T(8,128)(2,1)S(1)}, bf16[16,2,64,128]{3,2,1,0:T(8,128)(2,1)S(1)}, u32[]{:S(2)}, u32[]{:S(2)}) %collective-permute-start.25) | collective-permute-done | bytes 524320 | tf_op jit(solution)/shard_map/ppermute | solution.py:329
  370.4 19.3 %collective-permute-start.35 = (bf16[16,2,64,128]{3,2,1,0:T(8,128)(2,1)S(1)}, bf16[16,2,64,128]{3,2,1,0:T(8,128)(2,1)S(1)}, u32[]{:S(2)}, u32[]{:S(2)}) collective-permute-start(bf16[16,2,64,128]{3,2,1,0:T(8,128)(2,1)S(1)} %get-tuple-element.172), channel_id=1, source_target_pairs={{0,12},{4,0},{8,4},{12,8},{1,13},{5,1},{9,5},{13,9},{2,14},{6,2},{... | collective-permute-start | bytes 1572872 | tf_op jit(solution)/shard_map/ppermute | solution.py:329
  389.8 10.7 %collective-permute-done.22.refs_2_ = bf16[16,2,64,128]{3,2,1,0:T(8,128)(2,1)S(1)} collective-permute-done((bf16[16,2,64,128]{3,2,1,0:T(8,128)(2,1)S(1)}, bf16[16,2,64,128]{3,2,1,0:T(8,128)(2,1)S(1)}, u32[]{:S(2)}, u32[]{:S(2)}) %collective-permute-start.22) | collective-permute-done | bytes 524320 | tf_op jit(solution)/shard_map/ppermute | solution.py:329
  407.8 26.9 %collective-permute-start.38 = (bf16[16,2,64,128]{3,2,1,0:T(8,128)(2,1)S(1)}, bf16[16,2,64,128]{3,2,1,0:T(8,128)(2,1)S(1)}, u32[]{:S(2)}, u32[]{:S(2)}) collective-permute-start(bf16[16,2,64,128]{3,2,1,0:T(8,128)(2,1)S(1)} %get-tuple-element.179), channel_id=1, source_target_pairs={{0,12},{4,0},{8,4},{12,8},{1,13},{5,1},{9,5},{13,9},{2,14},{6,2},{... | collective-permute-start | bytes 1572872 | tf_op jit(solution)/shard_map/ppermute | solution.py:329
  434.7 10.7 %collective-permute-done.34.refs_2_ = bf16[16,2,64,128]{3,2,1,0:T(8,128)(2,1)S(1)} collective-permute-done((bf16[16,2,64,128]{3,2,1,0:T(8,128)(2,1)S(1)}, bf16[16,2,64,128]{3,2,1,0:T(8,128)(2,1)S(1)}, u32[]{:S(2)}, u32[]{:S(2)}) %collective-permute-start.34) | collective-permute-done | bytes 524320 | tf_op jit(solution)/shard_map/ppermute | solution.py:329
  445.4 34.2 %collective-permute-start.32 = (bf16[16,2,64,128]{3,2,1,0:T(8,128)(2,1)S(1)}, bf16[16,2,64,128]{3,2,1,0:T(8,128)(2,1)S(1)}, u32[]{:S(2)}, u32[]{:S(2)}) collective-permute-start(bf16[16,2,64,128]{3,2,1,0:T(8,128)(2,1)S(1)} %get-tuple-element.168), channel_id=1, source_target_pairs={{0,12},{4,0},{8,4},{12,8},{1,13},{5,1},{9,5},{13,9},{2,14},{6,2},{... | collective-permute-start | bytes 1572872 | tf_op jit(solution)/shard_map/ppermute | solution.py:329
  496.0 28.6 %collective-permute-start.47 = (bf16[16,2,64,128]{3,2,1,0:T(8,128)(2,1)S(1)}, bf16[16,2,64,128]{3,2,1,0:T(8,128)(2,1)S(1)}, u32[]{:S(2)}, u32[]{:S(2)}) collective-permute-start(bf16[16,2,64,128]{3,2,1,0:T(8,128)(2,1)S(1)} %get-tuple-element.196), channel_id=1, source_target_pairs={{0,12},{4,0},{8,4},{12,8},{1,13},{5,1},{9,5},{13,9},{2,14},{6,2},{... | collective-permute-start | bytes 1572872 | tf_op jit(solution)/shard_map/ppermute | solution.py:329
  550.2 19.3 %collective-permute-start.44 = (bf16[16,2,64,128]{3,2,1,0:T(8,128)(2,1)S(1)}, bf16[16,2,64,128]{3,2,1,0:T(8,128)(2,1)S(1)}, u32[]{:S(2)}, u32[]{:S(2)}) collective-permute-start(bf16[16,2,64,128]{3,2,1,0:T(8,128)(2,1)S(1)} %get-tuple-element.191), channel_id=1, source_target_pairs={{0,12},{4,0},{8,4},{12,8},{1,13},{5,1},{9,5},{13,9},{2,14},{6,2},{... | collective-permute-start | bytes 1572872 | tf_op jit(solution)/shard_map/ppermute | solution.py:329
  569.5 10.7 %collective-permute-done.46.refs_2_ = bf16[16,2,64,128]{3,2,1,0:T(8,128)(2,1)S(1)} collective-permute-done((bf16[16,2,64,128]{3,2,1,0:T(8,128)(2,1)S(1)}, bf16[16,2,64,128]{3,2,1,0:T(8,128)(2,1)S(1)}, u32[]{:S(2)}, u32[]{:S(2)}) %collective-permute-start.46) | collective-permute-done | bytes 524320 | tf_op jit(solution)/shard_map/ppermute | solution.py:329
  587.5 26.9 %collective-permute-start.41 = (bf16[16,2,64,128]{3,2,1,0:T(8,128)(2,1)S(1)}, bf16[16,2,64,128]{3,2,1,0:T(8,128)(2,1)S(1)}, u32[]{:S(2)}, u32[]{:S(2)}) collective-permute-start(bf16[16,2,64,128]{3,2,1,0:T(8,128)(2,1)S(1)} %get-tuple-element.187), channel_id=1, source_target_pairs={{0,12},{4,0},{8,4},{12,8},{1,13},{5,1},{9,5},{13,9},{2,14},{6,2},{... | collective-permute-start | bytes 1572872 | tf_op jit(solution)/shard_map/ppermute | solution.py:329
  614.5 10.7 %collective-permute-done.43.refs_2_ = bf16[16,2,64,128]{3,2,1,0:T(8,128)(2,1)S(1)} collective-permute-done((bf16[16,2,64,128]{3,2,1,0:T(8,128)(2,1)S(1)}, bf16[16,2,64,128]{3,2,1,0:T(8,128)(2,1)S(1)}, u32[]{:S(2)}, u32[]{:S(2)}) %collective-permute-start.43) | collective-permute-done | bytes 524320 | tf_op jit(solution)/shard_map/ppermute | solution.py:329
  632.6 26.8 %collective-permute-start.56 = (bf16[16,2,64,128]{3,2,1,0:T(8,128)(2,1)S(1)}, bf16[16,2,64,128]{3,2,1,0:T(8,128)(2,1)S(1)}, u32[]{:S(2)}, u32[]{:S(2)}) collective-permute-start(bf16[16,2,64,128]{3,2,1,0:T(8,128)(2,1)S(1)} %get-tuple-element.211), channel_id=1, source_target_pairs={{0,12},{4,0},{8,4},{12,8},{1,13},{5,1},{9,5},{13,9},{2,14},{6,2},{... | collective-permute-start | bytes 1572872 | tf_op jit(solution)/shard_map/ppermute | solution.py:329
  659.4 10.7 %collective-permute-done.40.refs_2_ = bf16[16,2,64,128]{3,2,1,0:T(8,128)(2,1)S(1)} collective-permute-done((bf16[16,2,64,128]{3,2,1,0:T(8,128)(2,1)S(1)}, bf16[16,2,64,128]{3,2,1,0:T(8,128)(2,1)S(1)}, u32[]{:S(2)}, u32[]{:S(2)}) %collective-permute-start.40) | collective-permute-done | bytes 524320 | tf_op jit(solution)/shard_map/ppermute | solution.py:329
  677.4 13.2 %collective-permute-start.53 = (bf16[16,2,48,128]{3,2,1,0:T(8,128)(2,1)S(1)}, bf16[16,2,48,128]{3,2,1,0:T(8,128)(2,1)S(1)}, u32[]{:S(2)}, u32[]{:S(2)}) collective-permute-start(bf16[16,2,48,128]{3,2,1,0:T(8,128)(2,1)S(1)} %get-tuple-element.207), channel_id=1, source_target_pairs={{0,8},{4,12},{8,0},{12,4},{1,9},{5,13},{9,1},{13,5},{2,10},{6,14},... | collective-permute-start | bytes 1179656 | tf_op jit(solution)/shard_map/ppermute | solution.py:329
  695.8 15.9 %collective-permute-start.50 = (bf16[16,2,16,128]{3,2,1,0:T(8,128)(2,1)S(1)}, bf16[16,2,16,128]{3,2,1,0:T(8,128)(2,1)S(1)}, u32[]{:S(2)}, u32[]{:S(2)}) collective-permute-start(bf16[16,2,16,128]{3,2,1,0:T(8,128)(2,1)S(1)} %get-tuple-element.203), channel_id=1, source_target_pairs={{0,8},{4,12},{8,0},{12,4},{1,9},{5,13},{9,1},{13,5},{2,10},{6,14},... | collective-permute-start | bytes 393224 | tf_op jit(solution)/shard_map/ppermute | solution.py:329
  711.7 12.4 %collective-permute-start.51 = (bf16[16,2,16,128]{3,2,1,0:T(8,128)(2,1)S(1)}, bf16[16,2,16,128]{3,2,1,0:T(8,128)(2,1)S(1)}, u32[]{:S(2)}, u32[]{:S(2)}) collective-permute-start(bf16[16,2,16,128]{3,2,1,0:T(8,128)(2,1)S(1)} %get-tuple-element.204), channel_id=1, source_target_pairs={{0,12},{4,0},{8,4},{12,8},{1,13},{5,1},{9,5},{13,9},{2,14},{6,2},{... | collective-permute-start | bytes 393224 | tf_op jit(solution)/shard_map/ppermute | solution.py:329
  (141 shorter events, 205.2 us)
Async XLA Ops:
  47.9 61.3 %collective-permute-start.6 = (bf16[16,2,64,128]{3,2,1,0:T(8,128)(2,1)}, bf16[16,2,64,128]{3,2,1,0:T(8,128)(2,1)}, u32[]{:S(2)}, u32[]{:S(2)}) collective-permute-start(bf16[16,2,64,128]{3,2,1,0:T(8,128)(2,1)} %get-tuple-element.120), channel_id=1, source_target_pairs={{0,4},{4,8},{8,12},{12,0},{1,5},{5,9},{9,13},{13,1},{2,6},{6,10},{... | collective-permute-start | bytes 1572872 | tf_op jit(solution)/shard_map/ppermute | solution.py:329
  51.2 79.5 %collective-permute-start.7 = (bf16[16,2,64,128]{3,2,1,0:T(8,128)(2,1)}, bf16[16,2,64,128]{3,2,1,0:T(8,128)(2,1)}, u32[]{:S(2)}, u32[]{:S(2)}) collective-permute-start(bf16[16,2,64,128]{3,2,1,0:T(8,128)(2,1)} %get-tuple-element.121), channel_id=1, source_target_pairs={{0,8},{4,12},{8,0},{12,4},{1,9},{5,13},{9,1},{13,5},{2,10},{6,14},... | collective-permute-start | bytes 1572872 | tf_op jit(solution)/shard_map/ppermute | solution.py:329
  63.2 67.6 %collective-permute-start.8 = (bf16[16,2,64,128]{3,2,1,0:T(8,128)(2,1)}, bf16[16,2,64,128]{3,2,1,0:T(8,128)(2,1)}, u32[]{:S(2)}, u32[]{:S(2)}) collective-permute-start(bf16[16,2,64,128]{3,2,1,0:T(8,128)(2,1)} %get-tuple-element.122), channel_id=1, source_target_pairs={{0,12},{4,0},{8,4},{12,8},{1,13},{5,1},{9,5},{13,9},{2,14},{6,2},{... | collective-permute-start | bytes 1572872 | tf_op jit(solution)/shard_map/ppermute | solution.py:329
  72.0 69.3 %collective-permute-start.15 = (bf16[16,2,64,128]{3,2,1,0:T(8,128)(2,1)}, bf16[16,2,64,128]{3,2,1,0:T(8,128)(2,1)}, u32[]{:S(2)}, u32[]{:S(2)}) collective-permute-start(bf16[16,2,64,128]{3,2,1,0:T(8,128)(2,1)} %get-tuple-element.135), channel_id=1, source_target_pairs={{0,4},{4,8},{8,12},{12,0},{1,5},{5,9},{9,13},{13,1},{2,6},{6,10},{... | collective-permute-start | bytes 1572872 | tf_op jit(solution)/shard_map/ppermute | solution.py:329
  80.9 94.9 %collective-permute-start.16 = (bf16[16,2,64,128]{3,2,1,0:T(8,128)(2,1)}, bf16[16,2,64,128]{3,2,1,0:T(8,128)(2,1)}, u32[]{:S(2)}, u32[]{:S(2)}) collective-permute-start(bf16[16,2,64,128]{3,2,1,0:T(8,128)(2,1)} %get-tuple-element.136), channel_id=1, source_target_pairs={{0,8},{4,12},{8,0},{12,4},{1,9},{5,13},{9,1},{13,5},{2,10},{6,14},... | collective-permute-start | bytes 1572872 | tf_op jit(solution)/shard_map/ppermute | solution.py:329
  109.2 67.2 %collective-permute-start.17 = (bf16[16,2,64,128]{3,2,1,0:T(8,128)(2,1)S(1)}, bf16[16,2,64,128]{3,2,1,0:T(8,128)(2,1)S(1)}, u32[]{:S(2)}, u32[]{:S(2)}) collective-permute-start(bf16[16,2,64,128]{3,2,1,0:T(8,128)(2,1)S(1)} %copy-done.7), channel_id=1, source_target_pairs={{0,12},{4,0},{8,4},{12,8},{1,13},{5,1},{9,5},{13,9},{2,14},{6,2},{... | collective-permute-start | bytes 1572872 | tf_op jit(solution)/shard_map/ppermute | solution.py:329
  130.8 89.8 %collective-permute-start.19 = (bf16[16,2,64,128]{3,2,1,0:T(8,128)(2,1)S(1)}, bf16[16,2,64,128]{3,2,1,0:T(8,128)(2,1)S(1)}, u32[]{:S(2)}, u32[]{:S(2)}) collective-permute-start(bf16[16,2,64,128]{3,2,1,0:T(8,128)(2,1)S(1)} %get-tuple-element.142), channel_id=1, source_target_pairs={{0,8},{4,12},{8,0},{12,4},{1,9},{5,13},{9,1},{13,5},{2,10},{6,14},... | collective-permute-start | bytes 1572872 | tf_op jit(solution)/shard_map/ppermute | solution.py:329
  141.3 79.3 %collective-permute-start.20 = (bf16[16,2,64,128]{3,2,1,0:T(8,128)(2,1)S(1)}, bf16[16,2,64,128]{3,2,1,0:T(8,128)(2,1)S(1)}, u32[]{:S(2)}, u32[]{:S(2)}) collective-permute-start(bf16[16,2,64,128]{3,2,1,0:T(8,128)(2,1)S(1)} %get-tuple-element.143), channel_id=1, source_target_pairs={{0,12},{4,0},{8,4},{12,8},{1,13},{5,1},{9,5},{13,9},{2,14},{6,2},{... | collective-permute-start | bytes 1572872 | tf_op jit(solution)/shard_map/ppermute | solution.py:329
  176.4 66.7 %collective-permute-start.13 = (bf16[16,2,64,128]{3,2,1,0:T(8,128)(2,1)S(1)}, bf16[16,2,64,128]{3,2,1,0:T(8,128)(2,1)S(1)}, u32[]{:S(2)}, u32[]{:S(2)}) collective-permute-start(bf16[16,2,64,128]{3,2,1,0:T(8,128)(2,1)S(1)} %get-tuple-element.132), channel_id=1, source_target_pairs={{0,8},{4,12},{8,0},{12,4},{1,9},{5,13},{9,1},{13,5},{2,10},{6,14},... | collective-permute-start | bytes 1572872 | tf_op jit(solution)/shard_map/ppermute | solution.py:329
  191.5 71.5 %collective-permute-start.14 = (bf16[16,2,64,128]{3,2,1,0:T(8,128)(2,1)S(1)}, bf16[16,2,64,128]{3,2,1,0:T(8,128)(2,1)S(1)}, u32[]{:S(2)}, u32[]{:S(2)}) collective-permute-start(bf16[16,2,64,128]{3,2,1,0:T(8,128)(2,1)S(1)} %get-tuple-element.133), channel_id=1, source_target_pairs={{0,12},{4,0},{8,4},{12,8},{1,13},{5,1},{9,5},{13,9},{2,14},{6,2},{... | collective-permute-start | bytes 1572872 | tf_op jit(solution)/shard_map/ppermute | solution.py:329
  227.9 63.0 %collective-permute-start.27 = (bf16[16,2,64,128]{3,2,1,0:T(8,128)(2,1)S(1)}, bf16[16,2,64,128]{3,2,1,0:T(8,128)(2,1)S(1)}, u32[]{:S(2)}, u32[]{:S(2)}) collective-permute-start(bf16[16,2,64,128]{3,2,1,0:T(8,128)(2,1)S(1)} %get-tuple-element.158), channel_id=1, source_target_pairs={{0,4},{4,8},{8,12},{12,0},{1,5},{5,9},{9,13},{13,1},{2,6},{6,10},{... | collective-permute-start | bytes 1572872 | tf_op jit(solution)/shard_map/ppermute | solution.py:329
  228.9 109.8 %collective-permute-start.28 = (bf16[16,2,64,128]{3,2,1,0:T(8,128)(2,1)S(1)}, bf16[16,2,64,128]{3,2,1,0:T(8,128)(2,1)S(1)}, u32[]{:S(2)}, u32[]{:S(2)}) collective-permute-start(bf16[16,2,64,128]{3,2,1,0:T(8,128)(2,1)S(1)} %get-tuple-element.159), channel_id=1, source_target_pairs={{0,8},{4,12},{8,0},{12,4},{1,9},{5,13},{9,1},{13,5},{2,10},{6,14},... | collective-permute-start | bytes 1572872 | tf_op jit(solution)/shard_map/ppermute | solution.py:329
  243.1 95.6 %collective-permute-start.29 = (bf16[16,2,64,128]{3,2,1,0:T(8,128)(2,1)S(1)}, bf16[16,2,64,128]{3,2,1,0:T(8,128)(2,1)S(1)}, u32[]{:S(2)}, u32[]{:S(2)}) collective-permute-start(bf16[16,2,64,128]{3,2,1,0:T(8,128)(2,1)S(1)} %get-tuple-element.160), channel_id=1, source_target_pairs={{0,12},{4,0},{8,4},{12,8},{1,13},{5,1},{9,5},{13,9},{2,14},{6,2},{... | collective-permute-start | bytes 1572872 | tf_op jit(solution)/shard_map/ppermute | solution.py:329
  263.0 92.5 %collective-permute-start.25 = (bf16[16,2,64,128]{3,2,1,0:T(8,128)(2,1)S(1)}, bf16[16,2,64,128]{3,2,1,0:T(8,128)(2,1)S(1)}, u32[]{:S(2)}, u32[]{:S(2)}) collective-permute-start(bf16[16,2,64,128]{3,2,1,0:T(8,128)(2,1)S(1)} %get-tuple-element.154), channel_id=1, source_target_pairs={{0,8},{4,12},{8,0},{12,4},{1,9},{5,13},{9,1},{13,5},{2,10},{6,14},... | collective-permute-start | bytes 1572872 | tf_op jit(solution)/shard_map/ppermute | solution.py:329
  276.1 79.4 %collective-permute-start.26 = (bf16[16,2,64,128]{3,2,1,0:T(8,128)(2,1)S(1)}, bf16[16,2,64,128]{3,2,1,0:T(8,128)(2,1)S(1)}, u32[]{:S(2)}, u32[]{:S(2)}) collective-permute-start(bf16[16,2,64,128]{3,2,1,0:T(8,128)(2,1)S(1)} %get-tuple-element.155), channel_id=1, source_target_pairs={{0,12},{4,0},{8,4},{12,8},{1,13},{5,1},{9,5},{13,9},{2,14},{6,2},{... | collective-permute-start | bytes 1572872 | tf_op jit(solution)/shard_map/ppermute | solution.py:329
  290.9 79.5 %collective-permute-start.21 = (bf16[16,2,64,128]{3,2,1,0:T(8,128)(2,1)S(1)}, bf16[16,2,64,128]{3,2,1,0:T(8,128)(2,1)S(1)}, u32[]{:S(2)}, u32[]{:S(2)}) collective-permute-start(bf16[16,2,64,128]{3,2,1,0:T(8,128)(2,1)S(1)} %get-tuple-element.149), channel_id=1, source_target_pairs={{0,4},{4,8},{8,12},{12,0},{1,5},{5,9},{9,13},{13,1},{2,6},{6,10},{... | collective-permute-start | bytes 1572872 | tf_op jit(solution)/shard_map/ppermute | solution.py:329
  338.6 61.8 %collective-permute-start.22 = (bf16[16,2,64,128]{3,2,1,0:T(8,128)(2,1)S(1)}, bf16[16,2,64,128]{3,2,1,0:T(8,128)(2,1)S(1)}, u32[]{:S(2)}, u32[]{:S(2)}) collective-permute-start(bf16[16,2,64,128]{3,2,1,0:T(8,128)(2,1)S(1)} %get-tuple-element.150), channel_id=1, source_target_pairs={{0,8},{4,12},{8,0},{12,4},{1,9},{5,13},{9,1},{13,5},{2,10},{6,14},... | collective-permute-start | bytes 1572872 | tf_op jit(solution)/shard_map/ppermute | solution.py:329
  338.6 61.8 %collective-permute-start.23 = (bf16[16,2,64,128]{3,2,1,0:T(8,128)(2,1)S(1)}, bf16[16,2,64,128]{3,2,1,0:T(8,128)(2,1)S(1)}, u32[]{:S(2)}, u32[]{:S(2)}) collective-permute-start(bf16[16,2,64,128]{3,2,1,0:T(8,128)(2,1)S(1)} %get-tuple-element.151), channel_id=1, source_target_pairs={{0,12},{4,0},{8,4},{12,8},{1,13},{5,1},{9,5},{13,9},{2,14},{6,2},{... | collective-permute-start | bytes 1572872 | tf_op jit(solution)/shard_map/ppermute | solution.py:329
  355.5 89.9 %collective-permute-start.34 = (bf16[16,2,64,128]{3,2,1,0:T(8,128)(2,1)S(1)}, bf16[16,2,64,128]{3,2,1,0:T(8,128)(2,1)S(1)}, u32[]{:S(2)}, u32[]{:S(2)}) collective-permute-start(bf16[16,2,64,128]{3,2,1,0:T(8,128)(2,1)S(1)} %get-tuple-element.171), channel_id=1, source_target_pairs={{0,8},{4,12},{8,0},{12,4},{1,9},{5,13},{9,1},{13,5},{2,10},{6,14},... | collective-permute-start | bytes 1572872 | tf_op jit(solution)/shard_map/ppermute | solution.py:329
  370.4 75.0 %collective-permute-start.35 = (bf16[16,2,64,128]{3,2,1,0:T(8,128)(2,1)S(1)}, bf16[16,2,64,128]{3,2,1,0:T(8,128)(2,1)S(1)}, u32[]{:S(2)}, u32[]{:S(2)}) collective-permute-start(bf16[16,2,64,128]{3,2,1,0:T(8,128)(2,1)S(1)} %get-tuple-element.172), channel_id=1, source_target_pairs={{0,12},{4,0},{8,4},{12,8},{1,13},{5,1},{9,5},{13,9},{2,14},{6,2},{... | collective-permute-start | bytes 1572872 | tf_op jit(solution)/shard_map/ppermute | solution.py:329
  400.4 94.0 %collective-permute-start.37 = (bf16[16,2,64,128]{3,2,1,0:T(8,128)(2,1)S(1)}, bf16[16,2,64,128]{3,2,1,0:T(8,128)(2,1)S(1)}, u32[]{:S(2)}, u32[]{:S(2)}) collective-permute-start(bf16[16,2,64,128]{3,2,1,0:T(8,128)(2,1)S(1)} %get-tuple-element.178), channel_id=1, source_target_pairs={{0,8},{4,12},{8,0},{12,4},{1,9},{5,13},{9,1},{13,5},{2,10},{6,14},... | collective-permute-start | bytes 1572872 | tf_op jit(solution)/shard_map/ppermute | solution.py:329
  407.8 86.7 %collective-permute-start.38 = (bf16[16,2,64,128]{3,2,1,0:T(8,128)(2,1)S(1)}, bf16[16,2,64,128]{3,2,1,0:T(8,128)(2,1)S(1)}, u32[]{:S(2)}, u32[]{:S(2)}) collective-permute-start(bf16[16,2,64,128]{3,2,1,0:T(8,128)(2,1)S(1)} %get-tuple-element.179), channel_id=1, source_target_pairs={{0,12},{4,0},{8,4},{12,8},{1,13},{5,1},{9,5},{13,9},{2,14},{6,2},{... | collective-permute-start | bytes 1572872 | tf_op jit(solution)/shard_map/ppermute | solution.py:329
  445.4 89.9 %collective-permute-start.31 = (bf16[16,2,64,128]{3,2,1,0:T(8,128)(2,1)S(1)}, bf16[16,2,64,128]{3,2,1,0:T(8,128)(2,1)S(1)}, u32[]{:S(2)}, u32[]{:S(2)}) collective-permute-start(bf16[16,2,64,128]{3,2,1,0:T(8,128)(2,1)S(1)} %get-tuple-element.167), channel_id=1, source_target_pairs={{0,8},{4,12},{8,0},{12,4},{1,9},{5,13},{9,1},{13,5},{2,10},{6,14},... | collective-permute-start | bytes 1572872 | tf_op jit(solution)/shard_map/ppermute | solution.py:329
  445.4 89.9 %collective-permute-start.32 = (bf16[16,2,64,128]{3,2,1,0:T(8,128)(2,1)S(1)}, bf16[16,2,64,128]{3,2,1,0:T(8,128)(2,1)S(1)}, u32[]{:S(2)}, u32[]{:S(2)}) collective-permute-start(bf16[16,2,64,128]{3,2,1,0:T(8,128)(2,1)S(1)} %get-tuple-element.168), channel_id=1, source_target_pairs={{0,12},{4,0},{8,4},{12,8},{1,13},{5,1},{9,5},{13,9},{2,14},{6,2},{... | collective-permute-start | bytes 1572872 | tf_op jit(solution)/shard_map/ppermute | solution.py:329
  494.5 85.7 %collective-permute-start.46 = (bf16[16,2,64,128]{3,2,1,0:T(8,128)(2,1)S(1)}, bf16[16,2,64,128]{3,2,1,0:T(8,128)(2,1)S(1)}, u32[]{:S(2)}, u32[]{:S(2)}) collective-permute-start(bf16[16,2,64,128]{3,2,1,0:T(8,128)(2,1)S(1)} %get-tuple-element.195), channel_id=1, source_target_pairs={{0,8},{4,12},{8,0},{12,4},{1,9},{5,13},{9,1},{13,5},{2,10},{6,14},... | collective-permute-start | bytes 1572872 | tf_op jit(solution)/shard_map/ppermute | solution.py:329
  496.0 84.3 %collective-permute-start.47 = (bf16[16,2,64,128]{3,2,1,0:T(8,128)(2,1)S(1)}, bf16[16,2,64,128]{3,2,1,0:T(8,128)(2,1)S(1)}, u32[]{:S(2)}, u32[]{:S(2)}) collective-permute-start(bf16[16,2,64,128]{3,2,1,0:T(8,128)(2,1)S(1)} %get-tuple-element.196), channel_id=1, source_target_pairs={{0,12},{4,0},{8,4},{12,8},{1,13},{5,1},{9,5},{13,9},{2,14},{6,2},{... | collective-permute-start | bytes 1572872 | tf_op jit(solution)/shard_map/ppermute | solution.py:329
  535.3 89.9 %collective-permute-start.43 = (bf16[16,2,64,128]{3,2,1,0:T(8,128)(2,1)S(1)}, bf16[16,2,64,128]{3,2,1,0:T(8,128)(2,1)S(1)}, u32[]{:S(2)}, u32[]{:S(2)}) collective-permute-start(bf16[16,2,64,128]{3,2,1,0:T(8,128)(2,1)S(1)} %get-tuple-element.190), channel_id=1, source_target_pairs={{0,8},{4,12},{8,0},{12,4},{1,9},{5,13},{9,1},{13,5},{2,10},{6,14},... | collective-permute-start | bytes 1572872 | tf_op jit(solution)/shard_map/ppermute | solution.py:329
  550.2 74.9 %collective-permute-start.44 = (bf16[16,2,64,128]{3,2,1,0:T(8,128)(2,1)S(1)}, bf16[16,2,64,128]{3,2,1,0:T(8,128)(2,1)S(1)}, u32[]{:S(2)}, u32[]{:S(2)}) collective-permute-start(bf16[16,2,64,128]{3,2,1,0:T(8,128)(2,1)S(1)} %get-tuple-element.191), channel_id=1, source_target_pairs={{0,12},{4,0},{8,4},{12,8},{1,13},{5,1},{9,5},{13,9},{2,14},{6,2},{... | collective-permute-start | bytes 1572872 | tf_op jit(solution)/shard_map/ppermute | solution.py:329
  580.2 89.9 %collective-permute-start.40 = (bf16[16,2,64,128]{3,2,1,0:T(8,128)(2,1)S(1)}, bf16[16,2,64,128]{3,2,1,0:T(8,128)(2,1)S(1)}, u32[]{:S(2)}, u32[]{:S(2)}) collective-permute-start(bf16[16,2,64,128]{3,2,1,0:T(8,128)(2,1)S(1)} %get-tuple-element.186), channel_id=1, source_target_pairs={{0,8},{4,12},{8,0},{12,4},{1,9},{5,13},{9,1},{13,5},{2,10},{6,14},... | collective-permute-start | bytes 1572872 | tf_op jit(solution)/shard_map/ppermute | solution.py:329
  587.5 82.6 %collective-permute-start.41 = (bf16[16,2,64,128]{3,2,1,0:T(8,128)(2,1)S(1)}, bf16[16,2,64,128]{3,2,1,0:T(8,128)(2,1)S(1)}, u32[]{:S(2)}, u32[]{:S(2)}) collective-permute-start(bf16[16,2,64,128]{3,2,1,0:T(8,128)(2,1)S(1)} %get-tuple-element.187), channel_id=1, source_target_pairs={{0,12},{4,0},{8,4},{12,8},{1,13},{5,1},{9,5},{13,9},{2,14},{6,2},{... | collective-permute-start | bytes 1572872 | tf_op jit(solution)/shard_map/ppermute | solution.py:329
  625.2 70.6 %collective-permute-start.55 = (bf16[16,2,64,128]{3,2,1,0:T(8,128)(2,1)S(1)}, bf16[16,2,64,128]{3,2,1,0:T(8,128)(2,1)S(1)}, u32[]{:S(2)}, u32[]{:S(2)}) collective-permute-start(bf16[16,2,64,128]{3,2,1,0:T(8,128)(2,1)S(1)} %get-tuple-element.210), channel_id=1, source_target_pairs={{0,8},{4,12},{8,0},{12,4},{1,9},{5,13},{9,1},{13,5},{2,10},{6,14},... | collective-permute-start | bytes 1572872 | tf_op jit(solution)/shard_map/ppermute | solution.py:329
  632.6 63.1 %collective-permute-start.56 = (bf16[16,2,64,128]{3,2,1,0:T(8,128)(2,1)S(1)}, bf16[16,2,64,128]{3,2,1,0:T(8,128)(2,1)S(1)}, u32[]{:S(2)}, u32[]{:S(2)}) collective-permute-start(bf16[16,2,64,128]{3,2,1,0:T(8,128)(2,1)S(1)} %get-tuple-element.211), channel_id=1, source_target_pairs={{0,12},{4,0},{8,4},{12,8},{1,13},{5,1},{9,5},{13,9},{2,14},{6,2},{... | collective-permute-start | bytes 1572872 | tf_op jit(solution)/shard_map/ppermute | solution.py:329
  (39 other events, 1401.0 us)

commit v5 on v4

--- a/solution.py
+++ b/solution.py
@@ -132,15 +132,18 @@
     ]
 
 
-def synthesize(field, halo, tables, curvature, walk_off, order_map, me, b, count, span, after):
+def synthesize(
+    field, halo, tables, curvature, walk_off, order_map, me, b, count, span, after,
+    apart=(), held=(),
+):
     low, high, halo_at = halo
-    parts, _, radial, _ = field.shape
+    parts, orders, radial, _ = field.shape
     kinds, _, block, _ = tables.shape
     share = block // count
     base, groups = span[0] // ROWS, span[1] // ROWS
 
     def kernel(map_ref, me_ref, x_ref, low_ref, high_ref, tab_ref, beta_ref, delta_ref, *refs):
-        outs, acc = refs[len(after) : len(after) + count], refs[-1]
+        outs, acc = refs[-count - 2 : -2], refs[-1]
         g = pl.program_id(0)
         beta = columns(beta_ref, b * block, block)
         delta = columns(delta_ref, b * block, block)
@@ -162,51 +165,50 @@
                 for c in range(parts):
                     outs[s][q, c] = acc[c, pl.ds(row, ROWS), :].astype(jnp.bfloat16)
 
-    piece = jax.ShapeDtypeStruct((share, parts, span[1], LANES), jnp.bfloat16)
+    def piece(s):
+        room = span[1] if s in apart else orders
+        return jax.ShapeDtypeStruct((share, parts, room, LANES), jnp.bfloat16)
+
+    def place(s):
+        first = 0 if s in apart else base
+        return pl.BlockSpec((share, parts, ROWS, LANES), lambda g, *_: (0, 0, g + first, 0))
+
+    joined = [s for s in range(count) if s not in apart]
     size = parts * span[1] * block * LANES * 2
-    *pieces, done = pl.pallas_call(
+    return pl.pallas_call(
         kernel,
-        out_shape=[piece] * count + [token()],
+        out_shape=[piece(s) for s in range(count)] + [token()],
         grid_spec=pltpu.PrefetchScalarGridSpec(
             num_scalar_prefetch=2,
             grid=(groups,),
             in_specs=radial_specs(parts, kinds, block, radial, b, halo_at, base)
-            + anywhere(len(after)),
-            out_specs=[
-                pl.BlockSpec((share, parts, ROWS, LANES), lambda g, *_: (0, 0, g, 0))
-            ]
-            * count
-            + anywhere(1),
+            + anywhere(len(held) + len(after)),
+            out_specs=[place(s) for s in range(count)] + anywhere(1),
             scratch_shapes=[pltpu.VMEM((parts, block * ROWS, LANES), jnp.float32)],
         ),
+        input_output_aliases={8 + k: s for k, s in enumerate(joined)} if held else {},
         compiler_params=params(),
         cost_estimate=cost(2 * size * block, 2 * size),
         name="synthesize",
-    )(order_map, me, field, low, high, tables, curvature, walk_off, *after)
-    return pieces, done
-
-
-def kerr_step(pieces, spans, out_spans, forward, backward, me, after):
-    count = len(pieces[0])
+    )(order_map, me, field, low, high, tables, curvature, walk_off, *held, *after)
+
+
+def kerr_step(pieces, out_spans, forward, backward, me, count, after):
     share, parts = pieces[0][0].shape[:2]
-    orders = sum(size for _, size in spans)
+    orders = sum(size for _, size in out_spans)
     every = count * orders
     width = 2
-    ins_count, outs_count = count * len(spans), count * len(out_spans)
+    outs_count = count * len(out_spans)
 
     def kernel(me_ref, f_ref, b_ref, *refs):
-        ins = refs[:ins_count]
-        outs = refs[ins_count + len(after) : ins_count + len(after) + outs_count]
+        ins, outs = refs[: len(pieces)], refs[-outs_count - 3 : -3]
         flat, back = refs[-2:]
-        for k, (start, size) in enumerate(spans):
-            for s in range(count):
-                source = lax.rem(me_ref[0] + count - s, count)
-                for c in range(parts):
-                    row = pl.multiple_of(c * every + source * orders + start, ROWS)
-                    for q in range(width):
-                        flat[pl.ds(row, size), q * LANES : (q + 1) * LANES] = ins[
-                            k * count + s
-                        ][q, c]
+        for piece, (_, s, (start, size)) in zip(ins, pieces, strict=True):
+            source = lax.rem(me_ref[0] + count - s, count)
+            for c in range(parts):
+                row = pl.multiple_of(c * every + source * orders + start, ROWS)
+                for q in range(width):
+                    flat[pl.ds(row, size), q * LANES : (q + 1) * LANES] = piece[q, c]
         angular = jnp.dot(f_ref[...], flat[...], preferred_element_type=jnp.float32)
         real, imag = angular[:every], angular[every:]
         power = kerr_gamma * (real * real + imag * imag)
@@ -224,12 +226,8 @@
                             pl.ds(row, size), q * LANES : (q + 1) * LANES
                         ]
 
-    def blocks(some):
-        return [
-            pl.BlockSpec((width, parts, size, LANES), lambda q, *_: (q, 0, 0, 0))
-            for _, size in some
-            for _ in range(count)
-        ]
+    def rows(size):
+        return pl.BlockSpec((width, parts, size, LANES), lambda q, *_: (q, 0, 0, 0))
 
     whole = pl.BlockSpec((parts * every, parts * every), lambda q, *_: (0, 0))
     lanes = share * LANES
@@ -244,8 +242,10 @@
         grid_spec=pltpu.PrefetchScalarGridSpec(
             num_scalar_prefetch=1,
             grid=(share // width,),
-            in_specs=[whole, whole] + blocks(spans) + anywhere(len(after)),
-            out_specs=blocks(out_spans) + anywhere(1),
+            in_specs=[whole, whole]
+            + [rows(size) for _, _, (_, size) in pieces]
+            + anywhere(len(after)),
+            out_specs=[rows(size) for _, size in out_spans for _ in range(count)] + anywhere(1),
             scratch_shapes=[
                 pltpu.VMEM((parts * every, width * LANES), jnp.bfloat16),
                 pltpu.VMEM((parts * every, width * LANES), jnp.bfloat16),
@@ -254,7 +254,7 @@
         compiler_params=params(),
         cost_estimate=cost(4 * (parts * every) ** 2 * lanes, 4 * parts * every * lanes),
         name="kerr",
-    )(me, forward, backward, *(piece for group in pieces for piece in group), *after)
+    )(me, forward, backward, *(piece for piece, _, _ in pieces), *after)
     return [back[k * count : (k + 1) * count] for k in range(len(out_spans))], done
 
 
@@ -324,10 +324,27 @@
     )
 
 
+def gate(arrays, before):
+    def kernel(*refs):
+        pass
+
+    return pl.pallas_call(
+        kernel,
+        out_shape=[jax.ShapeDtypeStruct(x.shape, x.dtype) for x in arrays] + [token()],
+        in_specs=anywhere(len(arrays) + len(before)),
+        out_specs=anywhere(len(arrays) + 1),
+        input_output_aliases={k: k for k in range(len(arrays))},
+        compiler_params=params(),
+        name="gate",
+    )(*arrays, *before)
+
+
+def step(piece, s):
+    return lax.ppermute(piece, "ang", ring("ang", s)) if s else piece
+
+
 def exchange(pieces):
-    return [pieces[0]] + [
-        lax.ppermute(pieces[s], "ang", ring("ang", s)) for s in range(1, len(pieces))
-    ]
+    return [step(piece, s) for s, piece in enumerate(pieces)]
 
 
 def spans_of(sizes):
@@ -344,8 +361,7 @@
     scaled = radial_tables.astype(jnp.float32) * weights.reshape(nblocks, block)[None, :, :, None]
     analysis = scaled.astype(jnp.bfloat16).transpose(0, 1, 3, 2)
     whole = spans_of([orders])
-    tail = spans_of([orders - ROWS, ROWS]) if orders > ROWS else whole
-    spans = {}
+    tail = spans_of([orders - ROWS, ROWS])
     out_spans = {nblocks - 1: tail}
     after = ()
     halos, sent, returned = {}, {}, {}
@@ -357,16 +373,37 @@
         high = lax.ppermute(ends, "tm", ring("tm", -1))
         return [(low, high, j) for j in range(some)], (done,)
 
-    def points(b, span, ends, after):
-        own, done = synthesize(
-            field, ends, radial_tables, curvature, walk_off, order_map, me, b, count, span, after
+    def radial_points(b, span, ends, after, **how):
+        *own, done = synthesize(
+            field, ends, radial_tables, curvature, walk_off, order_map, me, b, count, span, after,
+            **how,
         )
-        sent.setdefault(b, []).append(exchange(own))
-        return (done,)
+        return own, (done,)
+
+    def points(b, after):
+        own, after = radial_points(b, whole[0], halos[b], after)
+        sent[b] = [(piece, s, whole[0]) for s, piece in enumerate(exchange(own))]
+        return after
+
+    def first_points(after):
+        early, late = (0, ROWS), (ROWS, orders - ROWS)
+        far = count // 2
+        (ends,), after = halo(0, 1, early, after)
+        (halos[0],), after = halo(0, 1, whole[0], after)
+        own, after = radial_points(0, early, ends, after, apart=(far,))
+        ahead = step(own.pop(far), far)
+        own, after = radial_points(0, late, halos[0], after, apart=(far,), held=tuple(own))
+        *own, done = gate(own, (ahead,) + after)
+        after = (done,)
+        sent[0] = [
+            (piece, s, late if s == far else whole[0]) for s, piece in enumerate(exchange(own))
+        ]
+        sent[0].append((ahead, far, early))
+        return after
 
     def turn(b, after):
         back, done = kerr_step(
-            sent.pop(b), spans.get(b, whole), out_spans.get(b, whole), forward, backward, me, after
+            sent.pop(b), out_spans.get(b, whole), forward, backward, me, count, after
         )
         returned[b] = [exchange(group) for group in back]
         return (done,)
@@ -380,10 +417,9 @@
             after = (done,)
         return out, after
 
-    (halos[0],), after = halo(0, 1, whole[0], after)
-    after = points(0, whole[0], halos[0], after)
+    after = first_points(after)
     (halos[1],), after = halo(1, 1, whole[0], after)
-    after = points(1, whole[0], halos[1], after)
+    after = points(1, after)
     if nblocks > 2:
         rest, after = halo(2, nblocks - 2, whole[0], after)
         halos.update(zip(range(2, nblocks), rest, strict=True))
@@ -394,7 +430,7 @@
         if b >= 1:
             out, after = finish(b - 1, out, after)
         if b + 2 < nblocks:
-            after = points(b + 2, whole[0], halos[b + 2], after)
+            after = points(b + 2, after)
     out, after = finish(nblocks - 1, out, after)
     return out
 
@@ -460,8 +496,9 @@
     fits = (
         steps == LANES
         and orders % ROWS == 0
-        and 2 * orders <= LANES
+        and ROWS < orders <= LANES // 2
         and block % (2 * count) == 0
+        and count > 1
         and radial % LANES == 0
         and LANES % block == 0
         and nblocks >= 2

time: 743 us -> 748 us (level)
  starting transfers between devices: 350 us -> 236 us
  waiting for transfers between devices: 183 us -> 295 us
    ppermute x51 -> x52, starting transfers between devices: 348 us -> 234 us  [step(): return lax.ppermute(piece, 'ang', ring('ang', s)) if s else piece]
    ppermute x51 -> x52, waiting for transfers between devices: 172 us -> 284 us  [step(): return lax.ppermute(piece, 'ang', ring('ang', s)) if s else piece]
    pallas_call x8 -> x10, Pallas kernels: 59.8 us -> 61.3 us  [the longest x9 61.3 us: synthesize(): pl.pallas_call(kernel, out_shape=[piece(s) for s in range(count)] + [toke...]
    pallas_call x3 -> x4, Pallas kernels: 22 us -> 23.2 us  [edges(): pl.pallas_call(kernel, out_shape=[jax.ShapeDtypeStruct((parts, count * bl...]
  transfers between devices with their start and end apart: 57 -> 60, of which waited for: 20 -> 20; matrix products, arithmetic and copies ran while one was open for 0% -> 0% of each run, Pallas kernels for 26% -> 27%
where the time goes in v5:
time: 748 us; the launch traced here: 743 us
  waiting for transfers between devices  295 us (39%)
  starting transfers between devices  236 us (32%)
  Pallas kernels  206 us (28%)
    ppermute x52, waiting for transfers between devices, step(): return lax.ppermute(piece, 'ang', ring('ang', s)) if s else piece  284 us
    ppermute x52, starting transfers between devices, step(): return lax.ppermute(piece, 'ang', ring('ang', s)) if s else piece  234 us
    pallas_call x9, Pallas kernels, analyze(): pl.pallas_call(kernel, out_shape=[jax.ShapeDtypeStruct(field.shape, field...  62 us
    pallas_call x9, Pallas kernels, synthesize(): pl.pallas_call(kernel, out_shape=[piece(s) for s in range(count)] + [toke...  61.3 us
    pallas_call x8, Pallas kernels, kerr_step(): pl.pallas_call(kernel, out_shape=[jax.ShapeDtypeStruct((share, parts, siz...  59.9 us
    pallas_call x4, Pallas kernels, edges(): pl.pallas_call(kernel, out_shape=[jax.ShapeDtypeStruct((parts, count * bl...  23.2 us
  transfers between devices with their start and end apart: 60, of which 20 were waited for; matrix products, arithmetic and copies ran while one was open for 0% of the time, Pallas kernels for 27%

profile of v5, /device:TPU:24, one launch (start us, length us, event | category | flops | bytes accessed | tf_op | source)
XLA Modules:
  0.0 742.8 jit_solution(5358089797681907362)
XLA Ops:
  30.3 8.0 %synthesize.11 = (bf16[16,2,64,128]{3,2,1,0:T(8,128)(2,1)S(1)}, bf16[16,2,64,128]{3,2,1,0:T(8,128)(2,1)}, bf16[16,2,64,128]{3,2,1,0:T(8,128)(2,1)}, bf16[16,2,64,128]{3,2,1,0:T(8,128)(2,1)}, f32[8,128]{1,0:T(8,128)S(1)}) custom-call(s32[64]{0:T(128)S(1)} %copy-done.3, s32[1]{0:T(128)} %bitcast.me_ref, bf16[2,64,512,128]{3,2,1,0:T(8,128)(2,1)} %refs_4_.17, ...), custom_call_target="tpu_custom_call" | custom-call | flops 268435456 | bytes 4194304 | tf_op jit(solution)/shard_map/synthesize/pallas_call | solution.py:178
  38.3 16.2 %edges.7 = (bf16[2,384,128]{2,1,0:T(8,128)(2,1)S(1)}, f32[8,128]{1,0:T(8,128)S(1)}) custom-call(bf16[2,64,512,128]{3,2,1,0:T(8,128)(2,1)} %refs_4_.17, f32[8,128]{1,0:T(8,128)S(1)} %get-tuple-element.141.refs_0_), custom_call_target="tpu_custom_call" | custom-call | bytes 12582912 | tf_op jit(solution)/shard_map/edges/pallas_call | solution.py:79
  62.9 24.3 %collective-permute-start.11 = (bf16[16,2,64,128]{3,2,1,0:T(8,128)(2,1)}, bf16[16,2,64,128]{3,2,1,0:T(8,128)(2,1)}, u32[]{:S(2)}, u32[]{:S(2)}) collective-permute-start(bf16[16,2,64,128]{3,2,1,0:T(8,128)(2,1)} %get-tuple-element.146), channel_id=1, source_target_pairs={{0,12},{4,0},{8,4},{12,8},{1,13},{5,1},{9,5},{13,9},{2,14},{6,2},{... | collective-permute-start | bytes 1572872 | tf_op jit(solution)/shard_map/ppermute | solution.py:343
  87.2 8.1 %kerr.8 = (bf16[16,2,64,128]{3,2,1,0:T(8,128)(2,1)S(1)}, bf16[16,2,64,128]{3,2,1,0:T(8,128)(2,1)}, bf16[16,2,64,128]{3,2,1,0:T(8,128)(2,1)}, bf16[16,2,64,128]{3,2,1,0:T(8,128)(2,1)S(1)}, f32[8,128]{1,0:T(8,128)S(1)}) custom-call(s32[1]{0:T(128)} %bitcast.me_ref, bf16[512,512]{1,0:T(8,128)(2,1)S(1)} %copy-done.10, bf16[512,512]{1,0:T(8,128)(2,1)S(1)} %copy-done.8, ...), custom_call_target="tpu_custom_call" | custom-call | flops 2147483648 | bytes 4194304 | tf_op jit(solution)/shard_map/kerr/pallas_call | solution.py:234
  105.3 7.7 %synthesize.12 = (bf16[16,2,64,128]{3,2,1,0:T(8,128)(2,1)S(1)}, bf16[16,2,64,128]{3,2,1,0:T(8,128)(2,1)S(1)}, bf16[16,2,64,128]{3,2,1,0:T(8,128)(2,1)S(1)}, bf16...) custom-call(s32[64]{0:T(128)S(1)} %copy-done.3, s32[1]{0:T(128)} %bitcast.me_ref, bf16[2,64,512,128]{3,2,1,0:T(8,128)(2,1)} %refs_4_.17, ...), custom_call_target="tpu_custom_call" | custom-call | flops 268435456 | bytes 4194304 | tf_op jit(solution)/shard_map/synthesize/pallas_call | solution.py:178
  113.7 10.0 %collective-permute-start.21 = (bf16[16,2,64,128]{3,2,1,0:T(8,128)(2,1)S(1)}, bf16[16,2,64,128]{3,2,1,0:T(8,128)(2,1)S(1)}, u32[]{:S(2)}, u32[]{:S(2)}) collective-permute-start(bf16[16,2,64,128]{3,2,1,0:T(8,128)(2,1)S(1)} %get-tuple-element.165), channel_id=1, source_target_pairs={{0,4},{4,8},{8,12},{12,0},{1,5},{5,9},{9,13},{13,1},{2,6},{6,10},{... | collective-permute-start | bytes 1572872 | tf_op jit(solution)/shard_map/ppermute | solution.py:343
  123.7 28.7 %collective-permute-start.22 = (bf16[16,2,64,128]{3,2,1,0:T(8,128)(2,1)S(1)}, bf16[16,2,64,128]{3,2,1,0:T(8,128)(2,1)S(1)}, u32[]{:S(2)}, u32[]{:S(2)}) collective-permute-start(bf16[16,2,64,128]{3,2,1,0:T(8,128)(2,1)S(1)} %get-tuple-element.166), channel_id=1, source_target_pairs={{0,8},{4,12},{8,0},{12,4},{1,9},{5,13},{9,1},{13,5},{2,10},{6,14},... | collective-permute-start | bytes 1572872 | tf_op jit(solution)/shard_map/ppermute | solution.py:343
  152.4 8.3 %kerr.9 = (bf16[16,2,64,128]{3,2,1,0:T(8,128)(2,1)S(1)}, bf16[16,2,64,128]{3,2,1,0:T(8,128)(2,1)S(1)}, bf16[16,2,64,128]{3,2,1,0:T(8,128)(2,1)S(1)}, bf16[16,2,64,128]{3,2,1,0:T(8,128)(2,1)S(1)}, f32[8,128]{1,0:T(8,128)S(1)}) custom-call(s32[1]{0:T(128)} %bitcast.me_ref, bf16[512,512]{1,0:T(8,128)(2,1)S(1)} %copy-done.11, bf16[512,512]{1,0:T(8,128)(2,1)S(1)} %copy-done.9, ...), custom_call_target="tpu_custom_call" | custom-call | flops 2147483648 | bytes 4194304 | tf_op jit(solution)/shard_map/kerr/pallas_call | solution.py:234
  160.7 9.4 %collective-permute-start.15 = (bf16[16,2,64,128]{3,2,1,0:T(8,128)(2,1)S(1)}, bf16[16,2,64,128]{3,2,1,0:T(8,128)(2,1)S(1)}, u32[]{:S(2)}, u32[]{:S(2)}) collective-permute-start(bf16[16,2,64,128]{3,2,1,0:T(8,128)(2,1)S(1)} %get-tuple-element.155), channel_id=1, source_target_pairs={{0,4},{4,8},{8,12},{12,0},{1,5},{5,9},{9,13},{13,1},{2,6},{6,10},{... | collective-permute-start | bytes 1572872 | tf_op jit(solution)/shard_map/ppermute | solution.py:343
  170.8 20.8 %collective-permute-start.16 = (bf16[16,2,64,128]{3,2,1,0:T(8,128)(2,1)S(1)}, bf16[16,2,64,128]{3,2,1,0:T(8,128)(2,1)S(1)}, u32[]{:S(2)}, u32[]{:S(2)}) collective-permute-start(bf16[16,2,64,128]{3,2,1,0:T(8,128)(2,1)S(1)} %get-tuple-element.156), channel_id=1, source_target_pairs={{0,8},{4,12},{8,0},{12,4},{1,9},{5,13},{9,1},{13,5},{2,10},{6,14},... | collective-permute-start | bytes 1572872 | tf_op jit(solution)/shard_map/ppermute | solution.py:343
  191.6 7.5 %analyze.9 = (bf16[2,64,512,128]{3,2,1,0:T(8,128)(2,1)}, f32[8,128]{1,0:T(8,128)S(1)}) custom-call(s32[64]{0:T(128)S(1)} %copy-done.3, s32[1]{0:T(128)} %bitcast.me_ref, bf16[16,2,64,128]{3,2,1,0:T(8,128)(2,1)S(1)} %get-tuple-element.158.refs_0_, bf16[16,2,64,128]{3,2,1,0:T(8,128)(2,1)} %collective-permute-done.18.refs_1_, ...), custom_call_target="tpu_custom_call" | custom-call | flops 268435456 | bytes 6291456 | tf_op jit(solution)/shard_map/analyze/pallas_call | solution.py:300
  206.6 15.2 %collective-permute-done.22.refs_2_ = bf16[16,2,64,128]{3,2,1,0:T(8,128)(2,1)S(1)} collective-permute-done((bf16[16,2,64,128]{3,2,1,0:T(8,128)(2,1)S(1)}, bf16[16,2,64,128]{3,2,1,0:T(8,128)(2,1)S(1)}, u32[]{:S(2)}, u32[]{:S(2)}) %collective-permute-start.22) | collective-permute-done | bytes 524320 | tf_op jit(solution)/shard_map/ppermute | solution.py:343
  234.1 10.3 %collective-permute-done.16.refs_2_ = bf16[16,2,64,128]{3,2,1,0:T(8,128)(2,1)S(1)} collective-permute-done((bf16[16,2,64,128]{3,2,1,0:T(8,128)(2,1)S(1)}, bf16[16,2,64,128]{3,2,1,0:T(8,128)(2,1)S(1)}, u32[]{:S(2)}, u32[]{:S(2)}) %collective-permute-start.16) | collective-permute-done | bytes 524320 | tf_op jit(solution)/shard_map/ppermute | solution.py:343
  244.3 24.0 %collective-permute-start.32 = (bf16[16,2,64,128]{3,2,1,0:T(8,128)(2,1)S(1)}, bf16[16,2,64,128]{3,2,1,0:T(8,128)(2,1)S(1)}, u32[]{:S(2)}, u32[]{:S(2)}) collective-permute-start(bf16[16,2,64,128]{3,2,1,0:T(8,128)(2,1)S(1)} %get-tuple-element.184), channel_id=1, source_target_pairs={{0,12},{4,0},{8,4},{12,8},{1,13},{5,1},{9,5},{13,9},{2,14},{6,2},{... | collective-permute-start | bytes 1572872 | tf_op jit(solution)/shard_map/ppermute | solution.py:343
  268.4 13.1 %collective-permute-start.28 = (bf16[16,2,64,128]{3,2,1,0:T(8,128)(2,1)S(1)}, bf16[16,2,64,128]{3,2,1,0:T(8,128)(2,1)S(1)}, u32[]{:S(2)}, u32[]{:S(2)}) collective-permute-start(bf16[16,2,64,128]{3,2,1,0:T(8,128)(2,1)S(1)} %get-tuple-element.178), channel_id=1, source_target_pairs={{0,8},{4,12},{8,0},{12,4},{1,9},{5,13},{9,1},{13,5},{2,10},{6,14},... | collective-permute-start | bytes 1572872 | tf_op jit(solution)/shard_map/ppermute | solution.py:343
  300.1 22.9 %collective-permute-done.31.refs_2_ = bf16[16,2,64,128]{3,2,1,0:T(8,128)(2,1)S(1)} collective-permute-done((bf16[16,2,64,128]{3,2,1,0:T(8,128)(2,1)S(1)}, bf16[16,2,64,128]{3,2,1,0:T(8,128)(2,1)S(1)}, u32[]{:S(2)}, u32[]{:S(2)}) %collective-permute-start.31) | collective-permute-done | bytes 524320 | tf_op jit(solution)/shard_map/ppermute | solution.py:343
  331.8 24.9 %collective-permute-done.28.refs_2_ = bf16[16,2,64,128]{3,2,1,0:T(8,128)(2,1)S(1)} collective-permute-done((bf16[16,2,64,128]{3,2,1,0:T(8,128)(2,1)S(1)}, bf16[16,2,64,128]{3,2,1,0:T(8,128)(2,1)S(1)}, u32[]{:S(2)}, u32[]{:S(2)}) %collective-permute-start.28) | collective-permute-done | bytes 524320 | tf_op jit(solution)/shard_map/ppermute | solution.py:343
  360.2 7.5 %analyze.11 = (bf16[2,64,512,128]{3,2,1,0:T(8,128)(2,1)}, f32[8,128]{1,0:T(8,128)S(1)}) custom-call(s32[64]{0:T(128)S(1)} %copy-done.3, s32[1]{0:T(128)} %bitcast.me_ref, bf16[16,2,64,128]{3,2,1,0:T(8,128)(2,1)S(1)} %get-tuple-element.176.refs_0_, bf16[16,2,64,128]{3,2,1,0:T(8,128)(2,1)S(1)} %collective-permute-done.27.refs_1_, ...), custom_call_target="tpu_custom_call", output_to_operand_aliasing={{0}: (12, {})} | custom-call | flops 268435456 | bytes 6291456 | tf_op jit(solution)/shard_map/analyze/pallas_call | solution.py:300
  375.2 26.5 %collective-permute-done.25.refs_2_ = bf16[16,2,64,128]{3,2,1,0:T(8,128)(2,1)S(1)} collective-permute-done((bf16[16,2,64,128]{3,2,1,0:T(8,128)(2,1)S(1)}, bf16[16,2,64,128]{3,2,1,0:T(8,128)(2,1)S(1)}, u32[]{:S(2)}, u32[]{:S(2)}) %collective-permute-start.25) | collective-permute-done | bytes 524320 | tf_op jit(solution)/shard_map/ppermute | solution.py:343
  413.5 33.1 %collective-permute-done.37.refs_2_ = bf16[16,2,64,128]{3,2,1,0:T(8,128)(2,1)S(1)} collective-permute-done((bf16[16,2,64,128]{3,2,1,0:T(8,128)(2,1)S(1)}, bf16[16,2,64,128]{3,2,1,0:T(8,128)(2,1)S(1)}, u32[]{:S(2)}, u32[]{:S(2)}) %collective-permute-start.37) | collective-permute-done | bytes 524320 | tf_op jit(solution)/shard_map/ppermute | solution.py:343
  450.2 8.2 %collective-permute-start.35 = (bf16[16,2,64,128]{3,2,1,0:T(8,128)(2,1)S(1)}, bf16[16,2,64,128]{3,2,1,0:T(8,128)(2,1)S(1)}, u32[]{:S(2)}, u32[]{:S(2)}) collective-permute-start(bf16[16,2,64,128]{3,2,1,0:T(8,128)(2,1)S(1)} %get-tuple-element.192), channel_id=1, source_target_pairs={{0,12},{4,0},{8,4},{12,8},{1,13},{5,1},{9,5},{13,9},{2,14},{6,2},{... | collective-permute-start | bytes 1572872 | tf_op jit(solution)/shard_map/ppermute | solution.py:343
  458.4 7.5 %analyze.12 = (bf16[2,64,512,128]{3,2,1,0:T(8,128)(2,1)}, f32[8,128]{1,0:T(8,128)S(1)}) custom-call(s32[64]{0:T(128)S(1)} %copy-done.3, s32[1]{0:T(128)} %bitcast.me_ref, bf16[16,2,64,128]{3,2,1,0:T(8,128)(2,1)S(1)} %get-tuple-element.193.refs_0_, bf16[16,2,64,128]{3,2,1,0:T(8,128)(2,1)S(1)} %collective-permute-done.36.refs_1_, ...), custom_call_target="tpu_custom_call", output_to_operand_aliasing={{0}: (12, {})} | custom-call | flops 268435456 | bytes 6291456 | tf_op jit(solution)/shard_map/analyze/pallas_call | solution.py:300
  473.2 18.4 %collective-permute-done.40.refs_2_ = bf16[16,2,64,128]{3,2,1,0:T(8,128)(2,1)S(1)} collective-permute-done((bf16[16,2,64,128]{3,2,1,0:T(8,128)(2,1)S(1)}, bf16[16,2,64,128]{3,2,1,0:T(8,128)(2,1)S(1)}, u32[]{:S(2)}, u32[]{:S(2)}) %collective-permute-start.40) | collective-permute-done | bytes 524320 | tf_op jit(solution)/shard_map/ppermute | solution.py:343
  495.2 8.2 %collective-permute-start.50 = (bf16[16,2,64,128]{3,2,1,0:T(8,128)(2,1)S(1)}, bf16[16,2,64,128]{3,2,1,0:T(8,128)(2,1)S(1)}, u32[]{:S(2)}, u32[]{:S(2)}) collective-permute-start(bf16[16,2,64,128]{3,2,1,0:T(8,128)(2,1)S(1)} %get-tuple-element.220), channel_id=1, source_target_pairs={{0,12},{4,0},{8,4},{12,8},{1,13},{5,1},{9,5},{13,9},{2,14},{6,2},{... | collective-permute-start | bytes 1572872 | tf_op jit(solution)/shard_map/ppermute | solution.py:343
  510.6 25.9 %collective-permute-done.34.refs_2_ = bf16[16,2,64,128]{3,2,1,0:T(8,128)(2,1)S(1)} collective-permute-done((bf16[16,2,64,128]{3,2,1,0:T(8,128)(2,1)S(1)}, bf16[16,2,64,128]{3,2,1,0:T(8,128)(2,1)S(1)}, u32[]{:S(2)}, u32[]{:S(2)}) %collective-permute-start.34) | collective-permute-done | bytes 524320 | tf_op jit(solution)/shard_map/ppermute | solution.py:343
  540.2 7.5 %analyze.13 = (bf16[2,64,512,128]{3,2,1,0:T(8,128)(2,1)}, f32[8,128]{1,0:T(8,128)S(1)}) custom-call(s32[64]{0:T(128)S(1)} %copy-done.3, s32[1]{0:T(128)} %bitcast.me_ref, bf16[16,2,64,128]{3,2,1,0:T(8,128)(2,1)S(1)} %get-tuple-element.189.refs_0_, bf16[16,2,64,128]{3,2,1,0:T(8,128)(2,1)S(1)} %collective-permute-done.33.refs_1_, ...), custom_call_target="tpu_custom_call", output_to_operand_aliasing={{0}: (12, {})} | custom-call | flops 268435456 | bytes 6291456 | tf_op jit(solution)/shard_map/analyze/pallas_call | solution.py:300
  555.1 26.3 %collective-permute-done.49.refs_2_ = bf16[16,2,64,128]{3,2,1,0:T(8,128)(2,1)S(1)} collective-permute-done((bf16[16,2,64,128]{3,2,1,0:T(8,128)(2,1)S(1)}, bf16[16,2,64,128]{3,2,1,0:T(8,128)(2,1)S(1)}, u32[]{:S(2)}, u32[]{:S(2)}) %collective-permute-start.49) | collective-permute-done | bytes 524320 | tf_op jit(solution)/shard_map/ppermute | solution.py:343
  593.2 33.1 %collective-permute-done.46.refs_2_ = bf16[16,2,64,128]{3,2,1,0:T(8,128)(2,1)S(1)} collective-permute-done((bf16[16,2,64,128]{3,2,1,0:T(8,128)(2,1)S(1)}, bf16[16,2,64,128]{3,2,1,0:T(8,128)(2,1)S(1)}, u32[]{:S(2)}, u32[]{:S(2)}) %collective-permute-start.46) | collective-permute-done | bytes 524320 | tf_op jit(solution)/shard_map/ppermute | solution.py:343
  638.2 33.1 %collective-permute-done.43.refs_2_ = bf16[16,2,64,128]{3,2,1,0:T(8,128)(2,1)S(1)} collective-permute-done((bf16[16,2,64,128]{3,2,1,0:T(8,128)(2,1)S(1)}, bf16[16,2,64,128]{3,2,1,0:T(8,128)(2,1)S(1)}, u32[]{:S(2)}, u32[]{:S(2)}) %collective-permute-start.43) | collective-permute-done | bytes 524320 | tf_op jit(solution)/shard_map/ppermute | solution.py:343
  678.7 13.2 %collective-permute-start.56 = (bf16[16,2,48,128]{3,2,1,0:T(8,128)(2,1)S(1)}, bf16[16,2,48,128]{3,2,1,0:T(8,128)(2,1)S(1)}, u32[]{:S(2)}, u32[]{:S(2)}) collective-permute-start(bf16[16,2,48,128]{3,2,1,0:T(8,128)(2,1)S(1)} %get-tuple-element.231), channel_id=1, source_target_pairs={{0,8},{4,12},{8,0},{12,4},{1,9},{5,13},{9,1},{13,5},{2,10},{6,14},... | collective-permute-start | bytes 1179656 | tf_op jit(solution)/shard_map/ppermute | solution.py:343
  695.7 22.9 %collective-permute-start.53 = (bf16[16,2,16,128]{3,2,1,0:T(8,128)(2,1)S(1)}, bf16[16,2,16,128]{3,2,1,0:T(8,128)(2,1)S(1)}, u32[]{:S(2)}, u32[]{:S(2)}) collective-permute-start(bf16[16,2,16,128]{3,2,1,0:T(8,128)(2,1)S(1)} %get-tuple-element.227), channel_id=1, source_target_pairs={{0,8},{4,12},{8,0},{12,4},{1,9},{5,13},{9,1},{13,5},{2,10},{6,14},... | collective-permute-start | bytes 393224 | tf_op jit(solution)/shard_map/ppermute | solution.py:343
  720.4 7.5 %analyze.15 = (bf16[2,64,512,128]{3,2,1,0:T(8,128)(2,1)}, f32[8,128]{1,0:T(8,128)S(1)}) custom-call(s32[64]{0:T(128)S(1)} %copy-done.3, s32[1]{0:T(128)} %bitcast.me_ref, bf16[16,2,64,128]{3,2,1,0:T(8,128)(2,1)S(1)} %get-tuple-element.233.refs_0_, ...), custom_call_target="tpu_custom_call", output_to_operand_aliasing={{0}: (12, {})} | custom-call | flops 268435456 | bytes 6291456 | tf_op jit(solution)/shard_map/analyze/pallas_call | solution.py:300
  (150 shorter events, 204.1 us)
Async XLA Ops:
  21.9 65.3 %collective-permute-start.14 = (bf16[16,2,64,128]{3,2,1,0:T(8,128)(2,1)S(1)}, bf16[16,2,64,128]{3,2,1,0:T(8,128)(2,1)S(1)}, u32[]{:S(2)}, u32[]{:S(2)}) collective-permute-start(bf16[16,2,64,128]{3,2,1,0:T(8,128)(2,1)S(1)} %get-tuple-element.150), channel_id=1, source_target_pairs={{0,12},{4,0},{8,4},{12,8},{1,13},{5,1},{9,5},{13,9},{2,14},{6,2},{... | collective-permute-start | bytes 1572872 | tf_op jit(solution)/shard_map/ppermute | solution.py:343
  54.8 58.2 %collective-permute-start.9 = (bf16[16,2,64,128]{3,2,1,0:T(8,128)(2,1)}, bf16[16,2,64,128]{3,2,1,0:T(8,128)(2,1)}, u32[]{:S(2)}, u32[]{:S(2)}) collective-permute-start(bf16[16,2,64,128]{3,2,1,0:T(8,128)(2,1)} %get-tuple-element.144), channel_id=1, source_target_pairs={{0,4},{4,8},{8,12},{12,0},{1,5},{5,9},{9,13},{13,1},{2,6},{6,10},{... | collective-permute-start | bytes 1572872 | tf_op jit(solution)/shard_map/ppermute | solution.py:343
  62.9 60.7 %collective-permute-start.11 = (bf16[16,2,64,128]{3,2,1,0:T(8,128)(2,1)}, bf16[16,2,64,128]{3,2,1,0:T(8,128)(2,1)}, u32[]{:S(2)}, u32[]{:S(2)}) collective-permute-start(bf16[16,2,64,128]{3,2,1,0:T(8,128)(2,1)} %get-tuple-element.146), channel_id=1, source_target_pairs={{0,12},{4,0},{8,4},{12,8},{1,13},{5,1},{9,5},{13,9},{2,14},{6,2},{... | collective-permute-start | bytes 1572872 | tf_op jit(solution)/shard_map/ppermute | solution.py:343
  101.2 59.5 %collective-permute-start.19 = (bf16[16,2,64,128]{3,2,1,0:T(8,128)(2,1)}, bf16[16,2,64,128]{3,2,1,0:T(8,128)(2,1)}, u32[]{:S(2)}, u32[]{:S(2)}) collective-permute-start(bf16[16,2,64,128]{3,2,1,0:T(8,128)(2,1)} %get-tuple-element.160), channel_id=1, source_target_pairs={{0,8},{4,12},{8,0},{12,4},{1,9},{5,13},{9,1},{13,5},{2,10},{6,14},... | collective-permute-start | bytes 1572872 | tf_op jit(solution)/shard_map/ppermute | solution.py:343
  113.7 92.9 %collective-permute-start.21 = (bf16[16,2,64,128]{3,2,1,0:T(8,128)(2,1)S(1)}, bf16[16,2,64,128]{3,2,1,0:T(8,128)(2,1)S(1)}, u32[]{:S(2)}, u32[]{:S(2)}) collective-permute-start(bf16[16,2,64,128]{3,2,1,0:T(8,128)(2,1)S(1)} %get-tuple-element.165), channel_id=1, source_target_pairs={{0,4},{4,8},{8,12},{12,0},{1,5},{5,9},{9,13},{13,1},{2,6},{6,10},{... | collective-permute-start | bytes 1572872 | tf_op jit(solution)/shard_map/ppermute | solution.py:343
  123.7 98.2 %collective-permute-start.22 = (bf16[16,2,64,128]{3,2,1,0:T(8,128)(2,1)S(1)}, bf16[16,2,64,128]{3,2,1,0:T(8,128)(2,1)S(1)}, u32[]{:S(2)}, u32[]{:S(2)}) collective-permute-start(bf16[16,2,64,128]{3,2,1,0:T(8,128)(2,1)S(1)} %get-tuple-element.166), channel_id=1, source_target_pairs={{0,8},{4,12},{8,0},{12,4},{1,9},{5,13},{9,1},{13,5},{2,10},{6,14},... | collective-permute-start | bytes 1572872 | tf_op jit(solution)/shard_map/ppermute | solution.py:343
  152.4 69.5 %collective-permute-start.23 = (bf16[16,2,64,128]{3,2,1,0:T(8,128)(2,1)S(1)}, bf16[16,2,64,128]{3,2,1,0:T(8,128)(2,1)S(1)}, u32[]{:S(2)}, u32[]{:S(2)}) collective-permute-start(bf16[16,2,64,128]{3,2,1,0:T(8,128)(2,1)S(1)} %get-tuple-element.167), channel_id=1, source_target_pairs={{0,12},{4,0},{8,4},{12,8},{1,13},{5,1},{9,5},{13,9},{2,14},{6,2},{... | collective-permute-start | bytes 1572872 | tf_op jit(solution)/shard_map/ppermute | solution.py:343
  160.7 73.4 %collective-permute-start.15 = (bf16[16,2,64,128]{3,2,1,0:T(8,128)(2,1)S(1)}, bf16[16,2,64,128]{3,2,1,0:T(8,128)(2,1)S(1)}, u32[]{:S(2)}, u32[]{:S(2)}) collective-permute-start(bf16[16,2,64,128]{3,2,1,0:T(8,128)(2,1)S(1)} %get-tuple-element.155), channel_id=1, source_target_pairs={{0,4},{4,8},{8,12},{12,0},{1,5},{5,9},{9,13},{13,1},{2,6},{6,10},{... | collective-permute-start | bytes 1572872 | tf_op jit(solution)/shard_map/ppermute | solution.py:343
  170.8 73.6 %collective-permute-start.16 = (bf16[16,2,64,128]{3,2,1,0:T(8,128)(2,1)S(1)}, bf16[16,2,64,128]{3,2,1,0:T(8,128)(2,1)S(1)}, u32[]{:S(2)}, u32[]{:S(2)}) collective-permute-start(bf16[16,2,64,128]{3,2,1,0:T(8,128)(2,1)S(1)} %get-tuple-element.156), channel_id=1, source_target_pairs={{0,8},{4,12},{8,0},{12,4},{1,9},{5,13},{9,1},{13,5},{2,10},{6,14},... | collective-permute-start | bytes 1572872 | tf_op jit(solution)/shard_map/ppermute | solution.py:343
  206.5 61.8 %collective-permute-start.17 = (bf16[16,2,64,128]{3,2,1,0:T(8,128)(2,1)S(1)}, bf16[16,2,64,128]{3,2,1,0:T(8,128)(2,1)S(1)}, u32[]{:S(2)}, u32[]{:S(2)}) collective-permute-start(bf16[16,2,64,128]{3,2,1,0:T(8,128)(2,1)S(1)} %get-tuple-element.157), channel_id=1, source_target_pairs={{0,12},{4,0},{8,4},{12,8},{1,13},{5,1},{9,5},{13,9},{2,14},{6,2},{... | collective-permute-start | bytes 1572872 | tf_op jit(solution)/shard_map/ppermute | solution.py:343
  229.2 67.1 %collective-permute-start.30 = (bf16[16,2,64,128]{3,2,1,0:T(8,128)(2,1)S(1)}, bf16[16,2,64,128]{3,2,1,0:T(8,128)(2,1)S(1)}, u32[]{:S(2)}, u32[]{:S(2)}) collective-permute-start(bf16[16,2,64,128]{3,2,1,0:T(8,128)(2,1)S(1)} %get-tuple-element.182), channel_id=1, source_target_pairs={{0,4},{4,8},{8,12},{12,0},{1,5},{5,9},{9,13},{13,1},{2,6},{6,10},{... | collective-permute-start | bytes 1572872 | tf_op jit(solution)/shard_map/ppermute | solution.py:343
  234.1 89.0 %collective-permute-start.31 = (bf16[16,2,64,128]{3,2,1,0:T(8,128)(2,1)S(1)}, bf16[16,2,64,128]{3,2,1,0:T(8,128)(2,1)S(1)}, u32[]{:S(2)}, u32[]{:S(2)}) collective-permute-start(bf16[16,2,64,128]{3,2,1,0:T(8,128)(2,1)S(1)} %get-tuple-element.183), channel_id=1, source_target_pairs={{0,8},{4,12},{8,0},{12,4},{1,9},{5,13},{9,1},{13,5},{2,10},{6,14},... | collective-permute-start | bytes 1572872 | tf_op jit(solution)/shard_map/ppermute | solution.py:343
  244.3 78.8 %collective-permute-start.32 = (bf16[16,2,64,128]{3,2,1,0:T(8,128)(2,1)S(1)}, bf16[16,2,64,128]{3,2,1,0:T(8,128)(2,1)S(1)}, u32[]{:S(2)}, u32[]{:S(2)}) collective-permute-start(bf16[16,2,64,128]{3,2,1,0:T(8,128)(2,1)S(1)} %get-tuple-element.184), channel_id=1, source_target_pairs={{0,12},{4,0},{8,4},{12,8},{1,13},{5,1},{9,5},{13,9},{2,14},{6,2},{... | collective-permute-start | bytes 1572872 | tf_op jit(solution)/shard_map/ppermute | solution.py:343
  268.4 88.4 %collective-permute-start.28 = (bf16[16,2,64,128]{3,2,1,0:T(8,128)(2,1)S(1)}, bf16[16,2,64,128]{3,2,1,0:T(8,128)(2,1)S(1)}, u32[]{:S(2)}, u32[]{:S(2)}) collective-permute-start(bf16[16,2,64,128]{3,2,1,0:T(8,128)(2,1)S(1)} %get-tuple-element.178), channel_id=1, source_target_pairs={{0,8},{4,12},{8,0},{12,4},{1,9},{5,13},{9,1},{13,5},{2,10},{6,14},... | collective-permute-start | bytes 1572872 | tf_op jit(solution)/shard_map/ppermute | solution.py:343
  281.5 75.2 %collective-permute-start.29 = (bf16[16,2,64,128]{3,2,1,0:T(8,128)(2,1)S(1)}, bf16[16,2,64,128]{3,2,1,0:T(8,128)(2,1)S(1)}, u32[]{:S(2)}, u32[]{:S(2)}) collective-permute-start(bf16[16,2,64,128]{3,2,1,0:T(8,128)(2,1)S(1)} %get-tuple-element.179), channel_id=1, source_target_pairs={{0,12},{4,0},{8,4},{12,8},{1,13},{5,1},{9,5},{13,9},{2,14},{6,2},{... | collective-permute-start | bytes 1572872 | tf_op jit(solution)/shard_map/ppermute | solution.py:343
  296.3 78.9 %collective-permute-start.24 = (bf16[16,2,64,128]{3,2,1,0:T(8,128)(2,1)S(1)}, bf16[16,2,64,128]{3,2,1,0:T(8,128)(2,1)S(1)}, u32[]{:S(2)}, u32[]{:S(2)}) collective-permute-start(bf16[16,2,64,128]{3,2,1,0:T(8,128)(2,1)S(1)} %get-tuple-element.173), channel_id=1, source_target_pairs={{0,4},{4,8},{8,12},{12,0},{1,5},{5,9},{9,13},{13,1},{2,6},{6,10},{... | collective-permute-start | bytes 1572872 | tf_op jit(solution)/shard_map/ppermute | solution.py:343
  323.1 78.6 %collective-permute-start.25 = (bf16[16,2,64,128]{3,2,1,0:T(8,128)(2,1)S(1)}, bf16[16,2,64,128]{3,2,1,0:T(8,128)(2,1)S(1)}, u32[]{:S(2)}, u32[]{:S(2)}) collective-permute-start(bf16[16,2,64,128]{3,2,1,0:T(8,128)(2,1)S(1)} %get-tuple-element.174), channel_id=1, source_target_pairs={{0,8},{4,12},{8,0},{12,4},{1,9},{5,13},{9,1},{13,5},{2,10},{6,14},... | collective-permute-start | bytes 1572872 | tf_op jit(solution)/shard_map/ppermute | solution.py:343
  323.1 78.6 %collective-permute-start.26 = (bf16[16,2,64,128]{3,2,1,0:T(8,128)(2,1)S(1)}, bf16[16,2,64,128]{3,2,1,0:T(8,128)(2,1)S(1)}, u32[]{:S(2)}, u32[]{:S(2)}) collective-permute-start(bf16[16,2,64,128]{3,2,1,0:T(8,128)(2,1)S(1)} %get-tuple-element.175), channel_id=1, source_target_pairs={{0,12},{4,0},{8,4},{12,8},{1,13},{5,1},{9,5},{13,9},{2,14},{6,2},{... | collective-permute-start | bytes 1572872 | tf_op jit(solution)/shard_map/ppermute | solution.py:343
  356.7 89.9 %collective-permute-start.37 = (bf16[16,2,64,128]{3,2,1,0:T(8,128)(2,1)S(1)}, bf16[16,2,64,128]{3,2,1,0:T(8,128)(2,1)S(1)}, u32[]{:S(2)}, u32[]{:S(2)}) collective-permute-start(bf16[16,2,64,128]{3,2,1,0:T(8,128)(2,1)S(1)} %get-tuple-element.195), channel_id=1, source_target_pairs={{0,8},{4,12},{8,0},{12,4},{1,9},{5,13},{9,1},{13,5},{2,10},{6,14},... | collective-permute-start | bytes 1572872 | tf_op jit(solution)/shard_map/ppermute | solution.py:343
  375.2 71.5 %collective-permute-start.38 = (bf16[16,2,64,128]{3,2,1,0:T(8,128)(2,1)S(1)}, bf16[16,2,64,128]{3,2,1,0:T(8,128)(2,1)S(1)}, u32[]{:S(2)}, u32[]{:S(2)}) collective-permute-start(bf16[16,2,64,128]{3,2,1,0:T(8,128)(2,1)S(1)} %get-tuple-element.196), channel_id=1, source_target_pairs={{0,12},{4,0},{8,4},{12,8},{1,13},{5,1},{9,5},{13,9},{2,14},{6,2},{... | collective-permute-start | bytes 1572872 | tf_op jit(solution)/shard_map/ppermute | solution.py:343
  401.7 89.9 %collective-permute-start.40 = (bf16[16,2,64,128]{3,2,1,0:T(8,128)(2,1)S(1)}, bf16[16,2,64,128]{3,2,1,0:T(8,128)(2,1)S(1)}, u32[]{:S(2)}, u32[]{:S(2)}) collective-permute-start(bf16[16,2,64,128]{3,2,1,0:T(8,128)(2,1)S(1)} %get-tuple-element.202), channel_id=1, source_target_pairs={{0,8},{4,12},{8,0},{12,4},{1,9},{5,13},{9,1},{13,5},{2,10},{6,14},... | collective-permute-start | bytes 1572872 | tf_op jit(solution)/shard_map/ppermute | solution.py:343
  412.5 79.1 %collective-permute-start.41 = (bf16[16,2,64,128]{3,2,1,0:T(8,128)(2,1)S(1)}, bf16[16,2,64,128]{3,2,1,0:T(8,128)(2,1)S(1)}, u32[]{:S(2)}, u32[]{:S(2)}) collective-permute-start(bf16[16,2,64,128]{3,2,1,0:T(8,128)(2,1)S(1)} %get-tuple-element.203), channel_id=1, source_target_pairs={{0,12},{4,0},{8,4},{12,8},{1,13},{5,1},{9,5},{13,9},{2,14},{6,2},{... | collective-permute-start | bytes 1572872 | tf_op jit(solution)/shard_map/ppermute | solution.py:343
  446.6 89.9 %collective-permute-start.34 = (bf16[16,2,64,128]{3,2,1,0:T(8,128)(2,1)S(1)}, bf16[16,2,64,128]{3,2,1,0:T(8,128)(2,1)S(1)}, u32[]{:S(2)}, u32[]{:S(2)}) collective-permute-start(bf16[16,2,64,128]{3,2,1,0:T(8,128)(2,1)S(1)} %get-tuple-element.191), channel_id=1, source_target_pairs={{0,8},{4,12},{8,0},{12,4},{1,9},{5,13},{9,1},{13,5},{2,10},{6,14},... | collective-permute-start | bytes 1572872 | tf_op jit(solution)/shard_map/ppermute | solution.py:343
  450.2 86.3 %collective-permute-start.35 = (bf16[16,2,64,128]{3,2,1,0:T(8,128)(2,1)S(1)}, bf16[16,2,64,128]{3,2,1,0:T(8,128)(2,1)S(1)}, u32[]{:S(2)}, u32[]{:S(2)}) collective-permute-start(bf16[16,2,64,128]{3,2,1,0:T(8,128)(2,1)S(1)} %get-tuple-element.192), channel_id=1, source_target_pairs={{0,12},{4,0},{8,4},{12,8},{1,13},{5,1},{9,5},{13,9},{2,14},{6,2},{... | collective-permute-start | bytes 1572872 | tf_op jit(solution)/shard_map/ppermute | solution.py:343
  491.6 63.5 %collective-permute-start.48 = (bf16[16,2,64,128]{3,2,1,0:T(8,128)(2,1)S(1)}, bf16[16,2,64,128]{3,2,1,0:T(8,128)(2,1)S(1)}, u32[]{:S(2)}, u32[]{:S(2)}) collective-permute-start(bf16[16,2,64,128]{3,2,1,0:T(8,128)(2,1)S(1)} %get-tuple-element.218), channel_id=1, source_target_pairs={{0,4},{4,8},{8,12},{12,0},{1,5},{5,9},{9,13},{13,1},{2,6},{6,10},{... | collective-permute-start | bytes 1572872 | tf_op jit(solution)/shard_map/ppermute | solution.py:343
  491.6 89.9 %collective-permute-start.49 = (bf16[16,2,64,128]{3,2,1,0:T(8,128)(2,1)S(1)}, bf16[16,2,64,128]{3,2,1,0:T(8,128)(2,1)S(1)}, u32[]{:S(2)}, u32[]{:S(2)}) collective-permute-start(bf16[16,2,64,128]{3,2,1,0:T(8,128)(2,1)S(1)} %get-tuple-element.219), channel_id=1, source_target_pairs={{0,8},{4,12},{8,0},{12,4},{1,9},{5,13},{9,1},{13,5},{2,10},{6,14},... | collective-permute-start | bytes 1572872 | tf_op jit(solution)/shard_map/ppermute | solution.py:343
  495.2 86.3 %collective-permute-start.50 = (bf16[16,2,64,128]{3,2,1,0:T(8,128)(2,1)S(1)}, bf16[16,2,64,128]{3,2,1,0:T(8,128)(2,1)S(1)}, u32[]{:S(2)}, u32[]{:S(2)}) collective-permute-start(bf16[16,2,64,128]{3,2,1,0:T(8,128)(2,1)S(1)} %get-tuple-element.220), channel_id=1, source_target_pairs={{0,12},{4,0},{8,4},{12,8},{1,13},{5,1},{9,5},{13,9},{2,14},{6,2},{... | collective-permute-start | bytes 1572872 | tf_op jit(solution)/shard_map/ppermute | solution.py:343
  536.5 89.9 %collective-permute-start.46 = (bf16[16,2,64,128]{3,2,1,0:T(8,128)(2,1)S(1)}, bf16[16,2,64,128]{3,2,1,0:T(8,128)(2,1)S(1)}, u32[]{:S(2)}, u32[]{:S(2)}) collective-permute-start(bf16[16,2,64,128]{3,2,1,0:T(8,128)(2,1)S(1)} %get-tuple-element.214), channel_id=1, source_target_pairs={{0,8},{4,12},{8,0},{12,4},{1,9},{5,13},{9,1},{13,5},{2,10},{6,14},... | collective-permute-start | bytes 1572872 | tf_op jit(solution)/shard_map/ppermute | solution.py:343
  555.1 71.3 %collective-permute-start.47 = (bf16[16,2,64,128]{3,2,1,0:T(8,128)(2,1)S(1)}, bf16[16,2,64,128]{3,2,1,0:T(8,128)(2,1)S(1)}, u32[]{:S(2)}, u32[]{:S(2)}) collective-permute-start(bf16[16,2,64,128]{3,2,1,0:T(8,128)(2,1)S(1)} %get-tuple-element.215), channel_id=1, source_target_pairs={{0,12},{4,0},{8,4},{12,8},{1,13},{5,1},{9,5},{13,9},{2,14},{6,2},{... | collective-permute-start | bytes 1572872 | tf_op jit(solution)/shard_map/ppermute | solution.py:343
  581.4 89.9 %collective-permute-start.43 = (bf16[16,2,64,128]{3,2,1,0:T(8,128)(2,1)S(1)}, bf16[16,2,64,128]{3,2,1,0:T(8,128)(2,1)S(1)}, u32[]{:S(2)}, u32[]{:S(2)}) collective-permute-start(bf16[16,2,64,128]{3,2,1,0:T(8,128)(2,1)S(1)} %get-tuple-element.210), channel_id=1, source_target_pairs={{0,8},{4,12},{8,0},{12,4},{1,9},{5,13},{9,1},{13,5},{2,10},{6,14},... | collective-permute-start | bytes 1572872 | tf_op jit(solution)/shard_map/ppermute | solution.py:343
  592.4 78.9 %collective-permute-start.44 = (bf16[16,2,64,128]{3,2,1,0:T(8,128)(2,1)S(1)}, bf16[16,2,64,128]{3,2,1,0:T(8,128)(2,1)S(1)}, u32[]{:S(2)}, u32[]{:S(2)}) collective-permute-start(bf16[16,2,64,128]{3,2,1,0:T(8,128)(2,1)S(1)} %get-tuple-element.211), channel_id=1, source_target_pairs={{0,12},{4,0},{8,4},{12,8},{1,13},{5,1},{9,5},{13,9},{2,14},{6,2},{... | collective-permute-start | bytes 1572872 | tf_op jit(solution)/shard_map/ppermute | solution.py:343
  626.4 67.4 %collective-permute-start.58 = (bf16[16,2,64,128]{3,2,1,0:T(8,128)(2,1)S(1)}, bf16[16,2,64,128]{3,2,1,0:T(8,128)(2,1)S(1)}, u32[]{:S(2)}, u32[]{:S(2)}) collective-permute-start(bf16[16,2,64,128]{3,2,1,0:T(8,128)(2,1)S(1)} %get-tuple-element.234), channel_id=1, source_target_pairs={{0,8},{4,12},{8,0},{12,4},{1,9},{5,13},{9,1},{13,5},{2,10},{6,14},... | collective-permute-start | bytes 1572872 | tf_op jit(solution)/shard_map/ppermute | solution.py:343
  (42 other events, 1458.1 us)

commit v6 on v4

--- a/solution.py
+++ b/solution.py
@@ -56,25 +56,84 @@
     return jax.ShapeDtypeStruct((8, LANES), jnp.float32)
 
 
+def indices(shape):
+    return [lax.broadcasted_iota(jnp.int32, shape, axis) for axis in range(2)]
+
+
+def ones_where(mask):
+    return jnp.where(mask, 1.0, 0.0).astype(jnp.bfloat16)
+
+
+def fill_packer(ref):
+    ref[...] = jnp.zeros_like(ref)
+    row, lane = indices((ROWS, LANES))
+    for i in range(ROWS):
+        at = i * LANES
+        ref[at : at + ROWS, :] = ones_where((row == 0) & (lane == 2 * i))
+        at += LANES - ROWS
+        last = (2 * i - 1) % LANES
+        ref[at : at + ROWS, :] = ones_where((row == ROWS - 1) & (lane == last))
+
+
+def fill_picker(ref):
+    ref[...] = jnp.zeros_like(ref)
+    row, lane = indices((ROWS, LANES))
+    for i in range(ROWS):
+        first, last = 2 * i, (2 * i - 1) % LANES
+        for tile in {first // ROWS, last // ROWS}:
+            mask = ((lane == 0) & (row == first - tile * ROWS)) | (
+                (lane == LANES - 1) & (row == last - tile * ROWS)
+            )
+            ref[tile * ROWS : (tile + 1) * ROWS, i * LANES : (i + 1) * LANES] = ones_where(mask)
+
+
+def fill_stencil(ref):
+    row, lane = indices((LANES, LANES))
+    apart = row - lane
+    near = jnp.where((apart == 1) | (apart == -1), 1.0, 0.0)
+    side = jnp.where(apart == 1, 0.5, 0.0) - jnp.where(apart == -1, 0.5, 0.0)
+    low = (row == 0) & (lane == 0)
+    high = (row == LANES - 1) & (lane == LANES - 1)
+    ref[:LANES, :LANES] = (near - jnp.where(apart == 0, 2.0, 0.0)).astype(jnp.bfloat16)
+    ref[:LANES, LANES:] = side.astype(jnp.bfloat16)
+    ref[LANES:, :LANES] = ones_where(low | high)
+    ref[LANES:, LANES:] = (jnp.where(high, 0.5, 0.0) - jnp.where(low, 0.5, 0.0)).astype(
+        jnp.bfloat16
+    )
+
+
 def edges(field, first, count, block, span, after):
     parts = field.shape[0]
     base, groups = span[0] // ROWS, span[1] // ROWS
 
     def kernel(x_ref, *refs):
-        o_ref, _, acc = refs[-3:]
+        o_ref, _, acc, packer = refs[-4:]
         g = pl.program_id(1)
-        slot = ((lane_index(block) + 1) >> 1) & (LANES // 2 - 1)
-        for c in range(parts):
-            kept = acc[c]
-            for i in range(ROWS):
-                m = (g + base) * ROWS + i
-                row = roll(x_ref[c, i].astype(jnp.float32), 2 * m)
-                kept = jnp.where(slot == m, row, kept)
-            acc[c] = kept
+
+        @pl.when((pl.program_id(0) == 0) & (g == 0))
+        def _():
+            fill_packer(packer)
+
+        rows = [
+            jnp.concatenate([x_ref[c, i] for i in range(ROWS)], 1) for c in range(parts)
+        ]
+        packed = jnp.dot(
+            jnp.concatenate(rows, 0), packer[...], preferred_element_type=jnp.float32
+        )
+        packed = roll(packed, 2 * ROWS * (g + base))
+
+        @pl.when(g == 0)
+        def _():
+            acc[...] = packed
+
+        @pl.when(g > 0)
+        def _():
+            acc[...] += packed
 
         @pl.when(g == groups - 1)
         def _():
-            o_ref[...] = acc[...].astype(o_ref.dtype)
+            for c in range(parts):
+                o_ref[c] = acc[c * block : (c + 1) * block, :].astype(o_ref.dtype)
 
     return pl.pallas_call(
         kernel,
@@ -88,7 +147,10 @@
         ]
         + anywhere(len(after)),
         out_specs=[pl.BlockSpec((parts, block, LANES), lambda j, g: (0, j, 0))] + anywhere(1),
-        scratch_shapes=[pltpu.VMEM((parts, block, LANES), jnp.float32)],
+        scratch_shapes=[
+            pltpu.VMEM((parts * block, LANES), jnp.float32),
+            pltpu.VMEM((ROWS * LANES, LANES), jnp.bfloat16),
+        ],
         compiler_params=params(),
         cost_estimate=cost(0, parts * span[1] * count * block * LANES * 2),
         name="edges",
@@ -101,24 +163,69 @@
     return jnp.where((lane & 1) == 0, roll(low, 1), roll(high, LANES - 1))
 
 
+def parts_of(x):
+    found = []
+    for _ in range(3):
+        found.append(x.astype(jnp.bfloat16).astype(jnp.float32))
+        x = x - found[-1]
+    return jnp.concatenate(found, 0)
+
+
 def columns(ref, start, block):
     base = start // LANES * LANES
-    turned = jnp.transpose(ref[:, base : base + LANES])
-    return turned[start - base : start - base + block]
-
-
-def move(x, halo, beta, delta, m):
-    lane = lane_index(beta.shape[0])
-    second, first = [], []
-    for c in range(2):
-        ends = roll(halo[c], (LANES - 2 * m) & (LANES - 1))
-        left = jnp.where(lane == 0, ends, roll(x[c], 1))
-        right = jnp.where(lane == LANES - 1, ends, roll(x[c], LANES - 1))
-        second.append(right - 2.0 * x[c] + left)
-        first.append(0.5 * (right - left))
-    real = x[0] - beta * second[1] + delta * first[0]
-    imag = x[1] + beta * second[0] + delta * first[1]
-    return real, imag
+    turned = jnp.transpose(parts_of(ref[:, base : base + LANES]))
+    return turned[start - base : start - base + block].astype(jnp.bfloat16)
+
+
+def moving_scratch(parts, block):
+    return [
+        pltpu.VMEM((2 * LANES, 2 * LANES), jnp.bfloat16),
+        pltpu.VMEM((LANES, ROWS * LANES), jnp.bfloat16),
+        pltpu.VMEM((ROWS * parts * block, 2 * LANES), jnp.bfloat16),
+        pltpu.VMEM((ROWS * parts * block, 2 * LANES), jnp.float32),
+        pltpu.VMEM((2 * block, ROWS * LANES), jnp.float32),
+    ]
+
+
+def moving(x_ref, low_ref, high_ref, beta_ref, delta_ref, scratch, group, start):
+    parts, _, block, _ = x_ref.shape
+    stencil, picker, wide, change, rates = scratch
+
+    @pl.when(pl.program_id(0) == 0)
+    def _():
+        fill_stencil(stencil)
+        fill_picker(picker)
+
+    shift = (LANES - 2 * ROWS * group) & (LANES - 1)
+    halo = [roll(join_halo(low_ref[c], high_ref[c]), shift) for c in range(parts)]
+    halo = jnp.concatenate(halo, 0).astype(jnp.bfloat16)
+    ends = jnp.dot(halo, picker[...], preferred_element_type=jnp.float32).astype(jnp.bfloat16)
+    for i in range(ROWS):
+        for c in range(parts):
+            at = (i * parts + c) * block
+            wide[at : at + block, :LANES] = x_ref[c, i]
+            wide[at : at + block, LANES:] = ends[
+                c * block : (c + 1) * block, i * LANES : (i + 1) * LANES
+            ]
+    change[...] = jnp.dot(wide[...], stencil[...], preferred_element_type=jnp.float32)
+    factors = jnp.concatenate(
+        [columns(beta_ref, start, block), columns(delta_ref, start, block)], 0
+    )
+    row, lane = indices((3 * ROWS, ROWS * LANES))
+    spread = ones_where(row % ROWS == lane // LANES)
+    rates[...] = jnp.dot(factors, spread, preferred_element_type=jnp.float32)
+
+    def order(i):
+        lanes = slice(i * LANES, (i + 1) * LANES)
+        beta, delta = rates[:block, lanes], rates[block:, lanes]
+        at = [(i * parts + c) * block for c in range(parts)]
+        second = [change[a : a + block, :LANES] for a in at]
+        first = [change[a : a + block, LANES:] for a in at]
+        real = x_ref[0, i].astype(jnp.float32) - beta * second[1] + delta * first[0]
+        imag = x_ref[1, i].astype(jnp.float32) + beta * second[0] + delta * first[1]
+        return real, imag
+
+    return order
 
 
 def radial_specs(parts, kinds, block, radial, b, halo_at, base):
@@ -140,16 +247,14 @@
     base, groups = span[0] // ROWS, span[1] // ROWS
 
     def kernel(map_ref, me_ref, x_ref, low_ref, high_ref, tab_ref, beta_ref, delta_ref, *refs):
-        outs, acc = refs[len(after) : len(after) + count], refs[-1]
+        outs, acc, scratch = refs[len(after) : len(after) + count], refs[-6], refs[-5:]
         g = pl.program_id(0)
-        beta = columns(beta_ref, b * block, block)
-        delta = columns(delta_ref, b * block, block)
-        ends = [join_halo(low_ref[c], high_ref[c]) for c in range(parts)]
+        order = moving(
+            x_ref, low_ref, high_ref, beta_ref, delta_ref, scratch, g + base, b * block
+        )
         for i in range(ROWS):
             m = (g + base) * ROWS + i
-            x = [x_ref[c, i].astype(jnp.float32) for c in range(parts)]
-            moved = move(x, ends, beta[:, i : i + 1], delta[:, i : i + 1], m)
-            moved = jnp.concatenate(moved, 1).astype(jnp.bfloat16)
+            moved = jnp.concatenate(order(i), 1).astype(jnp.bfloat16)
             points = jnp.dot(
                 tab_ref[map_ref[m], 0], moved, preferred_element_type=jnp.float32
             )
@@ -177,7 +282,8 @@
             ]
             * count
             + anywhere(1),
-            scratch_shapes=[pltpu.VMEM((parts, block * ROWS, LANES), jnp.float32)],
+            scratch_shapes=[pltpu.VMEM((parts, block * ROWS, LANES), jnp.float32)]
+            + moving_scratch(parts, block),
         ),
         compiler_params=params(),
         cost_estimate=cost(2 * size * block, 2 * size),
@@ -272,7 +378,8 @@
     def kernel(map_ref, me_ref, *refs):
         ins = refs[:count]
         x_ref, low_ref, high_ref, tab_ref, beta_ref, delta_ref = refs[count : count + 6]
-        o_ref, _, acc = refs[-3:]
+        o_ref, _, acc = refs[-8:-5]
+        scratch = refs[-5:]
         g = pl.program_id(0)
         for s in range(count):
             source = lax.rem(me_ref[0] + count - s, count)
@@ -280,13 +387,12 @@
                 row = pl.multiple_of((source * share + q) * ROWS, ROWS)
                 for c in range(parts):
                     acc[c, pl.ds(row, ROWS), :] = ins[s][q, c].astype(jnp.float32)
-        beta = columns(beta_ref, b * block, block)
-        delta = columns(delta_ref, b * block, block)
-        ends = [join_halo(low_ref[c], high_ref[c]) for c in range(parts)]
+        order = moving(
+            x_ref, low_ref, high_ref, beta_ref, delta_ref, scratch, g + base, b * block
+        )
         for i in range(ROWS):
             m = (g + base) * ROWS + i
-            x = [x_ref[c, i].astype(jnp.float32) for c in range(parts)]
-            moved = move(x, ends, beta[:, i : i + 1], delta[:, i : i + 1], m)
+            moved = order(i)
             back = [acc[c, pl.ds(i, block, stride=ROWS), :] for c in range(parts)]
             back = jnp.concatenate(back, 1).astype(jnp.bfloat16)
             increment = jnp.dot(
@@ -313,7 +419,8 @@
                 pl.BlockSpec((parts, ROWS, block, LANES), lambda g, *_: (0, g + base, b, 0))
             ]
             + anywhere(1),
-            scratch_shapes=[pltpu.VMEM((parts, block * ROWS, LANES), jnp.float32)],
+            scratch_shapes=[pltpu.VMEM((parts, block * ROWS, LANES), jnp.float32)]
+            + moving_scratch(parts, block),
         ),
         input_output_aliases={2 + count + 6: 0} if held else {},
         compiler_params=params(),

time: 743 us -> 745 us (level)
  Pallas kernels: 204 us -> 215 us
  transfers between devices with their start and end apart: 57 -> 57, of which waited for: 20 -> 19; matrix products, arithmetic and copies ran while one was open for 0% -> 0% of each run, Pallas kernels for 26% -> 27%
where the time goes in v6:
time: 745 us; the launch traced here: 744 us
  starting transfers between devices  345 us (46%)
  Pallas kernels  215 us (29%)
  waiting for transfers between devices  179 us (24%)
    ppermute x51, starting transfers between devices, exchange(): lax.ppermute(pieces[s], 'ang', ring('ang', s))  343 us
    ppermute x51, waiting for transfers between devices, exchange(): lax.ppermute(pieces[s], 'ang', ring('ang', s))  167 us
    pallas_call x9, Pallas kernels, analyze(): pl.pallas_call(kernel, out_shape=[jax.ShapeDtypeStruct(field.shape, field...  68.4 us
    pallas_call x8, Pallas kernels, synthesize(): pl.pallas_call(kernel, out_shape=[piece] * count + [token()], grid_spec=p...  61.9 us
    pallas_call x8, Pallas kernels, kerr_step(): pl.pallas_call(kernel, out_shape=[jax.ShapeDtypeStruct((share, parts, siz...  59.9 us
    pallas_call x3, Pallas kernels, edges(): pl.pallas_call(kernel, out_shape=[jax.ShapeDtypeStruct((parts, count * bl...  25.1 us
  transfers between devices with their start and end apart: 57, of which 19 were waited for; matrix products, arithmetic and copies ran while one was open for 0% of the time, Pallas kernels for 27%

profile of v6, /device:TPU:24, one launch (start us, length us, event | category | flops | bytes accessed | tf_op | source)
XLA Modules:
  0.0 743.7 jit_solution(13001131078533349055)
XLA Ops:
  33.0 18.3 %edges.5 = (bf16[2,384,128]{2,1,0:T(8,128)(2,1)S(1)}, f32[8,128]{1,0:T(8,128)S(1)}) custom-call(bf16[2,64,512,128]{3,2,1,0:T(8,128)(2,1)} %refs_4_.17, f32[8,128]{1,0:T(8,128)S(1)} %get-tuple-element.117.refs_0_), custom_call_target="tpu_custom_call" | custom-call | bytes 12582912 | tf_op jit(solution)/shard_map/edges/pallas_call | solution.py:138
  54.9 9.2 %collective-permute-done.10.refs_2_ = bf16[16,2,64,128]{3,2,1,0:T(8,128)(2,1)S(1)} collective-permute-done((bf16[16,2,64,128]{3,2,1,0:T(8,128)(2,1)S(1)}, bf16[16,2,64,128]{3,2,1,0:T(8,128)(2,1)S(1)}, u32[]{:S(2)}, u32[]{:S(2)}) %collective-permute-start.10) | collective-permute-done | bytes 524320 | tf_op jit(solution)/shard_map/ppermute | solution.py:436
  81.7 17.9 %collective-permute-start.16 = (bf16[16,2,64,128]{3,2,1,0:T(8,128)(2,1)}, bf16[16,2,64,128]{3,2,1,0:T(8,128)(2,1)}, u32[]{:S(2)}, u32[]{:S(2)}) collective-permute-start(bf16[16,2,64,128]{3,2,1,0:T(8,128)(2,1)} %get-tuple-element.136), channel_id=1, source_target_pairs={{0,8},{4,12},{8,0},{12,4},{1,9},{5,13},{9,1},{13,5},{2,10},{6,14},... | collective-permute-start | bytes 1572872 | tf_op jit(solution)/shard_map/ppermute | solution.py:436
  112.5 19.1 %collective-permute-done.7.refs_2_ = bf16[16,2,64,128]{3,2,1,0:T(8,128)(2,1)} collective-permute-done((bf16[16,2,64,128]{3,2,1,0:T(8,128)(2,1)}, bf16[16,2,64,128]{3,2,1,0:T(8,128)(2,1)}, u32[]{:S(2)}, u32[]{:S(2)}) %collective-permute-start.7) | collective-permute-done | bytes 524320 | tf_op jit(solution)/shard_map/ppermute | solution.py:436
  131.6 10.5 %collective-permute-start.19 = (bf16[16,2,64,128]{3,2,1,0:T(8,128)(2,1)S(1)}, bf16[16,2,64,128]{3,2,1,0:T(8,128)(2,1)S(1)}, u32[]{:S(2)}, u32[]{:S(2)}) collective-permute-start(bf16[16,2,64,128]{3,2,1,0:T(8,128)(2,1)S(1)} %get-tuple-element.142), channel_id=1, source_target_pairs={{0,8},{4,12},{8,0},{12,4},{1,9},{5,13},{9,1},{13,5},{2,10},{6,14},... | collective-permute-start | bytes 1572872 | tf_op jit(solution)/shard_map/ppermute | solution.py:436
  142.2 23.8 %collective-permute-start.20 = (bf16[16,2,64,128]{3,2,1,0:T(8,128)(2,1)S(1)}, bf16[16,2,64,128]{3,2,1,0:T(8,128)(2,1)S(1)}, u32[]{:S(2)}, u32[]{:S(2)}) collective-permute-start(bf16[16,2,64,128]{3,2,1,0:T(8,128)(2,1)S(1)} %get-tuple-element.143), channel_id=1, source_target_pairs={{0,12},{4,0},{8,4},{12,8},{1,13},{5,1},{9,5},{13,9},{2,14},{6,2},{... | collective-permute-start | bytes 1572872 | tf_op jit(solution)/shard_map/ppermute | solution.py:436
  165.9 8.3 %kerr.9 = (bf16[16,2,64,128]{3,2,1,0:T(8,128)(2,1)S(1)}, bf16[16,2,64,128]{3,2,1,0:T(8,128)(2,1)S(1)}, bf16[16,2,64,128]{3,2,1,0:T(8,128)(2,1)S(1)}, bf16[16,2,64,128]{3,2,1,0:T(8,128)(2,1)S(1)}, f32[8,128]{1,0:T(8,128)S(1)}) custom-call(s32[1]{0:T(128)} %bitcast.me_ref, bf16[512,512]{1,0:T(8,128)(2,1)S(1)} %copy-done.11, bf16[512,512]{1,0:T(8,128)(2,1)S(1)} %copy-done.9, ...), custom_call_target="tpu_custom_call" | custom-call | flops 2147483648 | bytes 4194304 | tf_op jit(solution)/shard_map/kerr/pallas_call | solution.py:342
  193.2 17.5 %collective-permute-start.14 = (bf16[16,2,64,128]{3,2,1,0:T(8,128)(2,1)S(1)}, bf16[16,2,64,128]{3,2,1,0:T(8,128)(2,1)S(1)}, u32[]{:S(2)}, u32[]{:S(2)}) collective-permute-start(bf16[16,2,64,128]{3,2,1,0:T(8,128)(2,1)S(1)} %get-tuple-element.133), channel_id=1, source_target_pairs={{0,12},{4,0},{8,4},{12,8},{1,13},{5,1},{9,5},{13,9},{2,14},{6,2},{... | collective-permute-start | bytes 1572872 | tf_op jit(solution)/shard_map/ppermute | solution.py:436
  210.8 10.7 %collective-permute-done.19.refs_2_ = bf16[16,2,64,128]{3,2,1,0:T(8,128)(2,1)S(1)} collective-permute-done((bf16[16,2,64,128]{3,2,1,0:T(8,128)(2,1)S(1)}, bf16[16,2,64,128]{3,2,1,0:T(8,128)(2,1)S(1)}, u32[]{:S(2)}, u32[]{:S(2)}) %collective-permute-start.19) | collective-permute-done | bytes 524320 | tf_op jit(solution)/shard_map/ppermute | solution.py:436
  232.2 11.7 %collective-permute-done.13.refs_2_ = bf16[16,2,64,128]{3,2,1,0:T(8,128)(2,1)S(1)} collective-permute-done((bf16[16,2,64,128]{3,2,1,0:T(8,128)(2,1)S(1)}, bf16[16,2,64,128]{3,2,1,0:T(8,128)(2,1)S(1)}, u32[]{:S(2)}, u32[]{:S(2)}) %collective-permute-start.13) | collective-permute-done | bytes 524320 | tf_op jit(solution)/shard_map/ppermute | solution.py:436
  243.9 19.9 %collective-permute-start.29 = (bf16[16,2,64,128]{3,2,1,0:T(8,128)(2,1)S(1)}, bf16[16,2,64,128]{3,2,1,0:T(8,128)(2,1)S(1)}, u32[]{:S(2)}, u32[]{:S(2)}) collective-permute-start(bf16[16,2,64,128]{3,2,1,0:T(8,128)(2,1)S(1)} %get-tuple-element.160), channel_id=1, source_target_pairs={{0,12},{4,0},{8,4},{12,8},{1,13},{5,1},{9,5},{13,9},{2,14},{6,2},{... | collective-permute-start | bytes 1572872 | tf_op jit(solution)/shard_map/ppermute | solution.py:436
  263.8 13.1 %collective-permute-start.25 = (bf16[16,2,64,128]{3,2,1,0:T(8,128)(2,1)S(1)}, bf16[16,2,64,128]{3,2,1,0:T(8,128)(2,1)S(1)}, u32[]{:S(2)}, u32[]{:S(2)}) collective-permute-start(bf16[16,2,64,128]{3,2,1,0:T(8,128)(2,1)S(1)} %get-tuple-element.154), channel_id=1, source_target_pairs={{0,8},{4,12},{8,0},{12,4},{1,9},{5,13},{9,1},{13,5},{2,10},{6,14},... | collective-permute-start | bytes 1572872 | tf_op jit(solution)/shard_map/ppermute | solution.py:436
  296.7 42.8 %collective-permute-done.28.refs_2_ = bf16[16,2,64,128]{3,2,1,0:T(8,128)(2,1)S(1)} collective-permute-done((bf16[16,2,64,128]{3,2,1,0:T(8,128)(2,1)S(1)}, bf16[16,2,64,128]{3,2,1,0:T(8,128)(2,1)S(1)}, u32[]{:S(2)}, u32[]{:S(2)}) %collective-permute-start.28) | collective-permute-done | bytes 524320 | tf_op jit(solution)/shard_map/ppermute | solution.py:436
  346.8 9.6 %collective-permute-done.25.refs_2_ = bf16[16,2,64,128]{3,2,1,0:T(8,128)(2,1)S(1)} collective-permute-done((bf16[16,2,64,128]{3,2,1,0:T(8,128)(2,1)S(1)}, bf16[16,2,64,128]{3,2,1,0:T(8,128)(2,1)S(1)}, u32[]{:S(2)}, u32[]{:S(2)}) %collective-permute-start.25) | collective-permute-done | bytes 524320 | tf_op jit(solution)/shard_map/ppermute | solution.py:436
  356.4 8.3 %analyze.11 = (bf16[2,64,512,128]{3,2,1,0:T(8,128)(2,1)}, f32[8,128]{1,0:T(8,128)S(1)}) custom-call(s32[64]{0:T(128)S(1)} %copy-done.3, s32[1]{0:T(128)} %bitcast.me_ref, bf16[16,2,64,128]{3,2,1,0:T(8,128)(2,1)S(1)} %get-tuple-element.152.refs_0_, bf16[16,2,64,128]{3,2,1,0:T(8,128)(2,1)S(1)} %collective-permute-done.24.refs_1_, ...), custom_call_target="tpu_custom_call", output_to_operand_aliasing={{0}: (12, {})} | custom-call | flops 268435456 | bytes 6291456 | tf_op jit(solution)/shard_map/analyze/pallas_call | solution.py:406
  372.3 18.3 %collective-permute-start.35 = (bf16[16,2,64,128]{3,2,1,0:T(8,128)(2,1)S(1)}, bf16[16,2,64,128]{3,2,1,0:T(8,128)(2,1)S(1)}, u32[]{:S(2)}, u32[]{:S(2)}) collective-permute-start(bf16[16,2,64,128]{3,2,1,0:T(8,128)(2,1)S(1)} %get-tuple-element.172), channel_id=1, source_target_pairs={{0,12},{4,0},{8,4},{12,8},{1,13},{5,1},{9,5},{13,9},{2,14},{6,2},{... | collective-permute-start | bytes 1572872 | tf_op jit(solution)/shard_map/ppermute | solution.py:436
  390.6 10.7 %collective-permute-done.22.refs_2_ = bf16[16,2,64,128]{3,2,1,0:T(8,128)(2,1)S(1)} collective-permute-done((bf16[16,2,64,128]{3,2,1,0:T(8,128)(2,1)S(1)}, bf16[16,2,64,128]{3,2,1,0:T(8,128)(2,1)S(1)}, u32[]{:S(2)}, u32[]{:S(2)}) %collective-permute-start.22) | collective-permute-done | bytes 524320 | tf_op jit(solution)/shard_map/ppermute | solution.py:436
  408.6 26.9 %collective-permute-start.38 = (bf16[16,2,64,128]{3,2,1,0:T(8,128)(2,1)S(1)}, bf16[16,2,64,128]{3,2,1,0:T(8,128)(2,1)S(1)}, u32[]{:S(2)}, u32[]{:S(2)}) collective-permute-start(bf16[16,2,64,128]{3,2,1,0:T(8,128)(2,1)S(1)} %get-tuple-element.179), channel_id=1, source_target_pairs={{0,12},{4,0},{8,4},{12,8},{1,13},{5,1},{9,5},{13,9},{2,14},{6,2},{... | collective-permute-start | bytes 1572872 | tf_op jit(solution)/shard_map/ppermute | solution.py:436
  435.6 10.7 %collective-permute-done.34.refs_2_ = bf16[16,2,64,128]{3,2,1,0:T(8,128)(2,1)S(1)} collective-permute-done((bf16[16,2,64,128]{3,2,1,0:T(8,128)(2,1)S(1)}, bf16[16,2,64,128]{3,2,1,0:T(8,128)(2,1)S(1)}, u32[]{:S(2)}, u32[]{:S(2)}) %collective-permute-start.34) | collective-permute-done | bytes 524320 | tf_op jit(solution)/shard_map/ppermute | solution.py:436
  446.3 34.2 %collective-permute-start.32 = (bf16[16,2,64,128]{3,2,1,0:T(8,128)(2,1)S(1)}, bf16[16,2,64,128]{3,2,1,0:T(8,128)(2,1)S(1)}, u32[]{:S(2)}, u32[]{:S(2)}) collective-permute-start(bf16[16,2,64,128]{3,2,1,0:T(8,128)(2,1)S(1)} %get-tuple-element.168), channel_id=1, source_target_pairs={{0,12},{4,0},{8,4},{12,8},{1,13},{5,1},{9,5},{13,9},{2,14},{6,2},{... | collective-permute-start | bytes 1572872 | tf_op jit(solution)/shard_map/ppermute | solution.py:436
  498.0 27.5 %collective-permute-start.47 = (bf16[16,2,64,128]{3,2,1,0:T(8,128)(2,1)S(1)}, bf16[16,2,64,128]{3,2,1,0:T(8,128)(2,1)S(1)}, u32[]{:S(2)}, u32[]{:S(2)}) collective-permute-start(bf16[16,2,64,128]{3,2,1,0:T(8,128)(2,1)S(1)} %get-tuple-element.196), channel_id=1, source_target_pairs={{0,12},{4,0},{8,4},{12,8},{1,13},{5,1},{9,5},{13,9},{2,14},{6,2},{... | collective-permute-start | bytes 1572872 | tf_op jit(solution)/shard_map/ppermute | solution.py:436
  552.0 18.4 %collective-permute-start.44 = (bf16[16,2,64,128]{3,2,1,0:T(8,128)(2,1)S(1)}, bf16[16,2,64,128]{3,2,1,0:T(8,128)(2,1)S(1)}, u32[]{:S(2)}, u32[]{:S(2)}) collective-permute-start(bf16[16,2,64,128]{3,2,1,0:T(8,128)(2,1)S(1)} %get-tuple-element.191), channel_id=1, source_target_pairs={{0,12},{4,0},{8,4},{12,8},{1,13},{5,1},{9,5},{13,9},{2,14},{6,2},{... | collective-permute-start | bytes 1572872 | tf_op jit(solution)/shard_map/ppermute | solution.py:436
  570.4 10.7 %collective-permute-done.46.refs_2_ = bf16[16,2,64,128]{3,2,1,0:T(8,128)(2,1)S(1)} collective-permute-done((bf16[16,2,64,128]{3,2,1,0:T(8,128)(2,1)S(1)}, bf16[16,2,64,128]{3,2,1,0:T(8,128)(2,1)S(1)}, u32[]{:S(2)}, u32[]{:S(2)}) %collective-permute-start.46) | collective-permute-done | bytes 524320 | tf_op jit(solution)/shard_map/ppermute | solution.py:436
  588.4 26.9 %collective-permute-start.41 = (bf16[16,2,64,128]{3,2,1,0:T(8,128)(2,1)S(1)}, bf16[16,2,64,128]{3,2,1,0:T(8,128)(2,1)S(1)}, u32[]{:S(2)}, u32[]{:S(2)}) collective-permute-start(bf16[16,2,64,128]{3,2,1,0:T(8,128)(2,1)S(1)} %get-tuple-element.187), channel_id=1, source_target_pairs={{0,12},{4,0},{8,4},{12,8},{1,13},{5,1},{9,5},{13,9},{2,14},{6,2},{... | collective-permute-start | bytes 1572872 | tf_op jit(solution)/shard_map/ppermute | solution.py:436
  615.3 10.7 %collective-permute-done.43.refs_2_ = bf16[16,2,64,128]{3,2,1,0:T(8,128)(2,1)S(1)} collective-permute-done((bf16[16,2,64,128]{3,2,1,0:T(8,128)(2,1)S(1)}, bf16[16,2,64,128]{3,2,1,0:T(8,128)(2,1)S(1)}, u32[]{:S(2)}, u32[]{:S(2)}) %collective-permute-start.43) | collective-permute-done | bytes 524320 | tf_op jit(solution)/shard_map/ppermute | solution.py:436
  626.0 8.3 %analyze.14 = (bf16[2,64,512,128]{3,2,1,0:T(8,128)(2,1)}, f32[8,128]{1,0:T(8,128)S(1)}) custom-call(s32[64]{0:T(128)S(1)} %copy-done.3, s32[1]{0:T(128)} %bitcast.me_ref, bf16[16,2,64,128]{3,2,1,0:T(8,128)(2,1)S(1)} %get-tuple-element.188.refs_0_, bf16[16,2,64,128]{3,2,1,0:T(8,128)(2,1)S(1)} %collective-permute-done.42.refs_1_, ...), custom_call_target="tpu_custom_call", output_to_operand_aliasing={{0}: (12, {})} | custom-call | flops 268435456 | bytes 6291456 | tf_op jit(solution)/shard_map/analyze/pallas_call | solution.py:406
  634.3 25.9 %collective-permute-start.56 = (bf16[16,2,64,128]{3,2,1,0:T(8,128)(2,1)S(1)}, bf16[16,2,64,128]{3,2,1,0:T(8,128)(2,1)S(1)}, u32[]{:S(2)}, u32[]{:S(2)}) collective-permute-start(bf16[16,2,64,128]{3,2,1,0:T(8,128)(2,1)S(1)} %get-tuple-element.211), channel_id=1, source_target_pairs={{0,12},{4,0},{8,4},{12,8},{1,13},{5,1},{9,5},{13,9},{2,14},{6,2},{... | collective-permute-start | bytes 1572872 | tf_op jit(solution)/shard_map/ppermute | solution.py:436
  660.3 10.7 %collective-permute-done.40.refs_2_ = bf16[16,2,64,128]{3,2,1,0:T(8,128)(2,1)S(1)} collective-permute-done((bf16[16,2,64,128]{3,2,1,0:T(8,128)(2,1)S(1)}, bf16[16,2,64,128]{3,2,1,0:T(8,128)(2,1)S(1)}, u32[]{:S(2)}, u32[]{:S(2)}) %collective-permute-start.40) | collective-permute-done | bytes 524320 | tf_op jit(solution)/shard_map/ppermute | solution.py:436
  678.3 13.2 %collective-permute-start.53 = (bf16[16,2,48,128]{3,2,1,0:T(8,128)(2,1)S(1)}, bf16[16,2,48,128]{3,2,1,0:T(8,128)(2,1)S(1)}, u32[]{:S(2)}, u32[]{:S(2)}) collective-permute-start(bf16[16,2,48,128]{3,2,1,0:T(8,128)(2,1)S(1)} %get-tuple-element.207), channel_id=1, source_target_pairs={{0,8},{4,12},{8,0},{12,4},{1,9},{5,13},{9,1},{13,5},{2,10},{6,14},... | collective-permute-start | bytes 1179656 | tf_op jit(solution)/shard_map/ppermute | solution.py:436
  696.6 16.0 %collective-permute-start.50 = (bf16[16,2,16,128]{3,2,1,0:T(8,128)(2,1)S(1)}, bf16[16,2,16,128]{3,2,1,0:T(8,128)(2,1)S(1)}, u32[]{:S(2)}, u32[]{:S(2)}) collective-permute-start(bf16[16,2,16,128]{3,2,1,0:T(8,128)(2,1)S(1)} %get-tuple-element.203), channel_id=1, source_target_pairs={{0,8},{4,12},{8,0},{12,4},{1,9},{5,13},{9,1},{13,5},{2,10},{6,14},... | collective-permute-start | bytes 393224 | tf_op jit(solution)/shard_map/ppermute | solution.py:436
  712.6 12.4 %collective-permute-start.51 = (bf16[16,2,16,128]{3,2,1,0:T(8,128)(2,1)S(1)}, bf16[16,2,16,128]{3,2,1,0:T(8,128)(2,1)S(1)}, u32[]{:S(2)}, u32[]{:S(2)}) collective-permute-start(bf16[16,2,16,128]{3,2,1,0:T(8,128)(2,1)S(1)} %get-tuple-element.204), channel_id=1, source_target_pairs={{0,12},{4,0},{8,4},{12,8},{1,13},{5,1},{9,5},{13,9},{2,14},{6,2},{... | collective-permute-start | bytes 393224 | tf_op jit(solution)/shard_map/ppermute | solution.py:436
  724.9 8.3 %analyze.15 = (bf16[2,64,512,128]{3,2,1,0:T(8,128)(2,1)}, f32[8,128]{1,0:T(8,128)S(1)}) custom-call(s32[64]{0:T(128)S(1)} %copy-done.3, s32[1]{0:T(128)} %bitcast.me_ref, bf16[16,2,64,128]{3,2,1,0:T(8,128)(2,1)S(1)} %get-tuple-element.209.refs_0_, ...), custom_call_target="tpu_custom_call", output_to_operand_aliasing={{0}: (12, {})} | custom-call | flops 268435456 | bytes 6291456 | tf_op jit(solution)/shard_map/analyze/pallas_call | solution.py:406
  (141 shorter events, 212.9 us)
Async XLA Ops:
  54.9 76.7 %collective-permute-start.7 = (bf16[16,2,64,128]{3,2,1,0:T(8,128)(2,1)}, bf16[16,2,64,128]{3,2,1,0:T(8,128)(2,1)}, u32[]{:S(2)}, u32[]{:S(2)}) collective-permute-start(bf16[16,2,64,128]{3,2,1,0:T(8,128)(2,1)} %get-tuple-element.121), channel_id=1, source_target_pairs={{0,8},{4,12},{8,0},{12,4},{1,9},{5,13},{9,1},{13,5},{2,10},{6,14},... | collective-permute-start | bytes 1572872 | tf_op jit(solution)/shard_map/ppermute | solution.py:436
  64.0 67.6 %collective-permute-start.8 = (bf16[16,2,64,128]{3,2,1,0:T(8,128)(2,1)}, bf16[16,2,64,128]{3,2,1,0:T(8,128)(2,1)}, u32[]{:S(2)}, u32[]{:S(2)}) collective-permute-start(bf16[16,2,64,128]{3,2,1,0:T(8,128)(2,1)} %get-tuple-element.122), channel_id=1, source_target_pairs={{0,12},{4,0},{8,4},{12,8},{1,13},{5,1},{9,5},{13,9},{2,14},{6,2},{... | collective-permute-start | bytes 1572872 | tf_op jit(solution)/shard_map/ppermute | solution.py:436
  72.9 69.3 %collective-permute-start.15 = (bf16[16,2,64,128]{3,2,1,0:T(8,128)(2,1)}, bf16[16,2,64,128]{3,2,1,0:T(8,128)(2,1)}, u32[]{:S(2)}, u32[]{:S(2)}) collective-permute-start(bf16[16,2,64,128]{3,2,1,0:T(8,128)(2,1)} %get-tuple-element.135), channel_id=1, source_target_pairs={{0,4},{4,8},{8,12},{12,0},{1,5},{5,9},{9,13},{13,1},{2,6},{6,10},{... | collective-permute-start | bytes 1572872 | tf_op jit(solution)/shard_map/ppermute | solution.py:436
  81.7 94.9 %collective-permute-start.16 = (bf16[16,2,64,128]{3,2,1,0:T(8,128)(2,1)}, bf16[16,2,64,128]{3,2,1,0:T(8,128)(2,1)}, u32[]{:S(2)}, u32[]{:S(2)}) collective-permute-start(bf16[16,2,64,128]{3,2,1,0:T(8,128)(2,1)} %get-tuple-element.136), channel_id=1, source_target_pairs={{0,8},{4,12},{8,0},{12,4},{1,9},{5,13},{9,1},{13,5},{2,10},{6,14},... | collective-permute-start | bytes 1572872 | tf_op jit(solution)/shard_map/ppermute | solution.py:436
  110.4 66.8 %collective-permute-start.17 = (bf16[16,2,64,128]{3,2,1,0:T(8,128)(2,1)S(1)}, bf16[16,2,64,128]{3,2,1,0:T(8,128)(2,1)S(1)}, u32[]{:S(2)}, u32[]{:S(2)}) collective-permute-start(bf16[16,2,64,128]{3,2,1,0:T(8,128)(2,1)S(1)} %copy-done.7), channel_id=1, source_target_pairs={{0,12},{4,0},{8,4},{12,8},{1,13},{5,1},{9,5},{13,9},{2,14},{6,2},{... | collective-permute-start | bytes 1572872 | tf_op jit(solution)/shard_map/ppermute | solution.py:436
  131.6 61.6 %collective-permute-start.18 = (bf16[16,2,64,128]{3,2,1,0:T(8,128)(2,1)S(1)}, bf16[16,2,64,128]{3,2,1,0:T(8,128)(2,1)S(1)}, u32[]{:S(2)}, u32[]{:S(2)}) collective-permute-start(bf16[16,2,64,128]{3,2,1,0:T(8,128)(2,1)S(1)} %get-tuple-element.141), channel_id=1, source_target_pairs={{0,4},{4,8},{8,12},{12,0},{1,5},{5,9},{9,13},{13,1},{2,6},{6,10},{... | collective-permute-start | bytes 1572872 | tf_op jit(solution)/shard_map/ppermute | solution.py:436
  131.6 89.8 %collective-permute-start.19 = (bf16[16,2,64,128]{3,2,1,0:T(8,128)(2,1)S(1)}, bf16[16,2,64,128]{3,2,1,0:T(8,128)(2,1)S(1)}, u32[]{:S(2)}, u32[]{:S(2)}) collective-permute-start(bf16[16,2,64,128]{3,2,1,0:T(8,128)(2,1)S(1)} %get-tuple-element.142), channel_id=1, source_target_pairs={{0,8},{4,12},{8,0},{12,4},{1,9},{5,13},{9,1},{13,5},{2,10},{6,14},... | collective-permute-start | bytes 1572872 | tf_op jit(solution)/shard_map/ppermute | solution.py:436
  142.2 79.3 %collective-permute-start.20 = (bf16[16,2,64,128]{3,2,1,0:T(8,128)(2,1)S(1)}, bf16[16,2,64,128]{3,2,1,0:T(8,128)(2,1)S(1)}, u32[]{:S(2)}, u32[]{:S(2)}) collective-permute-start(bf16[16,2,64,128]{3,2,1,0:T(8,128)(2,1)S(1)} %get-tuple-element.143), channel_id=1, source_target_pairs={{0,12},{4,0},{8,4},{12,8},{1,13},{5,1},{9,5},{13,9},{2,14},{6,2},{... | collective-permute-start | bytes 1572872 | tf_op jit(solution)/shard_map/ppermute | solution.py:436
  177.3 66.7 %collective-permute-start.13 = (bf16[16,2,64,128]{3,2,1,0:T(8,128)(2,1)S(1)}, bf16[16,2,64,128]{3,2,1,0:T(8,128)(2,1)S(1)}, u32[]{:S(2)}, u32[]{:S(2)}) collective-permute-start(bf16[16,2,64,128]{3,2,1,0:T(8,128)(2,1)S(1)} %get-tuple-element.132), channel_id=1, source_target_pairs={{0,8},{4,12},{8,0},{12,4},{1,9},{5,13},{9,1},{13,5},{2,10},{6,14},... | collective-permute-start | bytes 1572872 | tf_op jit(solution)/shard_map/ppermute | solution.py:436
  193.2 70.6 %collective-permute-start.14 = (bf16[16,2,64,128]{3,2,1,0:T(8,128)(2,1)S(1)}, bf16[16,2,64,128]{3,2,1,0:T(8,128)(2,1)S(1)}, u32[]{:S(2)}, u32[]{:S(2)}) collective-permute-start(bf16[16,2,64,128]{3,2,1,0:T(8,128)(2,1)S(1)} %get-tuple-element.133), channel_id=1, source_target_pairs={{0,12},{4,0},{8,4},{12,8},{1,13},{5,1},{9,5},{13,9},{2,14},{6,2},{... | collective-permute-start | bytes 1572872 | tf_op jit(solution)/shard_map/ppermute | solution.py:436
  228.8 64.1 %collective-permute-start.27 = (bf16[16,2,64,128]{3,2,1,0:T(8,128)(2,1)S(1)}, bf16[16,2,64,128]{3,2,1,0:T(8,128)(2,1)S(1)}, u32[]{:S(2)}, u32[]{:S(2)}) collective-permute-start(bf16[16,2,64,128]{3,2,1,0:T(8,128)(2,1)S(1)} %get-tuple-element.158), channel_id=1, source_target_pairs={{0,4},{4,8},{8,12},{12,0},{1,5},{5,9},{9,13},{13,1},{2,6},{6,10},{... | collective-permute-start | bytes 1572872 | tf_op jit(solution)/shard_map/ppermute | solution.py:436
  229.7 109.8 %collective-permute-start.28 = (bf16[16,2,64,128]{3,2,1,0:T(8,128)(2,1)S(1)}, bf16[16,2,64,128]{3,2,1,0:T(8,128)(2,1)S(1)}, u32[]{:S(2)}, u32[]{:S(2)}) collective-permute-start(bf16[16,2,64,128]{3,2,1,0:T(8,128)(2,1)S(1)} %get-tuple-element.159), channel_id=1, source_target_pairs={{0,8},{4,12},{8,0},{12,4},{1,9},{5,13},{9,1},{13,5},{2,10},{6,14},... | collective-permute-start | bytes 1572872 | tf_op jit(solution)/shard_map/ppermute | solution.py:436
  243.9 95.6 %collective-permute-start.29 = (bf16[16,2,64,128]{3,2,1,0:T(8,128)(2,1)S(1)}, bf16[16,2,64,128]{3,2,1,0:T(8,128)(2,1)S(1)}, u32[]{:S(2)}, u32[]{:S(2)}) collective-permute-start(bf16[16,2,64,128]{3,2,1,0:T(8,128)(2,1)S(1)} %get-tuple-element.160), channel_id=1, source_target_pairs={{0,12},{4,0},{8,4},{12,8},{1,13},{5,1},{9,5},{13,9},{2,14},{6,2},{... | collective-permute-start | bytes 1572872 | tf_op jit(solution)/shard_map/ppermute | solution.py:436
  263.8 92.5 %collective-permute-start.25 = (bf16[16,2,64,128]{3,2,1,0:T(8,128)(2,1)S(1)}, bf16[16,2,64,128]{3,2,1,0:T(8,128)(2,1)S(1)}, u32[]{:S(2)}, u32[]{:S(2)}) collective-permute-start(bf16[16,2,64,128]{3,2,1,0:T(8,128)(2,1)S(1)} %get-tuple-element.154), channel_id=1, source_target_pairs={{0,8},{4,12},{8,0},{12,4},{1,9},{5,13},{9,1},{13,5},{2,10},{6,14},... | collective-permute-start | bytes 1572872 | tf_op jit(solution)/shard_map/ppermute | solution.py:436
  277.0 79.4 %collective-permute-start.26 = (bf16[16,2,64,128]{3,2,1,0:T(8,128)(2,1)S(1)}, bf16[16,2,64,128]{3,2,1,0:T(8,128)(2,1)S(1)}, u32[]{:S(2)}, u32[]{:S(2)}) collective-permute-start(bf16[16,2,64,128]{3,2,1,0:T(8,128)(2,1)S(1)} %get-tuple-element.155), channel_id=1, source_target_pairs={{0,12},{4,0},{8,4},{12,8},{1,13},{5,1},{9,5},{13,9},{2,14},{6,2},{... | collective-permute-start | bytes 1572872 | tf_op jit(solution)/shard_map/ppermute | solution.py:436
  292.9 79.4 %collective-permute-start.21 = (bf16[16,2,64,128]{3,2,1,0:T(8,128)(2,1)S(1)}, bf16[16,2,64,128]{3,2,1,0:T(8,128)(2,1)S(1)}, u32[]{:S(2)}, u32[]{:S(2)}) collective-permute-start(bf16[16,2,64,128]{3,2,1,0:T(8,128)(2,1)S(1)} %get-tuple-element.149), channel_id=1, source_target_pairs={{0,4},{4,8},{8,12},{12,0},{1,5},{5,9},{9,13},{13,1},{2,6},{6,10},{... | collective-permute-start | bytes 1572872 | tf_op jit(solution)/shard_map/ppermute | solution.py:436
  339.5 61.8 %collective-permute-start.22 = (bf16[16,2,64,128]{3,2,1,0:T(8,128)(2,1)S(1)}, bf16[16,2,64,128]{3,2,1,0:T(8,128)(2,1)S(1)}, u32[]{:S(2)}, u32[]{:S(2)}) collective-permute-start(bf16[16,2,64,128]{3,2,1,0:T(8,128)(2,1)S(1)} %get-tuple-element.150), channel_id=1, source_target_pairs={{0,8},{4,12},{8,0},{12,4},{1,9},{5,13},{9,1},{13,5},{2,10},{6,14},... | collective-permute-start | bytes 1572872 | tf_op jit(solution)/shard_map/ppermute | solution.py:436
  339.5 61.8 %collective-permute-start.23 = (bf16[16,2,64,128]{3,2,1,0:T(8,128)(2,1)S(1)}, bf16[16,2,64,128]{3,2,1,0:T(8,128)(2,1)S(1)}, u32[]{:S(2)}, u32[]{:S(2)}) collective-permute-start(bf16[16,2,64,128]{3,2,1,0:T(8,128)(2,1)S(1)} %get-tuple-element.151), channel_id=1, source_target_pairs={{0,12},{4,0},{8,4},{12,8},{1,13},{5,1},{9,5},{13,9},{2,14},{6,2},{... | collective-permute-start | bytes 1572872 | tf_op jit(solution)/shard_map/ppermute | solution.py:436
  356.4 89.9 %collective-permute-start.34 = (bf16[16,2,64,128]{3,2,1,0:T(8,128)(2,1)S(1)}, bf16[16,2,64,128]{3,2,1,0:T(8,128)(2,1)S(1)}, u32[]{:S(2)}, u32[]{:S(2)}) collective-permute-start(bf16[16,2,64,128]{3,2,1,0:T(8,128)(2,1)S(1)} %get-tuple-element.171), channel_id=1, source_target_pairs={{0,8},{4,12},{8,0},{12,4},{1,9},{5,13},{9,1},{13,5},{2,10},{6,14},... | collective-permute-start | bytes 1572872 | tf_op jit(solution)/shard_map/ppermute | solution.py:436
  372.3 74.0 %collective-permute-start.35 = (bf16[16,2,64,128]{3,2,1,0:T(8,128)(2,1)S(1)}, bf16[16,2,64,128]{3,2,1,0:T(8,128)(2,1)S(1)}, u32[]{:S(2)}, u32[]{:S(2)}) collective-permute-start(bf16[16,2,64,128]{3,2,1,0:T(8,128)(2,1)S(1)} %get-tuple-element.172), channel_id=1, source_target_pairs={{0,12},{4,0},{8,4},{12,8},{1,13},{5,1},{9,5},{13,9},{2,14},{6,2},{... | collective-permute-start | bytes 1572872 | tf_op jit(solution)/shard_map/ppermute | solution.py:436
  401.3 95.1 %collective-permute-start.37 = (bf16[16,2,64,128]{3,2,1,0:T(8,128)(2,1)S(1)}, bf16[16,2,64,128]{3,2,1,0:T(8,128)(2,1)S(1)}, u32[]{:S(2)}, u32[]{:S(2)}) collective-permute-start(bf16[16,2,64,128]{3,2,1,0:T(8,128)(2,1)S(1)} %get-tuple-element.178), channel_id=1, source_target_pairs={{0,8},{4,12},{8,0},{12,4},{1,9},{5,13},{9,1},{13,5},{2,10},{6,14},... | collective-permute-start | bytes 1572872 | tf_op jit(solution)/shard_map/ppermute | solution.py:436
  408.6 87.8 %collective-permute-start.38 = (bf16[16,2,64,128]{3,2,1,0:T(8,128)(2,1)S(1)}, bf16[16,2,64,128]{3,2,1,0:T(8,128)(2,1)S(1)}, u32[]{:S(2)}, u32[]{:S(2)}) collective-permute-start(bf16[16,2,64,128]{3,2,1,0:T(8,128)(2,1)S(1)} %get-tuple-element.179), channel_id=1, source_target_pairs={{0,12},{4,0},{8,4},{12,8},{1,13},{5,1},{9,5},{13,9},{2,14},{6,2},{... | collective-permute-start | bytes 1572872 | tf_op jit(solution)/shard_map/ppermute | solution.py:436
  446.2 89.9 %collective-permute-start.31 = (bf16[16,2,64,128]{3,2,1,0:T(8,128)(2,1)S(1)}, bf16[16,2,64,128]{3,2,1,0:T(8,128)(2,1)S(1)}, u32[]{:S(2)}, u32[]{:S(2)}) collective-permute-start(bf16[16,2,64,128]{3,2,1,0:T(8,128)(2,1)S(1)} %get-tuple-element.167), channel_id=1, source_target_pairs={{0,8},{4,12},{8,0},{12,4},{1,9},{5,13},{9,1},{13,5},{2,10},{6,14},... | collective-permute-start | bytes 1572872 | tf_op jit(solution)/shard_map/ppermute | solution.py:436
  446.3 89.9 %collective-permute-start.32 = (bf16[16,2,64,128]{3,2,1,0:T(8,128)(2,1)S(1)}, bf16[16,2,64,128]{3,2,1,0:T(8,128)(2,1)S(1)}, u32[]{:S(2)}, u32[]{:S(2)}) collective-permute-start(bf16[16,2,64,128]{3,2,1,0:T(8,128)(2,1)S(1)} %get-tuple-element.168), channel_id=1, source_target_pairs={{0,12},{4,0},{8,4},{12,8},{1,13},{5,1},{9,5},{13,9},{2,14},{6,2},{... | collective-permute-start | bytes 1572872 | tf_op jit(solution)/shard_map/ppermute | solution.py:436
  496.4 84.6 %collective-permute-start.46 = (bf16[16,2,64,128]{3,2,1,0:T(8,128)(2,1)S(1)}, bf16[16,2,64,128]{3,2,1,0:T(8,128)(2,1)S(1)}, u32[]{:S(2)}, u32[]{:S(2)}) collective-permute-start(bf16[16,2,64,128]{3,2,1,0:T(8,128)(2,1)S(1)} %get-tuple-element.195), channel_id=1, source_target_pairs={{0,8},{4,12},{8,0},{12,4},{1,9},{5,13},{9,1},{13,5},{2,10},{6,14},... | collective-permute-start | bytes 1572872 | tf_op jit(solution)/shard_map/ppermute | solution.py:436
  498.0 83.1 %collective-permute-start.47 = (bf16[16,2,64,128]{3,2,1,0:T(8,128)(2,1)S(1)}, bf16[16,2,64,128]{3,2,1,0:T(8,128)(2,1)S(1)}, u32[]{:S(2)}, u32[]{:S(2)}) collective-permute-start(bf16[16,2,64,128]{3,2,1,0:T(8,128)(2,1)S(1)} %get-tuple-element.196), channel_id=1, source_target_pairs={{0,12},{4,0},{8,4},{12,8},{1,13},{5,1},{9,5},{13,9},{2,14},{6,2},{... | collective-permute-start | bytes 1572872 | tf_op jit(solution)/shard_map/ppermute | solution.py:436
  536.1 89.9 %collective-permute-start.43 = (bf16[16,2,64,128]{3,2,1,0:T(8,128)(2,1)S(1)}, bf16[16,2,64,128]{3,2,1,0:T(8,128)(2,1)S(1)}, u32[]{:S(2)}, u32[]{:S(2)}) collective-permute-start(bf16[16,2,64,128]{3,2,1,0:T(8,128)(2,1)S(1)} %get-tuple-element.190), channel_id=1, source_target_pairs={{0,8},{4,12},{8,0},{12,4},{1,9},{5,13},{9,1},{13,5},{2,10},{6,14},... | collective-permute-start | bytes 1572872 | tf_op jit(solution)/shard_map/ppermute | solution.py:436
  552.0 74.0 %collective-permute-start.44 = (bf16[16,2,64,128]{3,2,1,0:T(8,128)(2,1)S(1)}, bf16[16,2,64,128]{3,2,1,0:T(8,128)(2,1)S(1)}, u32[]{:S(2)}, u32[]{:S(2)}) collective-permute-start(bf16[16,2,64,128]{3,2,1,0:T(8,128)(2,1)S(1)} %get-tuple-element.191), channel_id=1, source_target_pairs={{0,12},{4,0},{8,4},{12,8},{1,13},{5,1},{9,5},{13,9},{2,14},{6,2},{... | collective-permute-start | bytes 1572872 | tf_op jit(solution)/shard_map/ppermute | solution.py:436
  581.1 89.9 %collective-permute-start.40 = (bf16[16,2,64,128]{3,2,1,0:T(8,128)(2,1)S(1)}, bf16[16,2,64,128]{3,2,1,0:T(8,128)(2,1)S(1)}, u32[]{:S(2)}, u32[]{:S(2)}) collective-permute-start(bf16[16,2,64,128]{3,2,1,0:T(8,128)(2,1)S(1)} %get-tuple-element.186), channel_id=1, source_target_pairs={{0,8},{4,12},{8,0},{12,4},{1,9},{5,13},{9,1},{13,5},{2,10},{6,14},... | collective-permute-start | bytes 1572872 | tf_op jit(solution)/shard_map/ppermute | solution.py:436
  588.4 82.6 %collective-permute-start.41 = (bf16[16,2,64,128]{3,2,1,0:T(8,128)(2,1)S(1)}, bf16[16,2,64,128]{3,2,1,0:T(8,128)(2,1)S(1)}, u32[]{:S(2)}, u32[]{:S(2)}) collective-permute-start(bf16[16,2,64,128]{3,2,1,0:T(8,128)(2,1)S(1)} %get-tuple-element.187), channel_id=1, source_target_pairs={{0,12},{4,0},{8,4},{12,8},{1,13},{5,1},{9,5},{13,9},{2,14},{6,2},{... | collective-permute-start | bytes 1572872 | tf_op jit(solution)/shard_map/ppermute | solution.py:436
  626.0 70.6 %collective-permute-start.55 = (bf16[16,2,64,128]{3,2,1,0:T(8,128)(2,1)S(1)}, bf16[16,2,64,128]{3,2,1,0:T(8,128)(2,1)S(1)}, u32[]{:S(2)}, u32[]{:S(2)}) collective-permute-start(bf16[16,2,64,128]{3,2,1,0:T(8,128)(2,1)S(1)} %get-tuple-element.210), channel_id=1, source_target_pairs={{0,8},{4,12},{8,0},{12,4},{1,9},{5,13},{9,1},{13,5},{2,10},{6,14},... | collective-permute-start | bytes 1572872 | tf_op jit(solution)/shard_map/ppermute | solution.py:436
  634.3 62.3 %collective-permute-start.56 = (bf16[16,2,64,128]{3,2,1,0:T(8,128)(2,1)S(1)}, bf16[16,2,64,128]{3,2,1,0:T(8,128)(2,1)S(1)}, u32[]{:S(2)}, u32[]{:S(2)}) collective-permute-start(bf16[16,2,64,128]{3,2,1,0:T(8,128)(2,1)S(1)} %get-tuple-element.211), channel_id=1, source_target_pairs={{0,12},{4,0},{8,4},{12,8},{1,13},{5,1},{9,5},{13,9},{2,14},{6,2},{... | collective-permute-start | bytes 1572872 | tf_op jit(solution)/shard_map/ppermute | solution.py:436
  (39 other events, 1407.8 us)

commit v7 on v4

--- a/solution.py
+++ b/solution.py
@@ -56,19 +56,63 @@
     return jax.ShapeDtypeStruct((8, LANES), jnp.float32)
 
 
+def indices(shape):
+    return [lax.broadcasted_iota(jnp.int32, shape, axis) for axis in range(2)]
+
+
+def ones_where(mask):
+    return jnp.where(mask, 1.0, 0.0).astype(jnp.bfloat16)
+
+
+HALVES = 2
+
+
+def field_specs(parts, block, place):
+    rows = ROWS // HALVES
+
+    def spec(c, half):
+        def index(*at):
+            group, b = place(*at)
+            return (c, group * HALVES + half, b, 0)
+
+        return pl.BlockSpec((1, rows, block, LANES), index)
+
+    return [spec(c, half) for c in range(parts) for half in range(HALVES)]
+
+
+def field_block(x_refs, c, i):
+    rows = ROWS // HALVES
+    return x_refs[c * HALVES + i // rows][0, i % rows]
+
+
+def fill_stencil(ref):
+    row, lane = indices((LANES, LANES))
+    apart = row - lane
+    near = jnp.where((apart == 1) | (apart == -1), 1.0, 0.0)
+    side = jnp.where(apart == 1, 0.5, 0.0) - jnp.where(apart == -1, 0.5, 0.0)
+    low = (row == 0) & (lane == 0)
+    high = (row == LANES - 1) & (lane == LANES - 1)
+    ref[:LANES, :LANES] = (near - jnp.where(apart == 0, 2.0, 0.0)).astype(jnp.bfloat16)
+    ref[:LANES, LANES:] = side.astype(jnp.bfloat16)
+    ref[LANES:, :LANES] = ones_where(low | high)
+    ref[LANES:, LANES:] = (jnp.where(high, 0.5, 0.0) - jnp.where(low, 0.5, 0.0)).astype(
+        jnp.bfloat16
+    )
+
+
 def edges(field, first, count, block, span, after):
     parts = field.shape[0]
     base, groups = span[0] // ROWS, span[1] // ROWS
 
-    def kernel(x_ref, *refs):
-        o_ref, _, acc = refs[-3:]
+    def kernel(*refs):
+        x_refs, (o_ref, _, acc) = refs[: parts * HALVES], refs[-3:]
         g = pl.program_id(1)
         slot = ((lane_index(block) + 1) >> 1) & (LANES // 2 - 1)
         for c in range(parts):
-            kept = acc[c]
+            kept = jnp.where(g == 0, 0.0, acc[c])
             for i in range(ROWS):
                 m = (g + base) * ROWS + i
-                row = roll(x_ref[c, i].astype(jnp.float32), 2 * m)
+                row = roll(field_block(x_refs, c, i).astype(jnp.float32), 2 * m)
                 kept = jnp.where(slot == m, row, kept)
             acc[c] = kept
 
@@ -83,16 +127,14 @@
             token(),
         ],
         grid=(count, groups),
-        in_specs=[
-            pl.BlockSpec((parts, ROWS, block, LANES), lambda j, g: (0, g + base, j + first, 0))
-        ]
+        in_specs=field_specs(parts, block, lambda j, g: (g + base, j + first))
         + anywhere(len(after)),
         out_specs=[pl.BlockSpec((parts, block, LANES), lambda j, g: (0, j, 0))] + anywhere(1),
         scratch_shapes=[pltpu.VMEM((parts, block, LANES), jnp.float32)],
         compiler_params=params(),
         cost_estimate=cost(0, parts * span[1] * count * block * LANES * 2),
         name="edges",
-    )(field, *after)
+    )(*[field] * (parts * HALVES), *after)
 
 
 def join_halo(low, high):
@@ -107,23 +149,47 @@
     return turned[start - base : start - base + block]
 
 
-def move(x, halo, beta, delta, m):
-    lane = lane_index(beta.shape[0])
-    second, first = [], []
-    for c in range(2):
-        ends = roll(halo[c], (LANES - 2 * m) & (LANES - 1))
-        left = jnp.where(lane == 0, ends, roll(x[c], 1))
-        right = jnp.where(lane == LANES - 1, ends, roll(x[c], LANES - 1))
-        second.append(right - 2.0 * x[c] + left)
-        first.append(0.5 * (right - left))
-    real = x[0] - beta * second[1] + delta * first[0]
-    imag = x[1] + beta * second[0] + delta * first[1]
-    return real, imag
+def moving_scratch(parts, block):
+    return [
+        pltpu.VMEM((2 * LANES, 2 * LANES), jnp.bfloat16),
+        pltpu.VMEM((ROWS * parts * block, 2 * LANES), jnp.bfloat16),
+        pltpu.VMEM((ROWS * parts * block, 2 * LANES), jnp.float32),
+    ]
+
+
+def moving(x_refs, low_ref, high_ref, beta_ref, delta_ref, scratch, group, start):
+    parts, block, _ = low_ref.shape
+    stencil, wide, change = scratch
+
+    @pl.when(pl.program_id(0) == 0)
+    def _():
+        fill_stencil(stencil)
+
+    halo = [join_halo(low_ref[c], high_ref[c]) for c in range(parts)]
+    for i in range(ROWS):
+        shift = (LANES - 2 * (ROWS * group + i)) & (LANES - 1)
+        for c in range(parts):
+            at = (i * parts + c) * block
+            wide[at : at + block, :LANES] = field_block(x_refs, c, i)
+            wide[at : at + block, LANES:] = roll(halo[c], shift).astype(jnp.bfloat16)
+    change[...] = jnp.dot(wide[...], stencil[...], preferred_element_type=jnp.float32)
+    beta = columns(beta_ref, start, block)
+    delta = columns(delta_ref, start, block)
+
+    def order(i):
+        at = [(i * parts + c) * block for c in range(parts)]
+        second = [change[a : a + block, :LANES] for a in at]
+        first = [change[a : a + block, LANES:] for a in at]
+        x = [field_block(x_refs, c, i).astype(jnp.float32) for c in range(parts)]
+        real = x[0] - beta[:, i : i + 1] * second[1] + delta[:, i : i + 1] * first[0]
+        imag = x[1] + beta[:, i : i + 1] * second[0] + delta[:, i : i + 1] * first[1]
+        return real, imag
+
+    return order
 
 
 def radial_specs(parts, kinds, block, radial, b, halo_at, base):
-    return [
-        pl.BlockSpec((parts, ROWS, block, LANES), lambda g, *_: (0, g + base, b, 0)),
+    return field_specs(parts, block, lambda g, *_: (g + base, b)) + [
         pl.BlockSpec((parts, block, LANES), lambda g, *_: (0, halo_at, 0)),
         pl.BlockSpec((parts, block, LANES), lambda g, *_: (0, halo_at, 0)),
         pl.BlockSpec((kinds, 1, block, block), lambda g, *_: (0, b, 0, 0)),
@@ -139,17 +205,17 @@
     share = block // count
     base, groups = span[0] // ROWS, span[1] // ROWS
 
-    def kernel(map_ref, me_ref, x_ref, low_ref, high_ref, tab_ref, beta_ref, delta_ref, *refs):
-        outs, acc = refs[len(after) : len(after) + count], refs[-1]
+    def kernel(map_ref, me_ref, *refs):
+        x_refs, refs = refs[: parts * HALVES], refs[parts * HALVES :]
+        low_ref, high_ref, tab_ref, beta_ref, delta_ref = refs[:5]
+        outs, acc, scratch = refs[-count - 5 : -5], refs[-4], refs[-3:]
         g = pl.program_id(0)
-        beta = columns(beta_ref, b * block, block)
-        delta = columns(delta_ref, b * block, block)
-        ends = [join_halo(low_ref[c], high_ref[c]) for c in range(parts)]
+        order = moving(
+            x_refs, low_ref, high_ref, beta_ref, delta_ref, scratch, g + base, b * block
+        )
         for i in range(ROWS):
             m = (g + base) * ROWS + i
-            x = [x_ref[c, i].astype(jnp.float32) for c in range(parts)]
-            moved = move(x, ends, beta[:, i : i + 1], delta[:, i : i + 1], m)
-            moved = jnp.concatenate(moved, 1).astype(jnp.bfloat16)
+            moved = jnp.concatenate(order(i), 1).astype(jnp.bfloat16)
             points = jnp.dot(
                 tab_ref[map_ref[m], 0], moved, preferred_element_type=jnp.float32
             )
@@ -177,12 +243,15 @@
             ]
             * count
             + anywhere(1),
-            scratch_shapes=[pltpu.VMEM((parts, block * ROWS, LANES), jnp.float32)],
+            scratch_shapes=[pltpu.VMEM((parts, block * ROWS, LANES), jnp.float32)]
+            + moving_scratch(parts, block),
         ),
         compiler_params=params(),
         cost_estimate=cost(2 * size * block, 2 * size),
         name="synthesize",
-    )(order_map, me, field, low, high, tables, curvature, walk_off, *after)
+    )(
+        order_map, me, *[field] * (parts * HALVES), low, high, tables, curvature, walk_off, *after
+    )
     return pieces, done
 
 
@@ -270,9 +339,11 @@
     held = () if out is None else (out,)
 
     def kernel(map_ref, me_ref, *refs):
-        ins = refs[:count]
-        x_ref, low_ref, high_ref, tab_ref, beta_ref, delta_ref = refs[count : count + 6]
-        o_ref, _, acc = refs[-3:]
+        ins, refs = refs[:count], refs[count:]
+        x_refs, refs = refs[: parts * HALVES], refs[parts * HALVES :]
+        low_ref, high_ref, tab_ref, beta_ref, delta_ref = refs[:5]
+        o_ref, _, acc = refs[-6:-3]
+        scratch = refs[-3:]
         g = pl.program_id(0)
         for s in range(count):
             source = lax.rem(me_ref[0] + count - s, count)
@@ -280,13 +351,12 @@
                 row = pl.multiple_of((source * share + q) * ROWS, ROWS)
                 for c in range(parts):
                     acc[c, pl.ds(row, ROWS), :] = ins[s][q, c].astype(jnp.float32)
-        beta = columns(beta_ref, b * block, block)
-        delta = columns(delta_ref, b * block, block)
-        ends = [join_halo(low_ref[c], high_ref[c]) for c in range(parts)]
+        order = moving(
+            x_refs, low_ref, high_ref, beta_ref, delta_ref, scratch, g + base, b * block
+        )
         for i in range(ROWS):
             m = (g + base) * ROWS + i
-            x = [x_ref[c, i].astype(jnp.float32) for c in range(parts)]
-            moved = move(x, ends, beta[:, i : i + 1], delta[:, i : i + 1], m)
+            moved = order(i)
             back = [acc[c, pl.ds(i, block, stride=ROWS), :] for c in range(parts)]
             back = jnp.concatenate(back, 1).astype(jnp.bfloat16)
             increment = jnp.dot(
@@ -313,14 +383,16 @@
                 pl.BlockSpec((parts, ROWS, block, LANES), lambda g, *_: (0, g + base, b, 0))
             ]
             + anywhere(1),
-            scratch_shapes=[pltpu.VMEM((parts, block * ROWS, LANES), jnp.float32)],
+            scratch_shapes=[pltpu.VMEM((parts, block * ROWS, LANES), jnp.float32)]
+            + moving_scratch(parts, block),
         ),
-        input_output_aliases={2 + count + 6: 0} if held else {},
+        input_output_aliases={2 + count + parts * HALVES + 5: 0} if held else {},
         compiler_params=params(),
         cost_estimate=cost(2 * size * block, 3 * size),
         name="analyze",
     )(
-        order_map, me, *pieces, field, low, high, tables, curvature, walk_off, *held, *after
+        order_map, me, *pieces, *[field] * (parts * HALVES), low, high, tables, curvature,
+        walk_off, *held, *after,
     )
 
 

time: 743 us -> 743 us (level)
  transfers between devices with their start and end apart: 57 -> 57, of which waited for: 20 -> 19; matrix products, arithmetic and copies ran while one was open for 0% -> 0% of each run, Pallas kernels for 26% -> 26%
where the time goes in v7:
time: 743 us; the launch traced here: 742 us
  starting transfers between devices  349 us (47%)
  Pallas kernels  207 us (28%)
  waiting for transfers between devices  182 us (24%)
    ppermute x51, starting transfers between devices, exchange(): lax.ppermute(pieces[s], 'ang', ring('ang', s))  347 us
    ppermute x51, waiting for transfers between devices, exchange(): lax.ppermute(pieces[s], 'ang', ring('ang', s))  171 us
    pallas_call x9, Pallas kernels, analyze(): pl.pallas_call(kernel, out_shape=[jax.ShapeDtypeStruct(field.shape, field...  65.8 us
    pallas_call x8, Pallas kernels, kerr_step(): pl.pallas_call(kernel, out_shape=[jax.ShapeDtypeStruct((share, parts, siz...  59.9 us
    pallas_call x8, Pallas kernels, synthesize(): pl.pallas_call(kernel, out_shape=[piece] * count + [token()], grid_spec=p...  58.5 us
    pallas_call x3, Pallas kernels, edges(): pl.pallas_call(kernel, out_shape=[jax.ShapeDtypeStruct((parts, count * bl...  22.5 us
  transfers between devices with their start and end apart: 57, of which 19 were waited for; matrix products, arithmetic and copies ran while one was open for 0% of the time, Pallas kernels for 26%

profile of v7, /device:TPU:24, one launch (start us, length us, event | category | flops | bytes accessed | tf_op | source)
XLA Modules:
  0.0 742.3 jit_solution(9002441105780061901)
XLA Ops:
  31.2 16.6 %edges.5 = (bf16[2,384,128]{2,1,0:T(8,128)(2,1)S(1)}, f32[8,128]{1,0:T(8,128)S(1)}) custom-call(bf16[2,64,512,128]{3,2,1,0:T(8,128)(2,1)} %refs_7_.33, bf16[2,64,512,128]{3,2,1,0:T(8,128)(2,1)} %refs_7_.33, bf16[2,64,512,128]{3,2,1,0:T(8,128)(2,1)} %refs_7_.33, bf16[2,64,512,128]{3,2,1,0:T(8,128)(2,1)} %refs_7_.33, f32[8,128]{1,0:T(8,128)S(1)} %get-tuple-element.117.refs_4_), custom_call_target="tpu_custom_call" | custom-call | bytes 12582912 | tf_op jit(solution)/shard_map/edges/pallas_call | solution.py:123
  51.5 11.7 %collective-permute-done.10.refs_2_ = bf16[16,2,64,128]{3,2,1,0:T(8,128)(2,1)S(1)} collective-permute-done((bf16[16,2,64,128]{3,2,1,0:T(8,128)(2,1)S(1)}, bf16[16,2,64,128]{3,2,1,0:T(8,128)(2,1)S(1)}, u32[]{:S(2)}, u32[]{:S(2)}) %collective-permute-start.10) | collective-permute-done | bytes 524320 | tf_op jit(solution)/shard_map/ppermute | solution.py:401
  63.2 8.0 %kerr.8 = (bf16[16,2,64,128]{3,2,1,0:T(8,128)(2,1)S(1)}, bf16[16,2,64,128]{3,2,1,0:T(8,128)(2,1)}, bf16[16,2,64,128]{3,2,1,0:T(8,128)(2,1)}, bf16[16,2,64,128]{3,2,1,0:T(8,128)(2,1)S(1)}, f32[8,128]{1,0:T(8,128)S(1)}) custom-call(s32[1]{0:T(128)} %bitcast.me_ref, bf16[512,512]{1,0:T(8,128)(2,1)S(1)} %copy-done.10, bf16[512,512]{1,0:T(8,128)(2,1)S(1)} %copy-done.8, ...), custom_call_target="tpu_custom_call" | custom-call | flops 2147483648 | bytes 4194304 | tf_op jit(solution)/shard_map/kerr/pallas_call | solution.py:305
  80.9 17.9 %collective-permute-start.16 = (bf16[16,2,64,128]{3,2,1,0:T(8,128)(2,1)}, bf16[16,2,64,128]{3,2,1,0:T(8,128)(2,1)}, u32[]{:S(2)}, u32[]{:S(2)}) collective-permute-start(bf16[16,2,64,128]{3,2,1,0:T(8,128)(2,1)} %get-tuple-element.136), channel_id=1, source_target_pairs={{0,8},{4,12},{8,0},{12,4},{1,9},{5,13},{9,1},{13,5},{2,10},{6,14},... | collective-permute-start | bytes 1572872 | tf_op jit(solution)/shard_map/ppermute | solution.py:401
  111.2 19.5 %collective-permute-done.7.refs_2_ = bf16[16,2,64,128]{3,2,1,0:T(8,128)(2,1)} collective-permute-done((bf16[16,2,64,128]{3,2,1,0:T(8,128)(2,1)}, bf16[16,2,64,128]{3,2,1,0:T(8,128)(2,1)}, u32[]{:S(2)}, u32[]{:S(2)}) %collective-permute-start.7) | collective-permute-done | bytes 524320 | tf_op jit(solution)/shard_map/ppermute | solution.py:401
  130.8 10.5 %collective-permute-start.19 = (bf16[16,2,64,128]{3,2,1,0:T(8,128)(2,1)S(1)}, bf16[16,2,64,128]{3,2,1,0:T(8,128)(2,1)S(1)}, u32[]{:S(2)}, u32[]{:S(2)}) collective-permute-start(bf16[16,2,64,128]{3,2,1,0:T(8,128)(2,1)S(1)} %get-tuple-element.142), channel_id=1, source_target_pairs={{0,8},{4,12},{8,0},{12,4},{1,9},{5,13},{9,1},{13,5},{2,10},{6,14},... | collective-permute-start | bytes 1572872 | tf_op jit(solution)/shard_map/ppermute | solution.py:401
  141.3 23.8 %collective-permute-start.20 = (bf16[16,2,64,128]{3,2,1,0:T(8,128)(2,1)S(1)}, bf16[16,2,64,128]{3,2,1,0:T(8,128)(2,1)S(1)}, u32[]{:S(2)}, u32[]{:S(2)}) collective-permute-start(bf16[16,2,64,128]{3,2,1,0:T(8,128)(2,1)S(1)} %get-tuple-element.143), channel_id=1, source_target_pairs={{0,12},{4,0},{8,4},{12,8},{1,13},{5,1},{9,5},{13,9},{2,14},{6,2},{... | collective-permute-start | bytes 1572872 | tf_op jit(solution)/shard_map/ppermute | solution.py:401
  165.1 8.3 %kerr.9 = (bf16[16,2,64,128]{3,2,1,0:T(8,128)(2,1)S(1)}, bf16[16,2,64,128]{3,2,1,0:T(8,128)(2,1)S(1)}, bf16[16,2,64,128]{3,2,1,0:T(8,128)(2,1)S(1)}, bf16[16,2,64,128]{3,2,1,0:T(8,128)(2,1)S(1)}, f32[8,128]{1,0:T(8,128)S(1)}) custom-call(s32[1]{0:T(128)} %bitcast.me_ref, bf16[512,512]{1,0:T(8,128)(2,1)S(1)} %copy-done.11, bf16[512,512]{1,0:T(8,128)(2,1)S(1)} %copy-done.9, ...), custom_call_target="tpu_custom_call" | custom-call | flops 2147483648 | bytes 4194304 | tf_op jit(solution)/shard_map/kerr/pallas_call | solution.py:305
  191.6 18.3 %collective-permute-start.14 = (bf16[16,2,64,128]{3,2,1,0:T(8,128)(2,1)S(1)}, bf16[16,2,64,128]{3,2,1,0:T(8,128)(2,1)S(1)}, u32[]{:S(2)}, u32[]{:S(2)}) collective-permute-start(bf16[16,2,64,128]{3,2,1,0:T(8,128)(2,1)S(1)} %get-tuple-element.133), channel_id=1, source_target_pairs={{0,12},{4,0},{8,4},{12,8},{1,13},{5,1},{9,5},{13,9},{2,14},{6,2},{... | collective-permute-start | bytes 1572872 | tf_op jit(solution)/shard_map/ppermute | solution.py:401
  209.9 10.7 %collective-permute-done.19.refs_2_ = bf16[16,2,64,128]{3,2,1,0:T(8,128)(2,1)S(1)} collective-permute-done((bf16[16,2,64,128]{3,2,1,0:T(8,128)(2,1)S(1)}, bf16[16,2,64,128]{3,2,1,0:T(8,128)(2,1)S(1)}, u32[]{:S(2)}, u32[]{:S(2)}) %collective-permute-start.19) | collective-permute-done | bytes 524320 | tf_op jit(solution)/shard_map/ppermute | solution.py:401
  231.4 11.7 %collective-permute-done.13.refs_2_ = bf16[16,2,64,128]{3,2,1,0:T(8,128)(2,1)S(1)} collective-permute-done((bf16[16,2,64,128]{3,2,1,0:T(8,128)(2,1)S(1)}, bf16[16,2,64,128]{3,2,1,0:T(8,128)(2,1)S(1)}, u32[]{:S(2)}, u32[]{:S(2)}) %collective-permute-start.13) | collective-permute-done | bytes 524320 | tf_op jit(solution)/shard_map/ppermute | solution.py:401
  243.1 19.9 %collective-permute-start.29 = (bf16[16,2,64,128]{3,2,1,0:T(8,128)(2,1)S(1)}, bf16[16,2,64,128]{3,2,1,0:T(8,128)(2,1)S(1)}, u32[]{:S(2)}, u32[]{:S(2)}) collective-permute-start(bf16[16,2,64,128]{3,2,1,0:T(8,128)(2,1)S(1)} %get-tuple-element.160), channel_id=1, source_target_pairs={{0,12},{4,0},{8,4},{12,8},{1,13},{5,1},{9,5},{13,9},{2,14},{6,2},{... | collective-permute-start | bytes 1572872 | tf_op jit(solution)/shard_map/ppermute | solution.py:401
  262.9 13.1 %collective-permute-start.25 = (bf16[16,2,64,128]{3,2,1,0:T(8,128)(2,1)S(1)}, bf16[16,2,64,128]{3,2,1,0:T(8,128)(2,1)S(1)}, u32[]{:S(2)}, u32[]{:S(2)}) collective-permute-start(bf16[16,2,64,128]{3,2,1,0:T(8,128)(2,1)S(1)} %get-tuple-element.154), channel_id=1, source_target_pairs={{0,8},{4,12},{8,0},{12,4},{1,9},{5,13},{9,1},{13,5},{2,10},{6,14},... | collective-permute-start | bytes 1572872 | tf_op jit(solution)/shard_map/ppermute | solution.py:401
  295.1 43.5 %collective-permute-done.28.refs_2_ = bf16[16,2,64,128]{3,2,1,0:T(8,128)(2,1)S(1)} collective-permute-done((bf16[16,2,64,128]{3,2,1,0:T(8,128)(2,1)S(1)}, bf16[16,2,64,128]{3,2,1,0:T(8,128)(2,1)S(1)}, u32[]{:S(2)}, u32[]{:S(2)}) %collective-permute-start.28) | collective-permute-done | bytes 524320 | tf_op jit(solution)/shard_map/ppermute | solution.py:401
  345.9 9.6 %collective-permute-done.25.refs_2_ = bf16[16,2,64,128]{3,2,1,0:T(8,128)(2,1)S(1)} collective-permute-done((bf16[16,2,64,128]{3,2,1,0:T(8,128)(2,1)S(1)}, bf16[16,2,64,128]{3,2,1,0:T(8,128)(2,1)S(1)}, u32[]{:S(2)}, u32[]{:S(2)}) %collective-permute-start.25) | collective-permute-done | bytes 524320 | tf_op jit(solution)/shard_map/ppermute | solution.py:401
  370.6 19.1 %collective-permute-start.35 = (bf16[16,2,64,128]{3,2,1,0:T(8,128)(2,1)S(1)}, bf16[16,2,64,128]{3,2,1,0:T(8,128)(2,1)S(1)}, u32[]{:S(2)}, u32[]{:S(2)}) collective-permute-start(bf16[16,2,64,128]{3,2,1,0:T(8,128)(2,1)S(1)} %get-tuple-element.172), channel_id=1, source_target_pairs={{0,12},{4,0},{8,4},{12,8},{1,13},{5,1},{9,5},{13,9},{2,14},{6,2},{... | collective-permute-start | bytes 1572872 | tf_op jit(solution)/shard_map/ppermute | solution.py:401
  389.8 10.7 %collective-permute-done.22.refs_2_ = bf16[16,2,64,128]{3,2,1,0:T(8,128)(2,1)S(1)} collective-permute-done((bf16[16,2,64,128]{3,2,1,0:T(8,128)(2,1)S(1)}, bf16[16,2,64,128]{3,2,1,0:T(8,128)(2,1)S(1)}, u32[]{:S(2)}, u32[]{:S(2)}) %collective-permute-start.22) | collective-permute-done | bytes 524320 | tf_op jit(solution)/shard_map/ppermute | solution.py:401
  407.8 26.9 %collective-permute-start.38 = (bf16[16,2,64,128]{3,2,1,0:T(8,128)(2,1)S(1)}, bf16[16,2,64,128]{3,2,1,0:T(8,128)(2,1)S(1)}, u32[]{:S(2)}, u32[]{:S(2)}) collective-permute-start(bf16[16,2,64,128]{3,2,1,0:T(8,128)(2,1)S(1)} %get-tuple-element.179), channel_id=1, source_target_pairs={{0,12},{4,0},{8,4},{12,8},{1,13},{5,1},{9,5},{13,9},{2,14},{6,2},{... | collective-permute-start | bytes 1572872 | tf_op jit(solution)/shard_map/ppermute | solution.py:401
  434.7 10.7 %collective-permute-done.34.refs_2_ = bf16[16,2,64,128]{3,2,1,0:T(8,128)(2,1)S(1)} collective-permute-done((bf16[16,2,64,128]{3,2,1,0:T(8,128)(2,1)S(1)}, bf16[16,2,64,128]{3,2,1,0:T(8,128)(2,1)S(1)}, u32[]{:S(2)}, u32[]{:S(2)}) %collective-permute-start.34) | collective-permute-done | bytes 524320 | tf_op jit(solution)/shard_map/ppermute | solution.py:401
  445.4 34.2 %collective-permute-start.32 = (bf16[16,2,64,128]{3,2,1,0:T(8,128)(2,1)S(1)}, bf16[16,2,64,128]{3,2,1,0:T(8,128)(2,1)S(1)}, u32[]{:S(2)}, u32[]{:S(2)}) collective-permute-start(bf16[16,2,64,128]{3,2,1,0:T(8,128)(2,1)S(1)} %get-tuple-element.168), channel_id=1, source_target_pairs={{0,12},{4,0},{8,4},{12,8},{1,13},{5,1},{9,5},{13,9},{2,14},{6,2},{... | collective-permute-start | bytes 1572872 | tf_op jit(solution)/shard_map/ppermute | solution.py:401
  479.6 8.0 %analyze.12 = (bf16[2,64,512,128]{3,2,1,0:T(8,128)(2,1)}, f32[8,128]{1,0:T(8,128)S(1)}) custom-call(s32[64]{0:T(128)S(1)} %copy-done.3, s32[1]{0:T(128)} %bitcast.me_ref, bf16[16,2,64,128]{3,2,1,0:T(8,128)(2,1)S(1)} %get-tuple-element.169.refs_0_, bf16[16,2,64,128]{3,2,1,0:T(8,128)(2,1)S(1)} %collective-permute-done.33.refs_1_, ...), custom_call_target="tpu_custom_call", output_to_operand_aliasing={{0}: (15, {})} | custom-call | flops 268435456 | bytes 6291456 | tf_op jit(solution)/shard_map/analyze/pallas_call | solution.py:370
  496.3 28.2 %collective-permute-start.47 = (bf16[16,2,64,128]{3,2,1,0:T(8,128)(2,1)S(1)}, bf16[16,2,64,128]{3,2,1,0:T(8,128)(2,1)S(1)}, u32[]{:S(2)}, u32[]{:S(2)}) collective-permute-start(bf16[16,2,64,128]{3,2,1,0:T(8,128)(2,1)S(1)} %get-tuple-element.196), channel_id=1, source_target_pairs={{0,12},{4,0},{8,4},{12,8},{1,13},{5,1},{9,5},{13,9},{2,14},{6,2},{... | collective-permute-start | bytes 1572872 | tf_op jit(solution)/shard_map/ppermute | solution.py:401
  550.4 19.1 %collective-permute-start.44 = (bf16[16,2,64,128]{3,2,1,0:T(8,128)(2,1)S(1)}, bf16[16,2,64,128]{3,2,1,0:T(8,128)(2,1)S(1)}, u32[]{:S(2)}, u32[]{:S(2)}) collective-permute-start(bf16[16,2,64,128]{3,2,1,0:T(8,128)(2,1)S(1)} %get-tuple-element.191), channel_id=1, source_target_pairs={{0,12},{4,0},{8,4},{12,8},{1,13},{5,1},{9,5},{13,9},{2,14},{6,2},{... | collective-permute-start | bytes 1572872 | tf_op jit(solution)/shard_map/ppermute | solution.py:401
  569.5 10.7 %collective-permute-done.46.refs_2_ = bf16[16,2,64,128]{3,2,1,0:T(8,128)(2,1)S(1)} collective-permute-done((bf16[16,2,64,128]{3,2,1,0:T(8,128)(2,1)S(1)}, bf16[16,2,64,128]{3,2,1,0:T(8,128)(2,1)S(1)}, u32[]{:S(2)}, u32[]{:S(2)}) %collective-permute-start.46) | collective-permute-done | bytes 524320 | tf_op jit(solution)/shard_map/ppermute | solution.py:401
  587.5 26.9 %collective-permute-start.41 = (bf16[16,2,64,128]{3,2,1,0:T(8,128)(2,1)S(1)}, bf16[16,2,64,128]{3,2,1,0:T(8,128)(2,1)S(1)}, u32[]{:S(2)}, u32[]{:S(2)}) collective-permute-start(bf16[16,2,64,128]{3,2,1,0:T(8,128)(2,1)S(1)} %get-tuple-element.187), channel_id=1, source_target_pairs={{0,12},{4,0},{8,4},{12,8},{1,13},{5,1},{9,5},{13,9},{2,14},{6,2},{... | collective-permute-start | bytes 1572872 | tf_op jit(solution)/shard_map/ppermute | solution.py:401
  614.5 10.7 %collective-permute-done.43.refs_2_ = bf16[16,2,64,128]{3,2,1,0:T(8,128)(2,1)S(1)} collective-permute-done((bf16[16,2,64,128]{3,2,1,0:T(8,128)(2,1)S(1)}, bf16[16,2,64,128]{3,2,1,0:T(8,128)(2,1)S(1)}, u32[]{:S(2)}, u32[]{:S(2)}) %collective-permute-start.43) | collective-permute-done | bytes 524320 | tf_op jit(solution)/shard_map/ppermute | solution.py:401
  625.2 8.0 %analyze.14 = (bf16[2,64,512,128]{3,2,1,0:T(8,128)(2,1)}, f32[8,128]{1,0:T(8,128)S(1)}) custom-call(s32[64]{0:T(128)S(1)} %copy-done.3, s32[1]{0:T(128)} %bitcast.me_ref, bf16[16,2,64,128]{3,2,1,0:T(8,128)(2,1)S(1)} %get-tuple-element.188.refs_0_, bf16[16,2,64,128]{3,2,1,0:T(8,128)(2,1)S(1)} %collective-permute-done.42.refs_1_, ...), custom_call_target="tpu_custom_call", output_to_operand_aliasing={{0}: (15, {})} | custom-call | flops 268435456 | bytes 6291456 | tf_op jit(solution)/shard_map/analyze/pallas_call | solution.py:370
  633.1 26.3 %collective-permute-start.56 = (bf16[16,2,64,128]{3,2,1,0:T(8,128)(2,1)S(1)}, bf16[16,2,64,128]{3,2,1,0:T(8,128)(2,1)S(1)}, u32[]{:S(2)}, u32[]{:S(2)}) collective-permute-start(bf16[16,2,64,128]{3,2,1,0:T(8,128)(2,1)S(1)} %get-tuple-element.211), channel_id=1, source_target_pairs={{0,12},{4,0},{8,4},{12,8},{1,13},{5,1},{9,5},{13,9},{2,14},{6,2},{... | collective-permute-start | bytes 1572872 | tf_op jit(solution)/shard_map/ppermute | solution.py:401
  659.4 10.7 %collective-permute-done.40.refs_2_ = bf16[16,2,64,128]{3,2,1,0:T(8,128)(2,1)S(1)} collective-permute-done((bf16[16,2,64,128]{3,2,1,0:T(8,128)(2,1)S(1)}, bf16[16,2,64,128]{3,2,1,0:T(8,128)(2,1)S(1)}, u32[]{:S(2)}, u32[]{:S(2)}) %collective-permute-start.40) | collective-permute-done | bytes 524320 | tf_op jit(solution)/shard_map/ppermute | solution.py:401
  677.4 13.2 %collective-permute-start.53 = (bf16[16,2,48,128]{3,2,1,0:T(8,128)(2,1)S(1)}, bf16[16,2,48,128]{3,2,1,0:T(8,128)(2,1)S(1)}, u32[]{:S(2)}, u32[]{:S(2)}) collective-permute-start(bf16[16,2,48,128]{3,2,1,0:T(8,128)(2,1)S(1)} %get-tuple-element.207), channel_id=1, source_target_pairs={{0,8},{4,12},{8,0},{12,4},{1,9},{5,13},{9,1},{13,5},{2,10},{6,14},... | collective-permute-start | bytes 1179656 | tf_op jit(solution)/shard_map/ppermute | solution.py:401
  695.8 15.8 %collective-permute-start.50 = (bf16[16,2,16,128]{3,2,1,0:T(8,128)(2,1)S(1)}, bf16[16,2,16,128]{3,2,1,0:T(8,128)(2,1)S(1)}, u32[]{:S(2)}, u32[]{:S(2)}) collective-permute-start(bf16[16,2,16,128]{3,2,1,0:T(8,128)(2,1)S(1)} %get-tuple-element.203), channel_id=1, source_target_pairs={{0,8},{4,12},{8,0},{12,4},{1,9},{5,13},{9,1},{13,5},{2,10},{6,14},... | collective-permute-start | bytes 393224 | tf_op jit(solution)/shard_map/ppermute | solution.py:401
  711.6 12.4 %collective-permute-start.51 = (bf16[16,2,16,128]{3,2,1,0:T(8,128)(2,1)S(1)}, bf16[16,2,16,128]{3,2,1,0:T(8,128)(2,1)S(1)}, u32[]{:S(2)}, u32[]{:S(2)}) collective-permute-start(bf16[16,2,16,128]{3,2,1,0:T(8,128)(2,1)S(1)} %get-tuple-element.204), channel_id=1, source_target_pairs={{0,12},{4,0},{8,4},{12,8},{1,13},{5,1},{9,5},{13,9},{2,14},{6,2},{... | collective-permute-start | bytes 393224 | tf_op jit(solution)/shard_map/ppermute | solution.py:401
  (141 shorter events, 207.0 us)
Async XLA Ops:
  48.1 61.1 %collective-permute-start.6 = (bf16[16,2,64,128]{3,2,1,0:T(8,128)(2,1)}, bf16[16,2,64,128]{3,2,1,0:T(8,128)(2,1)}, u32[]{:S(2)}, u32[]{:S(2)}) collective-permute-start(bf16[16,2,64,128]{3,2,1,0:T(8,128)(2,1)} %get-tuple-element.120), channel_id=1, source_target_pairs={{0,4},{4,8},{8,12},{12,0},{1,5},{5,9},{9,13},{13,1},{2,6},{6,10},{... | collective-permute-start | bytes 1572872 | tf_op jit(solution)/shard_map/ppermute | solution.py:401
  51.4 79.3 %collective-permute-start.7 = (bf16[16,2,64,128]{3,2,1,0:T(8,128)(2,1)}, bf16[16,2,64,128]{3,2,1,0:T(8,128)(2,1)}, u32[]{:S(2)}, u32[]{:S(2)}) collective-permute-start(bf16[16,2,64,128]{3,2,1,0:T(8,128)(2,1)} %get-tuple-element.121), channel_id=1, source_target_pairs={{0,8},{4,12},{8,0},{12,4},{1,9},{5,13},{9,1},{13,5},{2,10},{6,14},... | collective-permute-start | bytes 1572872 | tf_op jit(solution)/shard_map/ppermute | solution.py:401
  63.2 67.6 %collective-permute-start.8 = (bf16[16,2,64,128]{3,2,1,0:T(8,128)(2,1)}, bf16[16,2,64,128]{3,2,1,0:T(8,128)(2,1)}, u32[]{:S(2)}, u32[]{:S(2)}) collective-permute-start(bf16[16,2,64,128]{3,2,1,0:T(8,128)(2,1)} %get-tuple-element.122), channel_id=1, source_target_pairs={{0,12},{4,0},{8,4},{12,8},{1,13},{5,1},{9,5},{13,9},{2,14},{6,2},{... | collective-permute-start | bytes 1572872 | tf_op jit(solution)/shard_map/ppermute | solution.py:401
  72.0 69.2 %collective-permute-start.15 = (bf16[16,2,64,128]{3,2,1,0:T(8,128)(2,1)}, bf16[16,2,64,128]{3,2,1,0:T(8,128)(2,1)}, u32[]{:S(2)}, u32[]{:S(2)}) collective-permute-start(bf16[16,2,64,128]{3,2,1,0:T(8,128)(2,1)} %get-tuple-element.135), channel_id=1, source_target_pairs={{0,4},{4,8},{8,12},{12,0},{1,5},{5,9},{9,13},{13,1},{2,6},{6,10},{... | collective-permute-start | bytes 1572872 | tf_op jit(solution)/shard_map/ppermute | solution.py:401
  80.9 94.9 %collective-permute-start.16 = (bf16[16,2,64,128]{3,2,1,0:T(8,128)(2,1)}, bf16[16,2,64,128]{3,2,1,0:T(8,128)(2,1)}, u32[]{:S(2)}, u32[]{:S(2)}) collective-permute-start(bf16[16,2,64,128]{3,2,1,0:T(8,128)(2,1)} %get-tuple-element.136), channel_id=1, source_target_pairs={{0,8},{4,12},{8,0},{12,4},{1,9},{5,13},{9,1},{13,5},{2,10},{6,14},... | collective-permute-start | bytes 1572872 | tf_op jit(solution)/shard_map/ppermute | solution.py:401
  109.1 67.2 %collective-permute-start.17 = (bf16[16,2,64,128]{3,2,1,0:T(8,128)(2,1)S(1)}, bf16[16,2,64,128]{3,2,1,0:T(8,128)(2,1)S(1)}, u32[]{:S(2)}, u32[]{:S(2)}) collective-permute-start(bf16[16,2,64,128]{3,2,1,0:T(8,128)(2,1)S(1)} %copy-done.7), channel_id=1, source_target_pairs={{0,12},{4,0},{8,4},{12,8},{1,13},{5,1},{9,5},{13,9},{2,14},{6,2},{... | collective-permute-start | bytes 1572872 | tf_op jit(solution)/shard_map/ppermute | solution.py:401
  130.8 89.8 %collective-permute-start.19 = (bf16[16,2,64,128]{3,2,1,0:T(8,128)(2,1)S(1)}, bf16[16,2,64,128]{3,2,1,0:T(8,128)(2,1)S(1)}, u32[]{:S(2)}, u32[]{:S(2)}) collective-permute-start(bf16[16,2,64,128]{3,2,1,0:T(8,128)(2,1)S(1)} %get-tuple-element.142), channel_id=1, source_target_pairs={{0,8},{4,12},{8,0},{12,4},{1,9},{5,13},{9,1},{13,5},{2,10},{6,14},... | collective-permute-start | bytes 1572872 | tf_op jit(solution)/shard_map/ppermute | solution.py:401
  141.3 79.3 %collective-permute-start.20 = (bf16[16,2,64,128]{3,2,1,0:T(8,128)(2,1)S(1)}, bf16[16,2,64,128]{3,2,1,0:T(8,128)(2,1)S(1)}, u32[]{:S(2)}, u32[]{:S(2)}) collective-permute-start(bf16[16,2,64,128]{3,2,1,0:T(8,128)(2,1)S(1)} %get-tuple-element.143), channel_id=1, source_target_pairs={{0,12},{4,0},{8,4},{12,8},{1,13},{5,1},{9,5},{13,9},{2,14},{6,2},{... | collective-permute-start | bytes 1572872 | tf_op jit(solution)/shard_map/ppermute | solution.py:401
  176.4 66.7 %collective-permute-start.13 = (bf16[16,2,64,128]{3,2,1,0:T(8,128)(2,1)S(1)}, bf16[16,2,64,128]{3,2,1,0:T(8,128)(2,1)S(1)}, u32[]{:S(2)}, u32[]{:S(2)}) collective-permute-start(bf16[16,2,64,128]{3,2,1,0:T(8,128)(2,1)S(1)} %get-tuple-element.132), channel_id=1, source_target_pairs={{0,8},{4,12},{8,0},{12,4},{1,9},{5,13},{9,1},{13,5},{2,10},{6,14},... | collective-permute-start | bytes 1572872 | tf_op jit(solution)/shard_map/ppermute | solution.py:401
  191.6 71.4 %collective-permute-start.14 = (bf16[16,2,64,128]{3,2,1,0:T(8,128)(2,1)S(1)}, bf16[16,2,64,128]{3,2,1,0:T(8,128)(2,1)S(1)}, u32[]{:S(2)}, u32[]{:S(2)}) collective-permute-start(bf16[16,2,64,128]{3,2,1,0:T(8,128)(2,1)S(1)} %get-tuple-element.133), channel_id=1, source_target_pairs={{0,12},{4,0},{8,4},{12,8},{1,13},{5,1},{9,5},{13,9},{2,14},{6,2},{... | collective-permute-start | bytes 1572872 | tf_op jit(solution)/shard_map/ppermute | solution.py:401
  227.9 63.3 %collective-permute-start.27 = (bf16[16,2,64,128]{3,2,1,0:T(8,128)(2,1)S(1)}, bf16[16,2,64,128]{3,2,1,0:T(8,128)(2,1)S(1)}, u32[]{:S(2)}, u32[]{:S(2)}) collective-permute-start(bf16[16,2,64,128]{3,2,1,0:T(8,128)(2,1)S(1)} %get-tuple-element.158), channel_id=1, source_target_pairs={{0,4},{4,8},{8,12},{12,0},{1,5},{5,9},{9,13},{13,1},{2,6},{6,10},{... | collective-permute-start | bytes 1572872 | tf_op jit(solution)/shard_map/ppermute | solution.py:401
  228.9 109.8 %collective-permute-start.28 = (bf16[16,2,64,128]{3,2,1,0:T(8,128)(2,1)S(1)}, bf16[16,2,64,128]{3,2,1,0:T(8,128)(2,1)S(1)}, u32[]{:S(2)}, u32[]{:S(2)}) collective-permute-start(bf16[16,2,64,128]{3,2,1,0:T(8,128)(2,1)S(1)} %get-tuple-element.159), channel_id=1, source_target_pairs={{0,8},{4,12},{8,0},{12,4},{1,9},{5,13},{9,1},{13,5},{2,10},{6,14},... | collective-permute-start | bytes 1572872 | tf_op jit(solution)/shard_map/ppermute | solution.py:401
  243.1 95.6 %collective-permute-start.29 = (bf16[16,2,64,128]{3,2,1,0:T(8,128)(2,1)S(1)}, bf16[16,2,64,128]{3,2,1,0:T(8,128)(2,1)S(1)}, u32[]{:S(2)}, u32[]{:S(2)}) collective-permute-start(bf16[16,2,64,128]{3,2,1,0:T(8,128)(2,1)S(1)} %get-tuple-element.160), channel_id=1, source_target_pairs={{0,12},{4,0},{8,4},{12,8},{1,13},{5,1},{9,5},{13,9},{2,14},{6,2},{... | collective-permute-start | bytes 1572872 | tf_op jit(solution)/shard_map/ppermute | solution.py:401
  262.9 92.6 %collective-permute-start.25 = (bf16[16,2,64,128]{3,2,1,0:T(8,128)(2,1)S(1)}, bf16[16,2,64,128]{3,2,1,0:T(8,128)(2,1)S(1)}, u32[]{:S(2)}, u32[]{:S(2)}) collective-permute-start(bf16[16,2,64,128]{3,2,1,0:T(8,128)(2,1)S(1)} %get-tuple-element.154), channel_id=1, source_target_pairs={{0,8},{4,12},{8,0},{12,4},{1,9},{5,13},{9,1},{13,5},{2,10},{6,14},... | collective-permute-start | bytes 1572872 | tf_op jit(solution)/shard_map/ppermute | solution.py:401
  276.1 79.4 %collective-permute-start.26 = (bf16[16,2,64,128]{3,2,1,0:T(8,128)(2,1)S(1)}, bf16[16,2,64,128]{3,2,1,0:T(8,128)(2,1)S(1)}, u32[]{:S(2)}, u32[]{:S(2)}) collective-permute-start(bf16[16,2,64,128]{3,2,1,0:T(8,128)(2,1)S(1)} %get-tuple-element.155), channel_id=1, source_target_pairs={{0,12},{4,0},{8,4},{12,8},{1,13},{5,1},{9,5},{13,9},{2,14},{6,2},{... | collective-permute-start | bytes 1572872 | tf_op jit(solution)/shard_map/ppermute | solution.py:401
  291.2 79.4 %collective-permute-start.21 = (bf16[16,2,64,128]{3,2,1,0:T(8,128)(2,1)S(1)}, bf16[16,2,64,128]{3,2,1,0:T(8,128)(2,1)S(1)}, u32[]{:S(2)}, u32[]{:S(2)}) collective-permute-start(bf16[16,2,64,128]{3,2,1,0:T(8,128)(2,1)S(1)} %get-tuple-element.149), channel_id=1, source_target_pairs={{0,4},{4,8},{8,12},{12,0},{1,5},{5,9},{9,13},{13,1},{2,6},{6,10},{... | collective-permute-start | bytes 1572872 | tf_op jit(solution)/shard_map/ppermute | solution.py:401
  338.6 61.8 %collective-permute-start.22 = (bf16[16,2,64,128]{3,2,1,0:T(8,128)(2,1)S(1)}, bf16[16,2,64,128]{3,2,1,0:T(8,128)(2,1)S(1)}, u32[]{:S(2)}, u32[]{:S(2)}) collective-permute-start(bf16[16,2,64,128]{3,2,1,0:T(8,128)(2,1)S(1)} %get-tuple-element.150), channel_id=1, source_target_pairs={{0,8},{4,12},{8,0},{12,4},{1,9},{5,13},{9,1},{13,5},{2,10},{6,14},... | collective-permute-start | bytes 1572872 | tf_op jit(solution)/shard_map/ppermute | solution.py:401
  338.6 61.8 %collective-permute-start.23 = (bf16[16,2,64,128]{3,2,1,0:T(8,128)(2,1)S(1)}, bf16[16,2,64,128]{3,2,1,0:T(8,128)(2,1)S(1)}, u32[]{:S(2)}, u32[]{:S(2)}) collective-permute-start(bf16[16,2,64,128]{3,2,1,0:T(8,128)(2,1)S(1)} %get-tuple-element.151), channel_id=1, source_target_pairs={{0,12},{4,0},{8,4},{12,8},{1,13},{5,1},{9,5},{13,9},{2,14},{6,2},{... | collective-permute-start | bytes 1572872 | tf_op jit(solution)/shard_map/ppermute | solution.py:401
  355.5 89.9 %collective-permute-start.34 = (bf16[16,2,64,128]{3,2,1,0:T(8,128)(2,1)S(1)}, bf16[16,2,64,128]{3,2,1,0:T(8,128)(2,1)S(1)}, u32[]{:S(2)}, u32[]{:S(2)}) collective-permute-start(bf16[16,2,64,128]{3,2,1,0:T(8,128)(2,1)S(1)} %get-tuple-element.171), channel_id=1, source_target_pairs={{0,8},{4,12},{8,0},{12,4},{1,9},{5,13},{9,1},{13,5},{2,10},{6,14},... | collective-permute-start | bytes 1572872 | tf_op jit(solution)/shard_map/ppermute | solution.py:401
  370.6 74.8 %collective-permute-start.35 = (bf16[16,2,64,128]{3,2,1,0:T(8,128)(2,1)S(1)}, bf16[16,2,64,128]{3,2,1,0:T(8,128)(2,1)S(1)}, u32[]{:S(2)}, u32[]{:S(2)}) collective-permute-start(bf16[16,2,64,128]{3,2,1,0:T(8,128)(2,1)S(1)} %get-tuple-element.172), channel_id=1, source_target_pairs={{0,12},{4,0},{8,4},{12,8},{1,13},{5,1},{9,5},{13,9},{2,14},{6,2},{... | collective-permute-start | bytes 1572872 | tf_op jit(solution)/shard_map/ppermute | solution.py:401
  400.4 94.4 %collective-permute-start.37 = (bf16[16,2,64,128]{3,2,1,0:T(8,128)(2,1)S(1)}, bf16[16,2,64,128]{3,2,1,0:T(8,128)(2,1)S(1)}, u32[]{:S(2)}, u32[]{:S(2)}) collective-permute-start(bf16[16,2,64,128]{3,2,1,0:T(8,128)(2,1)S(1)} %get-tuple-element.178), channel_id=1, source_target_pairs={{0,8},{4,12},{8,0},{12,4},{1,9},{5,13},{9,1},{13,5},{2,10},{6,14},... | collective-permute-start | bytes 1572872 | tf_op jit(solution)/shard_map/ppermute | solution.py:401
  407.8 87.1 %collective-permute-start.38 = (bf16[16,2,64,128]{3,2,1,0:T(8,128)(2,1)S(1)}, bf16[16,2,64,128]{3,2,1,0:T(8,128)(2,1)S(1)}, u32[]{:S(2)}, u32[]{:S(2)}) collective-permute-start(bf16[16,2,64,128]{3,2,1,0:T(8,128)(2,1)S(1)} %get-tuple-element.179), channel_id=1, source_target_pairs={{0,12},{4,0},{8,4},{12,8},{1,13},{5,1},{9,5},{13,9},{2,14},{6,2},{... | collective-permute-start | bytes 1572872 | tf_op jit(solution)/shard_map/ppermute | solution.py:401
  445.4 89.9 %collective-permute-start.31 = (bf16[16,2,64,128]{3,2,1,0:T(8,128)(2,1)S(1)}, bf16[16,2,64,128]{3,2,1,0:T(8,128)(2,1)S(1)}, u32[]{:S(2)}, u32[]{:S(2)}) collective-permute-start(bf16[16,2,64,128]{3,2,1,0:T(8,128)(2,1)S(1)} %get-tuple-element.167), channel_id=1, source_target_pairs={{0,8},{4,12},{8,0},{12,4},{1,9},{5,13},{9,1},{13,5},{2,10},{6,14},... | collective-permute-start | bytes 1572872 | tf_op jit(solution)/shard_map/ppermute | solution.py:401
  445.4 89.9 %collective-permute-start.32 = (bf16[16,2,64,128]{3,2,1,0:T(8,128)(2,1)S(1)}, bf16[16,2,64,128]{3,2,1,0:T(8,128)(2,1)S(1)}, u32[]{:S(2)}, u32[]{:S(2)}) collective-permute-start(bf16[16,2,64,128]{3,2,1,0:T(8,128)(2,1)S(1)} %get-tuple-element.168), channel_id=1, source_target_pairs={{0,12},{4,0},{8,4},{12,8},{1,13},{5,1},{9,5},{13,9},{2,14},{6,2},{... | collective-permute-start | bytes 1572872 | tf_op jit(solution)/shard_map/ppermute | solution.py:401
  494.9 85.3 %collective-permute-start.46 = (bf16[16,2,64,128]{3,2,1,0:T(8,128)(2,1)S(1)}, bf16[16,2,64,128]{3,2,1,0:T(8,128)(2,1)S(1)}, u32[]{:S(2)}, u32[]{:S(2)}) collective-permute-start(bf16[16,2,64,128]{3,2,1,0:T(8,128)(2,1)S(1)} %get-tuple-element.195), channel_id=1, source_target_pairs={{0,8},{4,12},{8,0},{12,4},{1,9},{5,13},{9,1},{13,5},{2,10},{6,14},... | collective-permute-start | bytes 1572872 | tf_op jit(solution)/shard_map/ppermute | solution.py:401
  496.3 83.9 %collective-permute-start.47 = (bf16[16,2,64,128]{3,2,1,0:T(8,128)(2,1)S(1)}, bf16[16,2,64,128]{3,2,1,0:T(8,128)(2,1)S(1)}, u32[]{:S(2)}, u32[]{:S(2)}) collective-permute-start(bf16[16,2,64,128]{3,2,1,0:T(8,128)(2,1)S(1)} %get-tuple-element.196), channel_id=1, source_target_pairs={{0,12},{4,0},{8,4},{12,8},{1,13},{5,1},{9,5},{13,9},{2,14},{6,2},{... | collective-permute-start | bytes 1572872 | tf_op jit(solution)/shard_map/ppermute | solution.py:401
  535.3 89.9 %collective-permute-start.43 = (bf16[16,2,64,128]{3,2,1,0:T(8,128)(2,1)S(1)}, bf16[16,2,64,128]{3,2,1,0:T(8,128)(2,1)S(1)}, u32[]{:S(2)}, u32[]{:S(2)}) collective-permute-start(bf16[16,2,64,128]{3,2,1,0:T(8,128)(2,1)S(1)} %get-tuple-element.190), channel_id=1, source_target_pairs={{0,8},{4,12},{8,0},{12,4},{1,9},{5,13},{9,1},{13,5},{2,10},{6,14},... | collective-permute-start | bytes 1572872 | tf_op jit(solution)/shard_map/ppermute | solution.py:401
  550.4 74.8 %collective-permute-start.44 = (bf16[16,2,64,128]{3,2,1,0:T(8,128)(2,1)S(1)}, bf16[16,2,64,128]{3,2,1,0:T(8,128)(2,1)S(1)}, u32[]{:S(2)}, u32[]{:S(2)}) collective-permute-start(bf16[16,2,64,128]{3,2,1,0:T(8,128)(2,1)S(1)} %get-tuple-element.191), channel_id=1, source_target_pairs={{0,12},{4,0},{8,4},{12,8},{1,13},{5,1},{9,5},{13,9},{2,14},{6,2},{... | collective-permute-start | bytes 1572872 | tf_op jit(solution)/shard_map/ppermute | solution.py:401
  580.2 89.9 %collective-permute-start.40 = (bf16[16,2,64,128]{3,2,1,0:T(8,128)(2,1)S(1)}, bf16[16,2,64,128]{3,2,1,0:T(8,128)(2,1)S(1)}, u32[]{:S(2)}, u32[]{:S(2)}) collective-permute-start(bf16[16,2,64,128]{3,2,1,0:T(8,128)(2,1)S(1)} %get-tuple-element.186), channel_id=1, source_target_pairs={{0,8},{4,12},{8,0},{12,4},{1,9},{5,13},{9,1},{13,5},{2,10},{6,14},... | collective-permute-start | bytes 1572872 | tf_op jit(solution)/shard_map/ppermute | solution.py:401
  587.5 82.6 %collective-permute-start.41 = (bf16[16,2,64,128]{3,2,1,0:T(8,128)(2,1)S(1)}, bf16[16,2,64,128]{3,2,1,0:T(8,128)(2,1)S(1)}, u32[]{:S(2)}, u32[]{:S(2)}) collective-permute-start(bf16[16,2,64,128]{3,2,1,0:T(8,128)(2,1)S(1)} %get-tuple-element.187), channel_id=1, source_target_pairs={{0,12},{4,0},{8,4},{12,8},{1,13},{5,1},{9,5},{13,9},{2,14},{6,2},{... | collective-permute-start | bytes 1572872 | tf_op jit(solution)/shard_map/ppermute | solution.py:401
  625.2 70.6 %collective-permute-start.55 = (bf16[16,2,64,128]{3,2,1,0:T(8,128)(2,1)S(1)}, bf16[16,2,64,128]{3,2,1,0:T(8,128)(2,1)S(1)}, u32[]{:S(2)}, u32[]{:S(2)}) collective-permute-start(bf16[16,2,64,128]{3,2,1,0:T(8,128)(2,1)S(1)} %get-tuple-element.210), channel_id=1, source_target_pairs={{0,8},{4,12},{8,0},{12,4},{1,9},{5,13},{9,1},{13,5},{2,10},{6,14},... | collective-permute-start | bytes 1572872 | tf_op jit(solution)/shard_map/ppermute | solution.py:401
  633.1 62.6 %collective-permute-start.56 = (bf16[16,2,64,128]{3,2,1,0:T(8,128)(2,1)S(1)}, bf16[16,2,64,128]{3,2,1,0:T(8,128)(2,1)S(1)}, u32[]{:S(2)}, u32[]{:S(2)}) collective-permute-start(bf16[16,2,64,128]{3,2,1,0:T(8,128)(2,1)S(1)} %get-tuple-element.211), channel_id=1, source_target_pairs={{0,12},{4,0},{8,4},{12,8},{1,13},{5,1},{9,5},{13,9},{2,14},{6,2},{... | collective-permute-start | bytes 1572872 | tf_op jit(solution)/shard_map/ppermute | solution.py:401
  (39 other events, 1388.3 us)

commit v8 on v4

--- a/solution.py
+++ b/solution.py
@@ -12,6 +12,7 @@
 ORDERS = 256
 LANES = 128
 ROWS = 16
+STRIDE = ROWS + 1
 
 kerr_gamma = 0.00390625
 
@@ -154,13 +155,15 @@
                 tab_ref[map_ref[m], 0], moved, preferred_element_type=jnp.float32
             )
             for c in range(parts):
-                acc[c, pl.ds(i, block, stride=ROWS), :] = points[:, c * LANES : (c + 1) * LANES]
+                acc[c, pl.ds(i, block, stride=STRIDE), :] = points[:, c * LANES : (c + 1) * LANES]
         for s in range(count):
             owner = lax.rem(me_ref[0] + s, count)
-            for q in range(share):
-                row = pl.multiple_of((owner * share + q) * ROWS, ROWS)
-                for c in range(parts):
-                    outs[s][q, c] = acc[c, pl.ds(row, ROWS), :].astype(jnp.bfloat16)
+            start = pl.multiple_of(owner * share * STRIDE, 8)
+            for c in range(parts):
+                part = acc.at[c, pl.ds(start, share * STRIDE), :]
+                for q in range(share):
+                    row = q * STRIDE
+                    outs[s][q, c] = part[row : row + ROWS, :].astype(jnp.bfloat16)
 
     piece = jax.ShapeDtypeStruct((share, parts, span[1], LANES), jnp.bfloat16)
     size = parts * span[1] * block * LANES * 2
@@ -177,7 +180,7 @@
             ]
             * count
             + anywhere(1),
-            scratch_shapes=[pltpu.VMEM((parts, block * ROWS, LANES), jnp.float32)],
+            scratch_shapes=[pltpu.VMEM((parts, (block + 8) * STRIDE, LANES), jnp.float32)],
         ),
         compiler_params=params(),
         cost_estimate=cost(2 * size * block, 2 * size),
@@ -276,10 +279,12 @@
         g = pl.program_id(0)
         for s in range(count):
             source = lax.rem(me_ref[0] + count - s, count)
-            for q in range(share):
-                row = pl.multiple_of((source * share + q) * ROWS, ROWS)
-                for c in range(parts):
-                    acc[c, pl.ds(row, ROWS), :] = ins[s][q, c].astype(jnp.float32)
+            start = pl.multiple_of(source * share * STRIDE, 8)
+            for c in range(parts):
+                part = acc.at[c, pl.ds(start, share * STRIDE), :]
+                for q in range(share):
+                    row = q * STRIDE
+                    part[row : row + ROWS, :] = ins[s][q, c].astype(jnp.float32)
         beta = columns(beta_ref, b * block, block)
         delta = columns(delta_ref, b * block, block)
         ends = [join_halo(low_ref[c], high_ref[c]) for c in range(parts)]
@@ -287,7 +292,7 @@
             m = (g + base) * ROWS + i
             x = [x_ref[c, i].astype(jnp.float32) for c in range(parts)]
             moved = move(x, ends, beta[:, i : i + 1], delta[:, i : i + 1], m)
-            back = [acc[c, pl.ds(i, block, stride=ROWS), :] for c in range(parts)]
+            back = [acc[c, pl.ds(i, block, stride=STRIDE), :] for c in range(parts)]
             back = jnp.concatenate(back, 1).astype(jnp.bfloat16)
             increment = jnp.dot(
                 tab_ref[map_ref[m], 0], back, preferred_element_type=jnp.float32
@@ -313,7 +318,7 @@
                 pl.BlockSpec((parts, ROWS, block, LANES), lambda g, *_: (0, g + base, b, 0))
             ]
             + anywhere(1),
-            scratch_shapes=[pltpu.VMEM((parts, block * ROWS, LANES), jnp.float32)],
+            scratch_shapes=[pltpu.VMEM((parts, (block + 8) * STRIDE, LANES), jnp.float32)],
         ),
         input_output_aliases={2 + count + 6: 0} if held else {},
         compiler_params=params(),
@@ -461,7 +466,7 @@
         steps == LANES
         and orders % ROWS == 0
         and 2 * orders <= LANES
-        and block % (2 * count) == 0
+        and block % (8 * count) == 0
         and radial % LANES == 0
         and LANES % block == 0
         and nblocks >= 2

time: 743 us -> 742 us (level)
  Pallas kernels: 204 us -> 193 us
  transfers between devices with their start and end apart: 57 -> 57, of which waited for: 20 -> 20; matrix products, arithmetic and copies ran while one was open for 0% -> 0% of each run, Pallas kernels for 26% -> 24%
where the time goes in v8:
time: 742 us; the launch traced here: 740 us
  starting transfers between devices  356 us (48%)
  Pallas kernels  193 us (26%)
  waiting for transfers between devices  186 us (25%)
    ppermute x51, starting transfers between devices, exchange(): lax.ppermute(pieces[s], 'ang', ring('ang', s))  354 us
    ppermute x51, waiting for transfers between devices, exchange(): lax.ppermute(pieces[s], 'ang', ring('ang', s))  175 us
    pallas_call x8, Pallas kernels, kerr_step(): pl.pallas_call(kernel, out_shape=[jax.ShapeDtypeStruct((share, parts, siz...  59.9 us
    pallas_call x9, Pallas kernels, analyze(): pl.pallas_call(kernel, out_shape=[jax.ShapeDtypeStruct(field.shape, field...  57 us
    pallas_call x8, Pallas kernels, synthesize(): pl.pallas_call(kernel, out_shape=[piece] * count + [token()], grid_spec=p...  54.4 us
    pallas_call x3, Pallas kernels, edges(): pl.pallas_call(kernel, out_shape=[jax.ShapeDtypeStruct((parts, count * bl...  22 us
  transfers between devices with their start and end apart: 57, of which 20 were waited for; matrix products, arithmetic and copies ran while one was open for 0% of the time, Pallas kernels for 24%

profile of v8, /device:TPU:24, one launch (start us, length us, event | category | flops | bytes accessed | tf_op | source)
XLA Modules:
  0.0 740.3 jit_solution(3707282485841917254)
XLA Ops:
  22.7 7.3 synthesize.9
  30.0 16.2 %edges.5 = (bf16[2,384,128]{2,1,0:T(8,128)(2,1)S(1)}, f32[8,128]{1,0:T(8,128)S(1)}) custom-call(bf16[2,64,512,128]{3,2,1,0:T(8,128)(2,1)} %refs_4_.17, f32[8,128]{1,0:T(8,128)S(1)} %get-tuple-element.117.refs_0_), custom_call_target="tpu_custom_call" | custom-call | bytes 12582912 | tf_op jit(solution)/shard_map/edges/pallas_call | solution.py:80
  50.8 12.1 %collective-permute-done.10.refs_2_ = bf16[16,2,64,128]{3,2,1,0:T(8,128)(2,1)S(1)} collective-permute-done((bf16[16,2,64,128]{3,2,1,0:T(8,128)(2,1)S(1)}, bf16[16,2,64,128]{3,2,1,0:T(8,128)(2,1)S(1)}, u32[]{:S(2)}, u32[]{:S(2)}) %collective-permute-start.10) | collective-permute-done | bytes 524320 | tf_op jit(solution)/shard_map/ppermute | solution.py:334
  62.9 8.0 %kerr.8 = (bf16[16,2,64,128]{3,2,1,0:T(8,128)(2,1)S(1)}, bf16[16,2,64,128]{3,2,1,0:T(8,128)(2,1)}, bf16[16,2,64,128]{3,2,1,0:T(8,128)(2,1)}, bf16[16,2,64,128]{3,2,1,0:T(8,128)(2,1)S(1)}, f32[8,128]{1,0:T(8,128)S(1)}) custom-call(s32[1]{0:T(128)} %bitcast.me_ref, bf16[512,512]{1,0:T(8,128)(2,1)S(1)} %copy-done.10, bf16[512,512]{1,0:T(8,128)(2,1)S(1)} %copy-done.8, ...), custom_call_target="tpu_custom_call" | custom-call | flops 2147483648 | bytes 4194304 | tf_op jit(solution)/shard_map/kerr/pallas_call | solution.py:239
  80.6 17.6 %collective-permute-start.16 = (bf16[16,2,64,128]{3,2,1,0:T(8,128)(2,1)}, bf16[16,2,64,128]{3,2,1,0:T(8,128)(2,1)}, u32[]{:S(2)}, u32[]{:S(2)}) collective-permute-start(bf16[16,2,64,128]{3,2,1,0:T(8,128)(2,1)} %get-tuple-element.136), channel_id=1, source_target_pairs={{0,8},{4,12},{8,0},{12,4},{1,9},{5,13},{9,1},{13,5},{2,10},{6,14},... | collective-permute-start | bytes 1572872 | tf_op jit(solution)/shard_map/ppermute | solution.py:334
  109.9 20.1 %collective-permute-done.7.refs_2_ = bf16[16,2,64,128]{3,2,1,0:T(8,128)(2,1)} collective-permute-done((bf16[16,2,64,128]{3,2,1,0:T(8,128)(2,1)}, bf16[16,2,64,128]{3,2,1,0:T(8,128)(2,1)}, u32[]{:S(2)}, u32[]{:S(2)}) %collective-permute-start.7) | collective-permute-done | bytes 524320 | tf_op jit(solution)/shard_map/ppermute | solution.py:334
  130.1 10.5 %collective-permute-start.19 = (bf16[16,2,64,128]{3,2,1,0:T(8,128)(2,1)S(1)}, bf16[16,2,64,128]{3,2,1,0:T(8,128)(2,1)S(1)}, u32[]{:S(2)}, u32[]{:S(2)}) collective-permute-start(bf16[16,2,64,128]{3,2,1,0:T(8,128)(2,1)S(1)} %get-tuple-element.142), channel_id=1, source_target_pairs={{0,8},{4,12},{8,0},{12,4},{1,9},{5,13},{9,1},{13,5},{2,10},{6,14},... | collective-permute-start | bytes 1572872 | tf_op jit(solution)/shard_map/ppermute | solution.py:334
  140.6 23.8 %collective-permute-start.20 = (bf16[16,2,64,128]{3,2,1,0:T(8,128)(2,1)S(1)}, bf16[16,2,64,128]{3,2,1,0:T(8,128)(2,1)S(1)}, u32[]{:S(2)}, u32[]{:S(2)}) collective-permute-start(bf16[16,2,64,128]{3,2,1,0:T(8,128)(2,1)S(1)} %get-tuple-element.143), channel_id=1, source_target_pairs={{0,12},{4,0},{8,4},{12,8},{1,13},{5,1},{9,5},{13,9},{2,14},{6,2},{... | collective-permute-start | bytes 1572872 | tf_op jit(solution)/shard_map/ppermute | solution.py:334
  164.4 8.3 %kerr.9 = (bf16[16,2,64,128]{3,2,1,0:T(8,128)(2,1)S(1)}, bf16[16,2,64,128]{3,2,1,0:T(8,128)(2,1)S(1)}, bf16[16,2,64,128]{3,2,1,0:T(8,128)(2,1)S(1)}, bf16[16,2,64,128]{3,2,1,0:T(8,128)(2,1)S(1)}, f32[8,128]{1,0:T(8,128)S(1)}) custom-call(s32[1]{0:T(128)} %bitcast.me_ref, bf16[512,512]{1,0:T(8,128)(2,1)S(1)} %copy-done.11, bf16[512,512]{1,0:T(8,128)(2,1)S(1)} %copy-done.9, ...), custom_call_target="tpu_custom_call" | custom-call | flops 2147483648 | bytes 4194304 | tf_op jit(solution)/shard_map/kerr/pallas_call | solution.py:239
  189.6 19.7 %collective-permute-start.14 = (bf16[16,2,64,128]{3,2,1,0:T(8,128)(2,1)S(1)}, bf16[16,2,64,128]{3,2,1,0:T(8,128)(2,1)S(1)}, u32[]{:S(2)}, u32[]{:S(2)}) collective-permute-start(bf16[16,2,64,128]{3,2,1,0:T(8,128)(2,1)S(1)} %get-tuple-element.133), channel_id=1, source_target_pairs={{0,12},{4,0},{8,4},{12,8},{1,13},{5,1},{9,5},{13,9},{2,14},{6,2},{... | collective-permute-start | bytes 1572872 | tf_op jit(solution)/shard_map/ppermute | solution.py:334
  209.2 10.7 %collective-permute-done.19.refs_2_ = bf16[16,2,64,128]{3,2,1,0:T(8,128)(2,1)S(1)} collective-permute-done((bf16[16,2,64,128]{3,2,1,0:T(8,128)(2,1)S(1)}, bf16[16,2,64,128]{3,2,1,0:T(8,128)(2,1)S(1)}, u32[]{:S(2)}, u32[]{:S(2)}) %collective-permute-start.19) | collective-permute-done | bytes 524320 | tf_op jit(solution)/shard_map/ppermute | solution.py:334
  230.7 11.7 %collective-permute-done.13.refs_2_ = bf16[16,2,64,128]{3,2,1,0:T(8,128)(2,1)S(1)} collective-permute-done((bf16[16,2,64,128]{3,2,1,0:T(8,128)(2,1)S(1)}, bf16[16,2,64,128]{3,2,1,0:T(8,128)(2,1)S(1)}, u32[]{:S(2)}, u32[]{:S(2)}) %collective-permute-start.13) | collective-permute-done | bytes 524320 | tf_op jit(solution)/shard_map/ppermute | solution.py:334
  242.4 19.8 %collective-permute-start.29 = (bf16[16,2,64,128]{3,2,1,0:T(8,128)(2,1)S(1)}, bf16[16,2,64,128]{3,2,1,0:T(8,128)(2,1)S(1)}, u32[]{:S(2)}, u32[]{:S(2)}) collective-permute-start(bf16[16,2,64,128]{3,2,1,0:T(8,128)(2,1)S(1)} %get-tuple-element.160), channel_id=1, source_target_pairs={{0,12},{4,0},{8,4},{12,8},{1,13},{5,1},{9,5},{13,9},{2,14},{6,2},{... | collective-permute-start | bytes 1572872 | tf_op jit(solution)/shard_map/ppermute | solution.py:334
  262.2 13.1 %collective-permute-start.25 = (bf16[16,2,64,128]{3,2,1,0:T(8,128)(2,1)S(1)}, bf16[16,2,64,128]{3,2,1,0:T(8,128)(2,1)S(1)}, u32[]{:S(2)}, u32[]{:S(2)}) collective-permute-start(bf16[16,2,64,128]{3,2,1,0:T(8,128)(2,1)S(1)} %get-tuple-element.154), channel_id=1, source_target_pairs={{0,8},{4,12},{8,0},{12,4},{1,9},{5,13},{9,1},{13,5},{2,10},{6,14},... | collective-permute-start | bytes 1572872 | tf_op jit(solution)/shard_map/ppermute | solution.py:334
  292.7 45.2 %collective-permute-done.28.refs_2_ = bf16[16,2,64,128]{3,2,1,0:T(8,128)(2,1)S(1)} collective-permute-done((bf16[16,2,64,128]{3,2,1,0:T(8,128)(2,1)S(1)}, bf16[16,2,64,128]{3,2,1,0:T(8,128)(2,1)S(1)}, u32[]{:S(2)}, u32[]{:S(2)}) %collective-permute-start.28) | collective-permute-done | bytes 524320 | tf_op jit(solution)/shard_map/ppermute | solution.py:334
  345.3 9.6 %collective-permute-done.25.refs_2_ = bf16[16,2,64,128]{3,2,1,0:T(8,128)(2,1)S(1)} collective-permute-done((bf16[16,2,64,128]{3,2,1,0:T(8,128)(2,1)S(1)}, bf16[16,2,64,128]{3,2,1,0:T(8,128)(2,1)S(1)}, u32[]{:S(2)}, u32[]{:S(2)}) %collective-permute-start.25) | collective-permute-done | bytes 524320 | tf_op jit(solution)/shard_map/ppermute | solution.py:334
  368.4 20.7 %collective-permute-start.35 = (bf16[16,2,64,128]{3,2,1,0:T(8,128)(2,1)S(1)}, bf16[16,2,64,128]{3,2,1,0:T(8,128)(2,1)S(1)}, u32[]{:S(2)}, u32[]{:S(2)}) collective-permute-start(bf16[16,2,64,128]{3,2,1,0:T(8,128)(2,1)S(1)} %get-tuple-element.172), channel_id=1, source_target_pairs={{0,12},{4,0},{8,4},{12,8},{1,13},{5,1},{9,5},{13,9},{2,14},{6,2},{... | collective-permute-start | bytes 1572872 | tf_op jit(solution)/shard_map/ppermute | solution.py:334
  389.1 10.7 %collective-permute-done.22.refs_2_ = bf16[16,2,64,128]{3,2,1,0:T(8,128)(2,1)S(1)} collective-permute-done((bf16[16,2,64,128]{3,2,1,0:T(8,128)(2,1)S(1)}, bf16[16,2,64,128]{3,2,1,0:T(8,128)(2,1)S(1)}, u32[]{:S(2)}, u32[]{:S(2)}) %collective-permute-start.22) | collective-permute-done | bytes 524320 | tf_op jit(solution)/shard_map/ppermute | solution.py:334
  399.8 7.3 kerr.12
  407.1 26.9 %collective-permute-start.38 = (bf16[16,2,64,128]{3,2,1,0:T(8,128)(2,1)S(1)}, bf16[16,2,64,128]{3,2,1,0:T(8,128)(2,1)S(1)}, u32[]{:S(2)}, u32[]{:S(2)}) collective-permute-start(bf16[16,2,64,128]{3,2,1,0:T(8,128)(2,1)S(1)} %get-tuple-element.179), channel_id=1, source_target_pairs={{0,12},{4,0},{8,4},{12,8},{1,13},{5,1},{9,5},{13,9},{2,14},{6,2},{... | collective-permute-start | bytes 1572872 | tf_op jit(solution)/shard_map/ppermute | solution.py:334
  434.0 10.7 %collective-permute-done.34.refs_2_ = bf16[16,2,64,128]{3,2,1,0:T(8,128)(2,1)S(1)} collective-permute-done((bf16[16,2,64,128]{3,2,1,0:T(8,128)(2,1)S(1)}, bf16[16,2,64,128]{3,2,1,0:T(8,128)(2,1)S(1)}, u32[]{:S(2)}, u32[]{:S(2)}) %collective-permute-start.34) | collective-permute-done | bytes 524320 | tf_op jit(solution)/shard_map/ppermute | solution.py:334
  444.7 34.2 %collective-permute-start.32 = (bf16[16,2,64,128]{3,2,1,0:T(8,128)(2,1)S(1)}, bf16[16,2,64,128]{3,2,1,0:T(8,128)(2,1)S(1)}, u32[]{:S(2)}, u32[]{:S(2)}) collective-permute-start(bf16[16,2,64,128]{3,2,1,0:T(8,128)(2,1)S(1)} %get-tuple-element.168), channel_id=1, source_target_pairs={{0,12},{4,0},{8,4},{12,8},{1,13},{5,1},{9,5},{13,9},{2,14},{6,2},{... | collective-permute-start | bytes 1572872 | tf_op jit(solution)/shard_map/ppermute | solution.py:334
  494.0 30.0 %collective-permute-start.47 = (bf16[16,2,64,128]{3,2,1,0:T(8,128)(2,1)S(1)}, bf16[16,2,64,128]{3,2,1,0:T(8,128)(2,1)S(1)}, u32[]{:S(2)}, u32[]{:S(2)}) collective-permute-start(bf16[16,2,64,128]{3,2,1,0:T(8,128)(2,1)S(1)} %get-tuple-element.196), channel_id=1, source_target_pairs={{0,12},{4,0},{8,4},{12,8},{1,13},{5,1},{9,5},{13,9},{2,14},{6,2},{... | collective-permute-start | bytes 1572872 | tf_op jit(solution)/shard_map/ppermute | solution.py:334
  548.2 20.7 %collective-permute-start.44 = (bf16[16,2,64,128]{3,2,1,0:T(8,128)(2,1)S(1)}, bf16[16,2,64,128]{3,2,1,0:T(8,128)(2,1)S(1)}, u32[]{:S(2)}, u32[]{:S(2)}) collective-permute-start(bf16[16,2,64,128]{3,2,1,0:T(8,128)(2,1)S(1)} %get-tuple-element.191), channel_id=1, source_target_pairs={{0,12},{4,0},{8,4},{12,8},{1,13},{5,1},{9,5},{13,9},{2,14},{6,2},{... | collective-permute-start | bytes 1572872 | tf_op jit(solution)/shard_map/ppermute | solution.py:334
  568.9 10.7 %collective-permute-done.46.refs_2_ = bf16[16,2,64,128]{3,2,1,0:T(8,128)(2,1)S(1)} collective-permute-done((bf16[16,2,64,128]{3,2,1,0:T(8,128)(2,1)S(1)}, bf16[16,2,64,128]{3,2,1,0:T(8,128)(2,1)S(1)}, u32[]{:S(2)}, u32[]{:S(2)}) %collective-permute-start.46) | collective-permute-done | bytes 524320 | tf_op jit(solution)/shard_map/ppermute | solution.py:334
  586.9 26.9 %collective-permute-start.41 = (bf16[16,2,64,128]{3,2,1,0:T(8,128)(2,1)S(1)}, bf16[16,2,64,128]{3,2,1,0:T(8,128)(2,1)S(1)}, u32[]{:S(2)}, u32[]{:S(2)}) collective-permute-start(bf16[16,2,64,128]{3,2,1,0:T(8,128)(2,1)S(1)} %get-tuple-element.187), channel_id=1, source_target_pairs={{0,12},{4,0},{8,4},{12,8},{1,13},{5,1},{9,5},{13,9},{2,14},{6,2},{... | collective-permute-start | bytes 1572872 | tf_op jit(solution)/shard_map/ppermute | solution.py:334
  613.8 10.7 %collective-permute-done.43.refs_2_ = bf16[16,2,64,128]{3,2,1,0:T(8,128)(2,1)S(1)} collective-permute-done((bf16[16,2,64,128]{3,2,1,0:T(8,128)(2,1)S(1)}, bf16[16,2,64,128]{3,2,1,0:T(8,128)(2,1)S(1)}, u32[]{:S(2)}, u32[]{:S(2)}) %collective-permute-start.43) | collective-permute-done | bytes 524320 | tf_op jit(solution)/shard_map/ppermute | solution.py:334
  631.3 27.4 %collective-permute-start.56 = (bf16[16,2,64,128]{3,2,1,0:T(8,128)(2,1)S(1)}, bf16[16,2,64,128]{3,2,1,0:T(8,128)(2,1)S(1)}, u32[]{:S(2)}, u32[]{:S(2)}) collective-permute-start(bf16[16,2,64,128]{3,2,1,0:T(8,128)(2,1)S(1)} %get-tuple-element.211), channel_id=1, source_target_pairs={{0,12},{4,0},{8,4},{12,8},{1,13},{5,1},{9,5},{13,9},{2,14},{6,2},{... | collective-permute-start | bytes 1572872 | tf_op jit(solution)/shard_map/ppermute | solution.py:334
  658.7 10.7 %collective-permute-done.40.refs_2_ = bf16[16,2,64,128]{3,2,1,0:T(8,128)(2,1)S(1)} collective-permute-done((bf16[16,2,64,128]{3,2,1,0:T(8,128)(2,1)S(1)}, bf16[16,2,64,128]{3,2,1,0:T(8,128)(2,1)S(1)}, u32[]{:S(2)}, u32[]{:S(2)}) %collective-permute-start.40) | collective-permute-done | bytes 524320 | tf_op jit(solution)/shard_map/ppermute | solution.py:334
  676.7 13.2 %collective-permute-start.53 = (bf16[16,2,48,128]{3,2,1,0:T(8,128)(2,1)S(1)}, bf16[16,2,48,128]{3,2,1,0:T(8,128)(2,1)S(1)}, u32[]{:S(2)}, u32[]{:S(2)}) collective-permute-start(bf16[16,2,48,128]{3,2,1,0:T(8,128)(2,1)S(1)} %get-tuple-element.207), channel_id=1, source_target_pairs={{0,8},{4,12},{8,0},{12,4},{1,9},{5,13},{9,1},{13,5},{2,10},{6,14},... | collective-permute-start | bytes 1179656 | tf_op jit(solution)/shard_map/ppermute | solution.py:334
  695.1 15.8 %collective-permute-start.50 = (bf16[16,2,16,128]{3,2,1,0:T(8,128)(2,1)S(1)}, bf16[16,2,16,128]{3,2,1,0:T(8,128)(2,1)S(1)}, u32[]{:S(2)}, u32[]{:S(2)}) collective-permute-start(bf16[16,2,16,128]{3,2,1,0:T(8,128)(2,1)S(1)} %get-tuple-element.203), channel_id=1, source_target_pairs={{0,8},{4,12},{8,0},{12,4},{1,9},{5,13},{9,1},{13,5},{2,10},{6,14},... | collective-permute-start | bytes 393224 | tf_op jit(solution)/shard_map/ppermute | solution.py:334
  710.9 12.4 %collective-permute-start.51 = (bf16[16,2,16,128]{3,2,1,0:T(8,128)(2,1)S(1)}, bf16[16,2,16,128]{3,2,1,0:T(8,128)(2,1)S(1)}, u32[]{:S(2)}, u32[]{:S(2)}) collective-permute-start(bf16[16,2,16,128]{3,2,1,0:T(8,128)(2,1)S(1)} %get-tuple-element.204), channel_id=1, source_target_pairs={{0,12},{4,0},{8,4},{12,8},{1,13},{5,1},{9,5},{13,9},{2,14},{6,2},{... | collective-permute-start | bytes 393224 | tf_op jit(solution)/shard_map/ppermute | solution.py:334
  (141 shorter events, 197.1 us)
Async XLA Ops:
  46.5 61.4 %collective-permute-start.6 = (bf16[16,2,64,128]{3,2,1,0:T(8,128)(2,1)}, bf16[16,2,64,128]{3,2,1,0:T(8,128)(2,1)}, u32[]{:S(2)}, u32[]{:S(2)}) collective-permute-start(bf16[16,2,64,128]{3,2,1,0:T(8,128)(2,1)} %get-tuple-element.120), channel_id=1, source_target_pairs={{0,4},{4,8},{8,12},{12,0},{1,5},{5,9},{9,13},{13,1},{2,6},{6,10},{... | collective-permute-start | bytes 1572872 | tf_op jit(solution)/shard_map/ppermute | solution.py:334
  49.9 80.2 %collective-permute-start.7 = (bf16[16,2,64,128]{3,2,1,0:T(8,128)(2,1)}, bf16[16,2,64,128]{3,2,1,0:T(8,128)(2,1)}, u32[]{:S(2)}, u32[]{:S(2)}) collective-permute-start(bf16[16,2,64,128]{3,2,1,0:T(8,128)(2,1)} %get-tuple-element.121), channel_id=1, source_target_pairs={{0,8},{4,12},{8,0},{12,4},{1,9},{5,13},{9,1},{13,5},{2,10},{6,14},... | collective-permute-start | bytes 1572872 | tf_op jit(solution)/shard_map/ppermute | solution.py:334
  62.9 67.2 %collective-permute-start.8 = (bf16[16,2,64,128]{3,2,1,0:T(8,128)(2,1)}, bf16[16,2,64,128]{3,2,1,0:T(8,128)(2,1)}, u32[]{:S(2)}, u32[]{:S(2)}) collective-permute-start(bf16[16,2,64,128]{3,2,1,0:T(8,128)(2,1)} %get-tuple-element.122), channel_id=1, source_target_pairs={{0,12},{4,0},{8,4},{12,8},{1,13},{5,1},{9,5},{13,9},{2,14},{6,2},{... | collective-permute-start | bytes 1572872 | tf_op jit(solution)/shard_map/ppermute | solution.py:334
  71.7 68.9 %collective-permute-start.15 = (bf16[16,2,64,128]{3,2,1,0:T(8,128)(2,1)}, bf16[16,2,64,128]{3,2,1,0:T(8,128)(2,1)}, u32[]{:S(2)}, u32[]{:S(2)}) collective-permute-start(bf16[16,2,64,128]{3,2,1,0:T(8,128)(2,1)} %get-tuple-element.135), channel_id=1, source_target_pairs={{0,4},{4,8},{8,12},{12,0},{1,5},{5,9},{9,13},{13,1},{2,6},{6,10},{... | collective-permute-start | bytes 1572872 | tf_op jit(solution)/shard_map/ppermute | solution.py:334
  80.6 94.5 %collective-permute-start.16 = (bf16[16,2,64,128]{3,2,1,0:T(8,128)(2,1)}, bf16[16,2,64,128]{3,2,1,0:T(8,128)(2,1)}, u32[]{:S(2)}, u32[]{:S(2)}) collective-permute-start(bf16[16,2,64,128]{3,2,1,0:T(8,128)(2,1)} %get-tuple-element.136), channel_id=1, source_target_pairs={{0,8},{4,12},{8,0},{12,4},{1,9},{5,13},{9,1},{13,5},{2,10},{6,14},... | collective-permute-start | bytes 1572872 | tf_op jit(solution)/shard_map/ppermute | solution.py:334
  107.9 67.9 %collective-permute-start.17 = (bf16[16,2,64,128]{3,2,1,0:T(8,128)(2,1)S(1)}, bf16[16,2,64,128]{3,2,1,0:T(8,128)(2,1)S(1)}, u32[]{:S(2)}, u32[]{:S(2)}) collective-permute-start(bf16[16,2,64,128]{3,2,1,0:T(8,128)(2,1)S(1)} %copy-done.7), channel_id=1, source_target_pairs={{0,12},{4,0},{8,4},{12,8},{1,13},{5,1},{9,5},{13,9},{2,14},{6,2},{... | collective-permute-start | bytes 1572872 | tf_op jit(solution)/shard_map/ppermute | solution.py:334
  130.1 89.8 %collective-permute-start.19 = (bf16[16,2,64,128]{3,2,1,0:T(8,128)(2,1)S(1)}, bf16[16,2,64,128]{3,2,1,0:T(8,128)(2,1)S(1)}, u32[]{:S(2)}, u32[]{:S(2)}) collective-permute-start(bf16[16,2,64,128]{3,2,1,0:T(8,128)(2,1)S(1)} %get-tuple-element.142), channel_id=1, source_target_pairs={{0,8},{4,12},{8,0},{12,4},{1,9},{5,13},{9,1},{13,5},{2,10},{6,14},... | collective-permute-start | bytes 1572872 | tf_op jit(solution)/shard_map/ppermute | solution.py:334
  140.6 79.3 %collective-permute-start.20 = (bf16[16,2,64,128]{3,2,1,0:T(8,128)(2,1)S(1)}, bf16[16,2,64,128]{3,2,1,0:T(8,128)(2,1)S(1)}, u32[]{:S(2)}, u32[]{:S(2)}) collective-permute-start(bf16[16,2,64,128]{3,2,1,0:T(8,128)(2,1)S(1)} %get-tuple-element.143), channel_id=1, source_target_pairs={{0,12},{4,0},{8,4},{12,8},{1,13},{5,1},{9,5},{13,9},{2,14},{6,2},{... | collective-permute-start | bytes 1572872 | tf_op jit(solution)/shard_map/ppermute | solution.py:334
  175.7 66.7 %collective-permute-start.13 = (bf16[16,2,64,128]{3,2,1,0:T(8,128)(2,1)S(1)}, bf16[16,2,64,128]{3,2,1,0:T(8,128)(2,1)S(1)}, u32[]{:S(2)}, u32[]{:S(2)}) collective-permute-start(bf16[16,2,64,128]{3,2,1,0:T(8,128)(2,1)S(1)} %get-tuple-element.132), channel_id=1, source_target_pairs={{0,8},{4,12},{8,0},{12,4},{1,9},{5,13},{9,1},{13,5},{2,10},{6,14},... | collective-permute-start | bytes 1572872 | tf_op jit(solution)/shard_map/ppermute | solution.py:334
  189.6 72.7 %collective-permute-start.14 = (bf16[16,2,64,128]{3,2,1,0:T(8,128)(2,1)S(1)}, bf16[16,2,64,128]{3,2,1,0:T(8,128)(2,1)S(1)}, u32[]{:S(2)}, u32[]{:S(2)}) collective-permute-start(bf16[16,2,64,128]{3,2,1,0:T(8,128)(2,1)S(1)} %get-tuple-element.133), channel_id=1, source_target_pairs={{0,12},{4,0},{8,4},{12,8},{1,13},{5,1},{9,5},{13,9},{2,14},{6,2},{... | collective-permute-start | bytes 1572872 | tf_op jit(solution)/shard_map/ppermute | solution.py:334
  227.2 61.6 %collective-permute-start.27 = (bf16[16,2,64,128]{3,2,1,0:T(8,128)(2,1)S(1)}, bf16[16,2,64,128]{3,2,1,0:T(8,128)(2,1)S(1)}, u32[]{:S(2)}, u32[]{:S(2)}) collective-permute-start(bf16[16,2,64,128]{3,2,1,0:T(8,128)(2,1)S(1)} %get-tuple-element.158), channel_id=1, source_target_pairs={{0,4},{4,8},{8,12},{12,0},{1,5},{5,9},{9,13},{13,1},{2,6},{6,10},{... | collective-permute-start | bytes 1572872 | tf_op jit(solution)/shard_map/ppermute | solution.py:334
  228.2 109.8 %collective-permute-start.28 = (bf16[16,2,64,128]{3,2,1,0:T(8,128)(2,1)S(1)}, bf16[16,2,64,128]{3,2,1,0:T(8,128)(2,1)S(1)}, u32[]{:S(2)}, u32[]{:S(2)}) collective-permute-start(bf16[16,2,64,128]{3,2,1,0:T(8,128)(2,1)S(1)} %get-tuple-element.159), channel_id=1, source_target_pairs={{0,8},{4,12},{8,0},{12,4},{1,9},{5,13},{9,1},{13,5},{2,10},{6,14},... | collective-permute-start | bytes 1572872 | tf_op jit(solution)/shard_map/ppermute | solution.py:334
  242.4 95.6 %collective-permute-start.29 = (bf16[16,2,64,128]{3,2,1,0:T(8,128)(2,1)S(1)}, bf16[16,2,64,128]{3,2,1,0:T(8,128)(2,1)S(1)}, u32[]{:S(2)}, u32[]{:S(2)}) collective-permute-start(bf16[16,2,64,128]{3,2,1,0:T(8,128)(2,1)S(1)} %get-tuple-element.160), channel_id=1, source_target_pairs={{0,12},{4,0},{8,4},{12,8},{1,13},{5,1},{9,5},{13,9},{2,14},{6,2},{... | collective-permute-start | bytes 1572872 | tf_op jit(solution)/shard_map/ppermute | solution.py:334
  262.2 92.6 %collective-permute-start.25 = (bf16[16,2,64,128]{3,2,1,0:T(8,128)(2,1)S(1)}, bf16[16,2,64,128]{3,2,1,0:T(8,128)(2,1)S(1)}, u32[]{:S(2)}, u32[]{:S(2)}) collective-permute-start(bf16[16,2,64,128]{3,2,1,0:T(8,128)(2,1)S(1)} %get-tuple-element.154), channel_id=1, source_target_pairs={{0,8},{4,12},{8,0},{12,4},{1,9},{5,13},{9,1},{13,5},{2,10},{6,14},... | collective-permute-start | bytes 1572872 | tf_op jit(solution)/shard_map/ppermute | solution.py:334
  275.4 79.4 %collective-permute-start.26 = (bf16[16,2,64,128]{3,2,1,0:T(8,128)(2,1)S(1)}, bf16[16,2,64,128]{3,2,1,0:T(8,128)(2,1)S(1)}, u32[]{:S(2)}, u32[]{:S(2)}) collective-permute-start(bf16[16,2,64,128]{3,2,1,0:T(8,128)(2,1)S(1)} %get-tuple-element.155), channel_id=1, source_target_pairs={{0,12},{4,0},{8,4},{12,8},{1,13},{5,1},{9,5},{13,9},{2,14},{6,2},{... | collective-permute-start | bytes 1572872 | tf_op jit(solution)/shard_map/ppermute | solution.py:334
  288.9 79.5 %collective-permute-start.21 = (bf16[16,2,64,128]{3,2,1,0:T(8,128)(2,1)S(1)}, bf16[16,2,64,128]{3,2,1,0:T(8,128)(2,1)S(1)}, u32[]{:S(2)}, u32[]{:S(2)}) collective-permute-start(bf16[16,2,64,128]{3,2,1,0:T(8,128)(2,1)S(1)} %get-tuple-element.149), channel_id=1, source_target_pairs={{0,4},{4,8},{8,12},{12,0},{1,5},{5,9},{9,13},{13,1},{2,6},{6,10},{... | collective-permute-start | bytes 1572872 | tf_op jit(solution)/shard_map/ppermute | solution.py:334
  338.0 61.8 %collective-permute-start.22 = (bf16[16,2,64,128]{3,2,1,0:T(8,128)(2,1)S(1)}, bf16[16,2,64,128]{3,2,1,0:T(8,128)(2,1)S(1)}, u32[]{:S(2)}, u32[]{:S(2)}) collective-permute-start(bf16[16,2,64,128]{3,2,1,0:T(8,128)(2,1)S(1)} %get-tuple-element.150), channel_id=1, source_target_pairs={{0,8},{4,12},{8,0},{12,4},{1,9},{5,13},{9,1},{13,5},{2,10},{6,14},... | collective-permute-start | bytes 1572872 | tf_op jit(solution)/shard_map/ppermute | solution.py:334
  338.0 61.8 %collective-permute-start.23 = (bf16[16,2,64,128]{3,2,1,0:T(8,128)(2,1)S(1)}, bf16[16,2,64,128]{3,2,1,0:T(8,128)(2,1)S(1)}, u32[]{:S(2)}, u32[]{:S(2)}) collective-permute-start(bf16[16,2,64,128]{3,2,1,0:T(8,128)(2,1)S(1)} %get-tuple-element.151), channel_id=1, source_target_pairs={{0,12},{4,0},{8,4},{12,8},{1,13},{5,1},{9,5},{13,9},{2,14},{6,2},{... | collective-permute-start | bytes 1572872 | tf_op jit(solution)/shard_map/ppermute | solution.py:334
  354.8 89.9 %collective-permute-start.34 = (bf16[16,2,64,128]{3,2,1,0:T(8,128)(2,1)S(1)}, bf16[16,2,64,128]{3,2,1,0:T(8,128)(2,1)S(1)}, u32[]{:S(2)}, u32[]{:S(2)}) collective-permute-start(bf16[16,2,64,128]{3,2,1,0:T(8,128)(2,1)S(1)} %get-tuple-element.171), channel_id=1, source_target_pairs={{0,8},{4,12},{8,0},{12,4},{1,9},{5,13},{9,1},{13,5},{2,10},{6,14},... | collective-permute-start | bytes 1572872 | tf_op jit(solution)/shard_map/ppermute | solution.py:334
  368.4 76.3 %collective-permute-start.35 = (bf16[16,2,64,128]{3,2,1,0:T(8,128)(2,1)S(1)}, bf16[16,2,64,128]{3,2,1,0:T(8,128)(2,1)S(1)}, u32[]{:S(2)}, u32[]{:S(2)}) collective-permute-start(bf16[16,2,64,128]{3,2,1,0:T(8,128)(2,1)S(1)} %get-tuple-element.172), channel_id=1, source_target_pairs={{0,12},{4,0},{8,4},{12,8},{1,13},{5,1},{9,5},{13,9},{2,14},{6,2},{... | collective-permute-start | bytes 1572872 | tf_op jit(solution)/shard_map/ppermute | solution.py:334
  399.8 92.7 %collective-permute-start.37 = (bf16[16,2,64,128]{3,2,1,0:T(8,128)(2,1)S(1)}, bf16[16,2,64,128]{3,2,1,0:T(8,128)(2,1)S(1)}, u32[]{:S(2)}, u32[]{:S(2)}) collective-permute-start(bf16[16,2,64,128]{3,2,1,0:T(8,128)(2,1)S(1)} %get-tuple-element.178), channel_id=1, source_target_pairs={{0,8},{4,12},{8,0},{12,4},{1,9},{5,13},{9,1},{13,5},{2,10},{6,14},... | collective-permute-start | bytes 1572872 | tf_op jit(solution)/shard_map/ppermute | solution.py:334
  407.1 85.4 %collective-permute-start.38 = (bf16[16,2,64,128]{3,2,1,0:T(8,128)(2,1)S(1)}, bf16[16,2,64,128]{3,2,1,0:T(8,128)(2,1)S(1)}, u32[]{:S(2)}, u32[]{:S(2)}) collective-permute-start(bf16[16,2,64,128]{3,2,1,0:T(8,128)(2,1)S(1)} %get-tuple-element.179), channel_id=1, source_target_pairs={{0,12},{4,0},{8,4},{12,8},{1,13},{5,1},{9,5},{13,9},{2,14},{6,2},{... | collective-permute-start | bytes 1572872 | tf_op jit(solution)/shard_map/ppermute | solution.py:334
  444.7 89.9 %collective-permute-start.31 = (bf16[16,2,64,128]{3,2,1,0:T(8,128)(2,1)S(1)}, bf16[16,2,64,128]{3,2,1,0:T(8,128)(2,1)S(1)}, u32[]{:S(2)}, u32[]{:S(2)}) collective-permute-start(bf16[16,2,64,128]{3,2,1,0:T(8,128)(2,1)S(1)} %get-tuple-element.167), channel_id=1, source_target_pairs={{0,8},{4,12},{8,0},{12,4},{1,9},{5,13},{9,1},{13,5},{2,10},{6,14},... | collective-permute-start | bytes 1572872 | tf_op jit(solution)/shard_map/ppermute | solution.py:334
  444.7 89.9 %collective-permute-start.32 = (bf16[16,2,64,128]{3,2,1,0:T(8,128)(2,1)S(1)}, bf16[16,2,64,128]{3,2,1,0:T(8,128)(2,1)S(1)}, u32[]{:S(2)}, u32[]{:S(2)}) collective-permute-start(bf16[16,2,64,128]{3,2,1,0:T(8,128)(2,1)S(1)} %get-tuple-element.168), channel_id=1, source_target_pairs={{0,12},{4,0},{8,4},{12,8},{1,13},{5,1},{9,5},{13,9},{2,14},{6,2},{... | collective-permute-start | bytes 1572872 | tf_op jit(solution)/shard_map/ppermute | solution.py:334
  492.5 87.0 %collective-permute-start.46 = (bf16[16,2,64,128]{3,2,1,0:T(8,128)(2,1)S(1)}, bf16[16,2,64,128]{3,2,1,0:T(8,128)(2,1)S(1)}, u32[]{:S(2)}, u32[]{:S(2)}) collective-permute-start(bf16[16,2,64,128]{3,2,1,0:T(8,128)(2,1)S(1)} %get-tuple-element.195), channel_id=1, source_target_pairs={{0,8},{4,12},{8,0},{12,4},{1,9},{5,13},{9,1},{13,5},{2,10},{6,14},... | collective-permute-start | bytes 1572872 | tf_op jit(solution)/shard_map/ppermute | solution.py:334
  494.0 85.6 %collective-permute-start.47 = (bf16[16,2,64,128]{3,2,1,0:T(8,128)(2,1)S(1)}, bf16[16,2,64,128]{3,2,1,0:T(8,128)(2,1)S(1)}, u32[]{:S(2)}, u32[]{:S(2)}) collective-permute-start(bf16[16,2,64,128]{3,2,1,0:T(8,128)(2,1)S(1)} %get-tuple-element.196), channel_id=1, source_target_pairs={{0,12},{4,0},{8,4},{12,8},{1,13},{5,1},{9,5},{13,9},{2,14},{6,2},{... | collective-permute-start | bytes 1572872 | tf_op jit(solution)/shard_map/ppermute | solution.py:334
  534.6 89.9 %collective-permute-start.43 = (bf16[16,2,64,128]{3,2,1,0:T(8,128)(2,1)S(1)}, bf16[16,2,64,128]{3,2,1,0:T(8,128)(2,1)S(1)}, u32[]{:S(2)}, u32[]{:S(2)}) collective-permute-start(bf16[16,2,64,128]{3,2,1,0:T(8,128)(2,1)S(1)} %get-tuple-element.190), channel_id=1, source_target_pairs={{0,8},{4,12},{8,0},{12,4},{1,9},{5,13},{9,1},{13,5},{2,10},{6,14},... | collective-permute-start | bytes 1572872 | tf_op jit(solution)/shard_map/ppermute | solution.py:334
  548.2 76.3 %collective-permute-start.44 = (bf16[16,2,64,128]{3,2,1,0:T(8,128)(2,1)S(1)}, bf16[16,2,64,128]{3,2,1,0:T(8,128)(2,1)S(1)}, u32[]{:S(2)}, u32[]{:S(2)}) collective-permute-start(bf16[16,2,64,128]{3,2,1,0:T(8,128)(2,1)S(1)} %get-tuple-element.191), channel_id=1, source_target_pairs={{0,12},{4,0},{8,4},{12,8},{1,13},{5,1},{9,5},{13,9},{2,14},{6,2},{... | collective-permute-start | bytes 1572872 | tf_op jit(solution)/shard_map/ppermute | solution.py:334
  579.5 89.9 %collective-permute-start.40 = (bf16[16,2,64,128]{3,2,1,0:T(8,128)(2,1)S(1)}, bf16[16,2,64,128]{3,2,1,0:T(8,128)(2,1)S(1)}, u32[]{:S(2)}, u32[]{:S(2)}) collective-permute-start(bf16[16,2,64,128]{3,2,1,0:T(8,128)(2,1)S(1)} %get-tuple-element.186), channel_id=1, source_target_pairs={{0,8},{4,12},{8,0},{12,4},{1,9},{5,13},{9,1},{13,5},{2,10},{6,14},... | collective-permute-start | bytes 1572872 | tf_op jit(solution)/shard_map/ppermute | solution.py:334
  586.9 82.6 %collective-permute-start.41 = (bf16[16,2,64,128]{3,2,1,0:T(8,128)(2,1)S(1)}, bf16[16,2,64,128]{3,2,1,0:T(8,128)(2,1)S(1)}, u32[]{:S(2)}, u32[]{:S(2)}) collective-permute-start(bf16[16,2,64,128]{3,2,1,0:T(8,128)(2,1)S(1)} %get-tuple-element.187), channel_id=1, source_target_pairs={{0,12},{4,0},{8,4},{12,8},{1,13},{5,1},{9,5},{13,9},{2,14},{6,2},{... | collective-permute-start | bytes 1572872 | tf_op jit(solution)/shard_map/ppermute | solution.py:334
  624.5 70.6 %collective-permute-start.55 = (bf16[16,2,64,128]{3,2,1,0:T(8,128)(2,1)S(1)}, bf16[16,2,64,128]{3,2,1,0:T(8,128)(2,1)S(1)}, u32[]{:S(2)}, u32[]{:S(2)}) collective-permute-start(bf16[16,2,64,128]{3,2,1,0:T(8,128)(2,1)S(1)} %get-tuple-element.210), channel_id=1, source_target_pairs={{0,8},{4,12},{8,0},{12,4},{1,9},{5,13},{9,1},{13,5},{2,10},{6,14},... | collective-permute-start | bytes 1572872 | tf_op jit(solution)/shard_map/ppermute | solution.py:334
  631.3 63.8 %collective-permute-start.56 = (bf16[16,2,64,128]{3,2,1,0:T(8,128)(2,1)S(1)}, bf16[16,2,64,128]{3,2,1,0:T(8,128)(2,1)S(1)}, u32[]{:S(2)}, u32[]{:S(2)}) collective-permute-start(bf16[16,2,64,128]{3,2,1,0:T(8,128)(2,1)S(1)} %get-tuple-element.211), channel_id=1, source_target_pairs={{0,12},{4,0},{8,4},{12,8},{1,13},{5,1},{9,5},{13,9},{2,14},{6,2},{... | collective-permute-start | bytes 1572872 | tf_op jit(solution)/shard_map/ppermute | solution.py:334
  (39 other events, 1398.2 us)

commit v9 on v8

--- a/solution.py
+++ b/solution.py
@@ -13,6 +13,7 @@
 LANES = 128
 ROWS = 16
 STRIDE = ROWS + 1
+TEAM = 4
 
 kerr_gamma = 0.00390625
 
@@ -66,12 +67,12 @@
         g = pl.program_id(1)
         slot = ((lane_index(block) + 1) >> 1) & (LANES // 2 - 1)
         for c in range(parts):
-            kept = acc[c]
+            kept = jnp.zeros((block, LANES), jnp.float32)
             for i in range(ROWS):
-                m = (g + base) * ROWS + i
-                row = roll(x_ref[c, i].astype(jnp.float32), 2 * m)
-                kept = jnp.where(slot == m, row, kept)
-            acc[c] = kept
+                row = roll(x_ref[c, i].astype(jnp.float32), 2 * i)
+                kept = jnp.where(slot == i, row, kept)
+            kept = roll(kept, 2 * ROWS * (g + base))
+            acc[c] = jnp.where(slot // ROWS == g + base, kept, acc[c])
 
         @pl.when(g == groups - 1)
         def _():
@@ -112,7 +113,7 @@
     lane = lane_index(beta.shape[0])
     second, first = [], []
     for c in range(2):
-        ends = roll(halo[c], (LANES - 2 * m) & (LANES - 1))
+        ends = roll(halo[c], (LANES - 2 * m) % LANES)
         left = jnp.where(lane == 0, ends, roll(x[c], 1))
         right = jnp.where(lane == LANES - 1, ends, roll(x[c], LANES - 1))
         second.append(right - 2.0 * x[c] + left)
@@ -120,6 +121,24 @@
     real = x[0] - beta * second[1] + delta * first[0]
     imag = x[1] + beta * second[0] + delta * first[1]
     return real, imag
+
+
+def team_scratch(block):
+    size = TEAM * block
+    return [
+        pltpu.VMEM((ROWS // TEAM, size, size), jnp.bfloat16),
+        pltpu.VMEM((ROWS // TEAM, size, 2 * LANES), jnp.bfloat16),
+    ]
+
+
+def team_product(diagonal, stacked, team, tables, operands):
+    block = tables[0].shape[0]
+    for k in range(TEAM):
+        rows = slice(k * block, (k + 1) * block)
+        diagonal[team, rows, rows] = tables[k]
+        stacked[team, rows, :] = operands[k]
+    product = jnp.dot(diagonal[team], stacked[team], preferred_element_type=jnp.float32)
+    return [product[k * block : (k + 1) * block] for k in range(TEAM)]
 
 
 def radial_specs(parts, kinds, block, radial, b, halo_at, base):
@@ -141,21 +160,31 @@
     base, groups = span[0] // ROWS, span[1] // ROWS
 
     def kernel(map_ref, me_ref, x_ref, low_ref, high_ref, tab_ref, beta_ref, delta_ref, *refs):
-        outs, acc = refs[len(after) : len(after) + count], refs[-1]
+        outs, (acc, diagonal, stacked) = refs[len(after) : len(after) + count], refs[-3:]
         g = pl.program_id(0)
+
+        @pl.when(g == 0)
+        def _():
+            diagonal[...] = jnp.zeros_like(diagonal)
+
         beta = columns(beta_ref, b * block, block)
         delta = columns(delta_ref, b * block, block)
-        ends = [join_halo(low_ref[c], high_ref[c]) for c in range(parts)]
-        for i in range(ROWS):
-            m = (g + base) * ROWS + i
-            x = [x_ref[c, i].astype(jnp.float32) for c in range(parts)]
-            moved = move(x, ends, beta[:, i : i + 1], delta[:, i : i + 1], m)
-            moved = jnp.concatenate(moved, 1).astype(jnp.bfloat16)
-            points = jnp.dot(
-                tab_ref[map_ref[m], 0], moved, preferred_element_type=jnp.float32
-            )
-            for c in range(parts):
-                acc[c, pl.ds(i, block, stride=STRIDE), :] = points[:, c * LANES : (c + 1) * LANES]
+        shift = (LANES - 2 * ROWS * (g + base)) & (LANES - 1)
+        ends = [roll(join_halo(low_ref[c], high_ref[c]), shift) for c in range(parts)]
+        for team in range(ROWS // TEAM):
+            members = range(team * TEAM, (team + 1) * TEAM)
+            tables, operands = [], []
+            for i in members:
+                x = [x_ref[c, i].astype(jnp.float32) for c in range(parts)]
+                moved = move(x, ends, beta[:, i : i + 1], delta[:, i : i + 1], i)
+                operands.append(jnp.concatenate(moved, 1).astype(jnp.bfloat16))
+                tables.append(tab_ref[map_ref[(g + base) * ROWS + i], 0])
+            products = team_product(diagonal, stacked, team, tables, operands)
+            for i, points in zip(members, products, strict=True):
+                for c in range(parts):
+                    acc[c, pl.ds(i, block, stride=STRIDE), :] = points[
+                        :, c * LANES : (c + 1) * LANES
+                    ]
         for s in range(count):
             owner = lax.rem(me_ref[0] + s, count)
             start = pl.multiple_of(owner * share * STRIDE, 8)
@@ -180,7 +209,8 @@
             ]
             * count
             + anywhere(1),
-            scratch_shapes=[pltpu.VMEM((parts, (block + 8) * STRIDE, LANES), jnp.float32)],
+            scratch_shapes=[pltpu.VMEM((parts, (block + 8) * STRIDE, LANES), jnp.float32)]
+            + team_scratch(block),
         ),
         compiler_params=params(),
         cost_estimate=cost(2 * size * block, 2 * size),
@@ -275,8 +305,13 @@
     def kernel(map_ref, me_ref, *refs):
         ins = refs[:count]
         x_ref, low_ref, high_ref, tab_ref, beta_ref, delta_ref = refs[count : count + 6]
-        o_ref, _, acc = refs[-3:]
+        o_ref, _, acc, diagonal, stacked = refs[-5:]
         g = pl.program_id(0)
+
+        @pl.when(g == 0)
+        def _():
+            diagonal[...] = jnp.zeros_like(diagonal)
+
         for s in range(count):
             source = lax.rem(me_ref[0] + count - s, count)
             start = pl.multiple_of(source * share * STRIDE, 8)
@@ -287,19 +322,22 @@
                     part[row : row + ROWS, :] = ins[s][q, c].astype(jnp.float32)
         beta = columns(beta_ref, b * block, block)
         delta = columns(delta_ref, b * block, block)
-        ends = [join_halo(low_ref[c], high_ref[c]) for c in range(parts)]
-        for i in range(ROWS):
-            m = (g + base) * ROWS + i
-            x = [x_ref[c, i].astype(jnp.float32) for c in range(parts)]
-            moved = move(x, ends, beta[:, i : i + 1], delta[:, i : i + 1], m)
-            back = [acc[c, pl.ds(i, block, stride=STRIDE), :] for c in range(parts)]
-            back = jnp.concatenate(back, 1).astype(jnp.bfloat16)
-            increment = jnp.dot(
-                tab_ref[map_ref[m], 0], back, preferred_element_type=jnp.float32
-            )
-            for c in range(parts):
-                total = moved[c] + increment[:, c * LANES : (c + 1) * LANES]
-                o_ref[c, i] = total.astype(jnp.bfloat16)
+        shift = (LANES - 2 * ROWS * (g + base)) & (LANES - 1)
+        ends = [roll(join_halo(low_ref[c], high_ref[c]), shift) for c in range(parts)]
+        for team in range(ROWS // TEAM):
+            members = range(team * TEAM, (team + 1) * TEAM)
+            tables, operands = [], []
+            for i in members:
+                back = [acc[c, pl.ds(i, block, stride=STRIDE), :] for c in range(parts)]
+                operands.append(jnp.concatenate(back, 1).astype(jnp.bfloat16))
+                tables.append(tab_ref[map_ref[(g + base) * ROWS + i], 0])
+            products = team_product(diagonal, stacked, team, tables, operands)
+            for i, increment in zip(members, products, strict=True):
+                x = [x_ref[c, i].astype(jnp.float32) for c in range(parts)]
+                moved = move(x, ends, beta[:, i : i + 1], delta[:, i : i + 1], i)
+                for c in range(parts):
+                    total = moved[c] + increment[:, c * LANES : (c + 1) * LANES]
+                    o_ref[c, i] = total.astype(jnp.bfloat16)
 
     size = parts * span[1] * block * LANES * 2
     return pl.pallas_call(
@@ -318,7 +356,8 @@
                 pl.BlockSpec((parts, ROWS, block, LANES), lambda g, *_: (0, g + base, b, 0))
             ]
             + anywhere(1),
-            scratch_shapes=[pltpu.VMEM((parts, (block + 8) * STRIDE, LANES), jnp.float32)],
+            scratch_shapes=[pltpu.VMEM((parts, (block + 8) * STRIDE, LANES), jnp.float32)]
+            + team_scratch(block),
         ),
         input_output_aliases={2 + count + 6: 0} if held else {},
         compiler_params=params(),

time: 742 us -> 743 us (level)
  Pallas kernels: 193 us -> 203 us
  transfers between devices with their start and end apart: 57 -> 57, of which waited for: 20 -> 20; matrix products, arithmetic and copies ran while one was open for 0% -> 0% of each run, Pallas kernels for 24% -> 25%
where the time goes in v9:
time: 743 us; the launch traced here: 741 us
  starting transfers between devices  351 us (47%)
  Pallas kernels  203 us (27%)
  waiting for transfers between devices  183 us (25%)
    ppermute x51, starting transfers between devices, exchange(): lax.ppermute(pieces[s], 'ang', ring('ang', s))  350 us
    ppermute x51, waiting for transfers between devices, exchange(): lax.ppermute(pieces[s], 'ang', ring('ang', s))  171 us
    pallas_call x9, Pallas kernels, analyze(): pl.pallas_call(kernel, out_shape=[jax.ShapeDtypeStruct(field.shape, field...  60.1 us
    pallas_call x8, Pallas kernels, kerr_step(): pl.pallas_call(kernel, out_shape=[jax.ShapeDtypeStruct((share, parts, siz...  59.9 us
    pallas_call x8, Pallas kernels, synthesize(): pl.pallas_call(kernel, out_shape=[piece] * count + [token()], grid_spec=p...  58.8 us
    pallas_call x3, Pallas kernels, edges(): pl.pallas_call(kernel, out_shape=[jax.ShapeDtypeStruct((parts, count * bl...  23.9 us
  transfers between devices with their start and end apart: 57, of which 20 were waited for; matrix products, arithmetic and copies ran while one was open for 0% of the time, Pallas kernels for 25%

profile of v9, /device:TPU:24, one launch (start us, length us, event | category | flops | bytes accessed | tf_op | source)
XLA Modules:
  0.0 741.5 jit_solution(11205725353004010153)
XLA Ops:
  23.7 8.0 %synthesize.9 = (bf16[16,2,64,128]{3,2,1,0:T(8,128)(2,1)S(1)}, bf16[16,2,64,128]{3,2,1,0:T(8,128)(2,1)}, bf16[16,2,64,128]{3,2,1,0:T(8,128)(2,1)}, bf16[16,2,64,128]{3,2,1,0:T(8,128)(2,1)}, f32[8,128]{1,0:T(8,128)S(1)}) custom-call(s32[64]{0:T(128)S(1)} %copy-done.3, s32[1]{0:T(128)} %bitcast.me_ref, bf16[2,64,512,128]{3,2,1,0:T(8,128)(2,1)} %refs_4_.17, ...), custom_call_target="tpu_custom_call" | custom-call | flops 268435456 | bytes 4194304 | tf_op jit(solution)/shard_map/synthesize/pallas_call | solution.py:199
  31.7 17.5 %edges.5 = (bf16[2,384,128]{2,1,0:T(8,128)(2,1)S(1)}, f32[8,128]{1,0:T(8,128)S(1)}) custom-call(bf16[2,64,512,128]{3,2,1,0:T(8,128)(2,1)} %refs_4_.17, f32[8,128]{1,0:T(8,128)S(1)} %get-tuple-element.117.refs_0_), custom_call_target="tpu_custom_call" | custom-call | bytes 12582912 | tf_op jit(solution)/shard_map/edges/pallas_call | solution.py:81
  52.9 10.3 %collective-permute-done.10.refs_2_ = bf16[16,2,64,128]{3,2,1,0:T(8,128)(2,1)S(1)} collective-permute-done((bf16[16,2,64,128]{3,2,1,0:T(8,128)(2,1)S(1)}, bf16[16,2,64,128]{3,2,1,0:T(8,128)(2,1)S(1)}, u32[]{:S(2)}, u32[]{:S(2)}) %collective-permute-start.10) | collective-permute-done | bytes 524320 | tf_op jit(solution)/shard_map/ppermute | solution.py:373
  63.2 8.0 %kerr.8 = (bf16[16,2,64,128]{3,2,1,0:T(8,128)(2,1)S(1)}, bf16[16,2,64,128]{3,2,1,0:T(8,128)(2,1)}, bf16[16,2,64,128]{3,2,1,0:T(8,128)(2,1)}, bf16[16,2,64,128]{3,2,1,0:T(8,128)(2,1)S(1)}, f32[8,128]{1,0:T(8,128)S(1)}) custom-call(s32[1]{0:T(128)} %bitcast.me_ref, bf16[512,512]{1,0:T(8,128)(2,1)S(1)} %copy-done.10, bf16[512,512]{1,0:T(8,128)(2,1)S(1)} %copy-done.8, ...), custom_call_target="tpu_custom_call" | custom-call | flops 2147483648 | bytes 4194304 | tf_op jit(solution)/shard_map/kerr/pallas_call | solution.py:269
  80.9 18.0 %collective-permute-start.16 = (bf16[16,2,64,128]{3,2,1,0:T(8,128)(2,1)}, bf16[16,2,64,128]{3,2,1,0:T(8,128)(2,1)}, u32[]{:S(2)}, u32[]{:S(2)}) collective-permute-start(bf16[16,2,64,128]{3,2,1,0:T(8,128)(2,1)} %get-tuple-element.136), channel_id=1, source_target_pairs={{0,8},{4,12},{8,0},{12,4},{1,9},{5,13},{9,1},{13,5},{2,10},{6,14},... | collective-permute-start | bytes 1572872 | tf_op jit(solution)/shard_map/ppermute | solution.py:373
  101.5 7.4 %synthesize.10 = (bf16[16,2,64,128]{3,2,1,0:T(8,128)(2,1)S(1)}, bf16[16,2,64,128]{3,2,1,0:T(8,128)(2,1)S(1)}, bf16[16,2,64,128]{3,2,1,0:T(8,128)(2,1)S(1)}, bf16...) custom-call(s32[64]{0:T(128)S(1)} %copy-done.3, s32[1]{0:T(128)} %bitcast.me_ref, bf16[2,64,512,128]{3,2,1,0:T(8,128)(2,1)} %refs_4_.17, ...), custom_call_target="tpu_custom_call" | custom-call | flops 268435456 | bytes 4194304 | tf_op jit(solution)/shard_map/synthesize/pallas_call | solution.py:199
  111.1 19.7 %collective-permute-done.7.refs_2_ = bf16[16,2,64,128]{3,2,1,0:T(8,128)(2,1)} collective-permute-done((bf16[16,2,64,128]{3,2,1,0:T(8,128)(2,1)}, bf16[16,2,64,128]{3,2,1,0:T(8,128)(2,1)}, u32[]{:S(2)}, u32[]{:S(2)}) %collective-permute-start.7) | collective-permute-done | bytes 524320 | tf_op jit(solution)/shard_map/ppermute | solution.py:373
  130.8 10.6 %collective-permute-start.19 = (bf16[16,2,64,128]{3,2,1,0:T(8,128)(2,1)S(1)}, bf16[16,2,64,128]{3,2,1,0:T(8,128)(2,1)S(1)}, u32[]{:S(2)}, u32[]{:S(2)}) collective-permute-start(bf16[16,2,64,128]{3,2,1,0:T(8,128)(2,1)S(1)} %get-tuple-element.142), channel_id=1, source_target_pairs={{0,8},{4,12},{8,0},{12,4},{1,9},{5,13},{9,1},{13,5},{2,10},{6,14},... | collective-permute-start | bytes 1572872 | tf_op jit(solution)/shard_map/ppermute | solution.py:373
  141.3 23.8 %collective-permute-start.20 = (bf16[16,2,64,128]{3,2,1,0:T(8,128)(2,1)S(1)}, bf16[16,2,64,128]{3,2,1,0:T(8,128)(2,1)S(1)}, u32[]{:S(2)}, u32[]{:S(2)}) collective-permute-start(bf16[16,2,64,128]{3,2,1,0:T(8,128)(2,1)S(1)} %get-tuple-element.143), channel_id=1, source_target_pairs={{0,12},{4,0},{8,4},{12,8},{1,13},{5,1},{9,5},{13,9},{2,14},{6,2},{... | collective-permute-start | bytes 1572872 | tf_op jit(solution)/shard_map/ppermute | solution.py:373
  165.1 8.3 %kerr.9 = (bf16[16,2,64,128]{3,2,1,0:T(8,128)(2,1)S(1)}, bf16[16,2,64,128]{3,2,1,0:T(8,128)(2,1)S(1)}, bf16[16,2,64,128]{3,2,1,0:T(8,128)(2,1)S(1)}, bf16[16,2,64,128]{3,2,1,0:T(8,128)(2,1)S(1)}, f32[8,128]{1,0:T(8,128)S(1)}) custom-call(s32[1]{0:T(128)} %bitcast.me_ref, bf16[512,512]{1,0:T(8,128)(2,1)S(1)} %copy-done.11, bf16[512,512]{1,0:T(8,128)(2,1)S(1)} %copy-done.9, ...), custom_call_target="tpu_custom_call" | custom-call | flops 2147483648 | bytes 4194304 | tf_op jit(solution)/shard_map/kerr/pallas_call | solution.py:269
  191.2 18.7 %collective-permute-start.14 = (bf16[16,2,64,128]{3,2,1,0:T(8,128)(2,1)S(1)}, bf16[16,2,64,128]{3,2,1,0:T(8,128)(2,1)S(1)}, u32[]{:S(2)}, u32[]{:S(2)}) collective-permute-start(bf16[16,2,64,128]{3,2,1,0:T(8,128)(2,1)S(1)} %get-tuple-element.133), channel_id=1, source_target_pairs={{0,12},{4,0},{8,4},{12,8},{1,13},{5,1},{9,5},{13,9},{2,14},{6,2},{... | collective-permute-start | bytes 1572872 | tf_op jit(solution)/shard_map/ppermute | solution.py:373
  209.9 10.7 %collective-permute-done.19.refs_2_ = bf16[16,2,64,128]{3,2,1,0:T(8,128)(2,1)S(1)} collective-permute-done((bf16[16,2,64,128]{3,2,1,0:T(8,128)(2,1)S(1)}, bf16[16,2,64,128]{3,2,1,0:T(8,128)(2,1)S(1)}, u32[]{:S(2)}, u32[]{:S(2)}) %collective-permute-start.19) | collective-permute-done | bytes 524320 | tf_op jit(solution)/shard_map/ppermute | solution.py:373
  231.4 11.7 %collective-permute-done.13.refs_2_ = bf16[16,2,64,128]{3,2,1,0:T(8,128)(2,1)S(1)} collective-permute-done((bf16[16,2,64,128]{3,2,1,0:T(8,128)(2,1)S(1)}, bf16[16,2,64,128]{3,2,1,0:T(8,128)(2,1)S(1)}, u32[]{:S(2)}, u32[]{:S(2)}) %collective-permute-start.13) | collective-permute-done | bytes 524320 | tf_op jit(solution)/shard_map/ppermute | solution.py:373
  243.1 19.9 %collective-permute-start.29 = (bf16[16,2,64,128]{3,2,1,0:T(8,128)(2,1)S(1)}, bf16[16,2,64,128]{3,2,1,0:T(8,128)(2,1)S(1)}, u32[]{:S(2)}, u32[]{:S(2)}) collective-permute-start(bf16[16,2,64,128]{3,2,1,0:T(8,128)(2,1)S(1)} %get-tuple-element.160), channel_id=1, source_target_pairs={{0,12},{4,0},{8,4},{12,8},{1,13},{5,1},{9,5},{13,9},{2,14},{6,2},{... | collective-permute-start | bytes 1572872 | tf_op jit(solution)/shard_map/ppermute | solution.py:373
  263.0 13.1 %collective-permute-start.25 = (bf16[16,2,64,128]{3,2,1,0:T(8,128)(2,1)S(1)}, bf16[16,2,64,128]{3,2,1,0:T(8,128)(2,1)S(1)}, u32[]{:S(2)}, u32[]{:S(2)}) collective-permute-start(bf16[16,2,64,128]{3,2,1,0:T(8,128)(2,1)S(1)} %get-tuple-element.154), channel_id=1, source_target_pairs={{0,8},{4,12},{8,0},{12,4},{1,9},{5,13},{9,1},{13,5},{2,10},{6,14},... | collective-permute-start | bytes 1572872 | tf_op jit(solution)/shard_map/ppermute | solution.py:373
  294.4 44.3 %collective-permute-done.28.refs_2_ = bf16[16,2,64,128]{3,2,1,0:T(8,128)(2,1)S(1)} collective-permute-done((bf16[16,2,64,128]{3,2,1,0:T(8,128)(2,1)S(1)}, bf16[16,2,64,128]{3,2,1,0:T(8,128)(2,1)S(1)}, u32[]{:S(2)}, u32[]{:S(2)}) %collective-permute-start.28) | collective-permute-done | bytes 524320 | tf_op jit(solution)/shard_map/ppermute | solution.py:373
  346.0 9.6 %collective-permute-done.25.refs_2_ = bf16[16,2,64,128]{3,2,1,0:T(8,128)(2,1)S(1)} collective-permute-done((bf16[16,2,64,128]{3,2,1,0:T(8,128)(2,1)S(1)}, bf16[16,2,64,128]{3,2,1,0:T(8,128)(2,1)S(1)}, u32[]{:S(2)}, u32[]{:S(2)}) %collective-permute-start.25) | collective-permute-done | bytes 524320 | tf_op jit(solution)/shard_map/ppermute | solution.py:373
  370.1 19.7 %collective-permute-start.35 = (bf16[16,2,64,128]{3,2,1,0:T(8,128)(2,1)S(1)}, bf16[16,2,64,128]{3,2,1,0:T(8,128)(2,1)S(1)}, u32[]{:S(2)}, u32[]{:S(2)}) collective-permute-start(bf16[16,2,64,128]{3,2,1,0:T(8,128)(2,1)S(1)} %get-tuple-element.172), channel_id=1, source_target_pairs={{0,12},{4,0},{8,4},{12,8},{1,13},{5,1},{9,5},{13,9},{2,14},{6,2},{... | collective-permute-start | bytes 1572872 | tf_op jit(solution)/shard_map/ppermute | solution.py:373
  389.8 10.7 %collective-permute-done.22.refs_2_ = bf16[16,2,64,128]{3,2,1,0:T(8,128)(2,1)S(1)} collective-permute-done((bf16[16,2,64,128]{3,2,1,0:T(8,128)(2,1)S(1)}, bf16[16,2,64,128]{3,2,1,0:T(8,128)(2,1)S(1)}, u32[]{:S(2)}, u32[]{:S(2)}) %collective-permute-start.22) | collective-permute-done | bytes 524320 | tf_op jit(solution)/shard_map/ppermute | solution.py:373
  407.8 26.9 %collective-permute-start.38 = (bf16[16,2,64,128]{3,2,1,0:T(8,128)(2,1)S(1)}, bf16[16,2,64,128]{3,2,1,0:T(8,128)(2,1)S(1)}, u32[]{:S(2)}, u32[]{:S(2)}) collective-permute-start(bf16[16,2,64,128]{3,2,1,0:T(8,128)(2,1)S(1)} %get-tuple-element.179), channel_id=1, source_target_pairs={{0,12},{4,0},{8,4},{12,8},{1,13},{5,1},{9,5},{13,9},{2,14},{6,2},{... | collective-permute-start | bytes 1572872 | tf_op jit(solution)/shard_map/ppermute | solution.py:373
  434.7 10.7 %collective-permute-done.34.refs_2_ = bf16[16,2,64,128]{3,2,1,0:T(8,128)(2,1)S(1)} collective-permute-done((bf16[16,2,64,128]{3,2,1,0:T(8,128)(2,1)S(1)}, bf16[16,2,64,128]{3,2,1,0:T(8,128)(2,1)S(1)}, u32[]{:S(2)}, u32[]{:S(2)}) %collective-permute-start.34) | collective-permute-done | bytes 524320 | tf_op jit(solution)/shard_map/ppermute | solution.py:373
  445.4 34.2 %collective-permute-start.32 = (bf16[16,2,64,128]{3,2,1,0:T(8,128)(2,1)S(1)}, bf16[16,2,64,128]{3,2,1,0:T(8,128)(2,1)S(1)}, u32[]{:S(2)}, u32[]{:S(2)}) collective-permute-start(bf16[16,2,64,128]{3,2,1,0:T(8,128)(2,1)S(1)} %get-tuple-element.168), channel_id=1, source_target_pairs={{0,12},{4,0},{8,4},{12,8},{1,13},{5,1},{9,5},{13,9},{2,14},{6,2},{... | collective-permute-start | bytes 1572872 | tf_op jit(solution)/shard_map/ppermute | solution.py:373
  495.6 29.0 %collective-permute-start.47 = (bf16[16,2,64,128]{3,2,1,0:T(8,128)(2,1)S(1)}, bf16[16,2,64,128]{3,2,1,0:T(8,128)(2,1)S(1)}, u32[]{:S(2)}, u32[]{:S(2)}) collective-permute-start(bf16[16,2,64,128]{3,2,1,0:T(8,128)(2,1)S(1)} %get-tuple-element.196), channel_id=1, source_target_pairs={{0,12},{4,0},{8,4},{12,8},{1,13},{5,1},{9,5},{13,9},{2,14},{6,2},{... | collective-permute-start | bytes 1572872 | tf_op jit(solution)/shard_map/ppermute | solution.py:373
  549.8 19.7 %collective-permute-start.44 = (bf16[16,2,64,128]{3,2,1,0:T(8,128)(2,1)S(1)}, bf16[16,2,64,128]{3,2,1,0:T(8,128)(2,1)S(1)}, u32[]{:S(2)}, u32[]{:S(2)}) collective-permute-start(bf16[16,2,64,128]{3,2,1,0:T(8,128)(2,1)S(1)} %get-tuple-element.191), channel_id=1, source_target_pairs={{0,12},{4,0},{8,4},{12,8},{1,13},{5,1},{9,5},{13,9},{2,14},{6,2},{... | collective-permute-start | bytes 1572872 | tf_op jit(solution)/shard_map/ppermute | solution.py:373
  569.6 10.7 %collective-permute-done.46.refs_2_ = bf16[16,2,64,128]{3,2,1,0:T(8,128)(2,1)S(1)} collective-permute-done((bf16[16,2,64,128]{3,2,1,0:T(8,128)(2,1)S(1)}, bf16[16,2,64,128]{3,2,1,0:T(8,128)(2,1)S(1)}, u32[]{:S(2)}, u32[]{:S(2)}) %collective-permute-start.46) | collective-permute-done | bytes 524320 | tf_op jit(solution)/shard_map/ppermute | solution.py:373
  587.5 26.9 %collective-permute-start.41 = (bf16[16,2,64,128]{3,2,1,0:T(8,128)(2,1)S(1)}, bf16[16,2,64,128]{3,2,1,0:T(8,128)(2,1)S(1)}, u32[]{:S(2)}, u32[]{:S(2)}) collective-permute-start(bf16[16,2,64,128]{3,2,1,0:T(8,128)(2,1)S(1)} %get-tuple-element.187), channel_id=1, source_target_pairs={{0,12},{4,0},{8,4},{12,8},{1,13},{5,1},{9,5},{13,9},{2,14},{6,2},{... | collective-permute-start | bytes 1572872 | tf_op jit(solution)/shard_map/ppermute | solution.py:373
  614.5 10.7 %collective-permute-done.43.refs_2_ = bf16[16,2,64,128]{3,2,1,0:T(8,128)(2,1)S(1)} collective-permute-done((bf16[16,2,64,128]{3,2,1,0:T(8,128)(2,1)S(1)}, bf16[16,2,64,128]{3,2,1,0:T(8,128)(2,1)S(1)}, u32[]{:S(2)}, u32[]{:S(2)}) %collective-permute-start.43) | collective-permute-done | bytes 524320 | tf_op jit(solution)/shard_map/ppermute | solution.py:373
  632.5 26.9 %collective-permute-start.56 = (bf16[16,2,64,128]{3,2,1,0:T(8,128)(2,1)S(1)}, bf16[16,2,64,128]{3,2,1,0:T(8,128)(2,1)S(1)}, u32[]{:S(2)}, u32[]{:S(2)}) collective-permute-start(bf16[16,2,64,128]{3,2,1,0:T(8,128)(2,1)S(1)} %get-tuple-element.211), channel_id=1, source_target_pairs={{0,12},{4,0},{8,4},{12,8},{1,13},{5,1},{9,5},{13,9},{2,14},{6,2},{... | collective-permute-start | bytes 1572872 | tf_op jit(solution)/shard_map/ppermute | solution.py:373
  659.4 10.7 %collective-permute-done.40.refs_2_ = bf16[16,2,64,128]{3,2,1,0:T(8,128)(2,1)S(1)} collective-permute-done((bf16[16,2,64,128]{3,2,1,0:T(8,128)(2,1)S(1)}, bf16[16,2,64,128]{3,2,1,0:T(8,128)(2,1)S(1)}, u32[]{:S(2)}, u32[]{:S(2)}) %collective-permute-start.40) | collective-permute-done | bytes 524320 | tf_op jit(solution)/shard_map/ppermute | solution.py:373
  677.4 13.2 %collective-permute-start.53 = (bf16[16,2,48,128]{3,2,1,0:T(8,128)(2,1)S(1)}, bf16[16,2,48,128]{3,2,1,0:T(8,128)(2,1)S(1)}, u32[]{:S(2)}, u32[]{:S(2)}) collective-permute-start(bf16[16,2,48,128]{3,2,1,0:T(8,128)(2,1)S(1)} %get-tuple-element.207), channel_id=1, source_target_pairs={{0,8},{4,12},{8,0},{12,4},{1,9},{5,13},{9,1},{13,5},{2,10},{6,14},... | collective-permute-start | bytes 1179656 | tf_op jit(solution)/shard_map/ppermute | solution.py:373
  695.8 15.9 %collective-permute-start.50 = (bf16[16,2,16,128]{3,2,1,0:T(8,128)(2,1)S(1)}, bf16[16,2,16,128]{3,2,1,0:T(8,128)(2,1)S(1)}, u32[]{:S(2)}, u32[]{:S(2)}) collective-permute-start(bf16[16,2,16,128]{3,2,1,0:T(8,128)(2,1)S(1)} %get-tuple-element.203), channel_id=1, source_target_pairs={{0,8},{4,12},{8,0},{12,4},{1,9},{5,13},{9,1},{13,5},{2,10},{6,14},... | collective-permute-start | bytes 393224 | tf_op jit(solution)/shard_map/ppermute | solution.py:373
  711.7 12.4 %collective-permute-start.51 = (bf16[16,2,16,128]{3,2,1,0:T(8,128)(2,1)S(1)}, bf16[16,2,16,128]{3,2,1,0:T(8,128)(2,1)S(1)}, u32[]{:S(2)}, u32[]{:S(2)}) collective-permute-start(bf16[16,2,16,128]{3,2,1,0:T(8,128)(2,1)S(1)} %get-tuple-element.204), channel_id=1, source_target_pairs={{0,12},{4,0},{8,4},{12,8},{1,13},{5,1},{9,5},{13,9},{2,14},{6,2},{... | collective-permute-start | bytes 393224 | tf_op jit(solution)/shard_map/ppermute | solution.py:373
  (141 shorter events, 203.1 us)
Async XLA Ops:
  52.9 77.9 %collective-permute-start.7 = (bf16[16,2,64,128]{3,2,1,0:T(8,128)(2,1)}, bf16[16,2,64,128]{3,2,1,0:T(8,128)(2,1)}, u32[]{:S(2)}, u32[]{:S(2)}) collective-permute-start(bf16[16,2,64,128]{3,2,1,0:T(8,128)(2,1)} %get-tuple-element.121), channel_id=1, source_target_pairs={{0,8},{4,12},{8,0},{12,4},{1,9},{5,13},{9,1},{13,5},{2,10},{6,14},... | collective-permute-start | bytes 1572872 | tf_op jit(solution)/shard_map/ppermute | solution.py:373
  63.2 67.6 %collective-permute-start.8 = (bf16[16,2,64,128]{3,2,1,0:T(8,128)(2,1)}, bf16[16,2,64,128]{3,2,1,0:T(8,128)(2,1)}, u32[]{:S(2)}, u32[]{:S(2)}) collective-permute-start(bf16[16,2,64,128]{3,2,1,0:T(8,128)(2,1)} %get-tuple-element.122), channel_id=1, source_target_pairs={{0,12},{4,0},{8,4},{12,8},{1,13},{5,1},{9,5},{13,9},{2,14},{6,2},{... | collective-permute-start | bytes 1572872 | tf_op jit(solution)/shard_map/ppermute | solution.py:373
  72.1 69.3 %collective-permute-start.15 = (bf16[16,2,64,128]{3,2,1,0:T(8,128)(2,1)}, bf16[16,2,64,128]{3,2,1,0:T(8,128)(2,1)}, u32[]{:S(2)}, u32[]{:S(2)}) collective-permute-start(bf16[16,2,64,128]{3,2,1,0:T(8,128)(2,1)} %get-tuple-element.135), channel_id=1, source_target_pairs={{0,4},{4,8},{8,12},{12,0},{1,5},{5,9},{9,13},{13,1},{2,6},{6,10},{... | collective-permute-start | bytes 1572872 | tf_op jit(solution)/shard_map/ppermute | solution.py:373
  80.9 94.9 %collective-permute-start.16 = (bf16[16,2,64,128]{3,2,1,0:T(8,128)(2,1)}, bf16[16,2,64,128]{3,2,1,0:T(8,128)(2,1)}, u32[]{:S(2)}, u32[]{:S(2)}) collective-permute-start(bf16[16,2,64,128]{3,2,1,0:T(8,128)(2,1)} %get-tuple-element.136), channel_id=1, source_target_pairs={{0,8},{4,12},{8,0},{12,4},{1,9},{5,13},{9,1},{13,5},{2,10},{6,14},... | collective-permute-start | bytes 1572872 | tf_op jit(solution)/shard_map/ppermute | solution.py:373
  109.0 67.4 %collective-permute-start.17 = (bf16[16,2,64,128]{3,2,1,0:T(8,128)(2,1)S(1)}, bf16[16,2,64,128]{3,2,1,0:T(8,128)(2,1)S(1)}, u32[]{:S(2)}, u32[]{:S(2)}) collective-permute-start(bf16[16,2,64,128]{3,2,1,0:T(8,128)(2,1)S(1)} %copy-done.7), channel_id=1, source_target_pairs={{0,12},{4,0},{8,4},{12,8},{1,13},{5,1},{9,5},{13,9},{2,14},{6,2},{... | collective-permute-start | bytes 1572872 | tf_op jit(solution)/shard_map/ppermute | solution.py:373
  130.8 60.4 %collective-permute-start.18 = (bf16[16,2,64,128]{3,2,1,0:T(8,128)(2,1)S(1)}, bf16[16,2,64,128]{3,2,1,0:T(8,128)(2,1)S(1)}, u32[]{:S(2)}, u32[]{:S(2)}) collective-permute-start(bf16[16,2,64,128]{3,2,1,0:T(8,128)(2,1)S(1)} %get-tuple-element.141), channel_id=1, source_target_pairs={{0,4},{4,8},{8,12},{12,0},{1,5},{5,9},{9,13},{13,1},{2,6},{6,10},{... | collective-permute-start | bytes 1572872 | tf_op jit(solution)/shard_map/ppermute | solution.py:373
  130.8 89.8 %collective-permute-start.19 = (bf16[16,2,64,128]{3,2,1,0:T(8,128)(2,1)S(1)}, bf16[16,2,64,128]{3,2,1,0:T(8,128)(2,1)S(1)}, u32[]{:S(2)}, u32[]{:S(2)}) collective-permute-start(bf16[16,2,64,128]{3,2,1,0:T(8,128)(2,1)S(1)} %get-tuple-element.142), channel_id=1, source_target_pairs={{0,8},{4,12},{8,0},{12,4},{1,9},{5,13},{9,1},{13,5},{2,10},{6,14},... | collective-permute-start | bytes 1572872 | tf_op jit(solution)/shard_map/ppermute | solution.py:373
  141.3 79.3 %collective-permute-start.20 = (bf16[16,2,64,128]{3,2,1,0:T(8,128)(2,1)S(1)}, bf16[16,2,64,128]{3,2,1,0:T(8,128)(2,1)S(1)}, u32[]{:S(2)}, u32[]{:S(2)}) collective-permute-start(bf16[16,2,64,128]{3,2,1,0:T(8,128)(2,1)S(1)} %get-tuple-element.143), channel_id=1, source_target_pairs={{0,12},{4,0},{8,4},{12,8},{1,13},{5,1},{9,5},{13,9},{2,14},{6,2},{... | collective-permute-start | bytes 1572872 | tf_op jit(solution)/shard_map/ppermute | solution.py:373
  176.4 66.7 %collective-permute-start.13 = (bf16[16,2,64,128]{3,2,1,0:T(8,128)(2,1)S(1)}, bf16[16,2,64,128]{3,2,1,0:T(8,128)(2,1)S(1)}, u32[]{:S(2)}, u32[]{:S(2)}) collective-permute-start(bf16[16,2,64,128]{3,2,1,0:T(8,128)(2,1)S(1)} %get-tuple-element.132), channel_id=1, source_target_pairs={{0,8},{4,12},{8,0},{12,4},{1,9},{5,13},{9,1},{13,5},{2,10},{6,14},... | collective-permute-start | bytes 1572872 | tf_op jit(solution)/shard_map/ppermute | solution.py:373
  191.2 71.8 %collective-permute-start.14 = (bf16[16,2,64,128]{3,2,1,0:T(8,128)(2,1)S(1)}, bf16[16,2,64,128]{3,2,1,0:T(8,128)(2,1)S(1)}, u32[]{:S(2)}, u32[]{:S(2)}) collective-permute-start(bf16[16,2,64,128]{3,2,1,0:T(8,128)(2,1)S(1)} %get-tuple-element.133), channel_id=1, source_target_pairs={{0,12},{4,0},{8,4},{12,8},{1,13},{5,1},{9,5},{13,9},{2,14},{6,2},{... | collective-permute-start | bytes 1572872 | tf_op jit(solution)/shard_map/ppermute | solution.py:373
  227.9 62.6 %collective-permute-start.27 = (bf16[16,2,64,128]{3,2,1,0:T(8,128)(2,1)S(1)}, bf16[16,2,64,128]{3,2,1,0:T(8,128)(2,1)S(1)}, u32[]{:S(2)}, u32[]{:S(2)}) collective-permute-start(bf16[16,2,64,128]{3,2,1,0:T(8,128)(2,1)S(1)} %get-tuple-element.158), channel_id=1, source_target_pairs={{0,4},{4,8},{8,12},{12,0},{1,5},{5,9},{9,13},{13,1},{2,6},{6,10},{... | collective-permute-start | bytes 1572872 | tf_op jit(solution)/shard_map/ppermute | solution.py:373
  228.9 109.8 %collective-permute-start.28 = (bf16[16,2,64,128]{3,2,1,0:T(8,128)(2,1)S(1)}, bf16[16,2,64,128]{3,2,1,0:T(8,128)(2,1)S(1)}, u32[]{:S(2)}, u32[]{:S(2)}) collective-permute-start(bf16[16,2,64,128]{3,2,1,0:T(8,128)(2,1)S(1)} %get-tuple-element.159), channel_id=1, source_target_pairs={{0,8},{4,12},{8,0},{12,4},{1,9},{5,13},{9,1},{13,5},{2,10},{6,14},... | collective-permute-start | bytes 1572872 | tf_op jit(solution)/shard_map/ppermute | solution.py:373
  243.1 95.6 %collective-permute-start.29 = (bf16[16,2,64,128]{3,2,1,0:T(8,128)(2,1)S(1)}, bf16[16,2,64,128]{3,2,1,0:T(8,128)(2,1)S(1)}, u32[]{:S(2)}, u32[]{:S(2)}) collective-permute-start(bf16[16,2,64,128]{3,2,1,0:T(8,128)(2,1)S(1)} %get-tuple-element.160), channel_id=1, source_target_pairs={{0,12},{4,0},{8,4},{12,8},{1,13},{5,1},{9,5},{13,9},{2,14},{6,2},{... | collective-permute-start | bytes 1572872 | tf_op jit(solution)/shard_map/ppermute | solution.py:373
  263.0 92.5 %collective-permute-start.25 = (bf16[16,2,64,128]{3,2,1,0:T(8,128)(2,1)S(1)}, bf16[16,2,64,128]{3,2,1,0:T(8,128)(2,1)S(1)}, u32[]{:S(2)}, u32[]{:S(2)}) collective-permute-start(bf16[16,2,64,128]{3,2,1,0:T(8,128)(2,1)S(1)} %get-tuple-element.154), channel_id=1, source_target_pairs={{0,8},{4,12},{8,0},{12,4},{1,9},{5,13},{9,1},{13,5},{2,10},{6,14},... | collective-permute-start | bytes 1572872 | tf_op jit(solution)/shard_map/ppermute | solution.py:373
  276.1 79.4 %collective-permute-start.26 = (bf16[16,2,64,128]{3,2,1,0:T(8,128)(2,1)S(1)}, bf16[16,2,64,128]{3,2,1,0:T(8,128)(2,1)S(1)}, u32[]{:S(2)}, u32[]{:S(2)}) collective-permute-start(bf16[16,2,64,128]{3,2,1,0:T(8,128)(2,1)S(1)} %get-tuple-element.155), channel_id=1, source_target_pairs={{0,12},{4,0},{8,4},{12,8},{1,13},{5,1},{9,5},{13,9},{2,14},{6,2},{... | collective-permute-start | bytes 1572872 | tf_op jit(solution)/shard_map/ppermute | solution.py:373
  290.5 79.5 %collective-permute-start.21 = (bf16[16,2,64,128]{3,2,1,0:T(8,128)(2,1)S(1)}, bf16[16,2,64,128]{3,2,1,0:T(8,128)(2,1)S(1)}, u32[]{:S(2)}, u32[]{:S(2)}) collective-permute-start(bf16[16,2,64,128]{3,2,1,0:T(8,128)(2,1)S(1)} %get-tuple-element.149), channel_id=1, source_target_pairs={{0,4},{4,8},{8,12},{12,0},{1,5},{5,9},{9,13},{13,1},{2,6},{6,10},{... | collective-permute-start | bytes 1572872 | tf_op jit(solution)/shard_map/ppermute | solution.py:373
  338.7 61.8 %collective-permute-start.22 = (bf16[16,2,64,128]{3,2,1,0:T(8,128)(2,1)S(1)}, bf16[16,2,64,128]{3,2,1,0:T(8,128)(2,1)S(1)}, u32[]{:S(2)}, u32[]{:S(2)}) collective-permute-start(bf16[16,2,64,128]{3,2,1,0:T(8,128)(2,1)S(1)} %get-tuple-element.150), channel_id=1, source_target_pairs={{0,8},{4,12},{8,0},{12,4},{1,9},{5,13},{9,1},{13,5},{2,10},{6,14},... | collective-permute-start | bytes 1572872 | tf_op jit(solution)/shard_map/ppermute | solution.py:373
  338.7 61.8 %collective-permute-start.23 = (bf16[16,2,64,128]{3,2,1,0:T(8,128)(2,1)S(1)}, bf16[16,2,64,128]{3,2,1,0:T(8,128)(2,1)S(1)}, u32[]{:S(2)}, u32[]{:S(2)}) collective-permute-start(bf16[16,2,64,128]{3,2,1,0:T(8,128)(2,1)S(1)} %get-tuple-element.151), channel_id=1, source_target_pairs={{0,12},{4,0},{8,4},{12,8},{1,13},{5,1},{9,5},{13,9},{2,14},{6,2},{... | collective-permute-start | bytes 1572872 | tf_op jit(solution)/shard_map/ppermute | solution.py:373
  355.5 89.9 %collective-permute-start.34 = (bf16[16,2,64,128]{3,2,1,0:T(8,128)(2,1)S(1)}, bf16[16,2,64,128]{3,2,1,0:T(8,128)(2,1)S(1)}, u32[]{:S(2)}, u32[]{:S(2)}) collective-permute-start(bf16[16,2,64,128]{3,2,1,0:T(8,128)(2,1)S(1)} %get-tuple-element.171), channel_id=1, source_target_pairs={{0,8},{4,12},{8,0},{12,4},{1,9},{5,13},{9,1},{13,5},{2,10},{6,14},... | collective-permute-start | bytes 1572872 | tf_op jit(solution)/shard_map/ppermute | solution.py:373
  370.1 75.3 %collective-permute-start.35 = (bf16[16,2,64,128]{3,2,1,0:T(8,128)(2,1)S(1)}, bf16[16,2,64,128]{3,2,1,0:T(8,128)(2,1)S(1)}, u32[]{:S(2)}, u32[]{:S(2)}) collective-permute-start(bf16[16,2,64,128]{3,2,1,0:T(8,128)(2,1)S(1)} %get-tuple-element.172), channel_id=1, source_target_pairs={{0,12},{4,0},{8,4},{12,8},{1,13},{5,1},{9,5},{13,9},{2,14},{6,2},{... | collective-permute-start | bytes 1572872 | tf_op jit(solution)/shard_map/ppermute | solution.py:373
  400.5 93.6 %collective-permute-start.37 = (bf16[16,2,64,128]{3,2,1,0:T(8,128)(2,1)S(1)}, bf16[16,2,64,128]{3,2,1,0:T(8,128)(2,1)S(1)}, u32[]{:S(2)}, u32[]{:S(2)}) collective-permute-start(bf16[16,2,64,128]{3,2,1,0:T(8,128)(2,1)S(1)} %get-tuple-element.178), channel_id=1, source_target_pairs={{0,8},{4,12},{8,0},{12,4},{1,9},{5,13},{9,1},{13,5},{2,10},{6,14},... | collective-permute-start | bytes 1572872 | tf_op jit(solution)/shard_map/ppermute | solution.py:373
  407.8 86.4 %collective-permute-start.38 = (bf16[16,2,64,128]{3,2,1,0:T(8,128)(2,1)S(1)}, bf16[16,2,64,128]{3,2,1,0:T(8,128)(2,1)S(1)}, u32[]{:S(2)}, u32[]{:S(2)}) collective-permute-start(bf16[16,2,64,128]{3,2,1,0:T(8,128)(2,1)S(1)} %get-tuple-element.179), channel_id=1, source_target_pairs={{0,12},{4,0},{8,4},{12,8},{1,13},{5,1},{9,5},{13,9},{2,14},{6,2},{... | collective-permute-start | bytes 1572872 | tf_op jit(solution)/shard_map/ppermute | solution.py:373
  445.4 89.9 %collective-permute-start.31 = (bf16[16,2,64,128]{3,2,1,0:T(8,128)(2,1)S(1)}, bf16[16,2,64,128]{3,2,1,0:T(8,128)(2,1)S(1)}, u32[]{:S(2)}, u32[]{:S(2)}) collective-permute-start(bf16[16,2,64,128]{3,2,1,0:T(8,128)(2,1)S(1)} %get-tuple-element.167), channel_id=1, source_target_pairs={{0,8},{4,12},{8,0},{12,4},{1,9},{5,13},{9,1},{13,5},{2,10},{6,14},... | collective-permute-start | bytes 1572872 | tf_op jit(solution)/shard_map/ppermute | solution.py:373
  445.4 89.9 %collective-permute-start.32 = (bf16[16,2,64,128]{3,2,1,0:T(8,128)(2,1)S(1)}, bf16[16,2,64,128]{3,2,1,0:T(8,128)(2,1)S(1)}, u32[]{:S(2)}, u32[]{:S(2)}) collective-permute-start(bf16[16,2,64,128]{3,2,1,0:T(8,128)(2,1)S(1)} %get-tuple-element.168), channel_id=1, source_target_pairs={{0,12},{4,0},{8,4},{12,8},{1,13},{5,1},{9,5},{13,9},{2,14},{6,2},{... | collective-permute-start | bytes 1572872 | tf_op jit(solution)/shard_map/ppermute | solution.py:373
  494.1 86.1 %collective-permute-start.46 = (bf16[16,2,64,128]{3,2,1,0:T(8,128)(2,1)S(1)}, bf16[16,2,64,128]{3,2,1,0:T(8,128)(2,1)S(1)}, u32[]{:S(2)}, u32[]{:S(2)}) collective-permute-start(bf16[16,2,64,128]{3,2,1,0:T(8,128)(2,1)S(1)} %get-tuple-element.195), channel_id=1, source_target_pairs={{0,8},{4,12},{8,0},{12,4},{1,9},{5,13},{9,1},{13,5},{2,10},{6,14},... | collective-permute-start | bytes 1572872 | tf_op jit(solution)/shard_map/ppermute | solution.py:373
  495.6 84.7 %collective-permute-start.47 = (bf16[16,2,64,128]{3,2,1,0:T(8,128)(2,1)S(1)}, bf16[16,2,64,128]{3,2,1,0:T(8,128)(2,1)S(1)}, u32[]{:S(2)}, u32[]{:S(2)}) collective-permute-start(bf16[16,2,64,128]{3,2,1,0:T(8,128)(2,1)S(1)} %get-tuple-element.196), channel_id=1, source_target_pairs={{0,12},{4,0},{8,4},{12,8},{1,13},{5,1},{9,5},{13,9},{2,14},{6,2},{... | collective-permute-start | bytes 1572872 | tf_op jit(solution)/shard_map/ppermute | solution.py:373
  535.3 89.9 %collective-permute-start.43 = (bf16[16,2,64,128]{3,2,1,0:T(8,128)(2,1)S(1)}, bf16[16,2,64,128]{3,2,1,0:T(8,128)(2,1)S(1)}, u32[]{:S(2)}, u32[]{:S(2)}) collective-permute-start(bf16[16,2,64,128]{3,2,1,0:T(8,128)(2,1)S(1)} %get-tuple-element.190), channel_id=1, source_target_pairs={{0,8},{4,12},{8,0},{12,4},{1,9},{5,13},{9,1},{13,5},{2,10},{6,14},... | collective-permute-start | bytes 1572872 | tf_op jit(solution)/shard_map/ppermute | solution.py:373
  549.8 75.3 %collective-permute-start.44 = (bf16[16,2,64,128]{3,2,1,0:T(8,128)(2,1)S(1)}, bf16[16,2,64,128]{3,2,1,0:T(8,128)(2,1)S(1)}, u32[]{:S(2)}, u32[]{:S(2)}) collective-permute-start(bf16[16,2,64,128]{3,2,1,0:T(8,128)(2,1)S(1)} %get-tuple-element.191), channel_id=1, source_target_pairs={{0,12},{4,0},{8,4},{12,8},{1,13},{5,1},{9,5},{13,9},{2,14},{6,2},{... | collective-permute-start | bytes 1572872 | tf_op jit(solution)/shard_map/ppermute | solution.py:373
  580.2 89.9 %collective-permute-start.40 = (bf16[16,2,64,128]{3,2,1,0:T(8,128)(2,1)S(1)}, bf16[16,2,64,128]{3,2,1,0:T(8,128)(2,1)S(1)}, u32[]{:S(2)}, u32[]{:S(2)}) collective-permute-start(bf16[16,2,64,128]{3,2,1,0:T(8,128)(2,1)S(1)} %get-tuple-element.186), channel_id=1, source_target_pairs={{0,8},{4,12},{8,0},{12,4},{1,9},{5,13},{9,1},{13,5},{2,10},{6,14},... | collective-permute-start | bytes 1572872 | tf_op jit(solution)/shard_map/ppermute | solution.py:373
  587.5 82.6 %collective-permute-start.41 = (bf16[16,2,64,128]{3,2,1,0:T(8,128)(2,1)S(1)}, bf16[16,2,64,128]{3,2,1,0:T(8,128)(2,1)S(1)}, u32[]{:S(2)}, u32[]{:S(2)}) collective-permute-start(bf16[16,2,64,128]{3,2,1,0:T(8,128)(2,1)S(1)} %get-tuple-element.187), channel_id=1, source_target_pairs={{0,12},{4,0},{8,4},{12,8},{1,13},{5,1},{9,5},{13,9},{2,14},{6,2},{... | collective-permute-start | bytes 1572872 | tf_op jit(solution)/shard_map/ppermute | solution.py:373
  625.2 70.6 %collective-permute-start.55 = (bf16[16,2,64,128]{3,2,1,0:T(8,128)(2,1)S(1)}, bf16[16,2,64,128]{3,2,1,0:T(8,128)(2,1)S(1)}, u32[]{:S(2)}, u32[]{:S(2)}) collective-permute-start(bf16[16,2,64,128]{3,2,1,0:T(8,128)(2,1)S(1)} %get-tuple-element.210), channel_id=1, source_target_pairs={{0,8},{4,12},{8,0},{12,4},{1,9},{5,13},{9,1},{13,5},{2,10},{6,14},... | collective-permute-start | bytes 1572872 | tf_op jit(solution)/shard_map/ppermute | solution.py:373
  632.5 63.2 %collective-permute-start.56 = (bf16[16,2,64,128]{3,2,1,0:T(8,128)(2,1)S(1)}, bf16[16,2,64,128]{3,2,1,0:T(8,128)(2,1)S(1)}, u32[]{:S(2)}, u32[]{:S(2)}) collective-permute-start(bf16[16,2,64,128]{3,2,1,0:T(8,128)(2,1)S(1)} %get-tuple-element.211), channel_id=1, source_target_pairs={{0,12},{4,0},{8,4},{12,8},{1,13},{5,1},{9,5},{13,9},{2,14},{6,2},{... | collective-permute-start | bytes 1572872 | tf_op jit(solution)/shard_map/ppermute | solution.py:373
  (39 other events, 1400.3 us)

commit v10 on v8

--- a/solution.py
+++ b/solution.py
@@ -59,7 +59,8 @@
 
 def edges(field, first, count, block, span, after):
     parts = field.shape[0]
-    base, groups = span[0] // ROWS, span[1] // ROWS
+    some = 2 * ROWS if span[0] % (2 * ROWS) == 0 and span[1] % (2 * ROWS) == 0 else ROWS
+    base, groups = span[0] // some, span[1] // some
 
     def kernel(x_ref, *refs):
         o_ref, _, acc = refs[-3:]
@@ -67,8 +68,8 @@
         slot = ((lane_index(block) + 1) >> 1) & (LANES // 2 - 1)
         for c in range(parts):
             kept = acc[c]
-            for i in range(ROWS):
-                m = (g + base) * ROWS + i
+            for i in range(some):
+                m = (g + base) * some + i
                 row = roll(x_ref[c, i].astype(jnp.float32), 2 * m)
                 kept = jnp.where(slot == m, row, kept)
             acc[c] = kept
@@ -85,7 +86,7 @@
         ],
         grid=(count, groups),
         in_specs=[
-            pl.BlockSpec((parts, ROWS, block, LANES), lambda j, g: (0, g + base, j + first, 0))
+            pl.BlockSpec((parts, some, block, LANES), lambda j, g: (0, g + base, j + first, 0))
         ]
         + anywhere(len(after)),
         out_specs=[pl.BlockSpec((parts, block, LANES), lambda j, g: (0, j, 0))] + anywhere(1),

time: 742 us -> 741 us (level)
  waiting for transfers between devices: 186 us -> 205 us
  starting transfers between devices: 356 us -> 343 us
    ppermute x51, waiting for transfers between devices: 175 us -> 194 us  [exchange(): lax.ppermute(pieces[s], 'ang', ring('ang', s))]
    ppermute x51, starting transfers between devices: 354 us -> 342 us  [exchange(): lax.ppermute(pieces[s], 'ang', ring('ang', s))]
  transfers between devices with their start and end apart: 57 -> 57, of which waited for: 20 -> 19; matrix products, arithmetic and copies ran while one was open for 0% -> 0% of each run, Pallas kernels for 24% -> 24%
where the time goes in v10:
time: 741 us; the launch traced here: 740 us
  starting transfers between devices  343 us (46%)
  waiting for transfers between devices  205 us (28%)
  Pallas kernels  186 us (25%)
    ppermute x51, starting transfers between devices, exchange(): lax.ppermute(pieces[s], 'ang', ring('ang', s))  342 us
    ppermute x51, waiting for transfers between devices, exchange(): lax.ppermute(pieces[s], 'ang', ring('ang', s))  194 us
    pallas_call x8, Pallas kernels, kerr_step(): pl.pallas_call(kernel, out_shape=[jax.ShapeDtypeStruct((share, parts, siz...  59.9 us
    pallas_call x9, Pallas kernels, analyze(): pl.pallas_call(kernel, out_shape=[jax.ShapeDtypeStruct(field.shape, field...  57 us
    pallas_call x8, Pallas kernels, synthesize(): pl.pallas_call(kernel, out_shape=[piece] * count + [token()], grid_spec=p...  54.4 us
  transfers between devices with their start and end apart: 57, of which 19 were waited for; matrix products, arithmetic and copies ran while one was open for 0% of the time, Pallas kernels for 24%

profile of v10, /device:TPU:24, one launch (start us, length us, event | category | flops | bytes accessed | tf_op | source)
XLA Modules:
  0.0 739.5 jit_solution(12154290165869265194)
XLA Ops:
  21.0 7.3 synthesize.9
  28.3 10.7 %edges.5 = (bf16[2,384,128]{2,1,0:T(8,128)(2,1)S(1)}, f32[8,128]{1,0:T(8,128)S(1)}) custom-call(bf16[2,64,512,128]{3,2,1,0:T(8,128)(2,1)} %refs_4_.17, f32[8,128]{1,0:T(8,128)S(1)} %get-tuple-element.117.refs_0_), custom_call_target="tpu_custom_call" | custom-call | bytes 12582912 | tf_op jit(solution)/shard_map/edges/pallas_call | solution.py:81
  49.6 29.0 %collective-permute-done.10.refs_2_ = bf16[16,2,64,128]{3,2,1,0:T(8,128)(2,1)S(1)} collective-permute-done((bf16[16,2,64,128]{3,2,1,0:T(8,128)(2,1)S(1)}, bf16[16,2,64,128]{3,2,1,0:T(8,128)(2,1)S(1)}, u32[]{:S(2)}, u32[]{:S(2)}) %collective-permute-start.10) | collective-permute-done | bytes 524320 | tf_op jit(solution)/shard_map/ppermute | solution.py:335
  78.6 8.0 %kerr.8 = (bf16[16,2,64,128]{3,2,1,0:T(8,128)(2,1)S(1)}, bf16[16,2,64,128]{3,2,1,0:T(8,128)(2,1)}, bf16[16,2,64,128]{3,2,1,0:T(8,128)(2,1)}, bf16[16,2,64,128]{3,2,1,0:T(8,128)(2,1)S(1)}, f32[8,128]{1,0:T(8,128)S(1)}) custom-call(s32[1]{0:T(128)} %bitcast.me_ref, bf16[512,512]{1,0:T(8,128)(2,1)S(1)} %copy-done.10, bf16[512,512]{1,0:T(8,128)(2,1)S(1)} %copy-done.8, ...), custom_call_target="tpu_custom_call" | custom-call | flops 2147483648 | bytes 4194304 | tf_op jit(solution)/shard_map/kerr/pallas_call | solution.py:240
  116.5 13.2 %collective-permute-start.19 = (bf16[16,2,64,128]{3,2,1,0:T(8,128)(2,1)S(1)}, bf16[16,2,64,128]{3,2,1,0:T(8,128)(2,1)S(1)}, u32[]{:S(2)}, u32[]{:S(2)}) collective-permute-start(bf16[16,2,64,128]{3,2,1,0:T(8,128)(2,1)S(1)} %get-tuple-element.142), channel_id=1, source_target_pairs={{0,8},{4,12},{8,0},{12,4},{1,9},{5,13},{9,1},{13,5},{2,10},{6,14},... | collective-permute-start | bytes 1572872 | tf_op jit(solution)/shard_map/ppermute | solution.py:335
  129.8 11.3 %collective-permute-start.20 = (bf16[16,2,64,128]{3,2,1,0:T(8,128)(2,1)S(1)}, bf16[16,2,64,128]{3,2,1,0:T(8,128)(2,1)S(1)}, u32[]{:S(2)}, u32[]{:S(2)}) collective-permute-start(bf16[16,2,64,128]{3,2,1,0:T(8,128)(2,1)S(1)} %get-tuple-element.143), channel_id=1, source_target_pairs={{0,12},{4,0},{8,4},{12,8},{1,13},{5,1},{9,5},{13,9},{2,14},{6,2},{... | collective-permute-start | bytes 1572872 | tf_op jit(solution)/shard_map/ppermute | solution.py:335
  141.1 8.3 %kerr.9 = (bf16[16,2,64,128]{3,2,1,0:T(8,128)(2,1)S(1)}, bf16[16,2,64,128]{3,2,1,0:T(8,128)(2,1)S(1)}, bf16[16,2,64,128]{3,2,1,0:T(8,128)(2,1)S(1)}, bf16[16,2,64,128]{3,2,1,0:T(8,128)(2,1)S(1)}, f32[8,128]{1,0:T(8,128)S(1)}) custom-call(s32[1]{0:T(128)} %bitcast.me_ref, bf16[512,512]{1,0:T(8,128)(2,1)S(1)} %copy-done.11, bf16[512,512]{1,0:T(8,128)(2,1)S(1)} %copy-done.9, ...), custom_call_target="tpu_custom_call" | custom-call | flops 2147483648 | bytes 4194304 | tf_op jit(solution)/shard_map/kerr/pallas_call | solution.py:240
  149.3 24.9 %collective-permute-done.16.refs_2_ = bf16[16,2,64,128]{3,2,1,0:T(8,128)(2,1)} collective-permute-done((bf16[16,2,64,128]{3,2,1,0:T(8,128)(2,1)}, bf16[16,2,64,128]{3,2,1,0:T(8,128)(2,1)}, u32[]{:S(2)}, u32[]{:S(2)}) %collective-permute-start.16) | collective-permute-done | bytes 524320 | tf_op jit(solution)/shard_map/ppermute | solution.py:335
  188.7 19.7 %collective-permute-start.14 = (bf16[16,2,64,128]{3,2,1,0:T(8,128)(2,1)S(1)}, bf16[16,2,64,128]{3,2,1,0:T(8,128)(2,1)S(1)}, u32[]{:S(2)}, u32[]{:S(2)}) collective-permute-start(bf16[16,2,64,128]{3,2,1,0:T(8,128)(2,1)S(1)} %get-tuple-element.133), channel_id=1, source_target_pairs={{0,12},{4,0},{8,4},{12,8},{1,13},{5,1},{9,5},{13,9},{2,14},{6,2},{... | collective-permute-start | bytes 1572872 | tf_op jit(solution)/shard_map/ppermute | solution.py:335
  208.4 10.7 %collective-permute-done.19.refs_2_ = bf16[16,2,64,128]{3,2,1,0:T(8,128)(2,1)S(1)} collective-permute-done((bf16[16,2,64,128]{3,2,1,0:T(8,128)(2,1)S(1)}, bf16[16,2,64,128]{3,2,1,0:T(8,128)(2,1)S(1)}, u32[]{:S(2)}, u32[]{:S(2)}) %collective-permute-start.19) | collective-permute-done | bytes 524320 | tf_op jit(solution)/shard_map/ppermute | solution.py:335
  229.9 11.7 %collective-permute-done.13.refs_2_ = bf16[16,2,64,128]{3,2,1,0:T(8,128)(2,1)S(1)} collective-permute-done((bf16[16,2,64,128]{3,2,1,0:T(8,128)(2,1)S(1)}, bf16[16,2,64,128]{3,2,1,0:T(8,128)(2,1)S(1)}, u32[]{:S(2)}, u32[]{:S(2)}) %collective-permute-start.13) | collective-permute-done | bytes 524320 | tf_op jit(solution)/shard_map/ppermute | solution.py:335
  241.6 19.8 %collective-permute-start.29 = (bf16[16,2,64,128]{3,2,1,0:T(8,128)(2,1)S(1)}, bf16[16,2,64,128]{3,2,1,0:T(8,128)(2,1)S(1)}, u32[]{:S(2)}, u32[]{:S(2)}) collective-permute-start(bf16[16,2,64,128]{3,2,1,0:T(8,128)(2,1)S(1)} %get-tuple-element.160), channel_id=1, source_target_pairs={{0,12},{4,0},{8,4},{12,8},{1,13},{5,1},{9,5},{13,9},{2,14},{6,2},{... | collective-permute-start | bytes 1572872 | tf_op jit(solution)/shard_map/ppermute | solution.py:335
  261.4 13.1 %collective-permute-start.25 = (bf16[16,2,64,128]{3,2,1,0:T(8,128)(2,1)S(1)}, bf16[16,2,64,128]{3,2,1,0:T(8,128)(2,1)S(1)}, u32[]{:S(2)}, u32[]{:S(2)}) collective-permute-start(bf16[16,2,64,128]{3,2,1,0:T(8,128)(2,1)S(1)} %get-tuple-element.154), channel_id=1, source_target_pairs={{0,8},{4,12},{8,0},{12,4},{1,9},{5,13},{9,1},{13,5},{2,10},{6,14},... | collective-permute-start | bytes 1572872 | tf_op jit(solution)/shard_map/ppermute | solution.py:335
  291.9 45.3 %collective-permute-done.28.refs_2_ = bf16[16,2,64,128]{3,2,1,0:T(8,128)(2,1)S(1)} collective-permute-done((bf16[16,2,64,128]{3,2,1,0:T(8,128)(2,1)S(1)}, bf16[16,2,64,128]{3,2,1,0:T(8,128)(2,1)S(1)}, u32[]{:S(2)}, u32[]{:S(2)}) %collective-permute-start.28) | collective-permute-done | bytes 524320 | tf_op jit(solution)/shard_map/ppermute | solution.py:335
  337.2 7.3 kerr.11
  344.4 9.6 %collective-permute-done.25.refs_2_ = bf16[16,2,64,128]{3,2,1,0:T(8,128)(2,1)S(1)} collective-permute-done((bf16[16,2,64,128]{3,2,1,0:T(8,128)(2,1)S(1)}, bf16[16,2,64,128]{3,2,1,0:T(8,128)(2,1)S(1)}, u32[]{:S(2)}, u32[]{:S(2)}) %collective-permute-start.25) | collective-permute-done | bytes 524320 | tf_op jit(solution)/shard_map/ppermute | solution.py:335
  367.6 20.7 %collective-permute-start.35 = (bf16[16,2,64,128]{3,2,1,0:T(8,128)(2,1)S(1)}, bf16[16,2,64,128]{3,2,1,0:T(8,128)(2,1)S(1)}, u32[]{:S(2)}, u32[]{:S(2)}) collective-permute-start(bf16[16,2,64,128]{3,2,1,0:T(8,128)(2,1)S(1)} %get-tuple-element.172), channel_id=1, source_target_pairs={{0,12},{4,0},{8,4},{12,8},{1,13},{5,1},{9,5},{13,9},{2,14},{6,2},{... | collective-permute-start | bytes 1572872 | tf_op jit(solution)/shard_map/ppermute | solution.py:335
  388.3 10.7 %collective-permute-done.22.refs_2_ = bf16[16,2,64,128]{3,2,1,0:T(8,128)(2,1)S(1)} collective-permute-done((bf16[16,2,64,128]{3,2,1,0:T(8,128)(2,1)S(1)}, bf16[16,2,64,128]{3,2,1,0:T(8,128)(2,1)S(1)}, u32[]{:S(2)}, u32[]{:S(2)}) %collective-permute-start.22) | collective-permute-done | bytes 524320 | tf_op jit(solution)/shard_map/ppermute | solution.py:335
  406.3 26.9 %collective-permute-start.38 = (bf16[16,2,64,128]{3,2,1,0:T(8,128)(2,1)S(1)}, bf16[16,2,64,128]{3,2,1,0:T(8,128)(2,1)S(1)}, u32[]{:S(2)}, u32[]{:S(2)}) collective-permute-start(bf16[16,2,64,128]{3,2,1,0:T(8,128)(2,1)S(1)} %get-tuple-element.179), channel_id=1, source_target_pairs={{0,12},{4,0},{8,4},{12,8},{1,13},{5,1},{9,5},{13,9},{2,14},{6,2},{... | collective-permute-start | bytes 1572872 | tf_op jit(solution)/shard_map/ppermute | solution.py:335
  433.2 10.7 %collective-permute-done.34.refs_2_ = bf16[16,2,64,128]{3,2,1,0:T(8,128)(2,1)S(1)} collective-permute-done((bf16[16,2,64,128]{3,2,1,0:T(8,128)(2,1)S(1)}, bf16[16,2,64,128]{3,2,1,0:T(8,128)(2,1)S(1)}, u32[]{:S(2)}, u32[]{:S(2)}) %collective-permute-start.34) | collective-permute-done | bytes 524320 | tf_op jit(solution)/shard_map/ppermute | solution.py:335
  443.9 34.2 %collective-permute-start.32 = (bf16[16,2,64,128]{3,2,1,0:T(8,128)(2,1)S(1)}, bf16[16,2,64,128]{3,2,1,0:T(8,128)(2,1)S(1)}, u32[]{:S(2)}, u32[]{:S(2)}) collective-permute-start(bf16[16,2,64,128]{3,2,1,0:T(8,128)(2,1)S(1)} %get-tuple-element.168), channel_id=1, source_target_pairs={{0,12},{4,0},{8,4},{12,8},{1,13},{5,1},{9,5},{13,9},{2,14},{6,2},{... | collective-permute-start | bytes 1572872 | tf_op jit(solution)/shard_map/ppermute | solution.py:335
  493.1 30.0 %collective-permute-start.47 = (bf16[16,2,64,128]{3,2,1,0:T(8,128)(2,1)S(1)}, bf16[16,2,64,128]{3,2,1,0:T(8,128)(2,1)S(1)}, u32[]{:S(2)}, u32[]{:S(2)}) collective-permute-start(bf16[16,2,64,128]{3,2,1,0:T(8,128)(2,1)S(1)} %get-tuple-element.196), channel_id=1, source_target_pairs={{0,12},{4,0},{8,4},{12,8},{1,13},{5,1},{9,5},{13,9},{2,14},{6,2},{... | collective-permute-start | bytes 1572872 | tf_op jit(solution)/shard_map/ppermute | solution.py:335
  547.4 20.7 %collective-permute-start.44 = (bf16[16,2,64,128]{3,2,1,0:T(8,128)(2,1)S(1)}, bf16[16,2,64,128]{3,2,1,0:T(8,128)(2,1)S(1)}, u32[]{:S(2)}, u32[]{:S(2)}) collective-permute-start(bf16[16,2,64,128]{3,2,1,0:T(8,128)(2,1)S(1)} %get-tuple-element.191), channel_id=1, source_target_pairs={{0,12},{4,0},{8,4},{12,8},{1,13},{5,1},{9,5},{13,9},{2,14},{6,2},{... | collective-permute-start | bytes 1572872 | tf_op jit(solution)/shard_map/ppermute | solution.py:335
  568.0 10.7 %collective-permute-done.46.refs_2_ = bf16[16,2,64,128]{3,2,1,0:T(8,128)(2,1)S(1)} collective-permute-done((bf16[16,2,64,128]{3,2,1,0:T(8,128)(2,1)S(1)}, bf16[16,2,64,128]{3,2,1,0:T(8,128)(2,1)S(1)}, u32[]{:S(2)}, u32[]{:S(2)}) %collective-permute-start.46) | collective-permute-done | bytes 524320 | tf_op jit(solution)/shard_map/ppermute | solution.py:335
  578.7 7.3 kerr.14
  586.0 26.9 %collective-permute-start.41 = (bf16[16,2,64,128]{3,2,1,0:T(8,128)(2,1)S(1)}, bf16[16,2,64,128]{3,2,1,0:T(8,128)(2,1)S(1)}, u32[]{:S(2)}, u32[]{:S(2)}) collective-permute-start(bf16[16,2,64,128]{3,2,1,0:T(8,128)(2,1)S(1)} %get-tuple-element.187), channel_id=1, source_target_pairs={{0,12},{4,0},{8,4},{12,8},{1,13},{5,1},{9,5},{13,9},{2,14},{6,2},{... | collective-permute-start | bytes 1572872 | tf_op jit(solution)/shard_map/ppermute | solution.py:335
  613.0 10.7 %collective-permute-done.43.refs_2_ = bf16[16,2,64,128]{3,2,1,0:T(8,128)(2,1)S(1)} collective-permute-done((bf16[16,2,64,128]{3,2,1,0:T(8,128)(2,1)S(1)}, bf16[16,2,64,128]{3,2,1,0:T(8,128)(2,1)S(1)}, u32[]{:S(2)}, u32[]{:S(2)}) %collective-permute-start.43) | collective-permute-done | bytes 524320 | tf_op jit(solution)/shard_map/ppermute | solution.py:335
  630.5 27.4 %collective-permute-start.56 = (bf16[16,2,64,128]{3,2,1,0:T(8,128)(2,1)S(1)}, bf16[16,2,64,128]{3,2,1,0:T(8,128)(2,1)S(1)}, u32[]{:S(2)}, u32[]{:S(2)}) collective-permute-start(bf16[16,2,64,128]{3,2,1,0:T(8,128)(2,1)S(1)} %get-tuple-element.211), channel_id=1, source_target_pairs={{0,12},{4,0},{8,4},{12,8},{1,13},{5,1},{9,5},{13,9},{2,14},{6,2},{... | collective-permute-start | bytes 1572872 | tf_op jit(solution)/shard_map/ppermute | solution.py:335
  657.9 10.7 %collective-permute-done.40.refs_2_ = bf16[16,2,64,128]{3,2,1,0:T(8,128)(2,1)S(1)} collective-permute-done((bf16[16,2,64,128]{3,2,1,0:T(8,128)(2,1)S(1)}, bf16[16,2,64,128]{3,2,1,0:T(8,128)(2,1)S(1)}, u32[]{:S(2)}, u32[]{:S(2)}) %collective-permute-start.40) | collective-permute-done | bytes 524320 | tf_op jit(solution)/shard_map/ppermute | solution.py:335
  675.9 13.2 %collective-permute-start.53 = (bf16[16,2,48,128]{3,2,1,0:T(8,128)(2,1)S(1)}, bf16[16,2,48,128]{3,2,1,0:T(8,128)(2,1)S(1)}, u32[]{:S(2)}, u32[]{:S(2)}) collective-permute-start(bf16[16,2,48,128]{3,2,1,0:T(8,128)(2,1)S(1)} %get-tuple-element.207), channel_id=1, source_target_pairs={{0,8},{4,12},{8,0},{12,4},{1,9},{5,13},{9,1},{13,5},{2,10},{6,14},... | collective-permute-start | bytes 1179656 | tf_op jit(solution)/shard_map/ppermute | solution.py:335
  694.2 15.8 %collective-permute-start.50 = (bf16[16,2,16,128]{3,2,1,0:T(8,128)(2,1)S(1)}, bf16[16,2,16,128]{3,2,1,0:T(8,128)(2,1)S(1)}, u32[]{:S(2)}, u32[]{:S(2)}) collective-permute-start(bf16[16,2,16,128]{3,2,1,0:T(8,128)(2,1)S(1)} %get-tuple-element.203), channel_id=1, source_target_pairs={{0,8},{4,12},{8,0},{12,4},{1,9},{5,13},{9,1},{13,5},{2,10},{6,14},... | collective-permute-start | bytes 393224 | tf_op jit(solution)/shard_map/ppermute | solution.py:335
  710.1 12.5 %collective-permute-start.51 = (bf16[16,2,16,128]{3,2,1,0:T(8,128)(2,1)S(1)}, bf16[16,2,16,128]{3,2,1,0:T(8,128)(2,1)S(1)}, u32[]{:S(2)}, u32[]{:S(2)}) collective-permute-start(bf16[16,2,16,128]{3,2,1,0:T(8,128)(2,1)S(1)} %get-tuple-element.204), channel_id=1, source_target_pairs={{0,12},{4,0},{8,4},{12,8},{1,13},{5,1},{9,5},{13,9},{2,14},{6,2},{... | collective-permute-start | bytes 393224 | tf_op jit(solution)/shard_map/ppermute | solution.py:335
  (141 shorter events, 200.2 us)
Async XLA Ops:
  13.4 65.1 %collective-permute-start.10 = (bf16[16,2,64,128]{3,2,1,0:T(8,128)(2,1)S(1)}, bf16[16,2,64,128]{3,2,1,0:T(8,128)(2,1)S(1)}, u32[]{:S(2)}, u32[]{:S(2)}) collective-permute-start(bf16[16,2,64,128]{3,2,1,0:T(8,128)(2,1)S(1)} %get-tuple-element.125), channel_id=1, source_target_pairs={{0,8},{4,12},{8,0},{12,4},{1,9},{5,13},{9,1},{13,5},{2,10},{6,14},... | collective-permute-start | bytes 1572872 | tf_op jit(solution)/shard_map/ppermute | solution.py:335
  15.1 63.4 %collective-permute-start.11 = (bf16[16,2,64,128]{3,2,1,0:T(8,128)(2,1)S(1)}, bf16[16,2,64,128]{3,2,1,0:T(8,128)(2,1)S(1)}, u32[]{:S(2)}, u32[]{:S(2)}) collective-permute-start(bf16[16,2,64,128]{3,2,1,0:T(8,128)(2,1)S(1)} %get-tuple-element.126), channel_id=1, source_target_pairs={{0,12},{4,0},{8,4},{12,8},{1,13},{5,1},{9,5},{13,9},{2,14},{6,2},{... | collective-permute-start | bytes 1572872 | tf_op jit(solution)/shard_map/ppermute | solution.py:335
  39.3 73.3 %collective-permute-start.6 = (bf16[16,2,64,128]{3,2,1,0:T(8,128)(2,1)}, bf16[16,2,64,128]{3,2,1,0:T(8,128)(2,1)}, u32[]{:S(2)}, u32[]{:S(2)}) collective-permute-start(bf16[16,2,64,128]{3,2,1,0:T(8,128)(2,1)} %get-tuple-element.120), channel_id=1, source_target_pairs={{0,4},{4,8},{8,12},{12,0},{1,5},{5,9},{9,13},{13,1},{2,6},{6,10},{... | collective-permute-start | bytes 1572872 | tf_op jit(solution)/shard_map/ppermute | solution.py:335
  42.7 72.0 %collective-permute-start.7 = (bf16[16,2,64,128]{3,2,1,0:T(8,128)(2,1)}, bf16[16,2,64,128]{3,2,1,0:T(8,128)(2,1)}, u32[]{:S(2)}, u32[]{:S(2)}) collective-permute-start(bf16[16,2,64,128]{3,2,1,0:T(8,128)(2,1)} %get-tuple-element.121), channel_id=1, source_target_pairs={{0,8},{4,12},{8,0},{12,4},{1,9},{5,13},{9,1},{13,5},{2,10},{6,14},... | collective-permute-start | bytes 1572872 | tf_op jit(solution)/shard_map/ppermute | solution.py:335
  96.2 78.0 %collective-permute-start.16 = (bf16[16,2,64,128]{3,2,1,0:T(8,128)(2,1)}, bf16[16,2,64,128]{3,2,1,0:T(8,128)(2,1)}, u32[]{:S(2)}, u32[]{:S(2)}) collective-permute-start(bf16[16,2,64,128]{3,2,1,0:T(8,128)(2,1)} %get-tuple-element.136), channel_id=1, source_target_pairs={{0,8},{4,12},{8,0},{12,4},{1,9},{5,13},{9,1},{13,5},{2,10},{6,14},... | collective-permute-start | bytes 1572872 | tf_op jit(solution)/shard_map/ppermute | solution.py:335
  112.7 62.2 %collective-permute-start.17 = (bf16[16,2,64,128]{3,2,1,0:T(8,128)(2,1)S(1)}, bf16[16,2,64,128]{3,2,1,0:T(8,128)(2,1)S(1)}, u32[]{:S(2)}, u32[]{:S(2)}) collective-permute-start(bf16[16,2,64,128]{3,2,1,0:T(8,128)(2,1)S(1)} %copy-done.7), channel_id=1, source_target_pairs={{0,12},{4,0},{8,4},{12,8},{1,13},{5,1},{9,5},{13,9},{2,14},{6,2},{... | collective-permute-start | bytes 1572872 | tf_op jit(solution)/shard_map/ppermute | solution.py:335
  114.7 74.0 %collective-permute-start.18 = (bf16[16,2,64,128]{3,2,1,0:T(8,128)(2,1)S(1)}, bf16[16,2,64,128]{3,2,1,0:T(8,128)(2,1)S(1)}, u32[]{:S(2)}, u32[]{:S(2)}) collective-permute-start(bf16[16,2,64,128]{3,2,1,0:T(8,128)(2,1)S(1)} %get-tuple-element.141), channel_id=1, source_target_pairs={{0,4},{4,8},{8,12},{12,0},{1,5},{5,9},{9,13},{13,1},{2,6},{6,10},{... | collective-permute-start | bytes 1572872 | tf_op jit(solution)/shard_map/ppermute | solution.py:335
  116.5 102.5 %collective-permute-start.19 = (bf16[16,2,64,128]{3,2,1,0:T(8,128)(2,1)S(1)}, bf16[16,2,64,128]{3,2,1,0:T(8,128)(2,1)S(1)}, u32[]{:S(2)}, u32[]{:S(2)}) collective-permute-start(bf16[16,2,64,128]{3,2,1,0:T(8,128)(2,1)S(1)} %get-tuple-element.142), channel_id=1, source_target_pairs={{0,8},{4,12},{8,0},{12,4},{1,9},{5,13},{9,1},{13,5},{2,10},{6,14},... | collective-permute-start | bytes 1572872 | tf_op jit(solution)/shard_map/ppermute | solution.py:335
  129.8 89.3 %collective-permute-start.20 = (bf16[16,2,64,128]{3,2,1,0:T(8,128)(2,1)S(1)}, bf16[16,2,64,128]{3,2,1,0:T(8,128)(2,1)S(1)}, u32[]{:S(2)}, u32[]{:S(2)}) collective-permute-start(bf16[16,2,64,128]{3,2,1,0:T(8,128)(2,1)S(1)} %get-tuple-element.143), channel_id=1, source_target_pairs={{0,12},{4,0},{8,4},{12,8},{1,13},{5,1},{9,5},{13,9},{2,14},{6,2},{... | collective-permute-start | bytes 1572872 | tf_op jit(solution)/shard_map/ppermute | solution.py:335
  174.9 66.7 %collective-permute-start.13 = (bf16[16,2,64,128]{3,2,1,0:T(8,128)(2,1)S(1)}, bf16[16,2,64,128]{3,2,1,0:T(8,128)(2,1)S(1)}, u32[]{:S(2)}, u32[]{:S(2)}) collective-permute-start(bf16[16,2,64,128]{3,2,1,0:T(8,128)(2,1)S(1)} %get-tuple-element.132), channel_id=1, source_target_pairs={{0,8},{4,12},{8,0},{12,4},{1,9},{5,13},{9,1},{13,5},{2,10},{6,14},... | collective-permute-start | bytes 1572872 | tf_op jit(solution)/shard_map/ppermute | solution.py:335
  188.7 72.6 %collective-permute-start.14 = (bf16[16,2,64,128]{3,2,1,0:T(8,128)(2,1)S(1)}, bf16[16,2,64,128]{3,2,1,0:T(8,128)(2,1)S(1)}, u32[]{:S(2)}, u32[]{:S(2)}) collective-permute-start(bf16[16,2,64,128]{3,2,1,0:T(8,128)(2,1)S(1)} %get-tuple-element.133), channel_id=1, source_target_pairs={{0,12},{4,0},{8,4},{12,8},{1,13},{5,1},{9,5},{13,9},{2,14},{6,2},{... | collective-permute-start | bytes 1572872 | tf_op jit(solution)/shard_map/ppermute | solution.py:335
  227.4 109.8 %collective-permute-start.28 = (bf16[16,2,64,128]{3,2,1,0:T(8,128)(2,1)S(1)}, bf16[16,2,64,128]{3,2,1,0:T(8,128)(2,1)S(1)}, u32[]{:S(2)}, u32[]{:S(2)}) collective-permute-start(bf16[16,2,64,128]{3,2,1,0:T(8,128)(2,1)S(1)} %get-tuple-element.159), channel_id=1, source_target_pairs={{0,8},{4,12},{8,0},{12,4},{1,9},{5,13},{9,1},{13,5},{2,10},{6,14},... | collective-permute-start | bytes 1572872 | tf_op jit(solution)/shard_map/ppermute | solution.py:335
  241.6 95.6 %collective-permute-start.29 = (bf16[16,2,64,128]{3,2,1,0:T(8,128)(2,1)S(1)}, bf16[16,2,64,128]{3,2,1,0:T(8,128)(2,1)S(1)}, u32[]{:S(2)}, u32[]{:S(2)}) collective-permute-start(bf16[16,2,64,128]{3,2,1,0:T(8,128)(2,1)S(1)} %get-tuple-element.160), channel_id=1, source_target_pairs={{0,12},{4,0},{8,4},{12,8},{1,13},{5,1},{9,5},{13,9},{2,14},{6,2},{... | collective-permute-start | bytes 1572872 | tf_op jit(solution)/shard_map/ppermute | solution.py:335
  261.4 92.6 %collective-permute-start.25 = (bf16[16,2,64,128]{3,2,1,0:T(8,128)(2,1)S(1)}, bf16[16,2,64,128]{3,2,1,0:T(8,128)(2,1)S(1)}, u32[]{:S(2)}, u32[]{:S(2)}) collective-permute-start(bf16[16,2,64,128]{3,2,1,0:T(8,128)(2,1)S(1)} %get-tuple-element.154), channel_id=1, source_target_pairs={{0,8},{4,12},{8,0},{12,4},{1,9},{5,13},{9,1},{13,5},{2,10},{6,14},... | collective-permute-start | bytes 1572872 | tf_op jit(solution)/shard_map/ppermute | solution.py:335
  274.5 79.5 %collective-permute-start.26 = (bf16[16,2,64,128]{3,2,1,0:T(8,128)(2,1)S(1)}, bf16[16,2,64,128]{3,2,1,0:T(8,128)(2,1)S(1)}, u32[]{:S(2)}, u32[]{:S(2)}) collective-permute-start(bf16[16,2,64,128]{3,2,1,0:T(8,128)(2,1)S(1)} %get-tuple-element.155), channel_id=1, source_target_pairs={{0,12},{4,0},{8,4},{12,8},{1,13},{5,1},{9,5},{13,9},{2,14},{6,2},{... | collective-permute-start | bytes 1572872 | tf_op jit(solution)/shard_map/ppermute | solution.py:335
  288.0 79.6 %collective-permute-start.21 = (bf16[16,2,64,128]{3,2,1,0:T(8,128)(2,1)S(1)}, bf16[16,2,64,128]{3,2,1,0:T(8,128)(2,1)S(1)}, u32[]{:S(2)}, u32[]{:S(2)}) collective-permute-start(bf16[16,2,64,128]{3,2,1,0:T(8,128)(2,1)S(1)} %get-tuple-element.149), channel_id=1, source_target_pairs={{0,4},{4,8},{8,12},{12,0},{1,5},{5,9},{9,13},{13,1},{2,6},{6,10},{... | collective-permute-start | bytes 1572872 | tf_op jit(solution)/shard_map/ppermute | solution.py:335
  337.1 61.8 %collective-permute-start.22 = (bf16[16,2,64,128]{3,2,1,0:T(8,128)(2,1)S(1)}, bf16[16,2,64,128]{3,2,1,0:T(8,128)(2,1)S(1)}, u32[]{:S(2)}, u32[]{:S(2)}) collective-permute-start(bf16[16,2,64,128]{3,2,1,0:T(8,128)(2,1)S(1)} %get-tuple-element.150), channel_id=1, source_target_pairs={{0,8},{4,12},{8,0},{12,4},{1,9},{5,13},{9,1},{13,5},{2,10},{6,14},... | collective-permute-start | bytes 1572872 | tf_op jit(solution)/shard_map/ppermute | solution.py:335
  337.1 61.8 %collective-permute-start.23 = (bf16[16,2,64,128]{3,2,1,0:T(8,128)(2,1)S(1)}, bf16[16,2,64,128]{3,2,1,0:T(8,128)(2,1)S(1)}, u32[]{:S(2)}, u32[]{:S(2)}) collective-permute-start(bf16[16,2,64,128]{3,2,1,0:T(8,128)(2,1)S(1)} %get-tuple-element.151), channel_id=1, source_target_pairs={{0,12},{4,0},{8,4},{12,8},{1,13},{5,1},{9,5},{13,9},{2,14},{6,2},{... | collective-permute-start | bytes 1572872 | tf_op jit(solution)/shard_map/ppermute | solution.py:335
  354.0 89.9 %collective-permute-start.34 = (bf16[16,2,64,128]{3,2,1,0:T(8,128)(2,1)S(1)}, bf16[16,2,64,128]{3,2,1,0:T(8,128)(2,1)S(1)}, u32[]{:S(2)}, u32[]{:S(2)}) collective-permute-start(bf16[16,2,64,128]{3,2,1,0:T(8,128)(2,1)S(1)} %get-tuple-element.171), channel_id=1, source_target_pairs={{0,8},{4,12},{8,0},{12,4},{1,9},{5,13},{9,1},{13,5},{2,10},{6,14},... | collective-permute-start | bytes 1572872 | tf_op jit(solution)/shard_map/ppermute | solution.py:335
  367.6 76.3 %collective-permute-start.35 = (bf16[16,2,64,128]{3,2,1,0:T(8,128)(2,1)S(1)}, bf16[16,2,64,128]{3,2,1,0:T(8,128)(2,1)S(1)}, u32[]{:S(2)}, u32[]{:S(2)}) collective-permute-start(bf16[16,2,64,128]{3,2,1,0:T(8,128)(2,1)S(1)} %get-tuple-element.172), channel_id=1, source_target_pairs={{0,12},{4,0},{8,4},{12,8},{1,13},{5,1},{9,5},{13,9},{2,14},{6,2},{... | collective-permute-start | bytes 1572872 | tf_op jit(solution)/shard_map/ppermute | solution.py:335
  398.9 92.7 %collective-permute-start.37 = (bf16[16,2,64,128]{3,2,1,0:T(8,128)(2,1)S(1)}, bf16[16,2,64,128]{3,2,1,0:T(8,128)(2,1)S(1)}, u32[]{:S(2)}, u32[]{:S(2)}) collective-permute-start(bf16[16,2,64,128]{3,2,1,0:T(8,128)(2,1)S(1)} %get-tuple-element.178), channel_id=1, source_target_pairs={{0,8},{4,12},{8,0},{12,4},{1,9},{5,13},{9,1},{13,5},{2,10},{6,14},... | collective-permute-start | bytes 1572872 | tf_op jit(solution)/shard_map/ppermute | solution.py:335
  406.3 85.4 %collective-permute-start.38 = (bf16[16,2,64,128]{3,2,1,0:T(8,128)(2,1)S(1)}, bf16[16,2,64,128]{3,2,1,0:T(8,128)(2,1)S(1)}, u32[]{:S(2)}, u32[]{:S(2)}) collective-permute-start(bf16[16,2,64,128]{3,2,1,0:T(8,128)(2,1)S(1)} %get-tuple-element.179), channel_id=1, source_target_pairs={{0,12},{4,0},{8,4},{12,8},{1,13},{5,1},{9,5},{13,9},{2,14},{6,2},{... | collective-permute-start | bytes 1572872 | tf_op jit(solution)/shard_map/ppermute | solution.py:335
  443.9 89.9 %collective-permute-start.31 = (bf16[16,2,64,128]{3,2,1,0:T(8,128)(2,1)S(1)}, bf16[16,2,64,128]{3,2,1,0:T(8,128)(2,1)S(1)}, u32[]{:S(2)}, u32[]{:S(2)}) collective-permute-start(bf16[16,2,64,128]{3,2,1,0:T(8,128)(2,1)S(1)} %get-tuple-element.167), channel_id=1, source_target_pairs={{0,8},{4,12},{8,0},{12,4},{1,9},{5,13},{9,1},{13,5},{2,10},{6,14},... | collective-permute-start | bytes 1572872 | tf_op jit(solution)/shard_map/ppermute | solution.py:335
  443.9 89.9 %collective-permute-start.32 = (bf16[16,2,64,128]{3,2,1,0:T(8,128)(2,1)S(1)}, bf16[16,2,64,128]{3,2,1,0:T(8,128)(2,1)S(1)}, u32[]{:S(2)}, u32[]{:S(2)}) collective-permute-start(bf16[16,2,64,128]{3,2,1,0:T(8,128)(2,1)S(1)} %get-tuple-element.168), channel_id=1, source_target_pairs={{0,12},{4,0},{8,4},{12,8},{1,13},{5,1},{9,5},{13,9},{2,14},{6,2},{... | collective-permute-start | bytes 1572872 | tf_op jit(solution)/shard_map/ppermute | solution.py:335
  491.7 87.0 %collective-permute-start.46 = (bf16[16,2,64,128]{3,2,1,0:T(8,128)(2,1)S(1)}, bf16[16,2,64,128]{3,2,1,0:T(8,128)(2,1)S(1)}, u32[]{:S(2)}, u32[]{:S(2)}) collective-permute-start(bf16[16,2,64,128]{3,2,1,0:T(8,128)(2,1)S(1)} %get-tuple-element.195), channel_id=1, source_target_pairs={{0,8},{4,12},{8,0},{12,4},{1,9},{5,13},{9,1},{13,5},{2,10},{6,14},... | collective-permute-start | bytes 1572872 | tf_op jit(solution)/shard_map/ppermute | solution.py:335
  493.1 85.6 %collective-permute-start.47 = (bf16[16,2,64,128]{3,2,1,0:T(8,128)(2,1)S(1)}, bf16[16,2,64,128]{3,2,1,0:T(8,128)(2,1)S(1)}, u32[]{:S(2)}, u32[]{:S(2)}) collective-permute-start(bf16[16,2,64,128]{3,2,1,0:T(8,128)(2,1)S(1)} %get-tuple-element.196), channel_id=1, source_target_pairs={{0,12},{4,0},{8,4},{12,8},{1,13},{5,1},{9,5},{13,9},{2,14},{6,2},{... | collective-permute-start | bytes 1572872 | tf_op jit(solution)/shard_map/ppermute | solution.py:335
  533.8 89.9 %collective-permute-start.43 = (bf16[16,2,64,128]{3,2,1,0:T(8,128)(2,1)S(1)}, bf16[16,2,64,128]{3,2,1,0:T(8,128)(2,1)S(1)}, u32[]{:S(2)}, u32[]{:S(2)}) collective-permute-start(bf16[16,2,64,128]{3,2,1,0:T(8,128)(2,1)S(1)} %get-tuple-element.190), channel_id=1, source_target_pairs={{0,8},{4,12},{8,0},{12,4},{1,9},{5,13},{9,1},{13,5},{2,10},{6,14},... | collective-permute-start | bytes 1572872 | tf_op jit(solution)/shard_map/ppermute | solution.py:335
  547.4 76.3 %collective-permute-start.44 = (bf16[16,2,64,128]{3,2,1,0:T(8,128)(2,1)S(1)}, bf16[16,2,64,128]{3,2,1,0:T(8,128)(2,1)S(1)}, u32[]{:S(2)}, u32[]{:S(2)}) collective-permute-start(bf16[16,2,64,128]{3,2,1,0:T(8,128)(2,1)S(1)} %get-tuple-element.191), channel_id=1, source_target_pairs={{0,12},{4,0},{8,4},{12,8},{1,13},{5,1},{9,5},{13,9},{2,14},{6,2},{... | collective-permute-start | bytes 1572872 | tf_op jit(solution)/shard_map/ppermute | solution.py:335
  578.7 89.9 %collective-permute-start.40 = (bf16[16,2,64,128]{3,2,1,0:T(8,128)(2,1)S(1)}, bf16[16,2,64,128]{3,2,1,0:T(8,128)(2,1)S(1)}, u32[]{:S(2)}, u32[]{:S(2)}) collective-permute-start(bf16[16,2,64,128]{3,2,1,0:T(8,128)(2,1)S(1)} %get-tuple-element.186), channel_id=1, source_target_pairs={{0,8},{4,12},{8,0},{12,4},{1,9},{5,13},{9,1},{13,5},{2,10},{6,14},... | collective-permute-start | bytes 1572872 | tf_op jit(solution)/shard_map/ppermute | solution.py:335
  586.0 82.6 %collective-permute-start.41 = (bf16[16,2,64,128]{3,2,1,0:T(8,128)(2,1)S(1)}, bf16[16,2,64,128]{3,2,1,0:T(8,128)(2,1)S(1)}, u32[]{:S(2)}, u32[]{:S(2)}) collective-permute-start(bf16[16,2,64,128]{3,2,1,0:T(8,128)(2,1)S(1)} %get-tuple-element.187), channel_id=1, source_target_pairs={{0,12},{4,0},{8,4},{12,8},{1,13},{5,1},{9,5},{13,9},{2,14},{6,2},{... | collective-permute-start | bytes 1572872 | tf_op jit(solution)/shard_map/ppermute | solution.py:335
  623.7 70.6 %collective-permute-start.55 = (bf16[16,2,64,128]{3,2,1,0:T(8,128)(2,1)S(1)}, bf16[16,2,64,128]{3,2,1,0:T(8,128)(2,1)S(1)}, u32[]{:S(2)}, u32[]{:S(2)}) collective-permute-start(bf16[16,2,64,128]{3,2,1,0:T(8,128)(2,1)S(1)} %get-tuple-element.210), channel_id=1, source_target_pairs={{0,8},{4,12},{8,0},{12,4},{1,9},{5,13},{9,1},{13,5},{2,10},{6,14},... | collective-permute-start | bytes 1572872 | tf_op jit(solution)/shard_map/ppermute | solution.py:335
  630.5 63.7 %collective-permute-start.56 = (bf16[16,2,64,128]{3,2,1,0:T(8,128)(2,1)S(1)}, bf16[16,2,64,128]{3,2,1,0:T(8,128)(2,1)S(1)}, u32[]{:S(2)}, u32[]{:S(2)}) collective-permute-start(bf16[16,2,64,128]{3,2,1,0:T(8,128)(2,1)S(1)} %get-tuple-element.211), channel_id=1, source_target_pairs={{0,12},{4,0},{8,4},{12,8},{1,13},{5,1},{9,5},{13,9},{2,14},{6,2},{... | collective-permute-start | bytes 1572872 | tf_op jit(solution)/shard_map/ppermute | solution.py:335
  (39 other events, 1343.9 us)
